TPU v7x, 32 devices: a whole 2x2x4 slice. The times are simulated.
32 devices in a mesh: dp: 4 (over y, x), row: 2 (over core), col: 4 (over z).
Axes of the slice: x: 2, y: 2, z: 4, core: 2. Of those that a mesh axis runs over, the one named last changes fastest.
Arguments:
- tokens: bfloat16 [16384, 2048], P(('dp', 'col'), 'row'), may hold values from -76 to 76
- gain_attn: float32 [2048], P('row'), may hold values from 0.25 to 1.75
- gain_ffn: float32 [2048], P('row'), may hold values from 0.25 to 1.75
- w_query: bfloat16 [2048, 2048], P('row', 'col'), may hold values from -0.125 to 0.125
- w_key: bfloat16 [2048, 2048], P('row', 'col'), may hold values from -0.125 to 0.125
- w_value: bfloat16 [2048, 2048], P('row', 'col'), may hold values from -0.125 to 0.125
- w_out: bfloat16 [2048, 2048], P('col', 'row'), may hold values from -0.5 to 0.5
- w_gate: bfloat16 [2048, 8192], P('row', 'col'), may hold values from -0.125 to 0.125
- w_up: bfloat16 [2048, 8192], P('row', 'col'), may hold values from -0.125 to 0.125
- w_down: bfloat16 [8192, 2048], P('col', 'row'), may hold values from -0.0625 to 0.0625
- cotangent: bfloat16 [16384, 2048], P(('dp', 'col'), 'row'), may hold values from -76 to 76
Outputs:
- mixed: bfloat16 [16384, 2048], P(('dp', 'col'), 'row')
- input_grad: float32 [16384, 2048], P(('dp', 'col'), 'row')
- gain_attn_grad: float32 [2048], P('row')
- gain_ffn_grad: float32 [2048], P('row')
- w_query_grad: float32 [2048, 2048], P('row', 'col')
- w_key_grad: float32 [2048, 2048], P('row', 'col')
- w_value_grad: float32 [2048, 2048], P('row', 'col')
- w_out_grad: float32 [2048, 2048], P('col', 'row')
- w_gate_grad: float32 [2048, 8192], P('row', 'col')
- w_up_grad: float32 [2048, 8192], P('row', 'col')
- w_down_grad: float32 [8192, 2048], P('col', 'row')
All inputs are finite; a program needn't handle non-finite values.
Results may differ from a plain program's by a relative error of at most 0.012.
Values may be sent and summed in bfloat16 or wider, within the bound.
No kernel may reach another device: no remote copies, remote signals or barrier semaphores. Data moves between devices by JAX's collectives and lax.ppermute only.
A program may use at most 384 MiB of HBM per device.

v0:
```python
import jax
import jax.numpy as jnp
from jax import lax
from jax.sharding import PartitionSpec as P

D = 2048
HEAD_DIM = 64
SEQ_LEN = 1024


eps_norm = 1e-05
rope_base = 130000.0


def row_total(values):
    return lax.psum(values, "row")


def spread_cols(values):
    return lax.all_gather(values, "col", axis=0, tiled=True)


def column_sum(operands):
    summed = None
    for left_side, weight, inner_dim in operands:
        product = lax.dot_general(
            left_side, weight, (((1,), (inner_dim,)), ((), ())), preferred_element_type=jnp.float32
        )
        summed = product if summed is None else summed + product
    return lax.psum_scatter(summed, "col", scatter_dimension=0, tiled=True)


def norm_scale(stream):
    squares = row_total(jnp.sum(stream * stream, axis=1))
    return lax.rsqrt(squares / D + eps_norm)[:, None]


def norm_back(stream, scale, gain, upstream):
    weighted = upstream * gain
    inner_sum = row_total(jnp.sum(weighted * stream, axis=1))[:, None]
    back_grad = scale * weighted - stream * (scale * scale * scale) * (inner_sum / D)
    gain_part = jnp.sum(upstream * stream * scale, axis=0)
    return (back_grad, gain_part)


def rotation_tables():
    half_dim = HEAD_DIM // 2
    frequency = jnp.exp(
        -jnp.log(rope_base) * jnp.arange(half_dim, dtype=jnp.float32) * (2.0 / HEAD_DIM)
    )
    angles = jnp.arange(SEQ_LEN, dtype=jnp.float32)[:, None] * frequency[None, :]
    return (jnp.cos(angles)[:, None, :], jnp.sin(angles)[:, None, :])


def rotate(values, cosine, sine_table):
    half_dim = values.shape[-1] // 2
    first_half = values[..., :half_dim]
    second = values[..., half_dim:]
    return jnp.concatenate(
        (first_half * cosine - second * sine_table, second * cosine + first_half * sine_table),
        axis=-1,
    )


def contract_rows(left_side, right_side):
    return lax.dot_general(
        left_side, right_side, (((0,), (0,)), ((), ())), preferred_element_type=jnp.float32
    )


def on_device(
    tokens, gain_attn, gain_ffn, w_query, w_key, w_value, w_out, w_gate, w_up, w_down, cotangent
):
    local_rows = tokens.shape[0]
    group_rows = local_rows * lax.axis_size("col")
    head_rows = group_rows // lax.axis_size("row")
    width_heads = w_query.shape[1]
    hidden_width = w_gate.shape[1]
    seq_count = head_rows // SEQ_LEN
    score_scale = HEAD_DIM ** (-0.5)
    cosine, sine_table = rotation_tables()
    places = jnp.arange(SEQ_LEN)
    causal = places[:, None] >= places[None, :]

    def to_heads(flat):
        return flat.reshape(seq_count, SEQ_LEN, width_heads // HEAD_DIM, HEAD_DIM)

    stream = tokens.astype(jnp.float32)
    scale_attn = norm_scale(stream)
    normed = (stream * scale_attn * gain_attn).astype(jnp.bfloat16)
    normed_all = spread_cols(normed)
    w_joined = jnp.concatenate((w_query, w_key, w_value), axis=1)
    row_block = normed_all
    joined = lax.psum_scatter(
        jnp.dot(row_block, w_joined, preferred_element_type=jnp.float32),
        "row",
        scatter_dimension=0,
        tiled=True,
    )
    queries = rotate(to_heads(joined[:, :width_heads]), cosine, sine_table).astype(jnp.bfloat16)
    key_rows = rotate(
        to_heads(joined[:, width_heads : 2 * width_heads]), cosine, sine_table
    ).astype(jnp.bfloat16)
    values = to_heads(joined[:, 2 * width_heads :]).astype(jnp.bfloat16)

    def attend_forward(sequence):
        block_queries, block_keys, block_values = sequence
        scores = (
            jnp.einsum(
                "qhd,khd->hqk", block_queries, block_keys, preferred_element_type=jnp.float32
            )
            * score_scale
        )
        scores = jnp.where(causal[None], scores, -1e30)
        row_max = jnp.max(scores, axis=-1, keepdims=True)
        exponent = jnp.exp(scores - row_max)
        row_sums = jnp.sum(exponent, axis=-1, keepdims=True)
        weights = (exponent / row_sums).astype(jnp.bfloat16)
        log_totals = row_max[..., 0] + jnp.log(row_sums[..., 0])
        result = jnp.einsum(
            "hqk,khd->qhd", weights, block_values, preferred_element_type=jnp.float32
        )
        return (result, log_totals)

    attended, log_totals = lax.map(attend_forward, (queries, key_rows, values))
    attended = attended.reshape(head_rows, width_heads).astype(jnp.bfloat16)
    attended_all = lax.all_gather(attended, "row", axis=0, tiled=True)
    row_block = attended_all
    attn_branch = lax.psum_scatter(
        jnp.dot(row_block, w_out, preferred_element_type=jnp.float32),
        "col",
        scatter_dimension=0,
        tiled=True,
    )
    residual = stream + attn_branch
    scale_ffn = norm_scale(residual)
    normed_ffn = (residual * scale_ffn * gain_ffn).astype(jnp.bfloat16)
    normed_ffn_all = spread_cols(normed_ffn)
    w_gate_up = jnp.concatenate((w_gate, w_up), axis=1)
    row_block = normed_ffn_all
    gate_up = lax.psum_scatter(
        jnp.dot(row_block, w_gate_up, preferred_element_type=jnp.float32),
        "row",
        scatter_dimension=0,
        tiled=True,
    )
    gate_rows = gate_up[:, :hidden_width]
    up_rows = gate_up[:, hidden_width:]
    sigmoid_gate = jax.nn.sigmoid(gate_rows)
    activated = gate_rows * sigmoid_gate
    hidden = (activated * up_rows).astype(jnp.bfloat16)
    hidden_all = lax.all_gather(hidden, "row", axis=0, tiled=True)
    ffn_branch = column_sum(((hidden_all, w_down, 0),))
    mixed = (residual + ffn_branch).astype(jnp.bfloat16)
    grad_all = spread_cols(cotangent)
    row_block = grad_all
    grad_hidden = lax.psum_scatter(
        lax.dot_general(
            row_block, w_down, (((1,), (1,)), ((), ())), preferred_element_type=jnp.float32
        ),
        "row",
        scatter_dimension=0,
        tiled=True,
    )
    w_down_grad = contract_rows(hidden_all, grad_all)
    grad_gate = (
        grad_hidden * up_rows * sigmoid_gate * (1.0 + gate_rows * (1.0 - sigmoid_gate))
    ).astype(jnp.bfloat16)
    grad_up = (grad_hidden * activated).astype(jnp.bfloat16)
    grad_gate_all, grad_up_all = (
        lax.all_gather(grad_gate, "row", axis=0, tiled=True),
        lax.all_gather(grad_up, "row", axis=0, tiled=True),
    )
    w_gate_grad = contract_rows(normed_ffn_all, grad_gate_all)
    w_up_grad = contract_rows(normed_ffn_all, grad_up_all)
    grad_normed_ffn = column_sum(((grad_gate_all, w_gate, 1), (grad_up_all, w_up, 1)))
    back_ffn, gain_ffn_part = norm_back(residual, scale_ffn, gain_ffn, grad_normed_ffn)
    grad_residual = cotangent.astype(jnp.float32) + back_ffn
    grad_resid_all = spread_cols(grad_residual.astype(jnp.bfloat16))
    w_out_grad = contract_rows(attended_all, grad_resid_all)
    row_block = grad_resid_all
    grad_attended = lax.psum_scatter(
        lax.dot_general(
            row_block, w_out, (((1,), (1,)), ((), ())), preferred_element_type=jnp.float32
        ),
        "row",
        scatter_dimension=0,
        tiled=True,
    ).astype(jnp.bfloat16)

    def attend_backward(sequence):
        block_queries, block_keys, block_values, block_grad, block_logs = sequence
        scores = (
            jnp.einsum(
                "qhd,khd->hqk", block_queries, block_keys, preferred_element_type=jnp.float32
            )
            * score_scale
        )
        weights = jnp.where(causal[None], jnp.exp(scores - block_logs[..., None]), 0.0)
        grad_weights = jnp.einsum(
            "qhd,khd->hqk", block_grad, block_values, preferred_element_type=jnp.float32
        )
        delta_sum = jnp.sum(weights * grad_weights, axis=-1, keepdims=True)
        grad_scores = (weights * (grad_weights - delta_sum)).astype(jnp.bfloat16)
        grad_queries = (
            jnp.einsum("hqk,khd->qhd", grad_scores, block_keys, preferred_element_type=jnp.float32)
            * score_scale
        )
        grad_keys = (
            jnp.einsum(
                "hqk,qhd->khd", grad_scores, block_queries, preferred_element_type=jnp.float32
            )
            * score_scale
        )
        grad_values = jnp.einsum(
            "hqk,qhd->khd",
            weights.astype(jnp.bfloat16),
            block_grad,
            preferred_element_type=jnp.float32,
        )
        return (grad_queries, grad_keys, grad_values)

    grad_queries, grad_keys, grad_values = lax.map(
        attend_backward, (queries, key_rows, values, to_heads(grad_attended), log_totals)
    )
    grad_queries = (
        rotate(grad_queries, cosine, -sine_table)
        .reshape(head_rows, width_heads)
        .astype(jnp.bfloat16)
    )
    grad_keys = (
        rotate(grad_keys, cosine, -sine_table).reshape(head_rows, width_heads).astype(jnp.bfloat16)
    )
    grad_values = grad_values.reshape(head_rows, width_heads).astype(jnp.bfloat16)
    grad_q_all, grad_k_all, grad_v_all = (
        lax.all_gather(grad_queries, "row", axis=0, tiled=True),
        lax.all_gather(grad_keys, "row", axis=0, tiled=True),
        lax.all_gather(grad_values, "row", axis=0, tiled=True),
    )
    w_query_grad = contract_rows(normed_all, grad_q_all)
    w_key_grad = contract_rows(normed_all, grad_k_all)
    w_value_grad = contract_rows(normed_all, grad_v_all)
    grad_normed = column_sum(
        ((grad_q_all, w_query, 1), (grad_k_all, w_key, 1), (grad_v_all, w_value, 1))
    )
    back_attn, gain_attn_part = norm_back(stream, scale_attn, gain_attn, grad_normed)
    input_grad = grad_residual + back_attn
    gain_attn_grad, gain_ffn_grad = lax.psum((gain_attn_part, gain_ffn_part), ("dp", "col"))
    summed = lax.psum(
        (w_query_grad, w_key_grad, w_value_grad, w_out_grad, w_gate_grad, w_up_grad, w_down_grad),
        "dp",
    )
    return (
        mixed,
        input_grad,
        gain_attn_grad,
        gain_ffn_grad,
        summed[0],
        summed[1],
        summed[2],
        summed[3],
        summed[4],
        summed[5],
        summed[6],
    )


def solution(mesh):
    placed = (
        P(("dp", "col"), "row"),
        P("row"),
        P("row"),
        P("row", "col"),
        P("row", "col"),
        P("row", "col"),
        P("col", "row"),
        P("row", "col"),
        P("row", "col"),
        P("col", "row"),
        P(("dp", "col"), "row"),
    )
    return jax.shard_map(
        on_device,
        mesh=mesh,
        in_specs=placed,
        out_specs=(
            P(("dp", "col"), "row"),
            P(("dp", "col"), "row"),
            P("row"),
            P("row"),
            P("row", "col"),
            P("row", "col"),
            P("row", "col"),
            P("col", "row"),
            P("row", "col"),
            P("row", "col"),
            P("col", "row"),
        ),
        check_vma=False,
    )
```

profile of v0, /device:TPU:0, one launch (start us, length us, event | category | flops | bytes accessed | tf_op | source)
XLA Modules:
  0.0 3369.5 jit_solution(15705374965132607509)
XLA Ops:
  16.8 152.3 %all-gather.12.cloned.1.call-done = bf16[4096,1024]{1,0:T(8,128)(2,1)} async-done(((bf16[1024,1024]{1,0:T(8,128)(2,1)}), bf16[4096,1024]{1,0:T(8,128)(2,1)}) %all-gather.12.cloned.1.call-update) | async-done | bytes 8388624 | tf_op jit(solution)/shard_map/all_gather | solution.py:20
  169.1 20.5 fusion.61
  191.2 32.3 reduce-scatter.9.cloned.1.call-done
  286.7 90.4 %while.28 = (s32[]{:T(128)}, bf16[2,1024,8,64]{1,3,2,0:T(8,128)(2,1)}, f32[2,8,1024]{2,1,0:T(8,128)S(1)}, bf16[2,1024,8,64]{1,3,2,0:T(8,128)(2,1)}, bf16[2,1024,...) while((s32[]{:T(128)}, bf16[2,1024,8,64]{1,3,2,0:T(8,128)(2,1)}, ...), condition=%wide.region_6.7_spmd.clone, body=%wide.region_3.6_spmd.clone.sunk | while | flops 2249187328 | bytes 118753392 | solution.py:125
  287.6 14.8 fusion.137
  302.4 14.3 fusion.138
  316.8 15.4 bitcast_dynamic-update-slice_fusion.6
  332.5 14.8 fusion.137
  347.3 14.3 fusion.138
  361.7 15.4 bitcast_dynamic-update-slice_fusion.6
  383.6 14.9 all-gather.14.cloned.1.call-done
  409.8 280.8 %reduce-scatter.11.cloned.1.call-done = f32[1024,1024]{1,0:T(8,128)} async-done(((f32[4096,1024]{1,0:T(8,128)}), f32[1024,1024]{1,0:T(8,128)}) %reduce-scatter.11.cloned.1.call-update) | async-done | bytes 4194320 | tf_op jit(solution)/shard_map/reduce_scatter | solution.py:129
  703.5 139.0 %all-gather.20.cloned.1.call-done = bf16[4096,1024]{1,0:T(8,128)(2,1)} async-done(((bf16[1024,1024]{1,0:T(8,128)(2,1)}), bf16[4096,1024]{1,0:T(8,128)(2,1)}) %all-gather.20.cloned.1.call-update) | async-done | bytes 8388624 | tf_op jit(solution)/shard_map/all_gather | solution.py:20
  842.5 25.2 fusion.76
  867.8 124.7 %all-gather.16.cloned.1.call-done = bf16[4096,1024]{1,0:T(8,128)(2,1)} async-done(((bf16[1024,1024]{1,0:T(8,128)(2,1)}), bf16[4096,1024]{1,0:T(8,128)(2,1)}) %all-gather.16.cloned.1.call-update) | async-done | bytes 8388624 | tf_op jit(solution)/shard_map/all_gather | solution.py:20
  992.5 49.0 %fusion.48 = f32[4096,4096]{1,0:T(8,128)} fusion(bf16[4096,1024]{1,0:T(8,128)(2,1)} %all-gather.16.cloned.1.call-done, bf16[1024,2048]{1,0:T(8,128)(2,1)} %param.23, bf16[1024,2048]{1,0:T(8,128)(2,1)} %param.22), kind=kOutput, calls=%fused_computation.69 | convolution fusion | flops 34376515584 | bytes 83886080 | tf_op jit(solution)/shard_map/dot_general | solution.py:142
  1041.5 83.3 %reduce-scatter.13.cloned.1.call-done = f32[2048,4096]{1,0:T(8,128)} async-done(((f32[4096,4096]{1,0:T(8,128)}), f32[2048,4096]{1,0:T(8,128)}) %reduce-scatter.13.cloned.1.call-update) | async-done | bytes 33554448 | tf_op jit(solution)/shard_map/reduce_scatter | solution.py:141
  1124.8 27.9 multiply_convert_fusion.1
  1154.6 29.6 all-gather.22.cloned.1.call-done
  1184.2 24.6 fusion.77
  1217.5 30.5 convolution_add_fusion
  1251.0 23.4 fusion.75
  1274.7 260.2 %reduce-scatter.19.cloned.1.call-done = f32[1024,1024]{1,0:T(8,128)} async-done(((f32[4096,1024]{1,0:T(8,128)}), f32[1024,1024]{1,0:T(8,128)}) %reduce-scatter.19.cloned.1.call-update) | async-done | bytes 4194320 | tf_op jit(solution)/shard_map/reduce_scatter | solution.py:30
  1542.4 275.9 %reduce-scatter.15.cloned.1.call-done = f32[1024,1024]{1,0:T(8,128)} async-done(((f32[4096,1024]{1,0:T(8,128)}), f32[1024,1024]{1,0:T(8,128)}) %reduce-scatter.15.cloned.1.call-update) | async-done | bytes 4194320 | tf_op jit(solution)/shard_map/reduce_scatter | solution.py:30
  1825.7 150.5 %all-gather.26.cloned.1.call-done = bf16[4096,1024]{1,0:T(8,128)(2,1)} async-done(((bf16[1024,1024]{1,0:T(8,128)(2,1)}), bf16[4096,1024]{1,0:T(8,128)(2,1)}) %all-gather.26.cloned.1.call-update) | async-done | bytes 8388624 | tf_op jit(solution)/shard_map/all_gather | solution.py:20
  1986.5 15.1 reduce-scatter.21.cloned.1.call-done
  2014.9 365.4 %while.29 = (s32[]{:T(128)}, f32[2,1024,8,64]{1,0,3,2:T(2,128)}, f32[2,1024,8,64]{1,0,3,2:T(2,128)}, bf16[2,1024,8,64]{1,3,2,0:T(8,128)(2,1)}, bf16[2,1024,8,64]...) while((s32[]{:T(128)}, f32[2,1024,8,64]{1,0,3,2:T(2,128)}, ...), condition=%wide.region_19.20_spmd.clone, body=%wide.region_17.19_spmd.clone.sunk | while | flops 5496627200 | bytes 311660224 | solution.py:223
  2015.3 14.6 fusion.147
  2030.2 23.5 multiply_reduce_fusion.5
  2053.7 28.2 multiply_convert_fusion.6
  2081.9 12.3 multiply_bitcast_fusion.5
  2097.9 36.6 %dynamic_update_slice.34 = f32[2,1024,8,64]{1,0,3,2:T(2,128)} dynamic-update-slice(f32[2,1024,8,64]{1,0,3,2:T(2,128)} %get-tuple-element.384, f32[1,1024,8,64]{1,0,3,2:T(1,128)S(1)} %copy.79, s32[]{:T(128)} %get-tuple-element.382, s32[]{:T(128)} %constant.55.clone.1..sunk, s32[]{:T(128)} %constant.55.clone.1..sunk, s32[]{:T(128)} %constant.55.clone.1..sunk) | dynamic-update-slice | bytes 4194308 | tf_op jit(solution)/shard_map/while/body/jit(dynamic_update_index_in_dim)/dynamic_update_slice | solution.py:125
  2145.8 36.6 %dynamic_update_slice.33 = f32[2,1024,8,64]{1,0,3,2:T(2,128)} dynamic-update-slice(f32[2,1024,8,64]{1,0,3,2:T(2,128)} %get-tuple-element.383, f32[1,1024,8,64]{1,0,3,2:T(1,128)S(1)} %copy.78, s32[]{:T(128)} %get-tuple-element.382, s32[]{:T(128)} %constant.55.clone.1..sunk, s32[]{:T(128)} %constant.55.clone.1..sunk, s32[]{:T(128)} %constant.55.clone.1..sunk) | dynamic-update-slice | bytes 4194308 | tf_op jit(solution)/shard_map/while/body/jit(dynamic_update_index_in_dim)/dynamic_update_slice | solution.py:125
  2182.4 15.4 bitcast_dynamic-update-slice_fusion.8
  2197.7 14.6 fusion.147
  2212.6 23.5 multiply_reduce_fusion.5
  2236.2 28.2 multiply_convert_fusion.6
  2264.3 12.3 multiply_bitcast_fusion.5
  2280.4 36.6 %dynamic_update_slice.34 = f32[2,1024,8,64]{1,0,3,2:T(2,128)} dynamic-update-slice(f32[2,1024,8,64]{1,0,3,2:T(2,128)} %get-tuple-element.384, f32[1,1024,8,64]{1,0,3,2:T(1,128)S(1)} %copy.79, s32[]{:T(128)} %get-tuple-element.382, s32[]{:T(128)} %constant.55.clone.1..sunk, s32[]{:T(128)} %constant.55.clone.1..sunk, s32[]{:T(128)} %constant.55.clone.1..sunk) | dynamic-update-slice | bytes 4194308 | tf_op jit(solution)/shard_map/while/body/jit(dynamic_update_index_in_dim)/dynamic_update_slice | solution.py:125
  2328.2 36.6 %dynamic_update_slice.33 = f32[2,1024,8,64]{1,0,3,2:T(2,128)} dynamic-update-slice(f32[2,1024,8,64]{1,0,3,2:T(2,128)} %get-tuple-element.383, f32[1,1024,8,64]{1,0,3,2:T(1,128)S(1)} %copy.78, s32[]{:T(128)} %get-tuple-element.382, s32[]{:T(128)} %constant.55.clone.1..sunk, s32[]{:T(128)} %constant.55.clone.1..sunk, s32[]{:T(128)} %constant.55.clone.1..sunk) | dynamic-update-slice | bytes 4194308 | tf_op jit(solution)/shard_map/while/body/jit(dynamic_update_index_in_dim)/dynamic_update_slice | solution.py:125
  2364.8 15.4 bitcast_dynamic-update-slice_fusion.8
  2440.3 20.4 add_add_fusion
  2460.8 24.5 fusion.85
  2485.4 24.4 fusion.86
  2509.8 24.8 fusion.87
  2561.1 181.3 %reduce-scatter.23.cloned.1.call-done = f32[1024,1024]{1,0:T(8,128)} async-done(((f32[4096,1024]{1,0:T(8,128)}), f32[1024,1024]{1,0:T(8,128)}) %reduce-scatter.23.cloned.1.call-update) | async-done | bytes 4194320 | tf_op jit(solution)/shard_map/reduce_scatter | solution.py:30
  2748.4 43.6 %all-reduce = (f32[1024]{0:T(1024)}, f32[1024]{0:T(1024)}) all-reduce(f32[1024]{0:T(1024)S(1)} %get-tuple-element.174, f32[1024]{0:T(1024)S(1)} %copy-done.32), channel_id=1, replica_groups=mesh['dp'=4,'row'=2,'col'=4] {'dp','col'}, use_global_device_ids=true, to_apply=%region_24.25 | all-reduce | flops 2048 | bytes 16384 | tf_op jit(solution)/shard_map/psum | solution.py:248
  2797.4 540.6 %all-reduce.4.cloned.1.call-done = (f32[1024,512]{1,0:T(8,128)}, f32[1024,512]{1,0:T(8,128)}, f32[1024,512]{1,0:T(8,128)}, f32[512,1024]{1,0:T(8,128)}, f32[1024...) async-done(((f32[1024,512]{1,0:T(8,128)}, f32[1024,512]{1,0:T(8,128)}, f32[1024,512]{1,0:T(8,128)}, f32[512,1024]{1,0:T(8,128)}, f32[1024,2048]{1,0:T(8,128)}, ...) | async-done | bytes 33554448 | tf_op jit(solution)/shard_map/psum | solution.py:249
  (232 shorter events, 310.8 us)
Async XLA Ops:
  7.2 391.4 %copy-start = (bf16[512,1024]{1,0:T(8,128)(2,1)S(1)}, bf16[512,1024]{1,0:T(8,128)(2,1)}, u32[]{:S(2)}) copy-start(bf16[512,1024]{1,0:T(8,128)(2,1)} %param.21) | copy-start | bytes 3145732
  7.2 161.9 %copy-start.18 = (bf16[1024,512]{1,0:T(8,128)(2,1)S(1)}, bf16[1024,512]{1,0:T(8,128)(2,1)}, u32[]{:S(2)}) copy-start(bf16[1024,512]{1,0:T(8,128)(2,1)} %param.20) | copy-start | bytes 3145732
  7.2 161.9 %copy-start.36 = (bf16[1024,512]{1,0:T(8,128)(2,1)S(1)}, bf16[1024,512]{1,0:T(8,128)(2,1)}, u32[]{:S(2)}) copy-start(bf16[1024,512]{1,0:T(8,128)(2,1)} %param.19) | copy-start | bytes 3145732
  7.2 161.9 %all-gather.12.cloned.1.call-start = ((), (), s32[]{:S(2)}) async-start(), calls=%async_computation.8 | async-start | bytes 10485760 | tf_op jit(solution)/shard_map/all_gather | solution.py:20
  16.7 206.7 %reduce-scatter.9.cloned.1.call-start = ((), (), s32[]{:S(2)}) async-start(), calls=%async_computation.9 | async-start | bytes 37748736 | tf_op jit(solution)/shard_map/reduce_scatter | solution.py:94
  189.6 209.0 %all-gather.14.cloned.1.call-start = ((), (), s32[]{:S(2)}) async-start(), calls=%async_computation.10 | async-start | bytes 6291456 | tf_op jit(solution)/shard_map/all_gather | solution.py:127
  191.2 63.9 %copy-start.16 = (f32[1024,32]{0,1:T(8,128)}, f32[1024,32]{0,1:T(8,128)S(1)}, u32[]{:S(2)}) copy-start(f32[1024,32]{0,1:T(8,128)S(1)} %get-tuple-element.247) | copy-start | bytes 393220
  383.6 307.0 %reduce-scatter.11.cloned.1.call-start = ((), (), s32[]{:S(2)}) async-start(), calls=%async_computation.11 | async-start | bytes 20971520 | tf_op jit(solution)/shard_map/reduce_scatter | solution.py:129
  408.9 281.7 %copy-start.5 = (bf16[1024,1024]{1,0:T(8,128)(2,1)S(1)}, bf16[1024,1024]{1,0:T(8,128)(2,1)}, u32[]{:S(2)}) copy-start(bf16[1024,1024]{1,0:T(8,128)(2,1)} %param.15) | copy-start | bytes 6291460
  409.0 433.5 %all-gather.20.cloned.1.call-start = ((), (), s32[]{:S(2)}) async-start(), calls=%async_computation.16 | async-start | bytes 10485760 | tf_op jit(solution)/shard_map/all_gather | solution.py:20
  409.6 289.4 %copy-start.27 = (f32[1024]{0:T(1024)S(1)}, f32[1024]{0:T(1024)}, u32[]{:S(2)}) copy-start(f32[1024]{0:T(1024)} %param.17) | copy-start | bytes 12292
  409.6 582.9 %all-gather.16.cloned.1.call-start = ((), (), s32[]{:S(2)}) async-start(), calls=%async_computation.12 | async-start | bytes 10485760 | tf_op jit(solution)/shard_map/all_gather | solution.py:20
  703.5 338.1 %reduce-scatter.17.cloned.1.call-start = ((), (), s32[]{:S(2)}) async-start(), calls=%async_computation.17 | async-start | bytes 50331648 | tf_op jit(solution)/shard_map/reduce_scatter | solution.py:157
  867.7 257.1 %reduce-scatter.13.cloned.1.call-start = ((), (), s32[]{:S(2)}) async-start(), calls=%async_computation.13 | async-start | bytes 100663296 | tf_op jit(solution)/shard_map/reduce_scatter | solution.py:141
  1041.5 142.7 %all-gather.22.cloned.1.call-start = ((), (), s32[]{:S(2)}) async-start(), calls=%async_computation.18 | async-start | bytes 25165824 | tf_op jit(solution)/shard_map/all_gather | solution.py:171
  1152.8 64.7 %all-gather.24.cloned.1.call-start = ((), (), s32[]{:S(2)}) async-start(), calls=%async_computation.19 | async-start | bytes 25165824 | tf_op jit(solution)/shard_map/all_gather | solution.py:172
  1153.4 97.6 %all-gather.18.cloned.1.call-start = ((), (), s32[]{:S(2)}) async-start(), calls=%async_computation.14 | async-start | bytes 25165824 | tf_op jit(solution)/shard_map/all_gather | solution.py:152
  1154.1 380.7 %reduce-scatter.19.cloned.1.call-start = ((), (), s32[]{:S(2)}) async-start(), calls=%async_computation.20 | async-start | bytes 20971520 | tf_op jit(solution)/shard_map/reduce_scatter | solution.py:30
  1248.1 570.2 %reduce-scatter.15.cloned.1.call-start = ((), (), s32[]{:S(2)}) async-start(), calls=%async_computation.15 | async-start | bytes 20971520 | tf_op jit(solution)/shard_map/reduce_scatter | solution.py:30
  1274.4 260.4 %copy-start.24 = (f32[1024]{0:T(1024)S(1)}, f32[1024]{0:T(1024)}, u32[]{:S(2)}) copy-start(f32[1024]{0:T(1024)} %copy-done.23) | copy-start | bytes 12292
  1274.4 260.4 %copy-start.28 = (f32[1024]{0:T(1024)S(1)}, f32[1024]{0:T(1024)}, u32[]{:S(2)}) copy-start(f32[1024]{0:T(1024)} %param.17) | copy-start | bytes 12292
  1274.4 543.8 %copy-start.11 = (bf16[1024,1024]{1,0:T(8,128)(2,1)S(1)}, bf16[1024,1024]{1,0:T(8,128)(2,1)}, u32[]{:S(2)}) copy-start(bf16[1024,1024]{1,0:T(8,128)(2,1)} %param.25) | copy-start | bytes 6291460
  1274.4 543.8 %copy-start.31 = (f32[1024]{0:T(1024)S(1)}, f32[1024]{0:T(1024)}, u32[]{:S(2)}) copy-start(f32[1024]{0:T(1024)} %get-tuple-element.243) | copy-start | bytes 12292
  1274.4 701.8 %all-gather.26.cloned.1.call-start = ((), (), s32[]{:S(2)}) async-start(), calls=%async_computation.21 | async-start | bytes 10485760 | tf_op jit(solution)/shard_map/all_gather | solution.py:20
  1825.7 175.9 %reduce-scatter.21.cloned.1.call-start = ((), (), s32[]{:S(2)}) async-start(), calls=%async_computation.22 | async-start | bytes 12582912 | tf_op jit(solution)/shard_map/reduce_scatter | solution.py:182
  1986.4 420.2 %all-gather.30.cloned.1.call-start = ((), (), s32[]{:S(2)}) async-start(), calls=%async_computation.24 | async-start | bytes 6291456 | tf_op jit(solution)/shard_map/all_gather | solution.py:237
  2014.9 365.4 %copy-start.17 = (f32[1024,32]{0,1:T(8,128)S(1)}, f32[1024,32]{0,1:T(8,128)}, u32[]{:S(2)}) copy-start(f32[1024,32]{0,1:T(8,128)} %copy-done.16) | copy-start | bytes 393220
  2014.9 365.4 %copy-start.20 = (f32[1024,32]{0,1:T(8,128)S(1)}, f32[1024,32]{0,1:T(8,128)}, u32[]{:S(2)}) copy-start(f32[1024,32]{0,1:T(8,128)} %get-tuple-element.245) | copy-start | bytes 393220
  2182.4 15.4 copy-start.4
  2364.8 15.4 copy-start.4
  2391.5 31.9 all-gather.28.cloned.1.call-start
  2396.2 44.1 %all-gather.32.cloned.1.call-start = ((), (), s32[]{:S(2)}) async-start(), calls=%async_computation.25 | async-start | bytes 6291456 | tf_op jit(solution)/shard_map/all_gather | solution.py:238
  2400.4 23.0 copy-start.38
  2400.5 341.9 %reduce-scatter.23.cloned.1.call-start = ((), (), s32[]{:S(2)}) async-start(), calls=%async_computation.26 | async-start | bytes 20971520 | tf_op jit(solution)/shard_map/reduce_scatter | solution.py:30
  2417.7 22.6 copy-start.19
  2460.8 877.3 %all-reduce.4.cloned.1.call-start = ((), (), s32[]{:S(2)}) async-start(), calls=%async_computation.27 | async-start | bytes 67108864 | tf_op jit(solution)/shard_map/psum | solution.py:249
  2460.8 48.9 %slice-start.4 = ((s8[16777216]{0:T(1024)(128)(4,1)}), s8[4194304]{0:T(1024)(128)(4,1)S(1)}, s32[]{:S(2)}) async-start(s8[16777216]{0:T(1024)(128)(4,1)} %bitcast.163), calls=%async_computation.32 | async-start | bytes 8388608
  2460.8 48.9 %slice-start.5 = ((s8[16777216]{0:T(1024)(128)(4,1)}), s8[4194304]{0:T(1024)(128)(4,1)S(1)}, s32[]{:S(2)}) async-start(s8[16777216]{0:T(1024)(128)(4,1)} %bitcast.163), calls=%async_computation.33 | async-start | bytes 8388608
  2485.3 24.4 slice-start.6
  2485.3 24.4 slice-start.7
  2485.3 57.8 %slice-start.8 = ((s8[8388608]{0:T(1024)(128)(4,1)}), s8[4194304]{0:T(1024)(128)(4,1)S(1)}, s32[]{:S(2)}) async-start(s8[8388608]{0:T(1024)(128)(4,1)} %bitcast.165), calls=%async_computation.36 | async-start | bytes 8388608
  2509.7 24.9 copy-start.33
  2509.7 33.4 slice-start.9
  2561.0 181.4 %copy-start.6 = (bf16[1024,1024]{1,0:T(8,128)(2,1)S(1)}, bf16[1024,1024]{1,0:T(8,128)(2,1)}, u32[]{:S(2)}) copy-start(bf16[1024,1024]{1,0:T(8,128)(2,1)} %param.15) | copy-start | bytes 6291460
  2561.0 181.4 %copy-start.26 = (f32[1024]{0:T(1024)S(1)}, f32[1024]{0:T(1024)}, u32[]{:S(2)}) copy-start(f32[1024]{0:T(1024)} %copy-done.25) | copy-start | bytes 12292
  2561.0 181.4 %copy-start.29 = (f32[1024]{0:T(1024)S(1)}, f32[1024]{0:T(1024)}, u32[]{:S(2)}) copy-start(f32[1024]{0:T(1024)} %param.16) | copy-start | bytes 12292
  2561.0 187.3 %copy-start.32 = (f32[1024]{0:T(1024)S(1)}, f32[1024]{0:T(1024)}, u32[]{:S(2)}) copy-start(f32[1024]{0:T(1024)} %get-tuple-element.172) | copy-start | bytes 12292
  2561.1 231.0 %copy-start.30 = (f32[1024]{0:T(1024)S(1)}, f32[1024]{0:T(1024)}, u32[]{:S(2)}) copy-start(f32[1024]{0:T(1024)} %get-tuple-element.241) | copy-start | bytes 12292
  (25 other events, 197.8 us)
Sparse Core Ops, SparseCore 0:
  16.9 152.2 all-gather.11
  189.7 33.6 reduce-scatter.8
  383.7 14.8 all-gather.13
  409.1 281.4 reduce-scatter.10
  692.1 150.3 all-gather.19
  844.6 147.8 all-gather.15
  994.9 43.3 reduce-scatter.16
  1041.6 83.2 reduce-scatter.12
  1152.9 31.2 all-gather.21
  1186.2 31.2 all-gather.23
  1219.7 31.2 all-gather.17
  1253.3 281.4 reduce-scatter.18
  1537.2 281.0 reduce-scatter.14
  1825.8 150.3 all-gather.25
  1986.5 15.0 reduce-scatter.20
  2391.6 14.9 all-gather.29
  2408.6 14.8 all-gather.27
  2425.4 14.8 all-gather.31
  2460.9 281.4 reduce-scatter.22
  2748.8 589.1 all-reduce.3
where the time goes:
time: 3390 us; the launch traced here: 3370 us
  waiting for transfers between devices  2310 us (68%)
  matrix products  546 us (16%)
  local copies, waits for them, and re-layouts  260 us (8%)
  other arithmetic  179 us (5%)
  blocking collectives  53.6 us (2%)
    reduce_scatter x3, waiting for transfers between devices, column_sum(): return lax.psum_scatter(summed, 'col', scatter_dimension=0, tiled=True)  717 us
    all_gather x4, waiting for transfers between devices, spread_cols(): return lax.all_gather(values, 'col', axis=0, tiled=True)  566 us
    psum x1, waiting for transfers between devices, on_device(): lax.psum((w_query_grad, w_key_grad, w_value_grad, w_out_grad, w_gate_grad...  541 us
    reduce_scatter x1, waiting for transfers between devices, on_device(): lax.psum_scatter(jnp.dot(row_block, w_out, preferred_element_type=jnp.flo...  281 us
    dynamic_update_slice x8, local copies, waits for them, and re-layouts, on_device(): attended, log_totals = lax.map(attend_forward, (queries, key_rows, values))  158 us
    dot_general x6, matrix products, column_sum(): lax.dot_general(left_side, weight, (((1,), (inner_dim,)), ((), ())), pref...  121 us
    dot_general x7, matrix products, contract_rows(): lax.dot_general(left_side, right_side, (((0,), (0,)), ((), ())), preferre...  100 us
    reduce_scatter x1, waiting for transfers between devices, on_device(): lax.psum_scatter(jnp.dot(row_block, w_gate_up, preferred_element_type=jnp...  83.3 us
  transfers between devices with their start and end apart: 20, of which 19 were waited for; matrix products, arithmetic and copies ran while one was open for 9% of the time, Pallas kernels for 0%

commit v1 on v0

v1 whole, which is shorter than its diff:
```python
import jax
import jax.numpy as jnp
from jax import lax
from jax.experimental import pallas as pl
from jax.experimental.pallas import tpu as pltpu
from jax.sharding import PartitionSpec as P

D = 2048
HEAD_DIM = 64
SEQ_LEN = 1024
LANES = 128
EPS = 1e-05
ROPE_BASE = 130000.0
VMEM = 60 * 1024 * 1024
UNIT_TILE = 512
QB = 256
COST = 10**12
F32 = jnp.float32
BF16 = jnp.bfloat16


def dot(a, b, ca, cb):
    return lax.dot_general(a, b, (((ca,), (cb,)), ((), ())), preferred_element_type=F32)


def of(shape, dtype=BF16):
    return jax.ShapeDtypeStruct(tuple(shape), dtype)


class Line:
    waiting = []

    def __init__(self):
        self.last, self.marks = [], []

    def run(self, call, *values):
        Line.waiting = list(self.last)
        result = call(*values)
        self.last = jax.tree.leaves(result)[:1] + self.marks
        self.marks = []
        return result

    def tied(self, value):
        if not self.last:
            return value
        value, *self.last = lax.optimization_barrier((value, *self.last))
        return value

    def mix(self, call, first, *values):
        first = self.tied(first)
        result = call(first, *values)
        self.last = jax.tree.leaves(result)[:1] + list(self.last)
        return result

    def send(self, move, value):
        return move(self.tied(value))

    def ship(self, move, value):
        return move(value)

    def post(self, move, value):
        sent = move(value)
        mark = other_core(self.tied(self.stamp))
        self.run(short_kernel, self.stamp)
        self.last = self.last + [mark]
        return sent

    def swap(self, value):
        value = lax.all_to_all(self.tied(value), "row", split_axis=0, concat_axis=0, tiled=True)
        self.last = [value, *self.last]
        return value


def launch(kernel, arrays, in_specs, name, prefetch=(), **rest):
    held, Line.waiting = Line.waiting, []
    skip, count = len(held), len(prefetch) + len(arrays)

    def body(*refs):
        kernel(*refs[:count], *refs[count + skip :])

    in_specs = list(in_specs) + [pl.BlockSpec(memory_space=pl.ANY)] * skip
    out_shape = rest.pop("out_shape")
    if prefetch:
        layout = dict(
            grid_spec=pltpu.PrefetchScalarGridSpec(num_scalar_prefetch=len(prefetch), in_specs=in_specs, **rest)
        )
    else:
        layout = dict(in_specs=in_specs, **rest)
    return pl.pallas_call(
        body,
        out_shape=out_shape,
        compiler_params=pltpu.CompilerParams(vmem_limit_bytes=VMEM),
        cost_estimate=pl.CostEstimate(flops=COST, bytes_accessed=1, transcendentals=0),
        name=name,
        **layout,
    )(*prefetch, *arrays, *held)


def short_kernel(values):
    def kernel(in_ref, out_ref):
        out_ref[...] = in_ref[...]

    spec = pl.BlockSpec(values.shape, lambda: (0, 0))
    return launch(kernel, [values], [spec], "short", grid=(), out_specs=spec, out_shape=of(values.shape, values.dtype))


def extent(shape, index):
    sizes = []
    for size, at in zip(shape, index):
        if not isinstance(at, int):
            sizes.append(size if isinstance(at, slice) else at.size)
    return tuple(sizes)


def place(sources, outs, phases, where, name, kept=0):
    moves = [m for phase in phases for m in phase]
    shapes = [extent((sources[src] if src >= 0 else outs[-1 - src]).shape, src_at([0] * 8)) for src, src_at, _, _ in moves]
    count = len(sources)

    def kernel(where_ref, *refs):
        ins, out_refs, held = refs[:count], refs[count : count + len(outs)], refs[count + len(outs) : -2]
        in_sems, out_sems = refs[-2:]
        base = 0
        for phase in phases:
            loads, stores = [], []
            for n, (src, src_at, dst, dst_at) in enumerate(phase, base):
                src_ref = out_refs[-1 - src] if src < 0 else ins[src]
                loads.append(pltpu.make_async_copy(src_ref.at[src_at(where_ref)], held[n], in_sems.at[n]))
                stores.append(pltpu.make_async_copy(held[n], out_refs[dst].at[dst_at(where_ref)], out_sems.at[n]))
            for load in loads:
                load.start()
            for load, store in zip(loads, stores):
                load.wait()
                store.start()
            for store in stores:
                store.wait()
            base += len(phase)

    return launch(
        kernel,
        [where, *sources],
        [pl.BlockSpec(memory_space=pltpu.SMEM)] + [pl.BlockSpec(memory_space=pl.ANY)] * count,
        name,
        out_specs=[pl.BlockSpec(memory_space=pl.ANY)] * len(outs),
        out_shape=list(outs),
        scratch_shapes=[pltpu.VMEM(s, outs[m[2]].dtype) for s, m in zip(shapes, moves)] + [pltpu.SemaphoreType.DMA((len(moves),))] * 2,
        input_output_aliases={1 + count - kept + i: i for i in range(kept)},
    )


CORE, OTHER, QUARTER = 0, 1, 2


def full(_):
    return (slice(None), slice(None))


def rows_at(scalar, size, base=0):
    return lambda w: (pl.ds(pl.multiple_of(base + w[scalar] * size, size), size), slice(None))


def cols_at(scalar, size, lo=0, width=None):
    width = width or size
    return lambda w: (slice(None), pl.ds(pl.multiple_of(w[scalar] * size + lo, width), width))


def rows_span(scalar, size, lo, count):
    return lambda w: (pl.ds(pl.multiple_of(w[scalar] * size + lo, count), count), slice(None))


def rows_fixed(lo, count):
    return lambda w: (pl.ds(lo, count), slice(None))


def block_at(row_scalar, height, lo, width):
    return lambda w: (pl.ds(pl.multiple_of(w[row_scalar] * height, height), height), pl.ds(lo, width))


def rope_tables():
    half = HEAD_DIM // 2
    frequency = jnp.exp(-jnp.log(ROPE_BASE) * jnp.arange(half, dtype=F32) * (2.0 / HEAD_DIM))
    frequency = jnp.tile(frequency, 4)
    sign = jnp.where(jnp.arange(LANES) % HEAD_DIM < half, -1.0, 1.0)
    angles = jnp.arange(SEQ_LEN, dtype=F32)[:, None] * frequency[None, :]
    return jnp.cos(angles), jnp.sin(angles) * sign[None, :]


def swap_halves(values):
    half = HEAD_DIM // 2
    lane = lax.broadcasted_iota(jnp.int32, values.shape, 1)
    return jnp.where(lane % HEAD_DIM < half, pltpu.roll(values, LANES - half, 1), pltpu.roll(values, half, 1))


def qkv_kernel(first, x_ref, gain_ref, cos_ref, sin_ref, w_ref, *refs):
    q_ref, k_ref, v_ref = refs[-3:]
    if first:
        x = x_ref[...].astype(F32)
        scale = lax.rsqrt(jnp.sum(x * x, axis=1, keepdims=True) / D + EPS)
        refs[0][...] = (x * scale * gain_ref[...]).astype(BF16)
        normed = refs[0][...]
    else:
        normed = x_ref[...]
    cos, sin = cos_ref[...], sin_ref[...]
    width = q_ref.shape[1]
    projected = dot(normed, w_ref[...], 1, 0)
    for part, (out_ref, mult) in enumerate(((q_ref, HEAD_DIM**-0.5), (k_ref, 1.0))):
        for lo in range(0, width, LANES):
            piece = projected[:, part * width + lo : part * width + lo + LANES]
            out_ref[:, lo : lo + LANES] = ((piece * cos + swap_halves(piece) * sin).astype(BF16) * mult).astype(BF16)
    v_ref[...] = projected[:, 2 * width :].astype(BF16)


def project_qkv(x, gain, cos, sin, weight, first):
    rows, width = x.shape[0], weight.shape[1] // 3
    tile = min(512, rows)
    row_block = lambda n: pl.BlockSpec((tile, n), lambda i: (i, 0))
    whole = lambda a: pl.BlockSpec(a.shape, lambda i: (0, 0))
    outs = [D] * first + [width] * 3
    return launch(
        lambda *refs: qkv_kernel(first, *refs),
        [x, gain, cos, sin, weight],
        [row_block(D), whole(gain), row_block(LANES), row_block(LANES), whole(weight)],
        "qkv",
        grid=(rows // tile,),
        out_specs=[row_block(n) for n in outs],
        out_shape=[of((rows, n)) for n in outs],
    )


def head_of(values, head):
    lane = lax.broadcasted_iota(jnp.int32, values.shape, 1)
    return jnp.where((lane >= HEAD_DIM) == (head == 1), values, jnp.zeros_like(values))


def causal_scores(keys, queries, start):
    scores = dot(keys, queries, 1, 1)
    last = scores[start:]
    key_at = lax.broadcasted_iota(jnp.int32, last.shape, 0)
    query_at = lax.broadcasted_iota(jnp.int32, last.shape, 1)
    last = jnp.where(key_at <= query_at, last, -1e30)
    return last if start == 0 else jnp.concatenate((scores[:start], last), axis=0)


def attend_kernel(q_ref, k_ref, v_ref, o_ref, lse_ref):
    v_t = v_ref[...].T
    for start in range(0, SEQ_LEN, QB):
        stop = start + QB
        queries = q_ref[start:stop, :]
        outs = []
        for head in range(2):
            scores = causal_scores(k_ref[:stop, :], head_of(queries, head), start)
            top = jnp.max(scores, axis=0, keepdims=True)
            weights = jnp.exp(scores - top)
            total = jnp.sum(weights, axis=0, keepdims=True)
            lse_ref[0, 0, head : head + 1, start:stop] = top + jnp.log(total)
            out = dot(v_t[head * HEAD_DIM : (head + 1) * HEAD_DIM, :stop], weights.astype(BF16), 1, 0)
            outs.append(out / total)
        o_ref[start:stop, :] = jnp.concatenate(outs, axis=0).T.astype(BF16)


def attend(q, k, v):
    rows, width = q.shape
    seqs, pairs = rows // SEQ_LEN, width // LANES
    block = pl.BlockSpec((SEQ_LEN, LANES), lambda s, h: (s, h))
    return launch(
        attend_kernel,
        [q, k, v],
        [block] * 3,
        "attend",
        grid=(seqs, pairs),
        out_specs=[block, pl.BlockSpec((1, 1, 8, SEQ_LEN), lambda s, h: (s, h, 0, 0))],
        out_shape=[of((rows, width)), of((seqs, pairs, 8, SEQ_LEN), F32)],
    )


def attend_back_kernel(do_ref, q_ref, k_ref, v_ref, o_ref, lse_ref, cos_ref, sin_ref, dq_ref, dk_ref, dv_ref, dk_acc, dv_acc):
    k_t = k_ref[...].T
    dk_acc[...] = jnp.zeros_like(dk_acc)
    dv_acc[...] = jnp.zeros_like(dv_acc)
    for start in range(0, SEQ_LEN, QB):
        stop = start + QB
        queries, grads = q_ref[start:stop, :], do_ref[start:stop, :]
        inner = (grads.astype(F32) * o_ref[start:stop, :].astype(F32)).T
        back = []
        for head in range(2):
            one_q, one_g = head_of(queries, head), head_of(grads, head)
            scores = causal_scores(k_ref[:stop, :], one_q, start)
            weights = jnp.exp(scores - lse_ref[0, 0, head : head + 1, start:stop])
            grad_weights = dot(v_ref[:stop, :], one_g, 1, 1)
            delta = jnp.sum(inner[head * HEAD_DIM : (head + 1) * HEAD_DIM], axis=0, keepdims=True)
            grad_scores = (weights * (grad_weights - delta)).astype(BF16)
            dv_acc[:stop, :] += dot(weights.astype(BF16), one_g, 1, 0)
            dk_acc[:stop, :] += dot(grad_scores, one_q, 1, 0)
            back.append(dot(k_t[head * HEAD_DIM : (head + 1) * HEAD_DIM, :stop], grad_scores, 1, 0))
        dq = jnp.concatenate(back, axis=0).T * HEAD_DIM**-0.5
        cos, sin = cos_ref[start:stop, :], sin_ref[start:stop, :]
        dq_ref[start:stop, :] = (dq * cos - swap_halves(dq) * sin).astype(BF16)
    dk = dk_acc[...]
    dk_ref[...] = (dk * cos_ref[...] - swap_halves(dk) * sin_ref[...]).astype(BF16)
    dv_ref[...] = dv_acc[...].astype(BF16)


def attend_back(do, q, k, v, o, lse, cos, sin):
    rows, width = q.shape
    seqs, pairs = rows // SEQ_LEN, width // LANES
    block = pl.BlockSpec((SEQ_LEN, LANES), lambda s, h: (s, h))
    table = pl.BlockSpec((SEQ_LEN, LANES), lambda s, h: (0, 0))
    return launch(
        attend_back_kernel,
        [do, q, k, v, o, lse, cos, sin],
        [block] * 5 + [pl.BlockSpec((1, 1, 8, SEQ_LEN), lambda s, h: (s, h, 0, 0)), table, table],
        "attend_back",
        grid=(seqs, pairs),
        out_specs=[block] * 3,
        out_shape=[of((rows, width))] * 3,
        scratch_shapes=[pltpu.VMEM((SEQ_LEN, LANES), F32)] * 2,
    )


def ffn_kernel(nf_ref, cot_ref, wgu_ref, wd_ref, hidden_ref, ggu_ref):
    tile = wd_ref.shape[0]
    chunk = 256
    for lo in range(0, nf_ref.shape[0], chunk):
        rows = slice(lo, lo + chunk)
        both = dot(nf_ref[rows, :], wgu_ref[...], 1, 0)
        grad_hidden = dot(cot_ref[rows, :], wd_ref[...], 1, 1)
        gate, up = both[:, :tile], both[:, tile:]
        sig = jax.nn.sigmoid(gate)
        act = gate * sig
        hidden_ref[rows, :] = (act * up).astype(BF16)
        ggu_ref[rows, :tile] = (grad_hidden * up * (sig * (1.0 + gate * (1.0 - sig)))).astype(BF16)
        ggu_ref[rows, tile:] = (grad_hidden * act).astype(BF16)


def ffn(nf, cot, w_gu, w_down):
    rows, units = nf.shape[0], w_down.shape[0]
    tile = min(UNIT_TILE, units)
    whole = pl.BlockSpec((rows, D), lambda j: (0, 0))
    return launch(
        ffn_kernel,
        [nf, cot, w_gu, w_down],
        [
            whole,
            whole,
            pl.BlockSpec((D, 2 * tile), lambda j: (0, j)),
            pl.BlockSpec((tile, D), lambda j: (j, 0)),
        ],
        "ffn",
        grid=(units // tile,),
        out_specs=[pl.BlockSpec((rows, tile), lambda j: (0, j)), pl.BlockSpec((rows, 2 * tile), lambda j: (0, j))],
        out_shape=[of((rows, units)), of((rows, 2 * units))],
    )


def product(lhs, rhs, where=None, turned=False, name="product"):
    count = len(lhs)
    rows = lhs[0].shape[0]
    columns = rhs[0].shape[0 if turned else 1]
    wide = sum(a.shape[1] for a in lhs)
    tile = min(columns, 512 if wide > 1024 else 1024)
    parts = 1 if where is None else 2
    size = rows // parts

    def kernel(*refs):
        refs = refs[parts - 1 :]
        lhs_refs, rhs_refs, out_refs = refs[: parts * count], refs[parts * count : -parts], refs[-parts:]
        for i, out_ref in enumerate(out_refs):
            total = None
            for a, b in zip(lhs_refs[i * count : (i + 1) * count], rhs_refs):
                extra = dot(a[...], b[...], 1, 1 if turned else 0)
                total = extra if total is None else total + extra
            out_ref[...] = total.astype(BF16)

    if parts == 1:
        lhs_specs = [pl.BlockSpec((rows, a.shape[1]), lambda n, *w: (0, 0)) for a in lhs]
    else:
        lhs_specs = [
            pl.BlockSpec((size, a.shape[1]), (lambda s: lambda n, w: (w[s], 0))(s)) for s in (OTHER, CORE) for a in lhs
        ]
    if turned:
        rhs_specs = [pl.BlockSpec((tile, b.shape[1]), lambda n, *w: (n, 0)) for b in rhs]
    else:
        rhs_specs = [pl.BlockSpec((b.shape[0], tile), lambda n, *w: (0, n)) for b in rhs]
    result = launch(
        kernel,
        [*list(lhs) * parts, *rhs],
        lhs_specs + rhs_specs,
        name,
        [] if where is None else [where],
        grid=(columns // tile,),
        out_specs=[pl.BlockSpec((size, tile), lambda n, *w: (0, n))] * parts,
        out_shape=[of((size, columns))] * parts,
    )
    return result[0] if parts == 1 else result


def quarter_product(sets, kinds, near, far, where, scalars, name):
    rows = near[0].shape[0]
    part = D // 8
    width = near[0].shape[1]
    tile = min(width, 512)
    tiles = width // tile
    pieces = len(near)
    first, stride = scalars
    fixed_specs = [
        pl.BlockSpec((rows, part), (lambda k, h: lambda t, w: (0, 4 * h + w[first + stride * k]))(k, h))
        for _ in sets
        for _ in range(2)
        for k in range(2)
        for h in range(2)
    ]
    piece_specs = [
        pl.BlockSpec((rows, tile), (lambda i: lambda t, w: (0, jnp.clip(t - i * tiles, 0, tiles - 1)))(i))
        for i in range(pieces)
    ]
    count = len(fixed_specs)

    def kernel(where_ref, *refs):
        fixed, near_refs, far_refs = refs[:count], refs[count : count + pieces], refs[count + pieces : -2]
        out_ref, flat = refs[-2:]
        step = pl.program_id(0)

        @pl.when(step == 0)
        def _():
            for n, ref in enumerate(fixed):
                kind, chip, at = n // 8, n // 4 % 2, n % 4
                flat[kind, at * part : (at + 1) * part, chip * rows : (chip + 1) * rows] = ref[...].T

        for i, kind in enumerate(kinds):

            @pl.when((step >= i * tiles) & (step < (i + 1) * tiles))
            def _():
                total = dot(flat[kind, :, :rows], near_refs[i][...], 1, 0)
                total += dot(flat[kind, :, rows:], far_refs[i][...], 1, 0)
                out_ref[0] = total[: 2 * part].astype(BF16)
                out_ref[1] = total[2 * part :].astype(BF16)

    return launch(
        kernel,
        [*[a for pair in sets for a in pair for _ in range(4)], *near, *far],
        fixed_specs + piece_specs * 2,
        name,
        [where],
        grid=(tiles * pieces,),
        out_specs=pl.BlockSpec((2, 2 * part, tile), lambda t, w: (0, 0, t)),
        out_shape=of((2, 2 * part, width * pieces)),
        scratch_shapes=[pltpu.VMEM((len(sets), 4 * part, 2 * rows), BF16)],
    )


def row_call(kernel, rows, where, ins, outs, sums, name):
    tile = min(256, rows)
    steps = rows // tile
    specs, arrays = [], []
    for item in ins:
        array, scalar = item if isinstance(item, tuple) else (item, None)
        if scalar is not None:
            specs.append(pl.BlockSpec((tile, D), (lambda s: lambda i, w: (w[s] * steps + i, 0))(scalar)))
        elif array.shape[0] == 1:
            specs.append(pl.BlockSpec((1, D), lambda i, w: (0, 0)))
        else:
            specs.append(pl.BlockSpec((tile, D), lambda i, w: (i, 0)))
        arrays.append(array)
    out_specs = [pl.BlockSpec((tile, width), lambda i, w: (i, 0)) for _, width in outs]
    out_shape = [of((rows, width), dtype) for dtype, width in outs]
    return launch(
        kernel,
        arrays,
        specs,
        name,
        [where],
        grid=(steps,),
        out_specs=out_specs + [pl.BlockSpec((8, D), lambda i, w: (0, 0))] * sums,
        out_shape=out_shape + [of((8, D), F32)] * sums,
    )


def add_refs(*refs):
    total = refs[0][...].astype(F32)
    for ref in refs[1:]:
        total += ref[...].astype(F32)
    return total


def split_features(where_ref, total, mine_ref, other_ref):
    first = where_ref[CORE] == 0
    low, high = total[:, : D // 2], total[:, D // 2 :]
    mine_ref[...] = jnp.where(first, low, high).astype(mine_ref.dtype)
    other_ref[...] = jnp.where(first, high, low).astype(other_ref.dtype)


def norm_kernel(where_ref, one_ref, two_ref, far_ref, x_ref, gain_ref, residual_ref, normed_ref):
    residual = add_refs(x_ref, one_ref, two_ref, far_ref)
    scale = lax.rsqrt(jnp.sum(residual * residual, axis=1, keepdims=True) / D + EPS)
    residual_ref[...] = residual
    normed_ref[...] = (residual * scale * gain_ref[...]).astype(BF16)


def norm_back(stream, gain, upstream, sum_ref):
    scale = lax.rsqrt(jnp.sum(stream * stream, axis=1, keepdims=True) / D + EPS)
    weighted = upstream * gain
    inner = jnp.sum(weighted * stream, axis=1, keepdims=True)
    part = jnp.sum((upstream * stream * scale).reshape(-1, 8, D), axis=0)

    @pl.when(pl.program_id(0) == 0)
    def _():
        sum_ref[...] = jnp.zeros_like(sum_ref)

    sum_ref[...] += part
    return scale * weighted - stream * (scale * scale * scale) * (inner / D)


def ffn_back_kernel(where_ref, one_ref, two_ref, far_ref, residual_ref, cot_ref, gain_ref, grad_ref, low_ref, sum_ref):
    back = norm_back(residual_ref[...], gain_ref[...], add_refs(one_ref, two_ref, far_ref), sum_ref)
    grad = cot_ref[...].astype(F32) + back
    grad_ref[...] = grad
    low_ref[...] = grad.astype(BF16)


def input_back_kernel(where_ref, one_ref, two_ref, far_ref, x_ref, grad_ref, gain_ref, mine_ref, other_ref, sum_ref):
    back = norm_back(x_ref[...].astype(F32), gain_ref[...], add_refs(one_ref, two_ref, far_ref), sum_ref)
    split_features(where_ref, grad_ref[...] + back, mine_ref, other_ref)


def mixed_kernel(where_ref, *refs):
    split_features(where_ref, add_refs(*refs[:-2]), *refs[-2:])


def finish(pieces, spans, turned, where, name):
    shape = pieces[0].shape
    part = shape[1]
    sizes = [2 * sum(hi - lo for lo, hi in mine) for mine in spans]

    def kernel(where_ref, *refs):
        ins, outs = refs[:4], refs[4:]
        for k in range(4):

            @pl.when(pl.program_id(0) == k)
            def _():
                for out_ref, mine, flip in zip(outs, spans, turned):
                    at = 0
                    for core in range(2):
                        for lo, hi in mine:
                            block = ins[k][core, :, lo:hi]
                            if flip:
                                out_ref[at : at + hi - lo, :] = block.T.astype(F32)
                            else:
                                out_ref[:, at : at + hi - lo] = block.astype(F32)
                            at += hi - lo

    return launch(
        kernel,
        pieces,
        [pl.BlockSpec(shape, lambda k, w: (0, 0, 0))] * 4,
        name,
        [where],
        grid=(4,),
        out_specs=[
            pl.BlockSpec((n, part), lambda k, w: (0, w[QUARTER + k]))
            if flip
            else pl.BlockSpec((part, n), lambda k, w: (w[QUARTER + k], 0))
            for n, flip in zip(sizes, turned)
        ],
        out_shape=[of((n, 4 * part) if flip else (4 * part, n), F32) for n, flip in zip(sizes, turned)],
    )


def swap_axis(values, axis, distance):
    size = lax.axis_size(axis)
    return lax.ppermute(values, axis, [(i, i ^ distance) for i in range(size)])


def other_core(values):
    return swap_axis(values, "row", 1)


def other_chip(values):
    return swap_axis(values, "col", 1)


def far_plane(values):
    return swap_axis(values, "col", 2)


def hop(values, step):
    pairs = []
    for spot in range(4):
        for core in range(2):
            distance = 1 if (step == 1) == (core == 0) else 2
            pairs.append((spot * 2 + core, (spot ^ distance) * 2 + core))
    return lax.ppermute(values, ("dp", "row"), pairs)


def hop_one(values):
    return hop(values, 1)


def hop_two(values):
    return hop(values, 2)


def add32(*values):
    total = values[0].astype(F32)
    for value in values[1:]:
        total += value.astype(F32)
    return total


class Plan:
    def __init__(self, direct, blocks):
        self.blocks = blocks
        self.core = lax.axis_index("row")
        if direct:
            spot = lax.axis_index("dp")
            quarters = [spot ^ jnp.where(self.core == 0, k, (0, 2, 1, 3)[k]) for k in range(4)]
        else:
            quarters = [jnp.int32(k) for k in range(4)]
        self.where = jnp.stack([self.core, 1 - self.core] + quarters).astype(jnp.int32)
        self.line = Line()

    def run(self, call, *values):
        return self.line.run(call, *values)

    def mix(self, call, *values):
        return self.line.mix(call, *values)

    def send(self, move, value):
        return self.line.send(move, value)

    def ship(self, move, value):
        return self.line.ship(move, value)

    def post(self, move, value):
        return self.line.post(move, value)

    def pause(self):
        self.run(short_kernel, self.line.stamp)

    def swap(self, value):
        return self.line.swap(value)

    def place(self, sources, outs, phases, name, kept=0):
        return self.run(lambda first, *rest: place([first, *rest], outs, phases, self.where, name, kept), *sources)

    def by_core(self, low, high):
        return jnp.where(self.core == 0, low, high), jnp.where(self.core == 0, high, low)


class Group:
    def __init__(self, name, plan, sets, kinds, near, far, spans, turned):
        self.name, self.plan, self.sets, self.kinds = name, plan, sets, kinds
        self.near, self.far, self.spans, self.turned = near, far, spans, turned
        self.block = sum(a.shape[1] for a in near) // plan.blocks

    def produce(self, scalars):
        plan, count = self.plan, len(self.near)
        return plan.run(
            lambda first, *rest: quarter_product(
                self.sets, self.kinds, (first,) + rest[: count - 1], rest[count - 1 :], plan.where, scalars, self.name
            ),
            *self.near, *self.far,
        )

    def make(self):
        self.sent = self.produce((QUARTER + 1, 2))

    def leave(self):
        self.came = self.plan.post(hop_one, self.sent)

    def stay(self):
        self.kept = self.produce((QUARTER, 2))

    def second(self):
        def add(kept, came):
            return add32(kept[1], came[1]).astype(BF16)

        self.back = self.plan.post(hop_two, self.plan.mix(add, self.kept, self.came))

    def cross_plane(self):
        n = self.block

        def add(kept, came, back):
            return add32(kept[0, :, n:], came[0, :, n:], back[:, n:]).astype(BF16)

        self.arrived = self.plan.post(far_plane, self.plan.mix(add, self.kept, self.came, self.back))

    def total(self):
        n = self.block

        def add(arrived, kept, came, back):
            return add32(kept[0, :, :n], came[0, :, :n], back[:, :n], arrived).astype(BF16)

        whole = self.plan.swap(self.plan.mix(add, self.arrived, self.kept, self.came, self.back))
        self.both = whole.reshape(2, -1, n)

    def spread(self):
        self.one = self.plan.ship(hop_one, self.both)
        self.two = self.plan.ship(hop_two, self.both)

    def spread_last(self):
        self.three = self.plan.send(hop_two, self.one)

    def finish(self):
        return self.plan.run(
            lambda first, *rest: finish((first,) + rest, self.spans, self.turned, self.plan.where, "finish"),
            self.both, self.one, self.two, self.three,
        )

    def whole(self, groups):
        plan = self.plan
        pieces = []
        for k in range(2):
            made = self.produce((QUARTER + 2 * k, 1))
            for one in made:
                total = jnp.stack(jnp.split(one.astype(F32), plan.blocks, axis=1))
                total = lax.psum_scatter(total, "col", scatter_dimension=0, axis_index_groups=groups)
                total = lax.psum(total, "dp").astype(BF16)
                pieces.append(plan.swap(total).reshape(2, -1, total.shape[1]))
        return finish(pieces, self.spans, self.turned, plan.where, "finish")


class Sizes:
    def __init__(self, tokens, w_query, w_gate):
        self.rows = tokens.shape[0]
        self.half = self.rows // 2
        self.width = w_query.shape[1] // 2
        self.units = w_gate.shape[1] // 2
        self.tile = min(UNIT_TILE, self.units)
        self.split = D // 2


def interleaved(s):
    return [(p, lo) for lo in range(0, s.units, s.tile) for p in range(2)]


def gu_spans(s):
    return [[(lo + p * s.tile, lo + (p + 1) * s.tile) for lo in range(0, 2 * s.units, 2 * s.tile)] for p in range(2)]


def columns(lo, size):
    return lambda w: (slice(None), pl.ds(lo, size))


def join_features(plan, s, mine, theirs):
    return plan.place(
        [mine, theirs], [of((s.rows, D))],
        [[(0, full, 0, cols_at(CORE, s.split)), (1, full, 0, cols_at(OTHER, s.split))]], "join",
    )[0]


def join_rows(plan, s, mine, theirs):
    return plan.place(
        [mine, theirs], [of((s.rows, D))], [[(0, full, 0, rows_at(CORE, s.half)), (1, full, 0, rows_at(OTHER, s.half))]], "join"
    )[0]


def pack_in(plan, s, weights, parts, name):
    total = sum(size for _, _, size, _ in parts)
    moves, at = [], 0
    for i, lo, size, step in parts:
        moves.append((i, cols_at(OTHER, step, lo, size), 0, columns(at, size)))
        at += size
    return plan.place(weights, [of((s.split, total))], [moves], name)[0]


def own_in(plan, s, weights, got, parts):
    total = got.shape[1]
    moves, at = [], 0
    for i, lo, size, step in parts:
        moves.append((i, cols_at(CORE, step, lo, size), 0, block_at(CORE, s.split, at, size)))
        at += size
    moves.append((len(weights), full, 0, rows_at(OTHER, s.split)))
    return plan.place([*weights, got], [of((D, total))], [moves], "own")[0]


def own_out(plan, s, weight, got):
    rows = got.shape[0]
    return plan.place(
        [weight, got], [of((rows, D))], [[(0, rows_at(CORE, rows), 0, cols_at(CORE, s.split)), (1, full, 0, cols_at(OTHER, s.split))]],
        "own",
    )[0]


def both_gains(plan, mine, other):
    joined = plan.mix(lambda a, b: jnp.concatenate(plan.by_core(a, b), axis=1), mine, other)
    return joined[:1], joined[1:]


def norm_first(plan, s, near, far, x_near, gains):
    return plan.run(
        lambda *a: row_call(
            norm_kernel, s.half, plan.where, [*a[:3], (a[3], CORE), a[4]], [(F32, D), (BF16, D)], 0, "norm"
        ),
        *near, far, x_near, gains,
    )


def norm_ffn_back(plan, s, near, far, residual, cot_near, gains):
    return plan.run(
        lambda *a: row_call(
            ffn_back_kernel, s.half, plan.where, [*a[:4], (a[4], CORE), a[5]], [(F32, D), (BF16, D)], 1, "ffn_back"
        ),
        *near, far, residual, cot_near, gains,
    )


def norm_input_back(plan, s, near, far, x_near, grad_residual, gains):
    return plan.run(
        lambda *a: row_call(
            input_back_kernel, s.half, plan.where, [*a[:3], (a[3], CORE), *a[4:]],
            [(F32, D // 2), (F32, D // 2)], 1, "input_back",
        ),
        *near, far, x_near, grad_residual, gains,
    )


def add_mixed(plan, s, near, *others):
    return plan.run(
        lambda *a: row_call(mixed_kernel, s.half, plan.where, list(a), [(BF16, D // 2), (BF16, D // 2)], 0, "mixed"),
        *near, *others,
    )


def core_sum(plan, lhs, weights, turned, name):
    count = len(lhs)
    other, mine = plan.run(lambda *a: product(a[:count], a[count:], plan.where, turned, name), *lhs, *weights)
    return mine, plan.ship(other_core, other)


def add_pair(plan, pair):
    return plan.mix(lambda a, b: add32(a, b).astype(BF16), pair[1], pair[0])


def side_by_side(plan, s, mine, got):
    width = mine.shape[1]
    return plan.place(
        [mine, got], [of((s.rows, width), mine.dtype)],
        [[(0, full, 0, rows_at(CORE, s.half)), (1, full, 0, rows_at(OTHER, s.half))]], "sides",
    )[0]


def grad_attended(plan, gr, weight):
    return plan.run(lambda a: product([a], [weight], turned=True, name="grad_att"), gr)


def square(tokens, gain_attn, gain_ffn, w_query, w_key, w_value, w_out, w_gate, w_up, w_down, cotangent):
    plan = Plan(True, 2)
    s = Sizes(tokens, w_query, w_gate)
    run, mix, send, ship, post, where = plan.run, plan.mix, plan.send, plan.ship, plan.post, plan.where
    cos, sin = rope_tables()
    cos_rows, sin_rows = jnp.tile(cos, (s.rows // SEQ_LEN, 1)), jnp.tile(sin, (s.rows // SEQ_LEN, 1))
    qkv_parts = [(p, 0, s.width, s.width) for p in range(3)]
    gu_parts = [(p, lo, s.tile, s.units) for p, lo in interleaved(s)]
    eighth = D // 4 // 8

    far_tokens = other_chip(tokens)
    near_tokens = other_core(tokens)
    gains_mine = jnp.stack((gain_attn, gain_ffn))
    gains_other = other_core(gains_mine)
    plan.line.stamp = gains_mine[:, :LANES]
    got_qkv = ship(other_core, pack_in(plan, s, [w_query, w_key, w_value], qkv_parts, "pack"))
    pack_out = plan.place([w_out], [of((s.width, s.split))], [[(0, rows_at(OTHER, s.width), 0, full)]], "pack")[0]
    got_out = ship(other_core, pack_out)
    own_qkv = own_in(plan, s, [w_query, w_key, w_value], got_qkv, qkv_parts)
    own_o = own_out(plan, s, w_out, got_out)
    quarter, out_rows = D // 4, s.width // 4
    slots = quarter // out_rows
    out_cols = D // slots
    qkvo = plan.place(
        [own_qkv, own_o], [of((quarter, 3 * s.width + out_cols))],
        [
            [(0, rows_at(QUARTER, quarter), 0, columns(0, 3 * s.width))]
            + [
                (
                    1, (lambda j: lambda w: (pl.ds(pl.multiple_of(w[QUARTER] * out_rows, out_rows), out_rows), pl.ds(j * out_cols, out_cols)))(j),
                    0, (lambda j: lambda w: (pl.ds(j * out_rows, out_rows), pl.ds(3 * s.width, out_cols)))(j),
                )
                for j in range(slots)
            ]
        ],
        "quarter",
    )[0]
    qkvo_zero = ship(far_plane, qkvo)
    gains_attn, gains_ffn = both_gains(plan, gains_mine, gains_other)
    got_gu = ship(other_core, pack_in(plan, s, [w_gate, w_up], gu_parts, "pack"))
    pack_down = plan.place([w_down], [of((s.units, s.split))], [[(0, rows_at(OTHER, s.units), 0, full)]], "pack")[0]
    got_down = ship(other_core, pack_down)
    x_near = join_features(plan, s, tokens, near_tokens)
    own_gu = own_in(plan, s, [w_gate, w_up], got_gu, gu_parts)
    own_d = own_out(plan, s, w_down, got_down)
    down_rows = s.units // 4
    mixed_rows = quarter // 2 + down_rows // 2
    gud = [
        plan.place(
            [own_gu, own_d], [of((mixed_rows, D))],
            [[
                (0, (lambda i: rows_span(QUARTER, quarter, i * (quarter // 2), quarter // 2))(i), 0, rows_fixed(0, quarter // 2)),
                (1, (lambda i: rows_span(QUARTER, down_rows, i * (down_rows // 2), down_rows // 2))(i), 0, rows_fixed(quarter // 2, down_rows // 2)),
            ]],
            "quarter",
        )[0]
        for i in range(2)
    ]
    gud_zero = [None, None]

    def project(x, weight, first):
        return run(lambda a: project_qkv(a, gains_attn, cos_rows, sin_rows, weight, first), x)

    normed_near, *near_own = project(x_near, own_qkv, True)
    far_half = send(other_core, far_tokens)
    o_near_own = run(attend, *near_own)
    qkvo_one, qkvo_two = send(hop_one, qkvo_zero), send(hop_two, qkvo_zero)
    gud_zero[0] = send(far_plane, gud[0])
    x_far = join_features(plan, s, far_tokens, far_half)
    normed_far, *far_own = project(x_far, own_qkv, True)
    qkvo_three = send(hop_two, qkvo_one)
    o_far_own = run(attend, *far_own)
    pieces = [qkvo_zero, qkvo_one, qkvo_two, qkvo_three]
    for_qkv, for_o = plan.place(
        pieces, [of((D, 3 * s.width)), of((s.width, D))],
        [
            [(k, columns(0, 3 * s.width), 0, rows_at(QUARTER + k, quarter)) for k in range(4)]
            + [
                (
                    k, (lambda j: lambda w: (pl.ds(j * out_rows, out_rows), pl.ds(3 * s.width, out_cols)))(j),
                    1, (lambda k, j: lambda w: (pl.ds(pl.multiple_of(w[QUARTER + k] * out_rows, out_rows), out_rows), pl.ds(j * out_cols, out_cols)))(k, j),
                )
                for k in range(4)
                for j in range(slots)
            ]
        ],
        "other",
    )
    w_qkv, w_o = [own_qkv, for_qkv], [own_o, for_o]

    far_for = project(normed_far, for_qkv, False)
    gud_one, gud_two, gud_three = [None, None], [None, None], [None, None]
    o_far = [o_far_own, run(attend, *far_for)]
    far = core_sum(plan, [o[0] for o in o_far], w_o, False, "out")
    near_for = project(normed_near, for_qkv, False)
    far = post(other_chip, add_pair(plan, far))
    gud_one[0], gud_two[0] = send(hop_one, gud_zero[0]), send(hop_two, gud_zero[0])
    gud_zero[1] = send(far_plane, gud[1])
    near_cot = send(other_core, cotangent)
    o_near = [o_near_own, run(attend, *near_for)]
    near = core_sum(plan, [o[0] for o in o_near], w_o, False, "out")
    gud_three[0] = send(hop_two, gud_one[0])
    cot_near = join_features(plan, s, cotangent, near_cot)
    residual, normed_ffn = norm_first(plan, s, near, far, x_near, gains_ffn)
    nf_row = ship(other_core, normed_ffn)
    nf_chip = post(other_chip, normed_ffn)
    def spread_out(i, outs):
        count = quarter // 2, down_rows // 2
        return plan.place(
            [g[i] for g in (gud_zero, gud_one, gud_two, gud_three)] + outs, [of(own_gu.shape), of(own_d.shape)],
            [
                [(k, rows_fixed(0, count[0]), 0, rows_span(QUARTER + k, quarter, i * count[0], count[0])) for k in range(4)]
                + [(k, rows_fixed(count[0], count[1]), 1, rows_span(QUARTER + k, down_rows, i * count[1], count[1])) for k in range(4)]
            ],
            "other", len(outs),
        )

    gud_one[1], gud_two[1] = send(hop_one, gud_zero[1]), send(hop_two, gud_zero[1])
    nf_near = join_rows(plan, s, normed_ffn, nf_row)
    fed_near = [run(ffn, nf_near, cot_near, own_gu, own_d)]
    halves = spread_out(0, [])
    nf_far_row = send(other_core, nf_chip)
    gud_three[1] = send(hop_two, gud_one[1])
    far_cot = send(other_chip, cotangent)
    plan.pause()
    nf_far = join_rows(plan, s, nf_chip, nf_far_row)
    for_gu, for_d = spread_out(1, list(halves))
    w_gu, w_d = [own_gu, for_gu], [own_d, for_d]
    fed_near.append(run(ffn, nf_near, cot_near, for_gu, for_d))
    hid_near, ggu_near = [f[0] for f in fed_near], [f[1] for f in fed_near]
    mixed_near = core_sum(plan, hid_near, w_d, False, "down")
    cot_far_row = send(other_core, far_cot)
    plan.pause()
    cot_far = join_features(plan, s, far_cot, cot_far_row)
    fed_far = [run(ffn, nf_far, cot_far, own_gu, own_d), run(ffn, nf_far, cot_far, for_gu, for_d)]
    hid_far, ggu_far = [f[0] for f in fed_far], [f[1] for f in fed_far]

    ups = Group("gu_grad", plan, [(nf_near, nf_far)], [0, 0], ggu_near, ggu_far, gu_spans(s), [False, False])
    down = Group("down_grad", plan, [(cot_near, cot_far)], [0, 0], hid_near, hid_far, [[(0, s.units)]], [True])
    ups.make()
    ups.leave()
    far = core_sum(plan, ggu_far, w_gu, True, "ffn_in")
    mixed_near = [add_pair(plan, mixed_near)]
    plan.pause()
    far = post(other_chip, add_pair(plan, far))
    near = core_sum(plan, ggu_near, w_gu, True, "ffn_in")
    ups.stay()
    grad_residual, grad_low, gain_ffn_part = norm_ffn_back(plan, s, near, far, residual, cot_near, gains_ffn)
    gr_row = ship(other_core, grad_low)
    gr_chip = post(other_chip, grad_low)
    gr_near = join_rows(plan, s, grad_low, gr_row)
    ups.second()

    def back_one(gr, heads, outs, b):
        return run(attend_back, grad_attended(plan, gr, w_o[b]), *heads[b], *outs[b], cos, sin)

    near_heads, far_heads = [near_own, near_for], [far_own, far_for]
    back_near = [back_one(gr_near, near_heads, o_near, b) for b in range(2)]
    gr_far_row = send(other_core, gr_chip)
    down.make()
    ups.cross_plane()
    down.leave()
    gr_far = join_rows(plan, s, gr_chip, gr_far_row)
    back_far = [back_one(gr_far, far_heads, o_far, b) for b in range(2)]
    dqkv_far = [jnp.concatenate(b, axis=1) for b in back_far]
    far = core_sum(plan, dqkv_far, w_qkv, True, "qkv_in")
    down.stay()
    down.second()
    far = post(other_chip, add_pair(plan, far))
    heads = Group(
        "head_grad", plan, [(normed_near, normed_far), (gr_near, gr_far)], [0, 0, 0, 1] * 2,
        [a for b in range(2) for a in (*back_near[b], o_near[b][0])],
        [a for b in range(2) for a in (*back_far[b], o_far[b][0])],
        [[(p * s.width, (p + 1) * s.width)] for p in range(4)], [False, False, False, True],
    )
    heads.make()
    heads.leave()
    down.cross_plane()
    dqkv_near = [jnp.concatenate(b, axis=1) for b in back_near]
    near = core_sum(plan, dqkv_near, w_qkv, True, "qkv_in")
    heads.stay()
    input_mine, input_other, gain_attn_part = norm_input_back(plan, s, near, far, x_near, grad_residual, gains_attn)
    input_got = ship(other_core, input_other)
    gains = mix(lambda a, b: jnp.stack((jnp.sum(a, axis=0), jnp.sum(b, axis=0))), gain_attn_part, gain_ffn_part)
    gains_got = ship(other_core, gains)
    heads.second()
    ups.total()
    ups.spread()
    gains = mix(jnp.add, gains, gains_got)
    gains_got = send(other_chip, gains)
    mixed_far = core_sum(plan, hid_far, w_d, False, "down")
    input_grad = side_by_side(plan, s, input_mine, input_got)
    mixed_far = post(other_chip, add_pair(plan, mixed_far))
    gains = mix(jnp.add, gains, gains_got)
    heads.cross_plane()
    down.total()
    ups.spread_last()
    down.spread()
    mixed_mine, mixed_other = add_mixed(plan, s, mixed_near, mixed_far, residual)
    gains_got = send(far_plane, gains)
    mixed_got = ship(other_core, mixed_other)
    gate_grad, up_grad = ups.finish()
    gains = mix(jnp.add, gains, gains_got)
    heads.total()
    heads.spread()
    down.spread_last()
    gains_got = send(hop_one, gains)
    mixed = side_by_side(plan, s, mixed_mine, mixed_got)
    (down_grad,) = down.finish()
    heads.spread_last()
    gains = mix(jnp.add, gains, gains_got)
    gains_got = send(hop_two, gains)
    gains = mix(jnp.add, gains, gains_got)
    gains = jnp.where(plan.core == 0, gains[:, : s.split], gains[:, s.split :])
    q_grad, k_grad, v_grad, out_grad = heads.finish()
    return mixed, input_grad, gains[0], gains[1], q_grad, k_grad, v_grad, out_grad, gate_grad, up_grad, down_grad


def pair_order(near, far):
    member = lax.axis_index("col") % 2
    return jnp.concatenate((jnp.where(member == 0, near, far), jnp.where(member == 0, far, near)), axis=0)


def from_pair(joined):
    member = lax.axis_index("col") % 2
    first, second = jnp.split(joined, 2, axis=0)
    return jnp.where(member == 0, first, second), jnp.where(member == 0, second, first)


def general(tokens, gain_attn, gain_ffn, w_query, w_key, w_value, w_out, w_gate, w_up, w_down, cotangent):
    blocks = lax.axis_size("col") // 2
    groups = [[i for i in range(2 * blocks) if i % 2 == m] for m in range(2)]
    plan = Plan(False, blocks)
    s = Sizes(tokens, w_query, w_gate)
    run, where = plan.run, plan.where
    cos, sin = rope_tables()
    shared = s.rows % SEQ_LEN != 0
    qkv_parts = [(p, 0, s.width, s.width) for p in range(3)]
    gu_parts = [(p, lo, s.tile, s.units) for p, lo in interleaved(s)]

    def gathered(own):
        every = lax.all_gather(own, "col", axis=0, axis_index_groups=groups)
        return [every[b] for b in range(blocks)]

    def pack_rows(weight, rows):
        return plan.place([weight], [of((rows, s.split))], [[(0, rows_at(OTHER, rows), 0, full)]], "pack")[0]

    got = other_core(pack_in(plan, s, [w_query, w_key, w_value], qkv_parts, "pack"))
    w_qkv = gathered(own_in(plan, s, [w_query, w_key, w_value], got, qkv_parts))
    got = other_core(pack_in(plan, s, [w_gate, w_up], gu_parts, "pack"))
    w_gu = gathered(own_in(plan, s, [w_gate, w_up], got, gu_parts))
    w_o = gathered(own_out(plan, s, w_out, other_core(pack_rows(w_out, s.width))))
    w_d = gathered(own_out(plan, s, w_down, other_core(pack_rows(w_down, s.units))))
    gains_mine = jnp.stack((gain_attn, gain_ffn))
    gains_attn, gains_ffn = both_gains(plan, gains_mine, other_core(gains_mine))

    def both_chips(values):
        far = other_chip(values)
        return join_features(plan, s, values, other_core(values)), join_features(plan, s, far, other_core(far))

    x_near, x_far = both_chips(tokens)
    cot_near, cot_far = both_chips(cotangent)

    def tables(offset):
        if shared:
            return [lax.dynamic_slice_in_dim(t, offset, s.rows) for t in (cos, sin)]
        return [jnp.tile(t, (s.rows // SEQ_LEN, 1)) for t in (cos, sin)]

    first = (lax.axis_index("col") % 2) * s.rows
    chips = []
    for x, offset in ((x_near, first), (x_far, s.rows - first)):
        turn = tables(offset)
        normed, *heads = run(lambda a: project_qkv(a, gains_attn, *turn, w_qkv[0], True), x)
        every = [heads]
        for w in w_qkv[1:]:
            every.append(run(lambda a: project_qkv(a, gains_attn, *turn, w, False), normed))
        chips.append((normed, every))
    (normed_near, heads_near), (normed_far, heads_far) = chips

    def together(near, far):
        return pair_order(near, far) if shared else jnp.concatenate((near, far), axis=0)

    def apart(joined):
        return from_pair(joined) if shared else jnp.split(joined, 2, axis=0)

    joined_heads = [[together(a, b) for a, b in zip(n, f)] for n, f in zip(heads_near, heads_far)]
    outs = [run(attend, *h) for h in joined_heads]
    att = [apart(o[0]) for o in outs]
    att_near, att_far = [a[0] for a in att], [a[1] for a in att]

    def four_core_sum(near, far, weights, turned, name):
        far = other_chip(add_pair(plan, core_sum(plan, far, weights, turned, name)))
        return core_sum(plan, near, weights, turned, name), far

    def gather_tokens(values):
        far = other_chip(values)
        return join_rows(plan, s, values, other_core(values)), join_rows(plan, s, far, other_core(far))

    residual, normed_ffn = norm_first(plan, s, *four_core_sum(att_near, att_far, w_o, False, "out"), x_near, gains_ffn)
    nf_near, nf_far = gather_tokens(normed_ffn)
    fed_near = [run(ffn, nf_near, cot_near, w_gu[b], w_d[b]) for b in range(blocks)]
    fed_far = [run(ffn, nf_far, cot_far, w_gu[b], w_d[b]) for b in range(blocks)]
    hid_near, ggu_near = [f[0] for f in fed_near], [f[1] for f in fed_near]
    hid_far, ggu_far = [f[0] for f in fed_far], [f[1] for f in fed_far]
    kinds = [0] * blocks
    ups = Group("gu_grad", plan, [(nf_near, nf_far)], kinds, ggu_near, ggu_far, gu_spans(s), [False, False])
    down = Group("down_grad", plan, [(cot_near, cot_far)], kinds, hid_near, hid_far, [[(0, s.units)]], [True])
    grad_residual, grad_low, gain_ffn_part = norm_ffn_back(
        plan, s, *four_core_sum(ggu_near, ggu_far, w_gu, True, "ffn_in"), residual, cot_near, gains_ffn
    )
    gr_near, gr_far = gather_tokens(grad_low)
    gr = together(gr_near, gr_far)
    backs = []
    for b in range(blocks):
        grads = run(attend_back, grad_attended(plan, gr, w_o[b]), *joined_heads[b], *outs[b], cos, sin)
        backs.append([apart(g) for g in grads])
    back_near = [[g[0] for g in b] for b in backs]
    back_far = [[g[1] for g in b] for b in backs]
    heads = Group(
        "head_grad", plan, [(normed_near, normed_far), (gr_near, gr_far)], [0, 0, 0, 1] * blocks,
        [a for b in range(blocks) for a in (*back_near[b], att_near[b])],
        [a for b in range(blocks) for a in (*back_far[b], att_far[b])],
        [[(p * s.width, (p + 1) * s.width)] for p in range(4)], [False, False, False, True],
    )
    dqkv_near = [jnp.concatenate(b, axis=1) for b in back_near]
    dqkv_far = [jnp.concatenate(b, axis=1) for b in back_far]
    input_mine, input_other, gain_attn_part = norm_input_back(
        plan, s, *four_core_sum(dqkv_near, dqkv_far, w_qkv, True, "qkv_in"), x_near, grad_residual, gains_attn
    )
    mixed_mine, mixed_other = add_mixed(plan, s, *four_core_sum(hid_near, hid_far, w_d, False, "down"), residual)
    gains = lax.psum(jnp.stack((jnp.sum(gain_attn_part, axis=0), jnp.sum(gain_ffn_part, axis=0))), ("dp", "col", "row"))
    gains = jnp.where(plan.core == 0, gains[:, : s.split], gains[:, s.split :])
    mixed = side_by_side(plan, s, mixed_mine, other_core(mixed_other))
    input_grad = side_by_side(plan, s, input_mine, other_core(input_other))
    q_grad, k_grad, v_grad, out_grad = heads.whole(groups)
    gate_grad, up_grad = ups.whole(groups)
    (down_grad,) = down.whole(groups)
    return mixed, input_grad, gains[0], gains[1], q_grad, k_grad, v_grad, out_grad, gate_grad, up_grad, down_grad


def solution(mesh):
    stream = P(("dp", "col"), "row")
    gain = P("row")
    inward, outward = P("row", "col"), P("col", "row")
    weights = (inward, inward, inward, outward, inward, inward, outward)
    fits = mesh.shape["dp"] == 4 and mesh.shape["col"] == 4
    return jax.shard_map(
        lambda *args: square(*args) if fits and args[0].shape[0] % SEQ_LEN == 0 else general(*args),
        mesh=mesh,
        in_specs=(stream, gain, gain, *weights, stream),
        out_specs=(stream, stream, gain, gain, *weights),
        check_vma=False,
    )
```

time: 3390 us -> 1000 us (0.29)
  waiting for transfers between devices: 2310 us -> 192 us
  Pallas kernels: 0 us -> 641 us
  matrix products: 546 us -> 0 us
  local copies, waits for them, and re-layouts: 260 us -> 3.45 us
  other arithmetic: 179 us -> 77 us
  starting transfers between devices: 1.88 us -> 71.3 us
  blocking collectives: 53.6 us -> 6.3 us
    reduce_scatter x8 -> x0, waiting for transfers between devices: 1130 us -> none  [the longest x3 717 us: column_sum(): return lax.psum_scatter(summed, 'col', scatter_dimension=0, tiled=True)]
    pallas_call x0 -> x83, Pallas kernels: none -> 641 us  [launch(): pl.pallas_call(body, out_shape=out_shape, compiler_params=pltpu.CompilerP...]
    all_gather x11 -> x0, waiting for transfers between devices: 641 us -> none  [the longest x4 566 us: spread_cols(): return lax.all_gather(values, 'col', axis=0, tiled=True)]
    dot_general x32 -> x0, matrix products: 546 us -> none  [the longest x6 121 us: column_sum(): lax.dot_general(left_side, weight, (((1,), (inner_dim,)), ((), ())), pref...]
    psum x1 -> x0, waiting for transfers between devices: 541 us -> none  [on_device(): lax.psum((w_query_grad, w_key_grad, w_value_grad, w_out_grad, w_gate_grad...]
    ppermute x0 -> x81, waiting for transfers between devices: none -> 189 us  [the longest x55 106 us: swap_axis(): return lax.ppermute(values, axis, [(i, i ^ distance) for i in range(size)])]
    dynamic_update_slice x8 -> x0, local copies, waits for them, and re-layouts: 158 us -> none  [on_device(): attended, log_totals = lax.map(attend_forward, (queries, key_rows, values))]
    ppermute x0 -> x81, starting transfers between devices: none -> 62.5 us  [the longest x26 32.1 us: hop(): return lax.ppermute(values, ('dp', 'row'), pairs)]
  transfers between devices with their start and end apart: 20 -> 83, of which waited for: 19 -> 24; matrix products, arithmetic and copies ran while one was open for 9% -> 8% of each run, Pallas kernels for 0% -> 64%
where the time goes in v1:
time: 1000 us; the launch traced here: 993 us
  Pallas kernels  641 us (64%)
  waiting for transfers between devices  192 us (19%)
  other arithmetic  77 us (8%)
  starting transfers between devices  71.3 us (7%)
    pallas_call x83, Pallas kernels, launch(): pl.pallas_call(body, out_shape=out_shape, compiler_params=pltpu.CompilerP...  641 us
    ppermute x55, waiting for transfers between devices, swap_axis(): return lax.ppermute(values, axis, [(i, i ^ distance) for i in range(size)])  106 us
    ppermute x26, waiting for transfers between devices, hop(): return lax.ppermute(values, ('dp', 'row'), pairs)  83 us
    ppermute x26, starting transfers between devices, hop(): return lax.ppermute(values, ('dp', 'row'), pairs)  32.1 us
    ppermute x55, starting transfers between devices, swap_axis(): return lax.ppermute(values, axis, [(i, i ^ distance) for i in range(size)])  30.4 us
  transfers between devices with their start and end apart: 83, of which 24 were waited for; matrix products, arithmetic and copies ran while one was open for 8% of the time, Pallas kernels for 64%

profile of v1, /device:TPU:0, one launch (start us, length us, event | category | flops | bytes accessed | tf_op | source)
XLA Modules:
  0.0 992.8 jit_solution(1606395247980407699)
XLA Ops:
  43.3 7.8 own.6.refs_3_.refs_1_.refs_2_.refs_5_
  61.5 8.4 qkv.4
  72.8 9.7 attend.4
  91.4 8.4 qkv.5
  99.9 8.6 collective-permute-done.8.refs_2_
  110.2 9.9 %attend.5 = (bf16[1024,256]{1,0:T(8,128)(2,1)}, f32[1,2,8,1024]{3,2,1,0:T(8,128)}) custom-call(bf16[1024,256]{1,0:T(8,128)(2,1)} %get-tuple-element.288.refs_0_.refs_1_, bf16[1024,256]{1,0:T(8,128)(2,1)} %get-tuple-element.289.refs_1_.refs_2_, bf16[1024,256]{1,0:T(8,128)(2,1)} %get-tuple-element.290.refs_2_.refs_3_, ...), custom_call_target="tpu_custom_call" | custom-call | flops 999999995904 | bytes 1 | tf_op jit(solution)/shard_map/attend/pallas_call | solution.py:89
  128.1 7.6 qkv.6
  135.7 9.7 attend.6
  151.2 7.8 qkv.7
  171.3 9.7 attend.7
  181.0 17.2 %out.3 = (bf16[512,2048]{1,0:T(8,128)(2,1)}, bf16[512,2048]{1,0:T(8,128)(2,1)}) custom-call(s32[6]{0:T(128)} %stack.45.refs_0_, bf16[1024,256]{1,0:T(8,128)(2,1)} %get-tuple-element.285.refs_3_.refs_1_.refs_4_.refs_20_, bf16[1024,256]{1,0:T(8,128)(2,1)} %get-tuple-element.318.refs_2_.refs_4_.refs_7_.refs_24_, ...), custom_call_target="tpu_custom_call" | custom-call | flops 999999995904 | bytes 1 | tf_op jit(solution)/shard_map/out/pallas_call | solution.py:89
  198.3 6.7 collective-permute-done.18.refs_2_
  211.8 33.1 %collective-permute-done.16.refs_3_ = bf16[512,2048]{1,0:T(8,128)(2,1)} collective-permute-done((bf16[512,2048]{1,0:T(8,128)(2,1)}, bf16[512,2048]{1,0:T(8,128)(2,1)}, u32[]{:S(2)}, u32[]{:S(2)}) %collective-permute-start.16) | collective-permute-done | bytes 2097184 | tf_op jit(solution)/shard_map/ppermute | solution.py:570
  244.9 6.8 norm.1
  262.2 20.8 %ffn.4 = (bf16[1024,1024]{1,0:T(8,128)(2,1)}, bf16[1024,2048]{1,0:T(8,128)(2,1)}) custom-call(bf16[1024,2048]{1,0:T(8,128)(2,1)} %join.11.refs_0_.refs_4_.refs_1_.refs_2_.refs_3_, bf16[1024,2048]{1,0:T(8,128)(2,1)} %join.10.refs_6_.refs_1_.refs_5_.refs_2_.refs_3_.refs_4_, bf16[2048,2048]{1,0:T(8,128)(2,1)} %own.6.refs_3_.refs_1_.refs_2_.refs_5_, ...), custom_call_target="tpu_custom_call" | custom-call | flops 999999995904 | bytes 1 | tf_op jit(solution)/shard_map/ffn/pallas_call | solution.py:89
  289.0 12.4 %collective-permute-done.24.refs_1_ = bf16[512,2048]{1,0:T(8,128)(2,1)} collective-permute-done((bf16[512,2048]{1,0:T(8,128)(2,1)}, bf16[512,2048]{1,0:T(8,128)(2,1)}, u32[]{:S(2)}, u32[]{:S(2)}) %collective-permute-start.24) | collective-permute-done | bytes 2097184 | tf_op jit(solution)/shard_map/ppermute | solution.py:570
  310.2 13.1 %collective-permute-done.27.refs_4_ = bf16[384,2048]{1,0:T(8,128)(2,1)} collective-permute-done((bf16[384,2048]{1,0:T(8,128)(2,1)}, bf16[384,2048]{1,0:T(8,128)(2,1)}, u32[]{:S(2)}, u32[]{:S(2)}) %collective-permute-start.27) | collective-permute-done | bytes 1572896 | tf_op jit(solution)/shard_map/ppermute | solution.py:591
  323.3 6.0 other.5
  329.3 20.8 %ffn.5 = (bf16[1024,1024]{1,0:T(8,128)(2,1)}, bf16[1024,2048]{1,0:T(8,128)(2,1)}) custom-call(bf16[1024,2048]{1,0:T(8,128)(2,1)} %join.11.refs_0_.refs_4_.refs_1_.refs_2_.refs_3_, bf16[1024,2048]{1,0:T(8,128)(2,1)} %join.10.refs_6_.refs_1_.refs_5_.refs_2_.refs_3_.refs_4_, bf16[2048,2048]{1,0:T(8,128)(2,1)} %get-tuple-element.345.refs_2_.refs_4_.refs_6_, ...), custom_call_target="tpu_custom_call" | custom-call | flops 999999995904 | bytes 1 | tf_op jit(solution)/shard_map/ffn/pallas_call | solution.py:89
  350.1 13.8 %down.2 = (bf16[512,2048]{1,0:T(8,128)(2,1)}, bf16[512,2048]{1,0:T(8,128)(2,1)}) custom-call(s32[6]{0:T(128)} %stack.45.refs_0_, bf16[1024,1024]{1,0:T(8,128)(2,1)} %get-tuple-element.333.refs_5_.refs_1_.refs_3_.refs_9_, bf16[1024,1024]{1,0:T(8,128)(2,1)} %get-tuple-element.347.refs_2_.refs_4_.refs_7_.refs_10_, ...), custom_call_target="tpu_custom_call" | custom-call | flops 999999995904 | bytes 1 | tf_op jit(solution)/shard_map/down/pallas_call | solution.py:89
  375.7 21.2 %ffn.6 = (bf16[1024,1024]{1,0:T(8,128)(2,1)}, bf16[1024,2048]{1,0:T(8,128)(2,1)}) custom-call(bf16[1024,2048]{1,0:T(8,128)(2,1)} %join.12.refs_7_.refs_0_.refs_5_.refs_6_.refs_8_, bf16[1024,2048]{1,0:T(8,128)(2,1)} %join.13.refs_1_.refs_4_.refs_5_.refs_6_.refs_7_.refs_8_, bf16[2048,2048]{1,0:T(8,128)(2,1)} %own.6.refs_3_.refs_1_.refs_2_.refs_5_, ...), custom_call_target="tpu_custom_call" | custom-call | flops 999999995904 | bytes 1 | tf_op jit(solution)/shard_map/ffn/pallas_call | solution.py:89
  396.9 20.8 %ffn.7 = (bf16[1024,1024]{1,0:T(8,128)(2,1)}, bf16[1024,2048]{1,0:T(8,128)(2,1)}) custom-call(bf16[1024,2048]{1,0:T(8,128)(2,1)} %join.12.refs_7_.refs_0_.refs_5_.refs_6_.refs_8_, bf16[1024,2048]{1,0:T(8,128)(2,1)} %join.13.refs_1_.refs_4_.refs_5_.refs_6_.refs_7_.refs_8_, bf16[2048,2048]{1,0:T(8,128)(2,1)} %get-tuple-element.345.refs_2_.refs_4_.refs_6_, ...), custom_call_target="tpu_custom_call" | custom-call | flops 999999995904 | bytes 1 | tf_op jit(solution)/shard_map/ffn/pallas_call | solution.py:89
  417.7 26.0 %gu_grad.2.refs_1_ = bf16[2,512,4096]{2,1,0:T(8,128)(2,1)} custom-call(s32[6]{0:T(128)} %stack.45.refs_0_, bf16[1024,2048]{1,0:T(8,128)(2,1)} %join.11.refs_0_.refs_4_.refs_1_.refs_2_.refs_3_, bf16[1024,2048]{1,0:T(8,128)(2,1)} %join.11.refs_0_.refs_4_.refs_1_.refs_2_.refs_3_, bf16[1024,2048]{1,0:T(8,128)(2,1)} %join.11.refs_0_.refs_4_.refs_1_.refs_2_.refs_3_, ...), custom_call_target="tpu_custom_call" | custom-call | flops 999999995904 | bytes 1 | tf_op jit(solution)/shard_map/gu_grad/pallas_call | solution.py:89
  446.9 24.6 %ffn_in.2 = (bf16[512,2048]{1,0:T(8,128)(2,1)}, bf16[512,2048]{1,0:T(8,128)(2,1)}) custom-call(s32[6]{0:T(128)} %stack.45.refs_0_, bf16[1024,2048]{1,0:T(8,128)(2,1)} %get-tuple-element.352.refs_11_.refs_1_.refs_3_, bf16[1024,2048]{1,0:T(8,128)(2,1)} %get-tuple-element.354.refs_12_.refs_2_.refs_4_, ...), custom_call_target="tpu_custom_call" | custom-call | flops 999999995904 | bytes 1 | tf_op jit(solution)/shard_map/ffn_in/pallas_call | solution.py:89
  482.8 24.4 %ffn_in.3 = (bf16[512,2048]{1,0:T(8,128)(2,1)}, bf16[512,2048]{1,0:T(8,128)(2,1)}) custom-call(s32[6]{0:T(128)} %stack.45.refs_0_, bf16[1024,2048]{1,0:T(8,128)(2,1)} %get-tuple-element.355.refs_9_.refs_1_.refs_3_, bf16[1024,2048]{1,0:T(8,128)(2,1)} %get-tuple-element.356.refs_10_.refs_2_.refs_4_, ...), custom_call_target="tpu_custom_call" | custom-call | flops 999999995904 | bytes 1 | tf_op jit(solution)/shard_map/ffn_in/pallas_call | solution.py:89
  507.5 26.1 %gu_grad.3.refs_7_ = bf16[2,512,4096]{2,1,0:T(8,128)(2,1)} custom-call(s32[6]{0:T(128)} %stack.45.refs_0_, bf16[1024,2048]{1,0:T(8,128)(2,1)} %join.11.refs_0_.refs_4_.refs_1_.refs_2_.refs_3_, bf16[1024,2048]{1,0:T(8,128)(2,1)} %join.11.refs_0_.refs_4_.refs_1_.refs_2_.refs_3_, bf16[1024,2048]{1,0:T(8,128)(2,1)} %join.11.refs_0_.refs_4_.refs_1_.refs_2_.refs_3_, ...), custom_call_target="tpu_custom_call" | custom-call | flops 999999995904 | bytes 1 | tf_op jit(solution)/shard_map/gu_grad/pallas_call | solution.py:89
  533.6 8.9 ffn_back.1
  566.2 10.2 %attend_back.4 = (bf16[1024,256]{1,0:T(8,128)(2,1)}, bf16[1024,256]{1,0:T(8,128)(2,1)}, bf16[1024,256]{1,0:T(8,128)(2,1)}) custom-call(bf16[1024,256]{1,0:T(8,128)(2,1)} %grad_att.4.refs_0_.refs_8_, bf16[1024,256]{1,0:T(8,128)(2,1)} %get-tuple-element.274.refs_0_.refs_1_, bf16[1024,256]{1,0:T(8,128)(2,1)} %get-tuple-element.275.refs_1_.refs_2_, ...), custom_call_target="tpu_custom_call" | custom-call | flops 999999995904 | bytes 1 | tf_op jit(solution)/shard_map/attend_back/pallas_call | solution.py:89
  580.9 10.6 %attend_back.5 = (bf16[1024,256]{1,0:T(8,128)(2,1)}, bf16[1024,256]{1,0:T(8,128)(2,1)}, bf16[1024,256]{1,0:T(8,128)(2,1)}) custom-call(bf16[1024,256]{1,0:T(8,128)(2,1)} %grad_att.5.refs_0_.refs_8_, bf16[1024,256]{1,0:T(8,128)(2,1)} %get-tuple-element.308.refs_2_.refs_0_.refs_1_, bf16[1024,256]{1,0:T(8,128)(2,1)} %get-tuple-element.301.refs_1_.refs_2_, ...), custom_call_target="tpu_custom_call" | custom-call | flops 999999995904 | bytes 1 | tf_op jit(solution)/shard_map/attend_back/pallas_call | solution.py:89
  591.6 16.5 %down_grad.2.refs_2_ = bf16[2,512,2048]{2,1,0:T(8,128)(2,1)} custom-call(s32[6]{0:T(128)} %stack.45.refs_0_, bf16[1024,2048]{1,0:T(8,128)(2,1)} %join.10.refs_6_.refs_1_.refs_5_.refs_2_.refs_3_.refs_4_, bf16[1024,2048]{1,0:T(8,128)(2,1)} %join.10.refs_6_.refs_1_.refs_5_.refs_2_.refs_3_.refs_4_, ...), custom_call_target="tpu_custom_call" | custom-call | flops 999999995904 | bytes 1 | tf_op jit(solution)/shard_map/down_grad/pallas_call | solution.py:89
  630.8 10.4 %attend_back.6 = (bf16[1024,256]{1,0:T(8,128)(2,1)}, bf16[1024,256]{1,0:T(8,128)(2,1)}, bf16[1024,256]{1,0:T(8,128)(2,1)}) custom-call(bf16[1024,256]{1,0:T(8,128)(2,1)} %grad_att.6.refs_0_.refs_8_, bf16[1024,256]{1,0:T(8,128)(2,1)} %get-tuple-element.288.refs_0_.refs_1_, bf16[1024,256]{1,0:T(8,128)(2,1)} %get-tuple-element.289.refs_1_.refs_2_, ...), custom_call_target="tpu_custom_call" | custom-call | flops 999999995904 | bytes 1 | tf_op jit(solution)/shard_map/attend_back/pallas_call | solution.py:89
  645.8 10.2 %attend_back.7 = (bf16[1024,256]{1,0:T(8,128)(2,1)}, bf16[1024,256]{1,0:T(8,128)(2,1)}, bf16[1024,256]{1,0:T(8,128)(2,1)}) custom-call(bf16[1024,256]{1,0:T(8,128)(2,1)} %grad_att.7.refs_0_.refs_8_, bf16[1024,256]{1,0:T(8,128)(2,1)} %get-tuple-element.294.refs_0_.refs_3_.refs_1_, bf16[1024,256]{1,0:T(8,128)(2,1)} %get-tuple-element.295.refs_1_.refs_2_, ...), custom_call_target="tpu_custom_call" | custom-call | flops 999999995904 | bytes 1 | tf_op jit(solution)/shard_map/attend_back/pallas_call | solution.py:89
  659.0 11.3 %qkv_in.2 = (bf16[512,2048]{1,0:T(8,128)(2,1)}, bf16[512,2048]{1,0:T(8,128)(2,1)}) custom-call(s32[6]{0:T(128)} %stack.45.refs_0_, bf16[1024,768]{1,0:T(8,128)(2,1)} %get-tuple-element.541.refs_1_.refs_3_, bf16[1024,768]{1,0:T(8,128)(2,1)} %get-tuple-element.542.refs_2_.refs_4_, bf16[1024,768]{1,0:T(8,128)(2,1)} %get-tuple-element.541.refs_1_.refs_3_, ...), custom_call_target="tpu_custom_call" | custom-call | flops 999999995904 | bytes 1 | tf_op jit(solution)/shard_map/qkv_in/pallas_call | solution.py:89
  670.3 16.1 %down_grad.3.refs_2_ = bf16[2,512,2048]{2,1,0:T(8,128)(2,1)} custom-call(s32[6]{0:T(128)} %stack.45.refs_0_, bf16[1024,2048]{1,0:T(8,128)(2,1)} %join.10.refs_6_.refs_1_.refs_5_.refs_2_.refs_3_.refs_4_, bf16[1024,2048]{1,0:T(8,128)(2,1)} %join.10.refs_6_.refs_1_.refs_5_.refs_2_.refs_3_.refs_4_, ...), custom_call_target="tpu_custom_call" | custom-call | flops 999999995904 | bytes 1 | tf_op jit(solution)/shard_map/down_grad/pallas_call | solution.py:89
  700.4 21.8 %head_grad.2.refs_1_ = bf16[2,512,2048]{2,1,0:T(8,128)(2,1)} custom-call(s32[6]{0:T(128)} %stack.45.refs_0_, bf16[1024,2048]{1,0:T(8,128)(2,1)} %get-tuple-element.278.refs_3_.refs_0_.refs_1_.refs_2_.refs_4_, bf16[1024,2048]{1,0:T(8,128)(2,1)} %get-tuple-element.278.refs_3_.refs_0_.refs_1_.refs_2_.refs_4_, ...), custom_call_target="tpu_custom_call" | custom-call | flops 999999995904 | bytes 1 | tf_op jit(solution)/shard_map/head_grad/pallas_call | solution.py:89
  730.0 11.3 %qkv_in.3 = (bf16[512,2048]{1,0:T(8,128)(2,1)}, bf16[512,2048]{1,0:T(8,128)(2,1)}) custom-call(s32[6]{0:T(128)} %stack.45.refs_0_, bf16[1024,768]{1,0:T(8,128)(2,1)} %get-tuple-element.543.refs_1_.refs_3_, bf16[1024,768]{1,0:T(8,128)(2,1)} %get-tuple-element.544.refs_2_.refs_4_, bf16[1024,768]{1,0:T(8,128)(2,1)} %get-tuple-element.543.refs_1_.refs_3_, ...), custom_call_target="tpu_custom_call" | custom-call | flops 999999995904 | bytes 1 | tf_op jit(solution)/shard_map/qkv_in/pallas_call | solution.py:89
  741.7 21.5 %head_grad.3.refs_7_ = bf16[2,512,2048]{2,1,0:T(8,128)(2,1)} custom-call(s32[6]{0:T(128)} %stack.45.refs_0_, bf16[1024,2048]{1,0:T(8,128)(2,1)} %get-tuple-element.278.refs_3_.refs_0_.refs_1_.refs_2_.refs_4_, bf16[1024,2048]{1,0:T(8,128)(2,1)} %get-tuple-element.278.refs_3_.refs_0_.refs_1_.refs_2_.refs_4_, ...), custom_call_target="tpu_custom_call" | custom-call | flops 999999995904 | bytes 1 | tf_op jit(solution)/shard_map/head_grad/pallas_call | solution.py:89
  763.2 14.7 %collective-permute-done.54.refs_3_ = bf16[512,2048]{1,0:T(8,128)(2,1)} collective-permute-done((bf16[512,2048]{1,0:T(8,128)(2,1)}, bf16[512,2048]{1,0:T(8,128)(2,1)}, u32[]{:S(2)}, u32[]{:S(2)}) %collective-permute-start.54) | collective-permute-done | bytes 2097184 | tf_op jit(solution)/shard_map/ppermute | solution.py:570
  777.9 9.3 input_back.1
  801.2 6.3 all_to_all.36.refs_1_
  808.9 13.8 %down.3 = (bf16[512,2048]{1,0:T(8,128)(2,1)}, bf16[512,2048]{1,0:T(8,128)(2,1)}) custom-call(s32[6]{0:T(128)} %stack.45.refs_0_, bf16[1024,1024]{1,0:T(8,128)(2,1)} %get-tuple-element.353.refs_4_.refs_11_.refs_1_.refs_3_, bf16[1024,1024]{1,0:T(8,128)(2,1)} %get-tuple-element.357.refs_13_.refs_12_.refs_2_.refs_4_, ...), custom_call_target="tpu_custom_call" | custom-call | flops 999999995904 | bytes 1 | tf_op jit(solution)/shard_map/down/pallas_call | solution.py:89
  853.0 18.0 %collective-permute-done.62.refs_2_ = bf16[2,256,2048]{2,1,0:T(8,128)(2,1)} collective-permute-done((bf16[2,256,2048]{2,1,0:T(8,128)(2,1)}, bf16[2,256,2048]{2,1,0:T(8,128)(2,1)}, u32[]{:S(2)}, u32[]{:S(2)}) %collective-permute-start.62) | collective-permute-done | bytes 2097184 | tf_op jit(solution)/shard_map/ppermute | solution.py:591
  873.0 32.1 %collective-permute-done.61.refs_2_ = bf16[512,2048]{1,0:T(8,128)(2,1)} collective-permute-done((bf16[512,2048]{1,0:T(8,128)(2,1)}, bf16[512,2048]{1,0:T(8,128)(2,1)}, u32[]{:S(2)}, u32[]{:S(2)}) %collective-permute-start.61) | collective-permute-done | bytes 2097184 | tf_op jit(solution)/shard_map/ppermute | solution.py:570
  912.7 10.3 %finish.3 = (f32[1024,2048]{1,0:T(8,128)}, f32[1024,2048]{1,0:T(8,128)}) custom-call(s32[6]{0:T(128)} %stack.45.refs_0_, bf16[2,256,2048]{2,1,0:T(8,128)(2,1)} %all_to_all.36.refs_1_, bf16[2,256,2048]{2,1,0:T(8,128)(2,1)} %collective-permute-done.62.refs_2_, bf16[2,256,2048]{2,1,0:T(8,128)(2,1)} %collective-permute-done.69.refs_3_, ...), custom_call_target="tpu_custom_call" | custom-call | flops 999999995904 | bytes 1 | tf_op jit(solution)/shard_map/finish/pallas_call | solution.py:89
  941.7 19.3 %collective-permute-done.76.refs_4_ = bf16[2,256,1024]{2,1,0:T(8,128)(2,1)} collective-permute-done((bf16[2,256,1024]{2,1,0:T(8,128)(2,1)}, bf16[2,256,1024]{2,1,0:T(8,128)(2,1)}, u32[]{:S(2)}, u32[]{:S(2)}) %collective-permute-start.76) | collective-permute-done | bytes 1048608 | tf_op jit(solution)/shard_map/ppermute | solution.py:591
  960.9 7.0 finish.4.refs_7_
  974.0 10.2 %collective-permute-done.78 = f32[2,2048]{1,0:T(2,128)S(1)} collective-permute-done((f32[2,2048]{1,0:T(2,128)S(1)}, f32[2,2048]{1,0:T(2,128)S(1)}, u32[]{:S(2)}, u32[]{:S(2)}) %collective-permute-start.78) | collective-permute-done | bytes 16416 | tf_op jit(solution)/shard_map/ppermute | solution.py:591
  985.9 6.6 finish.5
  (293 shorter events, 313.3 us)
Async XLA Ops:
  0.6 38.3 %collective-permute-start = (bf16[1024,1024]{1,0:T(8,128)(2,1)}, bf16[1024,1024]{1,0:T(8,128)(2,1)}, u32[]{:S(2)}, u32[]{:S(2)}) collective-permute-start(bf16[1024,1024]{1,0:T(8,128)(2,1)} %refs_1_.16), channel_id=1, source_target_pairs={{0,4},{4,0},{1,5},{5,1},{2,6},{6,2},{3,7},{7,3},{8,12},{12,8},{9,1... | collective-permute-start | bytes 6291464 | tf_op jit(solution)/shard_map/ppermute | solution.py:570
  1.2 71.7 %collective-permute-start.6 = (bf16[1024,1024]{1,0:T(8,128)(2,1)}, bf16[1024,1024]{1,0:T(8,128)(2,1)}, u32[]{:S(2)}, u32[]{:S(2)}) collective-permute-start(bf16[1024,1024]{1,0:T(8,128)(2,1)} %refs_1_.16), channel_id=1, source_target_pairs={{0,1},{1,0},{2,3},{3,2},{4,5},{5,4},{6,7},{7,6},{8,9},{9,8},{10,11... | collective-permute-start | bytes 6291464 | tf_op jit(solution)/shard_map/ppermute | solution.py:570
  5.1 22.8 %collective-permute-start.3 = (f32[2,1024]{1,0:T(2,128)}, f32[2,1024]{1,0:T(2,128)}, u32[]{:S(2)}, u32[]{:S(2)}) collective-permute-start(f32[2,1024]{1,0:T(2,128)} %pad_maximum_fusion.6), channel_id=1, source_target_pairs={{0,4},{4,0},{1,5},{5,1},{2,6},{6,2},{3,7},{7,3},{8,12},{12,8},{9,1... | collective-permute-start | bytes 24584 | tf_op jit(solution)/shard_map/ppermute | solution.py:570
  25.2 57.3 %collective-permute-start.7 = (bf16[512,1024]{1,0:T(8,128)(2,1)}, bf16[512,1024]{1,0:T(8,128)(2,1)}, u32[]{:S(2)}, u32[]{:S(2)}) collective-permute-start(bf16[512,1024]{1,0:T(8,128)(2,1)} %quarter.3.refs_4_), channel_id=1, source_target_pairs={{0,2},{1,3},{2,0},{3,1},{4,6},{5,7},{6,4},{7,5},{8,10},{9,11},{10,... | collective-permute-start | bytes 3145736 | tf_op jit(solution)/shard_map/ppermute | solution.py:570
  82.5 37.6 %collective-permute-start.9 = (bf16[512,1024]{1,0:T(8,128)(2,1)}, bf16[512,1024]{1,0:T(8,128)(2,1)}, u32[]{:S(2)}, u32[]{:S(2)}) collective-permute-start(bf16[512,1024]{1,0:T(8,128)(2,1)} %collective-permute-done.7.refs_1_), channel_id=1, source_target_pairs={{0,16},{4,12},{8,24},{12,4},{16,0},{20,28},{24,8},{28,20},{1,17},{... | collective-permute-start | bytes 3145736 | tf_op jit(solution)/shard_map/ppermute | solution.py:591
  84.3 24.2 %collective-permute-start.8 = (bf16[512,1024]{1,0:T(8,128)(2,1)}, bf16[512,1024]{1,0:T(8,128)(2,1)}, u32[]{:S(2)}, u32[]{:S(2)}) collective-permute-start(bf16[512,1024]{1,0:T(8,128)(2,1)} %collective-permute-done.7.refs_1_), channel_id=1, source_target_pairs={{0,8},{4,20},{8,0},{12,28},{16,24},{20,4},{24,16},{28,12},{1,9},{5... | collective-permute-start | bytes 3145736 | tf_op jit(solution)/shard_map/ppermute | solution.py:591
  85.8 78.7 %collective-permute-start.12 = (bf16[384,2048]{1,0:T(8,128)(2,1)}, bf16[384,2048]{1,0:T(8,128)(2,1)}, u32[]{:S(2)}, u32[]{:S(2)}) collective-permute-start(bf16[384,2048]{1,0:T(8,128)(2,1)} %quarter.4.refs_3_), channel_id=1, source_target_pairs={{0,2},{1,3},{2,0},{3,1},{4,6},{5,7},{6,4},{7,5},{8,10},{9,11},{10,... | collective-permute-start | bytes 4718600 | tf_op jit(solution)/shard_map/ppermute | solution.py:570
  162.8 82.0 %collective-permute-start.16 = (bf16[512,2048]{1,0:T(8,128)(2,1)}, bf16[512,2048]{1,0:T(8,128)(2,1)}, u32[]{:S(2)}, u32[]{:S(2)}) collective-permute-start(bf16[512,2048]{1,0:T(8,128)(2,1)} %add_convert_fusion.7.refs_1_), channel_id=1, source_target_pairs={{0,1},{1,0},{2,3},{3,2},{4,5},{5,4},{6,7},{7,6},{8,9},{9,8},{10,11... | collective-permute-start | bytes 6291464 | tf_op jit(solution)/shard_map/ppermute | solution.py:570
  164.5 88.9 %collective-permute-start.20 = (bf16[384,2048]{1,0:T(8,128)(2,1)}, bf16[384,2048]{1,0:T(8,128)(2,1)}, u32[]{:S(2)}, u32[]{:S(2)}) collective-permute-start(bf16[384,2048]{1,0:T(8,128)(2,1)} %quarter.5.refs_5_), channel_id=1, source_target_pairs={{0,2},{1,3},{2,0},{3,1},{4,6},{5,7},{6,4},{7,5},{8,10},{9,11},{10,... | collective-permute-start | bytes 4718600 | tf_op jit(solution)/shard_map/ppermute | solution.py:570
  168.3 114.7 %collective-permute-start.25 = (bf16[384,2048]{1,0:T(8,128)(2,1)}, bf16[384,2048]{1,0:T(8,128)(2,1)}, u32[]{:S(2)}, u32[]{:S(2)}) collective-permute-start(bf16[384,2048]{1,0:T(8,128)(2,1)} %collective-permute-done.12.refs_1_), channel_id=1, source_target_pairs={{0,16},{4,12},{8,24},{12,4},{16,0},{20,28},{24,8},{28,20},{1,17},{... | collective-permute-start | bytes 4718600 | tf_op jit(solution)/shard_map/ppermute | solution.py:591
  169.8 35.1 %collective-permute-start.18 = (bf16[384,2048]{1,0:T(8,128)(2,1)}, bf16[384,2048]{1,0:T(8,128)(2,1)}, u32[]{:S(2)}, u32[]{:S(2)}) collective-permute-start(bf16[384,2048]{1,0:T(8,128)(2,1)} %collective-permute-done.12.refs_1_), channel_id=1, source_target_pairs={{0,8},{4,20},{8,0},{12,28},{16,24},{20,4},{24,16},{28,12},{1,9},{5... | collective-permute-start | bytes 4718600 | tf_op jit(solution)/shard_map/ppermute | solution.py:591
  171.3 34.7 %collective-permute-start.17 = (bf16[1024,1024]{1,0:T(8,128)(2,1)}, bf16[1024,1024]{1,0:T(8,128)(2,1)}, u32[]{:S(2)}, u32[]{:S(2)}) collective-permute-start(bf16[1024,1024]{1,0:T(8,128)(2,1)} %refs_1_.19), channel_id=1, source_target_pairs={{0,4},{4,0},{1,5},{5,1},{2,6},{6,2},{3,7},{7,3},{8,12},{12,8},{9,1... | collective-permute-start | bytes 6291464 | tf_op jit(solution)/shard_map/ppermute | solution.py:570
  204.9 39.9 %collective-permute-start.15 = (bf16[512,2048]{1,0:T(8,128)(2,1)}, bf16[512,2048]{1,0:T(8,128)(2,1)}, u32[]{:S(2)}, u32[]{:S(2)}) collective-permute-start(bf16[512,2048]{1,0:T(8,128)(2,1)} %get-tuple-element.323.refs_3_), channel_id=1, source_target_pairs={{0,4},{4,0},{1,5},{5,1},{2,6},{6,2},{3,7},{7,3},{8,12},{12,8},{9,1... | collective-permute-start | bytes 6291464 | tf_op jit(solution)/shard_map/ppermute | solution.py:570
  206.0 77.0 %collective-permute-start.26 = (bf16[384,2048]{1,0:T(8,128)(2,1)}, bf16[384,2048]{1,0:T(8,128)(2,1)}, u32[]{:S(2)}, u32[]{:S(2)}) collective-permute-start(bf16[384,2048]{1,0:T(8,128)(2,1)} %collective-permute-done.18.refs_2_), channel_id=1, source_target_pairs={{0,16},{4,12},{8,24},{12,4},{16,0},{20,28},{24,8},{28,20},{1,17},{... | collective-permute-start | bytes 4718600 | tf_op jit(solution)/shard_map/ppermute | solution.py:591
  253.4 47.9 %collective-permute-start.24 = (bf16[512,2048]{1,0:T(8,128)(2,1)}, bf16[512,2048]{1,0:T(8,128)(2,1)}, u32[]{:S(2)}, u32[]{:S(2)}) collective-permute-start(bf16[512,2048]{1,0:T(8,128)(2,1)} %get-tuple-element.324.refs_1_), channel_id=1, source_target_pairs={{0,1},{1,0},{2,3},{3,2},{4,5},{5,4},{6,7},{7,6},{8,9},{9,8},{10,11... | collective-permute-start | bytes 6291464 | tf_op jit(solution)/shard_map/ppermute | solution.py:570
  253.4 56.7 %collective-permute-start.23 = (bf16[384,2048]{1,0:T(8,128)(2,1)}, bf16[384,2048]{1,0:T(8,128)(2,1)}, u32[]{:S(2)}, u32[]{:S(2)}) collective-permute-start(bf16[384,2048]{1,0:T(8,128)(2,1)} %collective-permute-done.20.refs_1_), channel_id=1, source_target_pairs={{0,16},{4,12},{8,24},{12,4},{16,0},{20,28},{24,8},{28,20},{1,17},{... | collective-permute-start | bytes 4718600 | tf_op jit(solution)/shard_map/ppermute | solution.py:591
  256.3 45.0 %collective-permute-start.22 = (bf16[384,2048]{1,0:T(8,128)(2,1)}, bf16[384,2048]{1,0:T(8,128)(2,1)}, u32[]{:S(2)}, u32[]{:S(2)}) collective-permute-start(bf16[384,2048]{1,0:T(8,128)(2,1)} %collective-permute-done.20.refs_1_), channel_id=1, source_target_pairs={{0,8},{4,20},{8,0},{12,28},{16,24},{20,4},{24,16},{28,12},{1,9},{5... | collective-permute-start | bytes 4718600 | tf_op jit(solution)/shard_map/ppermute | solution.py:591
  302.6 20.7 %collective-permute-start.27 = (bf16[384,2048]{1,0:T(8,128)(2,1)}, bf16[384,2048]{1,0:T(8,128)(2,1)}, u32[]{:S(2)}, u32[]{:S(2)}) collective-permute-start(bf16[384,2048]{1,0:T(8,128)(2,1)} %collective-permute-done.22.refs_2_), channel_id=1, source_target_pairs={{0,16},{4,12},{8,24},{12,4},{16,0},{20,28},{24,8},{28,20},{1,17},{... | collective-permute-start | bytes 4718600 | tf_op jit(solution)/shard_map/ppermute | solution.py:591
  304.3 59.6 %collective-permute-start.30 = (bf16[1024,1024]{1,0:T(8,128)(2,1)}, bf16[1024,1024]{1,0:T(8,128)(2,1)}, u32[]{:S(2)}, u32[]{:S(2)}) collective-permute-start(bf16[1024,1024]{1,0:T(8,128)(2,1)} %refs_1_.19), channel_id=1, source_target_pairs={{0,1},{1,0},{2,3},{3,2},{4,5},{5,4},{6,7},{7,6},{8,9},{9,8},{10,11... | collective-permute-start | bytes 6291464 | tf_op jit(solution)/shard_map/ppermute | solution.py:570
  363.9 107.9 %collective-permute-start.29 = (bf16[512,2048]{1,0:T(8,128)(2,1)}, bf16[512,2048]{1,0:T(8,128)(2,1)}, u32[]{:S(2)}, u32[]{:S(2)}) collective-permute-start(bf16[512,2048]{1,0:T(8,128)(2,1)} %get-tuple-element.351.refs_1_), channel_id=1, source_target_pairs={{0,4},{4,0},{1,5},{5,1},{2,6},{6,2},{3,7},{7,3},{8,12},{12,8},{9,1... | collective-permute-start | bytes 6291464 | tf_op jit(solution)/shard_map/ppermute | solution.py:570
  443.7 109.3 %collective-permute-start.39 = (bf16[2,512,4096]{2,1,0:T(8,128)(2,1)}, bf16[2,512,4096]{2,1,0:T(8,128)(2,1)}, u32[]{:S(2)}, u32[]{:S(2)}) collective-permute-start(bf16[2,512,4096]{2,1,0:T(8,128)(2,1)} %gu_grad.2.refs_1_), channel_id=1, source_target_pairs={{0,8},{4,20},{8,0},{12,28},{16,24},{20,4},{24,16},{28,12},{1,9},{5... | collective-permute-start | bytes 25165832 | tf_op jit(solution)/shard_map/ppermute | solution.py:591
  481.0 52.6 %collective-permute-start.36 = (bf16[512,2048]{1,0:T(8,128)(2,1)}, bf16[512,2048]{1,0:T(8,128)(2,1)}, u32[]{:S(2)}, u32[]{:S(2)}) collective-permute-start(bf16[512,2048]{1,0:T(8,128)(2,1)} %add_convert_fusion.5.refs_1_), channel_id=1, source_target_pairs={{0,1},{1,0},{2,3},{3,2},{4,5},{5,4},{6,7},{7,6},{8,9},{9,8},{10,11... | collective-permute-start | bytes 6291464 | tf_op jit(solution)/shard_map/ppermute | solution.py:570
  507.2 26.4 %collective-permute-start.35 = (bf16[512,2048]{1,0:T(8,128)(2,1)}, bf16[512,2048]{1,0:T(8,128)(2,1)}, u32[]{:S(2)}, u32[]{:S(2)}) collective-permute-start(bf16[512,2048]{1,0:T(8,128)(2,1)} %get-tuple-element.371.refs_13_), channel_id=1, source_target_pairs={{0,4},{4,0},{1,5},{5,1},{2,6},{6,2},{3,7},{7,3},{8,12},{12,8},{9,1... | collective-permute-start | bytes 6291464 | tf_op jit(solution)/shard_map/ppermute | solution.py:570
  542.5 49.0 %collective-permute-start.41 = (bf16[512,2048]{1,0:T(8,128)(2,1)}, bf16[512,2048]{1,0:T(8,128)(2,1)}, u32[]{:S(2)}, u32[]{:S(2)}) collective-permute-start(bf16[512,2048]{1,0:T(8,128)(2,1)} %get-tuple-element.372.refs_1_), channel_id=1, source_target_pairs={{0,1},{1,0},{2,3},{3,2},{4,5},{5,4},{6,7},{7,6},{8,9},{9,8},{10,11... | collective-permute-start | bytes 6291464 | tf_op jit(solution)/shard_map/ppermute | solution.py:570
  558.6 51.7 %collective-permute-start.43 = (bf16[512,4096]{1,0:T(8,128)(2,1)}, bf16[512,4096]{1,0:T(8,128)(2,1)}, u32[]{:S(2)}, u32[]{:S(2)}) collective-permute-start(bf16[512,4096]{1,0:T(8,128)(2,1)} %fusion.refs_1_), channel_id=1, source_target_pairs={{0,16},{4,12},{8,24},{12,4},{16,0},{20,28},{24,8},{28,20},{1,17},{... | collective-permute-start | bytes 12582920 | tf_op jit(solution)/shard_map/ppermute | solution.py:591
  608.1 78.5 %collective-permute-start.47 = (bf16[2,512,2048]{2,1,0:T(8,128)(2,1)}, bf16[2,512,2048]{2,1,0:T(8,128)(2,1)}, u32[]{:S(2)}, u32[]{:S(2)}) collective-permute-start(bf16[2,512,2048]{2,1,0:T(8,128)(2,1)} %down_grad.2.refs_2_), channel_id=1, source_target_pairs={{0,8},{4,20},{8,0},{12,28},{16,24},{20,4},{24,16},{28,12},{1,9},{5... | collective-permute-start | bytes 12582920 | tf_op jit(solution)/shard_map/ppermute | solution.py:591
  615.9 179.1 %collective-permute-start.55 = (bf16[512,2048]{1,0:T(8,128)(2,1)}, bf16[512,2048]{1,0:T(8,128)(2,1)}, u32[]{:S(2)}, u32[]{:S(2)}) collective-permute-start(bf16[512,2048]{1,0:T(8,128)(2,1)} %fusion.3.refs_1_), channel_id=1, source_target_pairs={{0,2},{1,3},{2,0},{3,1},{4,6},{5,7},{6,4},{7,5},{8,10},{9,11},{10,... | collective-permute-start | bytes 6291464 | tf_op jit(solution)/shard_map/ppermute | solution.py:570
  691.0 33.3 %collective-permute-start.51 = (bf16[512,2048]{1,0:T(8,128)(2,1)}, bf16[512,2048]{1,0:T(8,128)(2,1)}, u32[]{:S(2)}, u32[]{:S(2)}) collective-permute-start(bf16[512,2048]{1,0:T(8,128)(2,1)} %fusion.4.refs_1_), channel_id=1, source_target_pairs={{0,16},{4,12},{8,24},{12,4},{16,0},{20,28},{24,8},{28,20},{1,17},{... | collective-permute-start | bytes 6291464 | tf_op jit(solution)/shard_map/ppermute | solution.py:591
  697.8 80.1 %collective-permute-start.54 = (bf16[512,2048]{1,0:T(8,128)(2,1)}, bf16[512,2048]{1,0:T(8,128)(2,1)}, u32[]{:S(2)}, u32[]{:S(2)}) collective-permute-start(bf16[512,2048]{1,0:T(8,128)(2,1)} %add_convert_fusion.3.refs_1_), channel_id=1, source_target_pairs={{0,1},{1,0},{2,3},{3,2},{4,5},{5,4},{6,7},{7,6},{8,9},{9,8},{10,11... | collective-permute-start | bytes 6291464 | tf_op jit(solution)/shard_map/ppermute | solution.py:570
  722.3 67.0 %collective-permute-start.56 = (bf16[2,512,2048]{2,1,0:T(8,128)(2,1)}, bf16[2,512,2048]{2,1,0:T(8,128)(2,1)}, u32[]{:S(2)}, u32[]{:S(2)}) collective-permute-start(bf16[2,512,2048]{2,1,0:T(8,128)(2,1)} %head_grad.2.refs_1_), channel_id=1, source_target_pairs={{0,8},{4,20},{8,0},{12,28},{16,24},{20,4},{24,16},{28,12},{1,9},{5... | collective-permute-start | bytes 12582920 | tf_op jit(solution)/shard_map/ppermute | solution.py:591
  727.8 114.9 %collective-permute-start.63 = (bf16[512,1024]{1,0:T(8,128)(2,1)}, bf16[512,1024]{1,0:T(8,128)(2,1)}, u32[]{:S(2)}, u32[]{:S(2)}) collective-permute-start(bf16[512,1024]{1,0:T(8,128)(2,1)} %fusion.11.refs_1_), channel_id=1, source_target_pairs={{0,2},{1,3},{2,0},{3,1},{4,6},{5,7},{6,4},{7,5},{8,10},{9,11},{10,... | collective-permute-start | bytes 3145736 | tf_op jit(solution)/shard_map/ppermute | solution.py:570
  741.2 36.7 %collective-permute-start.53 = (bf16[512,2048]{1,0:T(8,128)(2,1)}, bf16[512,2048]{1,0:T(8,128)(2,1)}, u32[]{:S(2)}, u32[]{:S(2)}) collective-permute-start(bf16[512,2048]{1,0:T(8,128)(2,1)} %get-tuple-element.431.refs_33_), channel_id=1, source_target_pairs={{0,4},{4,0},{1,5},{5,1},{2,6},{6,2},{3,7},{7,3},{8,12},{12,8},{9,1... | collective-permute-start | bytes 6291464 | tf_op jit(solution)/shard_map/ppermute | solution.py:570
  788.7 18.8 %collective-permute-start.58 = (f32[2,2048]{1,0:T(2,128)}, f32[2,2048]{1,0:T(2,128)}, u32[]{:S(2)}, u32[]{:S(2)}) collective-permute-start(f32[2,2048]{1,0:T(2,128)} %pad_maximum_fusion.5.refs_2_), channel_id=1, source_target_pairs={{0,4},{4,0},{1,5},{5,1},{2,6},{6,2},{3,7},{7,3},{8,12},{12,8},{9,1... | collective-permute-start | bytes 49160 | tf_op jit(solution)/shard_map/ppermute | solution.py:570
  788.8 34.0 %collective-permute-start.60 = (f32[512,1024]{1,0:T(8,128)}, f32[512,1024]{1,0:T(8,128)}, u32[]{:S(2)}, u32[]{:S(2)}) collective-permute-start(f32[512,1024]{1,0:T(8,128)} %get-tuple-element.462), channel_id=1, source_target_pairs={{0,4},{4,0},{1,5},{5,1},{2,6},{6,2},{3,7},{7,3},{8,12},{12,8},{9,1... | collective-permute-start | bytes 6291464 | tf_op jit(solution)/shard_map/ppermute | solution.py:570
  795.0 43.0 %collective-permute-start.66 = (bf16[512,2048]{1,0:T(8,128)(2,1)}, bf16[512,2048]{1,0:T(8,128)(2,1)}, u32[]{:S(2)}, u32[]{:S(2)}) collective-permute-start(bf16[512,2048]{1,0:T(8,128)(2,1)} %fusion.5.refs_1_), channel_id=1, source_target_pairs={{0,16},{4,12},{8,24},{12,4},{16,0},{20,28},{24,8},{28,20},{1,17},{... | collective-permute-start | bytes 6291464 | tf_op jit(solution)/shard_map/ppermute | solution.py:591
  808.9 25.8 %collective-permute-start.65 = (f32[2,2048]{1,0:T(2,128)}, f32[2,2048]{1,0:T(2,128)}, u32[]{:S(2)}, u32[]{:S(2)}) collective-permute-start(f32[2,2048]{1,0:T(2,128)} %add.147.refs_7_), channel_id=1, source_target_pairs={{0,1},{1,0},{2,3},{3,2},{4,5},{5,4},{6,7},{7,6},{8,9},{9,8},{10,11... | collective-permute-start | bytes 49160 | tf_op jit(solution)/shard_map/ppermute | solution.py:570
  822.8 89.5 %collective-permute-start.69 = (bf16[2,256,2048]{2,1,0:T(8,128)(2,1)}, bf16[2,256,2048]{2,1,0:T(8,128)(2,1)}, u32[]{:S(2)}, u32[]{:S(2)}) collective-permute-start(bf16[2,256,2048]{2,1,0:T(8,128)(2,1)} %all_to_all.36.refs_1_), channel_id=1, source_target_pairs={{0,16},{4,12},{8,24},{12,4},{16,0},{20,28},{24,8},{28,20},{1,17},{... | collective-permute-start | bytes 6291464 | tf_op jit(solution)/shard_map/ppermute | solution.py:591
  834.1 36.9 %collective-permute-start.62 = (bf16[2,256,2048]{2,1,0:T(8,128)(2,1)}, bf16[2,256,2048]{2,1,0:T(8,128)(2,1)}, u32[]{:S(2)}, u32[]{:S(2)}) collective-permute-start(bf16[2,256,2048]{2,1,0:T(8,128)(2,1)} %all_to_all.36.refs_1_), channel_id=1, source_target_pairs={{0,8},{4,20},{8,0},{12,28},{16,24},{20,4},{24,16},{28,12},{1,9},{5... | collective-permute-start | bytes 6291464 | tf_op jit(solution)/shard_map/ppermute | solution.py:591
  834.7 70.4 %collective-permute-start.61 = (bf16[512,2048]{1,0:T(8,128)(2,1)}, bf16[512,2048]{1,0:T(8,128)(2,1)}, u32[]{:S(2)}, u32[]{:S(2)}) collective-permute-start(bf16[512,2048]{1,0:T(8,128)(2,1)} %add_convert_fusion.1.refs_1_), channel_id=1, source_target_pairs={{0,1},{1,0},{2,3},{3,2},{4,5},{5,4},{6,7},{7,6},{8,9},{9,8},{10,11... | collective-permute-start | bytes 6291464 | tf_op jit(solution)/shard_map/ppermute | solution.py:570
  842.7 81.7 %collective-permute-start.73 = (bf16[512,1024]{1,0:T(8,128)(2,1)}, bf16[512,1024]{1,0:T(8,128)(2,1)}, u32[]{:S(2)}, u32[]{:S(2)}) collective-permute-start(bf16[512,1024]{1,0:T(8,128)(2,1)} %fusion.8.refs_1_), channel_id=1, source_target_pairs={{0,2},{1,3},{2,0},{3,1},{4,6},{5,7},{6,4},{7,5},{8,10},{9,11},{10,... | collective-permute-start | bytes 3145736 | tf_op jit(solution)/shard_map/ppermute | solution.py:570
  848.6 22.4 %all-to-all-start.1 = ((bf16[2,256,1024]{2,1,0:T(8,128)(2,1)}), bf16[2,256,1024]{2,1,0:T(8,128)(2,1)}, u32[]{:S(2)}, u32[]{:S(2)}) async-start(bf16[2,256,1024]{2,1,0:T(8,128)(2,1)} %bitcast.20), calls=%async_computation.1 | async-start | bytes 2097152 | tf_op jit(solution)/shard_map/all_to_all | solution.py:69
  871.0 41.7 %collective-permute-start.70 = (bf16[2,256,2048]{2,1,0:T(8,128)(2,1)}, bf16[2,256,2048]{2,1,0:T(8,128)(2,1)}, u32[]{:S(2)}, u32[]{:S(2)}) collective-permute-start(bf16[2,256,2048]{2,1,0:T(8,128)(2,1)} %collective-permute-done.62.refs_2_), channel_id=1, source_target_pairs={{0,16},{4,12},{8,24},{12,4},{16,0},{20,28},{24,8},{28,20},{1,17},{... | collective-permute-start | bytes 6291464 | tf_op jit(solution)/shard_map/ppermute | solution.py:591
  872.4 69.3 %collective-permute-start.75 = (bf16[2,256,1024]{2,1,0:T(8,128)(2,1)}, bf16[2,256,1024]{2,1,0:T(8,128)(2,1)}, u32[]{:S(2)}, u32[]{:S(2)}) collective-permute-start(bf16[2,256,1024]{2,1,0:T(8,128)(2,1)} %all-to-all-done.1.refs_1_), channel_id=1, source_target_pairs={{0,16},{4,12},{8,24},{12,4},{16,0},{20,28},{24,8},{28,20},{1,17},{... | collective-permute-start | bytes 3145736 | tf_op jit(solution)/shard_map/ppermute | solution.py:591
  905.1 27.8 %collective-permute-start.72 = (bf16[2,256,1024]{2,1,0:T(8,128)(2,1)}, bf16[2,256,1024]{2,1,0:T(8,128)(2,1)}, u32[]{:S(2)}, u32[]{:S(2)}) collective-permute-start(bf16[2,256,1024]{2,1,0:T(8,128)(2,1)} %all-to-all-done.1.refs_1_), channel_id=1, source_target_pairs={{0,8},{4,20},{8,0},{12,28},{16,24},{20,4},{24,16},{28,12},{1,9},{5... | collective-permute-start | bytes 3145736 | tf_op jit(solution)/shard_map/ppermute | solution.py:591
  912.7 25.7 %collective-permute-start.68 = (bf16[512,1024]{1,0:T(8,128)(2,1)}, bf16[512,1024]{1,0:T(8,128)(2,1)}, u32[]{:S(2)}, u32[]{:S(2)}) collective-permute-start(bf16[512,1024]{1,0:T(8,128)(2,1)} %get-tuple-element.494), channel_id=1, source_target_pairs={{0,4},{4,0},{1,5},{5,1},{2,6},{6,2},{3,7},{7,3},{8,12},{12,8},{9,1... | collective-permute-start | bytes 3145736 | tf_op jit(solution)/shard_map/ppermute | solution.py:570
  935.1 25.8 %collective-permute-start.76 = (bf16[2,256,1024]{2,1,0:T(8,128)(2,1)}, bf16[2,256,1024]{2,1,0:T(8,128)(2,1)}, u32[]{:S(2)}, u32[]{:S(2)}) collective-permute-start(bf16[2,256,1024]{2,1,0:T(8,128)(2,1)} %collective-permute-done.72.refs_2_), channel_id=1, source_target_pairs={{0,16},{4,12},{8,24},{12,4},{16,0},{20,28},{24,8},{28,20},{1,17},{... | collective-permute-start | bytes 3145736 | tf_op jit(solution)/shard_map/ppermute | solution.py:591
  936.7 48.2 %collective-permute-start.79 = (bf16[2,256,1024]{2,1,0:T(8,128)(2,1)}, bf16[2,256,1024]{2,1,0:T(8,128)(2,1)}, u32[]{:S(2)}, u32[]{:S(2)}) collective-permute-start(bf16[2,256,1024]{2,1,0:T(8,128)(2,1)} %all-to-all-done.2.refs_1_), channel_id=1, source_target_pairs={{0,16},{4,12},{8,24},{12,4},{16,0},{20,28},{24,8},{28,20},{1,17},{... | collective-permute-start | bytes 3145736 | tf_op jit(solution)/shard_map/ppermute | solution.py:591
  937.2 30.7 %collective-permute-start.74 = (bf16[2,256,1024]{2,1,0:T(8,128)(2,1)}, bf16[2,256,1024]{2,1,0:T(8,128)(2,1)}, u32[]{:S(2)}, u32[]{:S(2)}) collective-permute-start(bf16[2,256,1024]{2,1,0:T(8,128)(2,1)} %all-to-all-done.2.refs_1_), channel_id=1, source_target_pairs={{0,8},{4,20},{8,0},{12,28},{16,24},{20,4},{24,16},{28,12},{1,9},{5... | collective-permute-start | bytes 3145736 | tf_op jit(solution)/shard_map/ppermute | solution.py:591
  (62 other events, 432.9 us)

commit v2 on v1

--- a/solution.py
+++ b/solution.py
@@ -12,7 +12,7 @@
 EPS = 1e-05
 ROPE_BASE = 130000.0
 VMEM = 60 * 1024 * 1024
-UNIT_TILE = 512
+UNIT_TILE = 256
 QB = 256
 COST = 10**12
 F32 = jnp.float32
@@ -98,10 +98,12 @@
 
 def short_kernel(values):
     def kernel(in_ref, out_ref):
-        out_ref[...] = in_ref[...]
-
-    spec = pl.BlockSpec(values.shape, lambda: (0, 0))
-    return launch(kernel, [values], [spec], "short", grid=(), out_specs=spec, out_shape=of(values.shape, values.dtype))
+        out_ref[0, 0] = 0.0
+
+    return launch(
+        kernel, [values], [pl.BlockSpec(memory_space=pl.ANY)], "short",
+        out_specs=pl.BlockSpec(memory_space=pltpu.SMEM), out_shape=of((1, 1), F32),
+    )
 
 
 def extent(shape, index):
@@ -242,20 +244,20 @@
 
 
 def attend_kernel(q_ref, k_ref, v_ref, o_ref, lse_ref):
-    v_t = v_ref[...].T
+    values = [head_of(v_ref[...], head) for head in range(2)]
     for start in range(0, SEQ_LEN, QB):
         stop = start + QB
         queries = q_ref[start:stop, :]
-        outs = []
+        outs, scales = [], []
         for head in range(2):
             scores = causal_scores(k_ref[:stop, :], head_of(queries, head), start)
             top = jnp.max(scores, axis=0, keepdims=True)
             weights = jnp.exp(scores - top)
             total = jnp.sum(weights, axis=0, keepdims=True)
             lse_ref[0, 0, head : head + 1, start:stop] = top + jnp.log(total)
-            out = dot(v_t[head * HEAD_DIM : (head + 1) * HEAD_DIM, :stop], weights.astype(BF16), 1, 0)
-            outs.append(out / total)
-        o_ref[start:stop, :] = jnp.concatenate(outs, axis=0).T.astype(BF16)
+            outs.append(dot(weights.astype(BF16), values[head][:stop], 0, 0))
+            scales.append(jnp.broadcast_to(1.0 / total, (HEAD_DIM, QB)))
+        o_ref[start:stop, :] = ((outs[0] + outs[1]) * jnp.concatenate(scales, axis=0).T).astype(BF16)
 
 
 def attend(q, k, v):
@@ -695,9 +697,9 @@
 
     def spread(self):
         self.one = self.plan.ship(hop_one, self.both)
-        self.two = self.plan.ship(hop_two, self.both)
 
     def spread_last(self):
+        self.two = self.plan.send(hop_two, self.both)
         self.three = self.plan.send(hop_two, self.one)
 
     def finish(self):
@@ -911,6 +913,7 @@
     o_near_own = run(attend, *near_own)
     qkvo_one, qkvo_two = send(hop_one, qkvo_zero), send(hop_two, qkvo_zero)
     gud_zero[0] = send(far_plane, gud[0])
+    far_cot = send(other_chip, cotangent)
     x_far = join_features(plan, s, far_tokens, far_half)
     normed_far, *far_own = project(x_far, own_qkv, True)
     qkvo_three = send(hop_two, qkvo_one)
@@ -946,9 +949,9 @@
     near = core_sum(plan, [o[0] for o in o_near], w_o, False, "out")
     gud_three[0] = send(hop_two, gud_one[0])
     cot_near = join_features(plan, s, cotangent, near_cot)
-    residual, normed_ffn = norm_first(plan, s, near, far, x_near, gains_ffn)
-    nf_row = ship(other_core, normed_ffn)
-    nf_chip = post(other_chip, normed_ffn)
+    cot_far_row = send(other_core, far_cot)
+    plan.pause()
+    cot_far = join_features(plan, s, far_cot, cot_far_row)
     def spread_out(i, outs):
         count = quarter // 2, down_rows // 2
         return plan.place(
@@ -960,24 +963,23 @@
             "other", len(outs),
         )
 
+    halves = spread_out(0, [])
+    residual, normed_ffn = norm_first(plan, s, near, far, x_near, gains_ffn)
+    nf_row = ship(other_core, normed_ffn)
+    nf_chip = post(other_chip, normed_ffn)
     gud_one[1], gud_two[1] = send(hop_one, gud_zero[1]), send(hop_two, gud_zero[1])
     nf_near = join_rows(plan, s, normed_ffn, nf_row)
     fed_near = [run(ffn, nf_near, cot_near, own_gu, own_d)]
-    halves = spread_out(0, [])
     nf_far_row = send(other_core, nf_chip)
     gud_three[1] = send(hop_two, gud_one[1])
-    far_cot = send(other_chip, cotangent)
     plan.pause()
     nf_far = join_rows(plan, s, nf_chip, nf_far_row)
+    fed_far = [run(ffn, nf_far, cot_far, own_gu, own_d)]
     for_gu, for_d = spread_out(1, list(halves))
     w_gu, w_d = [own_gu, for_gu], [own_d, for_d]
+    fed_far.append(run(ffn, nf_far, cot_far, for_gu, for_d))
     fed_near.append(run(ffn, nf_near, cot_near, for_gu, for_d))
     hid_near, ggu_near = [f[0] for f in fed_near], [f[1] for f in fed_near]
-    mixed_near = core_sum(plan, hid_near, w_d, False, "down")
-    cot_far_row = send(other_core, far_cot)
-    plan.pause()
-    cot_far = join_features(plan, s, far_cot, cot_far_row)
-    fed_far = [run(ffn, nf_far, cot_far, own_gu, own_d), run(ffn, nf_far, cot_far, for_gu, for_d)]
     hid_far, ggu_far = [f[0] for f in fed_far], [f[1] for f in fed_far]
 
     ups = Group("gu_grad", plan, [(nf_near, nf_far)], [0, 0], ggu_near, ggu_far, gu_spans(s), [False, False])
@@ -985,7 +987,6 @@
     ups.make()
     ups.leave()
     far = core_sum(plan, ggu_far, w_gu, True, "ffn_in")
-    mixed_near = [add_pair(plan, mixed_near)]
     plan.pause()
     far = post(other_chip, add_pair(plan, far))
     near = core_sum(plan, ggu_near, w_gu, True, "ffn_in")
@@ -1009,9 +1010,6 @@
     back_far = [back_one(gr_far, far_heads, o_far, b) for b in range(2)]
     dqkv_far = [jnp.concatenate(b, axis=1) for b in back_far]
     far = core_sum(plan, dqkv_far, w_qkv, True, "qkv_in")
-    down.stay()
-    down.second()
-    far = post(other_chip, add_pair(plan, far))
     heads = Group(
         "head_grad", plan, [(normed_near, normed_far), (gr_near, gr_far)], [0, 0, 0, 1] * 2,
         [a for b in range(2) for a in (*back_near[b], o_near[b][0])],
@@ -1020,41 +1018,47 @@
     )
     heads.make()
     heads.leave()
-    down.cross_plane()
+    far = post(other_chip, add_pair(plan, far))
+    down.stay()
+    down.second()
+    ups.total()
     dqkv_near = [jnp.concatenate(b, axis=1) for b in back_near]
     near = core_sum(plan, dqkv_near, w_qkv, True, "qkv_in")
     heads.stay()
+    heads.second()
+    down.cross_plane()
     input_mine, input_other, gain_attn_part = norm_input_back(plan, s, near, far, x_near, grad_residual, gains_attn)
     input_got = ship(other_core, input_other)
     gains = mix(lambda a, b: jnp.stack((jnp.sum(a, axis=0), jnp.sum(b, axis=0))), gain_attn_part, gain_ffn_part)
     gains_got = ship(other_core, gains)
-    heads.second()
-    ups.total()
+    mixed_near = core_sum(plan, hid_near, w_d, False, "down")
+    input_grad = side_by_side(plan, s, input_mine, input_got)
+    gains = mix(jnp.add, gains, gains_got)
+    gains_got = ship(hop_one, gains)
+    heads.cross_plane()
+    mixed_far = core_sum(plan, hid_far, w_d, False, "down")
+    gains = mix(jnp.add, gains, gains_got)
+    gains_got = ship(hop_two, gains)
     ups.spread()
+    plan.pause()
+    mixed_far = post(other_chip, add_pair(plan, mixed_far))
+    down.total()
+    down.spread()
     gains = mix(jnp.add, gains, gains_got)
-    gains_got = send(other_chip, gains)
-    mixed_far = core_sum(plan, hid_far, w_d, False, "down")
-    input_grad = side_by_side(plan, s, input_mine, input_got)
-    mixed_far = post(other_chip, add_pair(plan, mixed_far))
-    gains = mix(jnp.add, gains, gains_got)
-    heads.cross_plane()
-    down.total()
+    gains_got = ship(other_chip, gains)
     ups.spread_last()
-    down.spread()
-    mixed_mine, mixed_other = add_mixed(plan, s, mixed_near, mixed_far, residual)
-    gains_got = send(far_plane, gains)
-    mixed_got = ship(other_core, mixed_other)
-    gate_grad, up_grad = ups.finish()
+    plan.pause()
     gains = mix(jnp.add, gains, gains_got)
     heads.total()
     heads.spread()
     down.spread_last()
-    gains_got = send(hop_one, gains)
+    gains_got = ship(far_plane, gains)
+    gate_grad, up_grad = ups.finish()
+    mixed_mine, mixed_other = add_mixed(plan, s, mixed_near, mixed_far, residual)
+    mixed_got = ship(other_core, mixed_other)
+    heads.spread_last()
+    (down_grad,) = down.finish()
     mixed = side_by_side(plan, s, mixed_mine, mixed_got)
-    (down_grad,) = down.finish()
-    heads.spread_last()
-    gains = mix(jnp.add, gains, gains_got)
-    gains_got = send(hop_two, gains)
     gains = mix(jnp.add, gains, gains_got)
     gains = jnp.where(plan.core == 0, gains[:, : s.split], gains[:, s.split :])
     q_grad, k_grad, v_grad, out_grad = heads.finish()

time: 1000 us -> 955 us (0.955)
  Pallas kernels: 641 us -> 617 us
  waiting for transfers between devices: 192 us -> 173 us
  blocking collectives: 6.3 us -> 17.5 us
  starting transfers between devices: 71.3 us -> 60.3 us
    ppermute x55, waiting for transfers between devices: 106 us -> 79 us  [swap_axis(): return lax.ppermute(values, axis, [(i, i ^ distance) for i in range(size)])]
    pallas_call x83 -> x85, Pallas kernels: 641 us -> 617 us  [launch(): pl.pallas_call(body, out_shape=out_shape, compiler_params=pltpu.CompilerP...]
    all_to_all x1 -> x3, blocking collectives: 6.3 us -> 17.5 us  [swap(): lax.all_to_all(self.tied(value), 'row', split_axis=0, concat_axis=0, tile...]
    ppermute x26, waiting for transfers between devices: 83 us -> 93.6 us  [hop(): return lax.ppermute(values, ('dp', 'row'), pairs)]
  transfers between devices with their start and end apart: 83 -> 81, of which waited for: 24 -> 35; matrix products, arithmetic and copies ran while one was open for 8% -> 8% of each run, Pallas kernels for 64% -> 57%
where the time goes in v2:
time: 955 us; the launch traced here: 944 us
  Pallas kernels  617 us (65%)
  waiting for transfers between devices  173 us (18%)
  other arithmetic  72.6 us (8%)
  starting transfers between devices  60.3 us (6%)
  blocking collectives  17.5 us (2%)
    pallas_call x85, Pallas kernels, launch(): pl.pallas_call(body, out_shape=out_shape, compiler_params=pltpu.CompilerP...  617 us
    ppermute x26, waiting for transfers between devices, hop(): return lax.ppermute(values, ('dp', 'row'), pairs)  93.6 us
    ppermute x55, waiting for transfers between devices, swap_axis(): return lax.ppermute(values, axis, [(i, i ^ distance) for i in range(size)])  79 us
    ppermute x55, starting transfers between devices, swap_axis(): return lax.ppermute(values, axis, [(i, i ^ distance) for i in range(size)])  31.1 us
    ppermute x26, starting transfers between devices, hop(): return lax.ppermute(values, ('dp', 'row'), pairs)  29.2 us
  transfers between devices with their start and end apart: 81, of which 35 were waited for; matrix products, arithmetic and copies ran while one was open for 8% of the time, Pallas kernels for 57%

profile of v2, /device:TPU:0, one launch (start us, length us, event | category | flops | bytes accessed | tf_op | source)
XLA Modules:
  0.0 944.0 jit_solution(17044312622321568463)
XLA Ops:
  42.9 7.9 own.6.refs_3_.refs_1_.refs_2_.refs_5_
  61.3 8.4 qkv.4
  72.8 7.3 attend.4
  91.9 8.4 qkv.5
  107.8 7.3 attend.5
  125.5 7.8 qkv.6
  133.3 7.3 attend.6
  146.3 7.8 qkv.7
  161.6 7.9 attend.7
  201.0 16.9 %collective-permute-done.19.refs_4_ = bf16[384,2048]{1,0:T(8,128)(2,1)} collective-permute-done((bf16[384,2048]{1,0:T(8,128)(2,1)}, bf16[384,2048]{1,0:T(8,128)(2,1)}, u32[]{:S(2)}, u32[]{:S(2)}) %collective-permute-start.19) | collective-permute-done | bytes 1572896 | tf_op jit(solution)/shard_map/ppermute | solution.py:593
  217.9 5.9 other.4
  223.8 12.4 %collective-permute-done.16.refs_3_ = bf16[512,2048]{1,0:T(8,128)(2,1)} collective-permute-done((bf16[512,2048]{1,0:T(8,128)(2,1)}, bf16[512,2048]{1,0:T(8,128)(2,1)}, u32[]{:S(2)}, u32[]{:S(2)}) %collective-permute-start.16) | collective-permute-done | bytes 2097184 | tf_op jit(solution)/shard_map/ppermute | solution.py:572
  236.3 7.3 norm.1
  244.6 9.4 collective-permute-done.24.refs_1_
  261.2 19.7 %ffn.4 = (bf16[1024,1024]{1,0:T(8,128)(2,1)}, bf16[1024,2048]{1,0:T(8,128)(2,1)}) custom-call(bf16[1024,2048]{1,0:T(8,128)(2,1)} %join.12.refs_0_.refs_4_.refs_1_.refs_2_.refs_3_, bf16[1024,2048]{1,0:T(8,128)(2,1)} %join.10.refs_1_.refs_5_.refs_2_.refs_3_.refs_4_, bf16[2048,2048]{1,0:T(8,128)(2,1)} %own.6.refs_3_.refs_1_.refs_2_.refs_5_, ...), custom_call_target="tpu_custom_call" | custom-call | flops 999999995904 | bytes 1 | tf_op jit(solution)/shard_map/ffn/pallas_call | solution.py:89
  280.9 17.9 %collective-permute-done.28.refs_1_ = bf16[512,2048]{1,0:T(8,128)(2,1)} collective-permute-done((bf16[512,2048]{1,0:T(8,128)(2,1)}, bf16[512,2048]{1,0:T(8,128)(2,1)}, u32[]{:S(2)}, u32[]{:S(2)}) %collective-permute-start.28) | collective-permute-done | bytes 2097184 | tf_op jit(solution)/shard_map/ppermute | solution.py:572
  310.0 19.7 %ffn.5 = (bf16[1024,1024]{1,0:T(8,128)(2,1)}, bf16[1024,2048]{1,0:T(8,128)(2,1)}) custom-call(bf16[1024,2048]{1,0:T(8,128)(2,1)} %join.13.refs_0_.refs_4_.refs_5_.refs_6_.refs_7_.refs_8_, bf16[1024,2048]{1,0:T(8,128)(2,1)} %join.11.refs_5_.refs_1_.refs_6_.refs_7_.refs_8_, bf16[2048,2048]{1,0:T(8,128)(2,1)} %own.6.refs_3_.refs_1_.refs_2_.refs_5_, ...), custom_call_target="tpu_custom_call" | custom-call | flops 999999995904 | bytes 1 | tf_op jit(solution)/shard_map/ffn/pallas_call | solution.py:89
  329.7 6.0 other.5
  335.6 19.7 %ffn.6 = (bf16[1024,1024]{1,0:T(8,128)(2,1)}, bf16[1024,2048]{1,0:T(8,128)(2,1)}) custom-call(bf16[1024,2048]{1,0:T(8,128)(2,1)} %join.13.refs_0_.refs_4_.refs_5_.refs_6_.refs_7_.refs_8_, bf16[1024,2048]{1,0:T(8,128)(2,1)} %join.11.refs_5_.refs_1_.refs_6_.refs_7_.refs_8_, bf16[2048,2048]{1,0:T(8,128)(2,1)} %get-tuple-element.339.refs_2_.refs_4_.refs_6_, ...), custom_call_target="tpu_custom_call" | custom-call | flops 999999995904 | bytes 1 | tf_op jit(solution)/shard_map/ffn/pallas_call | solution.py:89
  355.3 19.9 %ffn.7 = (bf16[1024,1024]{1,0:T(8,128)(2,1)}, bf16[1024,2048]{1,0:T(8,128)(2,1)}) custom-call(bf16[1024,2048]{1,0:T(8,128)(2,1)} %join.12.refs_0_.refs_4_.refs_1_.refs_2_.refs_3_, bf16[1024,2048]{1,0:T(8,128)(2,1)} %join.10.refs_1_.refs_5_.refs_2_.refs_3_.refs_4_, bf16[2048,2048]{1,0:T(8,128)(2,1)} %get-tuple-element.339.refs_2_.refs_4_.refs_6_, ...), custom_call_target="tpu_custom_call" | custom-call | flops 999999995904 | bytes 1 | tf_op jit(solution)/shard_map/ffn/pallas_call | solution.py:89
  375.1 25.9 %gu_grad.2.refs_1_ = bf16[2,512,4096]{2,1,0:T(8,128)(2,1)} custom-call(s32[6]{0:T(128)} %stack.45.refs_0_, bf16[1024,2048]{1,0:T(8,128)(2,1)} %join.12.refs_0_.refs_4_.refs_1_.refs_2_.refs_3_, bf16[1024,2048]{1,0:T(8,128)(2,1)} %join.12.refs_0_.refs_4_.refs_1_.refs_2_.refs_3_, bf16[1024,2048]{1,0:T(8,128)(2,1)} %join.12.refs_0_.refs_4_.refs_1_.refs_2_.refs_3_, ...), custom_call_target="tpu_custom_call" | custom-call | flops 999999995904 | bytes 1 | tf_op jit(solution)/shard_map/gu_grad/pallas_call | solution.py:89
  403.1 25.1 %ffn_in.2 = (bf16[512,2048]{1,0:T(8,128)(2,1)}, bf16[512,2048]{1,0:T(8,128)(2,1)}) custom-call(s32[6]{0:T(128)} %stack.45.refs_0_, bf16[1024,2048]{1,0:T(8,128)(2,1)} %get-tuple-element.345.refs_11_.refs_1_.refs_3_, bf16[1024,2048]{1,0:T(8,128)(2,1)} %get-tuple-element.346.refs_12_.refs_2_.refs_4_, ...), custom_call_target="tpu_custom_call" | custom-call | flops 999999995904 | bytes 1 | tf_op jit(solution)/shard_map/ffn_in/pallas_call | solution.py:89
  437.9 25.3 %ffn_in.3 = (bf16[512,2048]{1,0:T(8,128)(2,1)}, bf16[512,2048]{1,0:T(8,128)(2,1)}) custom-call(s32[6]{0:T(128)} %stack.45.refs_0_, bf16[1024,2048]{1,0:T(8,128)(2,1)} %get-tuple-element.343.refs_9_.refs_1_.refs_3_, bf16[1024,2048]{1,0:T(8,128)(2,1)} %get-tuple-element.344.refs_10_.refs_2_.refs_4_, ...), custom_call_target="tpu_custom_call" | custom-call | flops 999999995904 | bytes 1 | tf_op jit(solution)/shard_map/ffn_in/pallas_call | solution.py:89
  463.4 25.9 %gu_grad.3.refs_7_ = bf16[2,512,4096]{2,1,0:T(8,128)(2,1)} custom-call(s32[6]{0:T(128)} %stack.45.refs_0_, bf16[1024,2048]{1,0:T(8,128)(2,1)} %join.12.refs_0_.refs_4_.refs_1_.refs_2_.refs_3_, bf16[1024,2048]{1,0:T(8,128)(2,1)} %join.12.refs_0_.refs_4_.refs_1_.refs_2_.refs_3_, bf16[1024,2048]{1,0:T(8,128)(2,1)} %join.12.refs_0_.refs_4_.refs_1_.refs_2_.refs_3_, ...), custom_call_target="tpu_custom_call" | custom-call | flops 999999995904 | bytes 1 | tf_op jit(solution)/shard_map/gu_grad/pallas_call | solution.py:89
  489.3 9.0 ffn_back.1
  521.2 10.6 %attend_back.4 = (bf16[1024,256]{1,0:T(8,128)(2,1)}, bf16[1024,256]{1,0:T(8,128)(2,1)}, bf16[1024,256]{1,0:T(8,128)(2,1)}) custom-call(bf16[1024,256]{1,0:T(8,128)(2,1)} %grad_att.4.refs_0_.refs_8_, bf16[1024,256]{1,0:T(8,128)(2,1)} %get-tuple-element.264.refs_0_.refs_1_, bf16[1024,256]{1,0:T(8,128)(2,1)} %get-tuple-element.265.refs_1_.refs_2_, ...), custom_call_target="tpu_custom_call" | custom-call | flops 999999995904 | bytes 1 | tf_op jit(solution)/shard_map/attend_back/pallas_call | solution.py:89
  536.3 10.1 %attend_back.5 = (bf16[1024,256]{1,0:T(8,128)(2,1)}, bf16[1024,256]{1,0:T(8,128)(2,1)}, bf16[1024,256]{1,0:T(8,128)(2,1)}) custom-call(bf16[1024,256]{1,0:T(8,128)(2,1)} %grad_att.5.refs_0_.refs_8_, bf16[1024,256]{1,0:T(8,128)(2,1)} %get-tuple-element.299.refs_2_.refs_0_.refs_1_, bf16[1024,256]{1,0:T(8,128)(2,1)} %get-tuple-element.292.refs_1_.refs_2_, ...), custom_call_target="tpu_custom_call" | custom-call | flops 999999995904 | bytes 1 | tf_op jit(solution)/shard_map/attend_back/pallas_call | solution.py:89
  547.0 16.3 %down_grad.2.refs_2_ = bf16[2,512,2048]{2,1,0:T(8,128)(2,1)} custom-call(s32[6]{0:T(128)} %stack.45.refs_0_, bf16[1024,2048]{1,0:T(8,128)(2,1)} %join.10.refs_1_.refs_5_.refs_2_.refs_3_.refs_4_, bf16[1024,2048]{1,0:T(8,128)(2,1)} %join.10.refs_1_.refs_5_.refs_2_.refs_3_.refs_4_, bf16[1024,2048]{1,0:T(8,128)(2,1)} %join.10.refs_1_.refs_5_.refs_2_.refs_3_.refs_4_, ...), custom_call_target="tpu_custom_call" | custom-call | flops 999999995904 | bytes 1 | tf_op jit(solution)/shard_map/down_grad/pallas_call | solution.py:89
  587.4 10.2 %attend_back.6 = (bf16[1024,256]{1,0:T(8,128)(2,1)}, bf16[1024,256]{1,0:T(8,128)(2,1)}, bf16[1024,256]{1,0:T(8,128)(2,1)}) custom-call(bf16[1024,256]{1,0:T(8,128)(2,1)} %grad_att.6.refs_0_.refs_8_, bf16[1024,256]{1,0:T(8,128)(2,1)} %get-tuple-element.279.refs_0_.refs_1_, bf16[1024,256]{1,0:T(8,128)(2,1)} %get-tuple-element.280.refs_1_.refs_2_, ...), custom_call_target="tpu_custom_call" | custom-call | flops 999999995904 | bytes 1 | tf_op jit(solution)/shard_map/attend_back/pallas_call | solution.py:89
  602.2 10.3 %attend_back.7 = (bf16[1024,256]{1,0:T(8,128)(2,1)}, bf16[1024,256]{1,0:T(8,128)(2,1)}, bf16[1024,256]{1,0:T(8,128)(2,1)}) custom-call(bf16[1024,256]{1,0:T(8,128)(2,1)} %grad_att.7.refs_0_.refs_8_, bf16[1024,256]{1,0:T(8,128)(2,1)} %get-tuple-element.285.refs_0_.refs_3_.refs_1_, bf16[1024,256]{1,0:T(8,128)(2,1)} %get-tuple-element.286.refs_1_.refs_2_, ...), custom_call_target="tpu_custom_call" | custom-call | flops 999999995904 | bytes 1 | tf_op jit(solution)/shard_map/attend_back/pallas_call | solution.py:89
  615.4 11.3 %qkv_in.2 = (bf16[512,2048]{1,0:T(8,128)(2,1)}, bf16[512,2048]{1,0:T(8,128)(2,1)}) custom-call(s32[6]{0:T(128)} %stack.45.refs_0_, bf16[1024,768]{1,0:T(8,128)(2,1)} %get-tuple-element.521.refs_1_.refs_3_, bf16[1024,768]{1,0:T(8,128)(2,1)} %get-tuple-element.522.refs_2_.refs_4_, bf16[1024,768]{1,0:T(8,128)(2,1)} %get-tuple-element.521.refs_1_.refs_3_, ...), custom_call_target="tpu_custom_call" | custom-call | flops 999999995904 | bytes 1 | tf_op jit(solution)/shard_map/qkv_in/pallas_call | solution.py:89
  627.0 21.8 %head_grad.2.refs_1_ = bf16[2,512,2048]{2,1,0:T(8,128)(2,1)} custom-call(s32[6]{0:T(128)} %stack.45.refs_0_, bf16[1024,2048]{1,0:T(8,128)(2,1)} %get-tuple-element.268.refs_3_.refs_0_.refs_1_.refs_2_.refs_4_, bf16[1024,2048]{1,0:T(8,128)(2,1)} %get-tuple-element.268.refs_3_.refs_0_.refs_1_.refs_2_.refs_4_, ...), custom_call_target="tpu_custom_call" | custom-call | flops 999999995904 | bytes 1 | tf_op jit(solution)/shard_map/head_grad/pallas_call | solution.py:89
  656.5 16.8 %down_grad.3.refs_2_ = bf16[2,512,2048]{2,1,0:T(8,128)(2,1)} custom-call(s32[6]{0:T(128)} %stack.45.refs_0_, bf16[1024,2048]{1,0:T(8,128)(2,1)} %join.10.refs_1_.refs_5_.refs_2_.refs_3_.refs_4_, bf16[1024,2048]{1,0:T(8,128)(2,1)} %join.10.refs_1_.refs_5_.refs_2_.refs_3_.refs_4_, bf16[1024,2048]{1,0:T(8,128)(2,1)} %join.10.refs_1_.refs_5_.refs_2_.refs_3_.refs_4_, ...), custom_call_target="tpu_custom_call" | custom-call | flops 999999995904 | bytes 1 | tf_op jit(solution)/shard_map/down_grad/pallas_call | solution.py:89
  686.0 6.5 all_to_all.35.refs_1_
  692.5 11.9 %qkv_in.3 = (bf16[512,2048]{1,0:T(8,128)(2,1)}, bf16[512,2048]{1,0:T(8,128)(2,1)}) custom-call(s32[6]{0:T(128)} %stack.45.refs_0_, bf16[1024,768]{1,0:T(8,128)(2,1)} %get-tuple-element.523.refs_1_.refs_3_, bf16[1024,768]{1,0:T(8,128)(2,1)} %get-tuple-element.524.refs_2_.refs_4_, bf16[1024,768]{1,0:T(8,128)(2,1)} %get-tuple-element.523.refs_1_.refs_3_, ...), custom_call_target="tpu_custom_call" | custom-call | flops 999999995904 | bytes 1 | tf_op jit(solution)/shard_map/qkv_in/pallas_call | solution.py:89
  704.5 21.5 %head_grad.3.refs_2_ = bf16[2,512,2048]{2,1,0:T(8,128)(2,1)} custom-call(s32[6]{0:T(128)} %stack.45.refs_0_, bf16[1024,2048]{1,0:T(8,128)(2,1)} %get-tuple-element.268.refs_3_.refs_0_.refs_1_.refs_2_.refs_4_, bf16[1024,2048]{1,0:T(8,128)(2,1)} %get-tuple-element.268.refs_3_.refs_0_.refs_1_.refs_2_.refs_4_, ...), custom_call_target="tpu_custom_call" | custom-call | flops 999999995904 | bytes 1 | tf_op jit(solution)/shard_map/head_grad/pallas_call | solution.py:89
  740.5 9.7 %input_back.1 = (f32[512,1024]{1,0:T(8,128)}, f32[512,1024]{1,0:T(8,128)}, f32[8,2048]{1,0:T(8,128)}) custom-call(s32[6]{0:T(128)} %stack.45.refs_0_, bf16[512,2048]{1,0:T(8,128)(2,1)} %get-tuple-element.416.refs_1_, bf16[512,2048]{1,0:T(8,128)(2,1)} %collective-permute-done.51.refs_2_, bf16[512,2048]{1,0:T(8,128)(2,1)} %collective-permute-done.52.refs_3_, ...), custom_call_target="tpu_custom_call" | custom-call | flops 999999995904 | bytes 1 | tf_op jit(solution)/shard_map/input_back/pallas_call | solution.py:89
  752.2 13.8 %down.2 = (bf16[512,2048]{1,0:T(8,128)(2,1)}, bf16[512,2048]{1,0:T(8,128)(2,1)}) custom-call(s32[6]{0:T(128)} %stack.45.refs_0_, bf16[1024,1024]{1,0:T(8,128)(2,1)} %get-tuple-element.337.refs_1_.refs_9_.refs_3_, bf16[1024,1024]{1,0:T(8,128)(2,1)} %get-tuple-element.342.refs_13_.refs_10_.refs_2_.refs_4_, ...), custom_call_target="tpu_custom_call" | custom-call | flops 999999995904 | bytes 1 | tf_op jit(solution)/shard_map/down/pallas_call | solution.py:89
  781.0 14.4 %down.3 = (bf16[512,2048]{1,0:T(8,128)(2,1)}, bf16[512,2048]{1,0:T(8,128)(2,1)}) custom-call(s32[6]{0:T(128)} %stack.45.refs_0_, bf16[1024,1024]{1,0:T(8,128)(2,1)} %get-tuple-element.338.refs_7_.refs_11_.refs_1_.refs_3_, bf16[1024,1024]{1,0:T(8,128)(2,1)} %get-tuple-element.341.refs_4_.refs_12_.refs_2_, ...), custom_call_target="tpu_custom_call" | custom-call | flops 999999995904 | bytes 1 | tf_op jit(solution)/shard_map/down/pallas_call | solution.py:89
  824.5 8.9 collective-permute-done.73
  851.2 7.1 collective-permute-done.69.refs_3_
  858.9 21.9 %collective-permute-done.70.refs_4_ = bf16[2,256,2048]{2,1,0:T(8,128)(2,1)} collective-permute-done((bf16[2,256,2048]{2,1,0:T(8,128)(2,1)}, bf16[2,256,2048]{2,1,0:T(8,128)(2,1)}, u32[]{:S(2)}, u32[]{:S(2)}) %collective-permute-start.70) | collective-permute-done | bytes 2097184 | tf_op jit(solution)/shard_map/ppermute | solution.py:593
  881.3 11.0 %finish.3 = (f32[1024,2048]{1,0:T(8,128)}, f32[1024,2048]{1,0:T(8,128)}) custom-call(s32[6]{0:T(128)} %stack.45.refs_0_, bf16[2,256,2048]{2,1,0:T(8,128)(2,1)} %all_to_all.35.refs_1_, bf16[2,256,2048]{2,1,0:T(8,128)(2,1)} %collective-permute-done.65.refs_2_, bf16[2,256,2048]{2,1,0:T(8,128)(2,1)} %collective-permute-done.69.refs_3_, ...), custom_call_target="tpu_custom_call" | custom-call | flops 999999995904 | bytes 1 | tf_op jit(solution)/shard_map/finish/pallas_call | solution.py:89
  893.8 6.3 mixed.1
  900.0 7.1 collective-permute-done.77.refs_2_
  914.5 6.9 finish.4.refs_3_
  926.0 11.0 %collective-permute-done.80.refs_4_ = bf16[2,256,1024]{2,1,0:T(8,128)(2,1)} collective-permute-done((bf16[2,256,1024]{2,1,0:T(8,128)(2,1)}, bf16[2,256,1024]{2,1,0:T(8,128)(2,1)}, u32[]{:S(2)}, u32[]{:S(2)}) %collective-permute-start.80) | collective-permute-done | bytes 1048608 | tf_op jit(solution)/shard_map/ppermute | solution.py:593
  936.9 6.6 finish.5
  (288 shorter events, 334.3 us)
Async XLA Ops:
  0.6 37.9 %collective-permute-start = (bf16[1024,1024]{1,0:T(8,128)(2,1)}, bf16[1024,1024]{1,0:T(8,128)(2,1)}, u32[]{:S(2)}, u32[]{:S(2)}) collective-permute-start(bf16[1024,1024]{1,0:T(8,128)(2,1)} %refs_1_.16), channel_id=1, source_target_pairs={{0,4},{4,0},{1,5},{5,1},{2,6},{6,2},{3,7},{7,3},{8,12},{12,8},{9,1... | collective-permute-start | bytes 6291464 | tf_op jit(solution)/shard_map/ppermute | solution.py:572
  1.2 71.7 %collective-permute-start.6 = (bf16[1024,1024]{1,0:T(8,128)(2,1)}, bf16[1024,1024]{1,0:T(8,128)(2,1)}, u32[]{:S(2)}, u32[]{:S(2)}) collective-permute-start(bf16[1024,1024]{1,0:T(8,128)(2,1)} %refs_1_.16), channel_id=1, source_target_pairs={{0,1},{1,0},{2,3},{3,2},{4,5},{5,4},{6,7},{7,6},{8,9},{9,8},{10,11... | collective-permute-start | bytes 6291464 | tf_op jit(solution)/shard_map/ppermute | solution.py:572
  24.4 55.7 %collective-permute-start.7 = (bf16[512,1024]{1,0:T(8,128)(2,1)}, bf16[512,1024]{1,0:T(8,128)(2,1)}, u32[]{:S(2)}, u32[]{:S(2)}) collective-permute-start(bf16[512,1024]{1,0:T(8,128)(2,1)} %quarter.3.refs_4_), channel_id=1, source_target_pairs={{0,2},{1,3},{2,0},{3,1},{4,6},{5,7},{6,4},{7,5},{8,10},{9,11},{10,... | collective-permute-start | bytes 3145736 | tf_op jit(solution)/shard_map/ppermute | solution.py:572
  80.1 25.5 %collective-permute-start.8 = (bf16[512,1024]{1,0:T(8,128)(2,1)}, bf16[512,1024]{1,0:T(8,128)(2,1)}, u32[]{:S(2)}, u32[]{:S(2)}) collective-permute-start(bf16[512,1024]{1,0:T(8,128)(2,1)} %collective-permute-done.7.refs_1_), channel_id=1, source_target_pairs={{0,8},{4,20},{8,0},{12,28},{16,24},{20,4},{24,16},{28,12},{1,9},{5... | collective-permute-start | bytes 3145736 | tf_op jit(solution)/shard_map/ppermute | solution.py:593
  81.9 33.3 %collective-permute-start.9 = (bf16[512,1024]{1,0:T(8,128)(2,1)}, bf16[512,1024]{1,0:T(8,128)(2,1)}, u32[]{:S(2)}, u32[]{:S(2)}) collective-permute-start(bf16[512,1024]{1,0:T(8,128)(2,1)} %collective-permute-done.7.refs_1_), channel_id=1, source_target_pairs={{0,16},{4,12},{8,24},{12,4},{16,0},{20,28},{24,8},{28,20},{1,17},{... | collective-permute-start | bytes 3145736 | tf_op jit(solution)/shard_map/ppermute | solution.py:593
  83.4 75.6 %collective-permute-start.12 = (bf16[384,2048]{1,0:T(8,128)(2,1)}, bf16[384,2048]{1,0:T(8,128)(2,1)}, u32[]{:S(2)}, u32[]{:S(2)}) collective-permute-start(bf16[384,2048]{1,0:T(8,128)(2,1)} %quarter.4.refs_3_), channel_id=1, source_target_pairs={{0,2},{1,3},{2,0},{3,1},{4,6},{5,7},{6,4},{7,5},{8,10},{9,11},{10,... | collective-permute-start | bytes 4718600 | tf_op jit(solution)/shard_map/ppermute | solution.py:572
  85.1 105.7 %collective-permute-start.20 = (bf16[1024,1024]{1,0:T(8,128)(2,1)}, bf16[1024,1024]{1,0:T(8,128)(2,1)}, u32[]{:S(2)}, u32[]{:S(2)}) collective-permute-start(bf16[1024,1024]{1,0:T(8,128)(2,1)} %refs_1_.19), channel_id=1, source_target_pairs={{0,1},{1,0},{2,3},{3,2},{4,5},{5,4},{6,7},{7,6},{8,9},{9,8},{10,11... | collective-permute-start | bytes 6291464 | tf_op jit(solution)/shard_map/ppermute | solution.py:572
  157.9 78.4 %collective-permute-start.16 = (bf16[512,2048]{1,0:T(8,128)(2,1)}, bf16[512,2048]{1,0:T(8,128)(2,1)}, u32[]{:S(2)}, u32[]{:S(2)}) collective-permute-start(bf16[512,2048]{1,0:T(8,128)(2,1)} %add_convert_fusion.6.refs_1_), channel_id=1, source_target_pairs={{0,1},{1,0},{2,3},{3,2},{4,5},{5,4},{6,7},{7,6},{8,9},{9,8},{10,11... | collective-permute-start | bytes 6291464 | tf_op jit(solution)/shard_map/ppermute | solution.py:572
  159.6 20.7 %collective-permute-start.17 = (bf16[384,2048]{1,0:T(8,128)(2,1)}, bf16[384,2048]{1,0:T(8,128)(2,1)}, u32[]{:S(2)}, u32[]{:S(2)}) collective-permute-start(bf16[384,2048]{1,0:T(8,128)(2,1)} %collective-permute-done.12.refs_1_), channel_id=1, source_target_pairs={{0,8},{4,20},{8,0},{12,28},{16,24},{20,4},{24,16},{28,12},{1,9},{5... | collective-permute-start | bytes 4718600 | tf_op jit(solution)/shard_map/ppermute | solution.py:593
  161.2 21.1 %collective-permute-start.21 = (bf16[1024,1024]{1,0:T(8,128)(2,1)}, bf16[1024,1024]{1,0:T(8,128)(2,1)}, u32[]{:S(2)}, u32[]{:S(2)}) collective-permute-start(bf16[1024,1024]{1,0:T(8,128)(2,1)} %refs_1_.19), channel_id=1, source_target_pairs={{0,4},{4,0},{1,5},{5,1},{2,6},{6,2},{3,7},{7,3},{8,12},{12,8},{9,1... | collective-permute-start | bytes 6291464 | tf_op jit(solution)/shard_map/ppermute | solution.py:572
  175.2 61.0 %collective-permute-start.15 = (bf16[512,2048]{1,0:T(8,128)(2,1)}, bf16[512,2048]{1,0:T(8,128)(2,1)}, u32[]{:S(2)}, u32[]{:S(2)}) collective-permute-start(bf16[512,2048]{1,0:T(8,128)(2,1)} %get-tuple-element.317.refs_3_), channel_id=1, source_target_pairs={{0,4},{4,0},{1,5},{5,1},{2,6},{6,2},{3,7},{7,3},{8,12},{12,8},{9,1... | collective-permute-start | bytes 6291464 | tf_op jit(solution)/shard_map/ppermute | solution.py:572
  180.3 20.7 %collective-permute-start.18 = (bf16[384,2048]{1,0:T(8,128)(2,1)}, bf16[384,2048]{1,0:T(8,128)(2,1)}, u32[]{:S(2)}, u32[]{:S(2)}) collective-permute-start(bf16[384,2048]{1,0:T(8,128)(2,1)} %collective-permute-done.12.refs_1_), channel_id=1, source_target_pairs={{0,16},{4,12},{8,24},{12,4},{16,0},{20,28},{24,8},{28,20},{1,17},{... | collective-permute-start | bytes 4718600 | tf_op jit(solution)/shard_map/ppermute | solution.py:593
  182.3 71.7 %collective-permute-start.24 = (bf16[384,2048]{1,0:T(8,128)(2,1)}, bf16[384,2048]{1,0:T(8,128)(2,1)}, u32[]{:S(2)}, u32[]{:S(2)}) collective-permute-start(bf16[384,2048]{1,0:T(8,128)(2,1)} %quarter.5.refs_5_), channel_id=1, source_target_pairs={{0,2},{1,3},{2,0},{3,1},{4,6},{5,7},{6,4},{7,5},{8,10},{9,11},{10,... | collective-permute-start | bytes 4718600 | tf_op jit(solution)/shard_map/ppermute | solution.py:572
  195.4 22.5 %collective-permute-start.19 = (bf16[384,2048]{1,0:T(8,128)(2,1)}, bf16[384,2048]{1,0:T(8,128)(2,1)}, u32[]{:S(2)}, u32[]{:S(2)}) collective-permute-start(bf16[384,2048]{1,0:T(8,128)(2,1)} %collective-permute-done.17.refs_2_), channel_id=1, source_target_pairs={{0,16},{4,12},{8,24},{12,4},{16,0},{20,28},{24,8},{28,20},{1,17},{... | collective-permute-start | bytes 4718600 | tf_op jit(solution)/shard_map/ppermute | solution.py:593
  243.6 55.2 %collective-permute-start.28 = (bf16[512,2048]{1,0:T(8,128)(2,1)}, bf16[512,2048]{1,0:T(8,128)(2,1)}, u32[]{:S(2)}, u32[]{:S(2)}) collective-permute-start(bf16[512,2048]{1,0:T(8,128)(2,1)} %get-tuple-element.321.refs_1_), channel_id=1, source_target_pairs={{0,1},{1,0},{2,3},{3,2},{4,5},{5,4},{6,7},{7,6},{8,9},{9,8},{10,11... | collective-permute-start | bytes 6291464 | tf_op jit(solution)/shard_map/ppermute | solution.py:572
  254.0 44.8 %collective-permute-start.26 = (bf16[384,2048]{1,0:T(8,128)(2,1)}, bf16[384,2048]{1,0:T(8,128)(2,1)}, u32[]{:S(2)}, u32[]{:S(2)}) collective-permute-start(bf16[384,2048]{1,0:T(8,128)(2,1)} %collective-permute-done.24.refs_1_), channel_id=1, source_target_pairs={{0,8},{4,20},{8,0},{12,28},{16,24},{20,4},{24,16},{28,12},{1,9},{5... | collective-permute-start | bytes 4718600 | tf_op jit(solution)/shard_map/ppermute | solution.py:593
  254.5 75.1 %collective-permute-start.27 = (bf16[384,2048]{1,0:T(8,128)(2,1)}, bf16[384,2048]{1,0:T(8,128)(2,1)}, u32[]{:S(2)}, u32[]{:S(2)}) collective-permute-start(bf16[384,2048]{1,0:T(8,128)(2,1)} %collective-permute-done.24.refs_1_), channel_id=1, source_target_pairs={{0,16},{4,12},{8,24},{12,4},{16,0},{20,28},{24,8},{28,20},{1,17},{... | collective-permute-start | bytes 4718600 | tf_op jit(solution)/shard_map/ppermute | solution.py:593
  298.8 30.8 %collective-permute-start.29 = (bf16[384,2048]{1,0:T(8,128)(2,1)}, bf16[384,2048]{1,0:T(8,128)(2,1)}, u32[]{:S(2)}, u32[]{:S(2)}) collective-permute-start(bf16[384,2048]{1,0:T(8,128)(2,1)} %collective-permute-done.26.refs_2_), channel_id=1, source_target_pairs={{0,16},{4,12},{8,24},{12,4},{16,0},{20,28},{24,8},{28,20},{1,17},{... | collective-permute-start | bytes 4718600 | tf_op jit(solution)/shard_map/ppermute | solution.py:593
  401.0 106.7 %collective-permute-start.38 = (bf16[2,512,4096]{2,1,0:T(8,128)(2,1)}, bf16[2,512,4096]{2,1,0:T(8,128)(2,1)}, u32[]{:S(2)}, u32[]{:S(2)}) collective-permute-start(bf16[2,512,4096]{2,1,0:T(8,128)(2,1)} %gu_grad.2.refs_1_), channel_id=1, source_target_pairs={{0,8},{4,20},{8,0},{12,28},{16,24},{20,4},{24,16},{28,12},{1,9},{5... | collective-permute-start | bytes 25165832 | tf_op jit(solution)/shard_map/ppermute | solution.py:593
  436.4 52.9 %collective-permute-start.35 = (bf16[512,2048]{1,0:T(8,128)(2,1)}, bf16[512,2048]{1,0:T(8,128)(2,1)}, u32[]{:S(2)}, u32[]{:S(2)}) collective-permute-start(bf16[512,2048]{1,0:T(8,128)(2,1)} %add_convert_fusion.5.refs_1_), channel_id=1, source_target_pairs={{0,1},{1,0},{2,3},{3,2},{4,5},{5,4},{6,7},{7,6},{8,9},{9,8},{10,11... | collective-permute-start | bytes 6291464 | tf_op jit(solution)/shard_map/ppermute | solution.py:572
  463.2 26.1 %collective-permute-start.34 = (bf16[512,2048]{1,0:T(8,128)(2,1)}, bf16[512,2048]{1,0:T(8,128)(2,1)}, u32[]{:S(2)}, u32[]{:S(2)}) collective-permute-start(bf16[512,2048]{1,0:T(8,128)(2,1)} %get-tuple-element.357.refs_13_), channel_id=1, source_target_pairs={{0,4},{4,0},{1,5},{5,1},{2,6},{6,2},{3,7},{7,3},{8,12},{12,8},{9,1... | collective-permute-start | bytes 6291464 | tf_op jit(solution)/shard_map/ppermute | solution.py:572
  498.6 48.4 %collective-permute-start.41 = (bf16[512,2048]{1,0:T(8,128)(2,1)}, bf16[512,2048]{1,0:T(8,128)(2,1)}, u32[]{:S(2)}, u32[]{:S(2)}) collective-permute-start(bf16[512,2048]{1,0:T(8,128)(2,1)} %get-tuple-element.358.refs_1_), channel_id=1, source_target_pairs={{0,1},{1,0},{2,3},{3,2},{4,5},{5,4},{6,7},{7,6},{8,9},{9,8},{10,11... | collective-permute-start | bytes 6291464 | tf_op jit(solution)/shard_map/ppermute | solution.py:572
  513.3 53.4 %collective-permute-start.40 = (bf16[512,4096]{1,0:T(8,128)(2,1)}, bf16[512,4096]{1,0:T(8,128)(2,1)}, u32[]{:S(2)}, u32[]{:S(2)}) collective-permute-start(bf16[512,4096]{1,0:T(8,128)(2,1)} %fusion.refs_1_), channel_id=1, source_target_pairs={{0,16},{4,12},{8,24},{12,4},{16,0},{20,28},{24,8},{28,20},{1,17},{... | collective-permute-start | bytes 12582920 | tf_op jit(solution)/shard_map/ppermute | solution.py:593
  563.3 110.0 %collective-permute-start.49 = (bf16[2,512,2048]{2,1,0:T(8,128)(2,1)}, bf16[2,512,2048]{2,1,0:T(8,128)(2,1)}, u32[]{:S(2)}, u32[]{:S(2)}) collective-permute-start(bf16[2,512,2048]{2,1,0:T(8,128)(2,1)} %down_grad.2.refs_2_), channel_id=1, source_target_pairs={{0,8},{4,20},{8,0},{12,28},{16,24},{20,4},{24,16},{28,12},{1,9},{5... | collective-permute-start | bytes 12582920 | tf_op jit(solution)/shard_map/ppermute | solution.py:593
  572.3 107.5 %collective-permute-start.42 = (bf16[512,2048]{1,0:T(8,128)(2,1)}, bf16[512,2048]{1,0:T(8,128)(2,1)}, u32[]{:S(2)}, u32[]{:S(2)}) collective-permute-start(bf16[512,2048]{1,0:T(8,128)(2,1)} %fusion.1.refs_1_), channel_id=1, source_target_pairs={{0,2},{1,3},{2,0},{3,1},{4,6},{5,7},{6,4},{7,5},{8,10},{9,11},{10,... | collective-permute-start | bytes 6291464 | tf_op jit(solution)/shard_map/ppermute | solution.py:572
  626.7 24.1 %collective-permute-start.46 = (bf16[512,2048]{1,0:T(8,128)(2,1)}, bf16[512,2048]{1,0:T(8,128)(2,1)}, u32[]{:S(2)}, u32[]{:S(2)}) collective-permute-start(bf16[512,2048]{1,0:T(8,128)(2,1)} %get-tuple-element.393.refs_33_), channel_id=1, source_target_pairs={{0,4},{4,0},{1,5},{5,1},{2,6},{6,2},{3,7},{7,3},{8,12},{12,8},{9,1... | collective-permute-start | bytes 6291464 | tf_op jit(solution)/shard_map/ppermute | solution.py:572
  648.7 78.0 %collective-permute-start.53 = (bf16[2,512,2048]{2,1,0:T(8,128)(2,1)}, bf16[2,512,2048]{2,1,0:T(8,128)(2,1)}, u32[]{:S(2)}, u32[]{:S(2)}) collective-permute-start(bf16[2,512,2048]{2,1,0:T(8,128)(2,1)} %head_grad.2.refs_1_), channel_id=1, source_target_pairs={{0,8},{4,20},{8,0},{12,28},{16,24},{20,4},{24,16},{28,12},{1,9},{5... | collective-permute-start | bytes 12582920 | tf_op jit(solution)/shard_map/ppermute | solution.py:593
  654.9 83.8 %collective-permute-start.52 = (bf16[512,2048]{1,0:T(8,128)(2,1)}, bf16[512,2048]{1,0:T(8,128)(2,1)}, u32[]{:S(2)}, u32[]{:S(2)}) collective-permute-start(bf16[512,2048]{1,0:T(8,128)(2,1)} %add_convert_fusion.4.refs_1_), channel_id=1, source_target_pairs={{0,1},{1,0},{2,3},{3,2},{4,5},{5,4},{6,7},{7,6},{8,9},{9,8},{10,11... | collective-permute-start | bytes 6291464 | tf_op jit(solution)/shard_map/ppermute | solution.py:572
  677.8 56.3 %collective-permute-start.55 = (bf16[512,2048]{1,0:T(8,128)(2,1)}, bf16[512,2048]{1,0:T(8,128)(2,1)}, u32[]{:S(2)}, u32[]{:S(2)}) collective-permute-start(bf16[512,2048]{1,0:T(8,128)(2,1)} %fusion.4.refs_1_), channel_id=1, source_target_pairs={{0,16},{4,12},{8,24},{12,4},{16,0},{20,28},{24,8},{28,20},{1,17},{... | collective-permute-start | bytes 6291464 | tf_op jit(solution)/shard_map/ppermute | solution.py:593
  704.4 36.1 %collective-permute-start.51 = (bf16[512,2048]{1,0:T(8,128)(2,1)}, bf16[512,2048]{1,0:T(8,128)(2,1)}, u32[]{:S(2)}, u32[]{:S(2)}) collective-permute-start(bf16[512,2048]{1,0:T(8,128)(2,1)} %get-tuple-element.417.refs_33_), channel_id=1, source_target_pairs={{0,4},{4,0},{1,5},{5,1},{2,6},{6,2},{3,7},{7,3},{8,12},{12,8},{9,1... | collective-permute-start | bytes 6291464 | tf_op jit(solution)/shard_map/ppermute | solution.py:572
  726.0 95.3 %collective-permute-start.65 = (bf16[2,256,2048]{2,1,0:T(8,128)(2,1)}, bf16[2,256,2048]{2,1,0:T(8,128)(2,1)}, u32[]{:S(2)}, u32[]{:S(2)}) collective-permute-start(bf16[2,256,2048]{2,1,0:T(8,128)(2,1)} %all_to_all.35.refs_1_), channel_id=1, source_target_pairs={{0,8},{4,20},{8,0},{12,28},{16,24},{20,4},{24,16},{28,12},{1,9},{5... | collective-permute-start | bytes 6291464 | tf_op jit(solution)/shard_map/ppermute | solution.py:593
  732.6 41.7 %collective-permute-start.60 = (bf16[512,2048]{1,0:T(8,128)(2,1)}, bf16[512,2048]{1,0:T(8,128)(2,1)}, u32[]{:S(2)}, u32[]{:S(2)}) collective-permute-start(bf16[512,2048]{1,0:T(8,128)(2,1)} %fusion.5.refs_1_), channel_id=1, source_target_pairs={{0,16},{4,12},{8,24},{12,4},{16,0},{20,28},{24,8},{28,20},{1,17},{... | collective-permute-start | bytes 6291464 | tf_op jit(solution)/shard_map/ppermute | solution.py:593
  738.7 72.2 %collective-permute-start.66 = (bf16[512,1024]{1,0:T(8,128)(2,1)}, bf16[512,1024]{1,0:T(8,128)(2,1)}, u32[]{:S(2)}, u32[]{:S(2)}) collective-permute-start(bf16[512,1024]{1,0:T(8,128)(2,1)} %fusion.11.refs_1_), channel_id=1, source_target_pairs={{0,2},{1,3},{2,0},{3,1},{4,6},{5,7},{6,4},{7,5},{8,10},{9,11},{10,... | collective-permute-start | bytes 3145736 | tf_op jit(solution)/shard_map/ppermute | solution.py:572
  771.7 23.8 %collective-permute-start.63 = (f32[2,2048]{1,0:T(2,128)}, f32[2,2048]{1,0:T(2,128)}, u32[]{:S(2)}, u32[]{:S(2)}) collective-permute-start(f32[2,2048]{1,0:T(2,128)} %add.143.refs_2_), channel_id=1, source_target_pairs={{0,8},{4,20},{8,0},{12,28},{16,24},{20,4},{24,16},{28,12},{1,9},{5... | collective-permute-start | bytes 49160 | tf_op jit(solution)/shard_map/ppermute | solution.py:593
  777.8 56.9 %collective-permute-start.72 = (bf16[512,1024]{1,0:T(8,128)(2,1)}, bf16[512,1024]{1,0:T(8,128)(2,1)}, u32[]{:S(2)}, u32[]{:S(2)}) collective-permute-start(bf16[512,1024]{1,0:T(8,128)(2,1)} %fusion.10.refs_1_), channel_id=1, source_target_pairs={{0,2},{1,3},{2,0},{3,1},{4,6},{5,7},{6,4},{7,5},{8,10},{9,11},{10,... | collective-permute-start | bytes 3145736 | tf_op jit(solution)/shard_map/ppermute | solution.py:572
  796.9 22.4 %collective-permute-start.68 = (f32[2,2048]{1,0:T(2,128)}, f32[2,2048]{1,0:T(2,128)}, u32[]{:S(2)}, u32[]{:S(2)}) collective-permute-start(f32[2,2048]{1,0:T(2,128)} %add.147.refs_1_), channel_id=1, source_target_pairs={{0,16},{4,12},{8,24},{12,4},{16,0},{20,28},{24,8},{28,20},{1,17},{... | collective-permute-start | bytes 49160 | tf_op jit(solution)/shard_map/ppermute | solution.py:593
  820.7 37.6 %collective-permute-start.69 = (bf16[2,256,2048]{2,1,0:T(8,128)(2,1)}, bf16[2,256,2048]{2,1,0:T(8,128)(2,1)}, u32[]{:S(2)}, u32[]{:S(2)}) collective-permute-start(bf16[2,256,2048]{2,1,0:T(8,128)(2,1)} %all_to_all.35.refs_1_), channel_id=1, source_target_pairs={{0,16},{4,12},{8,24},{12,4},{16,0},{20,28},{24,8},{28,20},{1,17},{... | collective-permute-start | bytes 6291464 | tf_op jit(solution)/shard_map/ppermute | solution.py:593
  821.3 59.4 %collective-permute-start.70 = (bf16[2,256,2048]{2,1,0:T(8,128)(2,1)}, bf16[2,256,2048]{2,1,0:T(8,128)(2,1)}, u32[]{:S(2)}, u32[]{:S(2)}) collective-permute-start(bf16[2,256,2048]{2,1,0:T(8,128)(2,1)} %collective-permute-done.65.refs_2_), channel_id=1, source_target_pairs={{0,16},{4,12},{8,24},{12,4},{16,0},{20,28},{24,8},{28,20},{1,17},{... | collective-permute-start | bytes 6291464 | tf_op jit(solution)/shard_map/ppermute | solution.py:593
  822.7 26.4 %collective-permute-start.71 = (bf16[2,256,1024]{2,1,0:T(8,128)(2,1)}, bf16[2,256,1024]{2,1,0:T(8,128)(2,1)}, u32[]{:S(2)}, u32[]{:S(2)}) collective-permute-start(bf16[2,256,1024]{2,1,0:T(8,128)(2,1)} %all_to_all.36.refs_1_), channel_id=1, source_target_pairs={{0,8},{4,20},{8,0},{12,28},{16,24},{20,4},{24,16},{28,12},{1,9},{5... | collective-permute-start | bytes 3145736 | tf_op jit(solution)/shard_map/ppermute | solution.py:593
  833.3 59.0 %collective-permute-start.57 = (bf16[512,2048]{1,0:T(8,128)(2,1)}, bf16[512,2048]{1,0:T(8,128)(2,1)}, u32[]{:S(2)}, u32[]{:S(2)}) collective-permute-start(bf16[512,2048]{1,0:T(8,128)(2,1)} %get-tuple-element.436.refs_3_), channel_id=1, source_target_pairs={{0,4},{4,0},{1,5},{5,1},{2,6},{6,2},{3,7},{7,3},{8,12},{12,8},{9,1... | collective-permute-start | bytes 6291464 | tf_op jit(solution)/shard_map/ppermute | solution.py:572
  834.7 59.1 %collective-permute-start.64 = (bf16[512,2048]{1,0:T(8,128)(2,1)}, bf16[512,2048]{1,0:T(8,128)(2,1)}, u32[]{:S(2)}, u32[]{:S(2)}) collective-permute-start(bf16[512,2048]{1,0:T(8,128)(2,1)} %add_convert_fusion.1.refs_1_), channel_id=1, source_target_pairs={{0,1},{1,0},{2,3},{3,2},{4,5},{5,4},{6,7},{7,6},{8,9},{9,8},{10,11... | collective-permute-start | bytes 6291464 | tf_op jit(solution)/shard_map/ppermute | solution.py:572
  849.1 75.4 %collective-permute-start.78 = (f32[2,2048]{1,0:T(2,128)}, f32[2,2048]{1,0:T(2,128)}, u32[]{:S(2)}, u32[]{:S(2)}) collective-permute-start(f32[2,2048]{1,0:T(2,128)} %add.157.refs_7_), channel_id=1, source_target_pairs={{0,2},{1,3},{2,0},{3,1},{4,6},{5,7},{6,4},{7,5},{8,10},{9,11},{10,... | collective-permute-start | bytes 49160 | tf_op jit(solution)/shard_map/ppermute | solution.py:572
  858.3 49.5 %collective-permute-start.75 = (bf16[2,256,1024]{2,1,0:T(8,128)(2,1)}, bf16[2,256,1024]{2,1,0:T(8,128)(2,1)}, u32[]{:S(2)}, u32[]{:S(2)}) collective-permute-start(bf16[2,256,1024]{2,1,0:T(8,128)(2,1)} %all_to_all.36.refs_1_), channel_id=1, source_target_pairs={{0,16},{4,12},{8,24},{12,4},{16,0},{20,28},{24,8},{28,20},{1,17},{... | collective-permute-start | bytes 3145736 | tf_op jit(solution)/shard_map/ppermute | solution.py:593
  880.8 26.4 %collective-permute-start.77 = (bf16[2,256,1024]{2,1,0:T(8,128)(2,1)}, bf16[2,256,1024]{2,1,0:T(8,128)(2,1)}, u32[]{:S(2)}, u32[]{:S(2)}) collective-permute-start(bf16[2,256,1024]{2,1,0:T(8,128)(2,1)} %all_to_all.37.refs_1_), channel_id=1, source_target_pairs={{0,8},{4,20},{8,0},{12,28},{16,24},{20,4},{24,16},{28,12},{1,9},{5... | collective-permute-start | bytes 3145736 | tf_op jit(solution)/shard_map/ppermute | solution.py:593
  892.3 22.2 %collective-permute-start.76 = (bf16[2,256,1024]{2,1,0:T(8,128)(2,1)}, bf16[2,256,1024]{2,1,0:T(8,128)(2,1)}, u32[]{:S(2)}, u32[]{:S(2)}) collective-permute-start(bf16[2,256,1024]{2,1,0:T(8,128)(2,1)} %collective-permute-done.71.refs_2_), channel_id=1, source_target_pairs={{0,16},{4,12},{8,24},{12,4},{16,0},{20,28},{24,8},{28,20},{1,17},{... | collective-permute-start | bytes 3145736 | tf_op jit(solution)/shard_map/ppermute | solution.py:593
  900.0 21.3 %collective-permute-start.74 = (bf16[512,1024]{1,0:T(8,128)(2,1)}, bf16[512,1024]{1,0:T(8,128)(2,1)}, u32[]{:S(2)}, u32[]{:S(2)}) collective-permute-start(bf16[512,1024]{1,0:T(8,128)(2,1)} %get-tuple-element.499), channel_id=1, source_target_pairs={{0,4},{4,0},{1,5},{5,1},{2,6},{6,2},{3,7},{7,3},{8,12},{12,8},{9,1... | collective-permute-start | bytes 3145736 | tf_op jit(solution)/shard_map/ppermute | solution.py:572
  907.2 18.8 %collective-permute-start.79 = (bf16[2,256,1024]{2,1,0:T(8,128)(2,1)}, bf16[2,256,1024]{2,1,0:T(8,128)(2,1)}, u32[]{:S(2)}, u32[]{:S(2)}) collective-permute-start(bf16[2,256,1024]{2,1,0:T(8,128)(2,1)} %all_to_all.37.refs_1_), channel_id=1, source_target_pairs={{0,16},{4,12},{8,24},{12,4},{16,0},{20,28},{24,8},{28,20},{1,17},{... | collective-permute-start | bytes 3145736 | tf_op jit(solution)/shard_map/ppermute | solution.py:593
  907.8 29.1 %collective-permute-start.80 = (bf16[2,256,1024]{2,1,0:T(8,128)(2,1)}, bf16[2,256,1024]{2,1,0:T(8,128)(2,1)}, u32[]{:S(2)}, u32[]{:S(2)}) collective-permute-start(bf16[2,256,1024]{2,1,0:T(8,128)(2,1)} %collective-permute-done.77.refs_2_), channel_id=1, source_target_pairs={{0,16},{4,12},{8,24},{12,4},{16,0},{20,28},{24,8},{28,20},{1,17},{... | collective-permute-start | bytes 3145736 | tf_op jit(solution)/shard_map/ppermute | solution.py:593
  (58 other events, 478.0 us)

commit v3 on v2

--- a/solution.py
+++ b/solution.py
@@ -11,7 +11,7 @@
 LANES = 128
 EPS = 1e-05
 ROPE_BASE = 130000.0
-VMEM = 60 * 1024 * 1024
+VMEM = 40 * 1024 * 1024
 UNIT_TILE = 256
 QB = 256
 COST = 10**12
@@ -69,6 +69,9 @@
         value = lax.all_to_all(self.tied(value), "row", split_axis=0, concat_axis=0, tiled=True)
         self.last = [value, *self.last]
         return value
+
+
+ONCE = pl.Buffered(1)
 
 
 def launch(kernel, arrays, in_specs, name, prefetch=(), **rest):
@@ -216,7 +219,7 @@
     rows, width = x.shape[0], weight.shape[1] // 3
     tile = min(512, rows)
     row_block = lambda n: pl.BlockSpec((tile, n), lambda i: (i, 0))
-    whole = lambda a: pl.BlockSpec(a.shape, lambda i: (0, 0))
+    whole = lambda a: pl.BlockSpec(a.shape, lambda i: (0, 0), pipeline_mode=ONCE)
     outs = [D] * first + [width] * 3
     return launch(
         lambda *refs: qkv_kernel(first, *refs),
@@ -337,7 +340,7 @@
 def ffn(nf, cot, w_gu, w_down):
     rows, units = nf.shape[0], w_down.shape[0]
     tile = min(UNIT_TILE, units)
-    whole = pl.BlockSpec((rows, D), lambda j: (0, 0))
+    whole = pl.BlockSpec((rows, D), lambda j: (0, 0), pipeline_mode=ONCE)
     return launch(
         ffn_kernel,
         [nf, cot, w_gu, w_down],
@@ -374,10 +377,12 @@
             out_ref[...] = total.astype(BF16)
 
     if parts == 1:
-        lhs_specs = [pl.BlockSpec((rows, a.shape[1]), lambda n, *w: (0, 0)) for a in lhs]
+        lhs_specs = [pl.BlockSpec((rows, a.shape[1]), lambda n, *w: (0, 0), pipeline_mode=ONCE) for a in lhs]
     else:
         lhs_specs = [
-            pl.BlockSpec((size, a.shape[1]), (lambda s: lambda n, w: (w[s], 0))(s)) for s in (OTHER, CORE) for a in lhs
+            pl.BlockSpec((size, a.shape[1]), (lambda s: lambda n, w: (w[s], 0))(s), pipeline_mode=ONCE)
+            for s in (OTHER, CORE)
+            for a in lhs
         ]
     if turned:
         rhs_specs = [pl.BlockSpec((tile, b.shape[1]), lambda n, *w: (n, 0)) for b in rhs]
@@ -405,7 +410,7 @@
     pieces = len(near)
     first, stride = scalars
     fixed_specs = [
-        pl.BlockSpec((rows, part), (lambda k, h: lambda t, w: (0, 4 * h + w[first + stride * k]))(k, h))
+        pl.BlockSpec((rows, part), (lambda k, h: lambda t, w: (0, 4 * h + w[first + stride * k]))(k, h), pipeline_mode=ONCE)
         for _ in sets
         for _ in range(2)
         for k in range(2)
@@ -553,7 +558,7 @@
     return launch(
         kernel,
         pieces,
-        [pl.BlockSpec(shape, lambda k, w: (0, 0, 0))] * 4,
+        [pl.BlockSpec(shape, lambda k, w: (0, 0, 0), pipeline_mode=ONCE)] * 4,
         name,
         [where],
         grid=(4,),
@@ -1006,8 +1011,10 @@
     down.make()
     ups.cross_plane()
     down.leave()
+    down.stay()
     gr_far = join_rows(plan, s, gr_chip, gr_far_row)
     back_far = [back_one(gr_far, far_heads, o_far, b) for b in range(2)]
+    down.second()
     dqkv_far = [jnp.concatenate(b, axis=1) for b in back_far]
     far = core_sum(plan, dqkv_far, w_qkv, True, "qkv_in")
     heads = Group(
@@ -1019,39 +1026,38 @@
     heads.make()
     heads.leave()
     far = post(other_chip, add_pair(plan, far))
-    down.stay()
-    down.second()
-    ups.total()
     dqkv_near = [jnp.concatenate(b, axis=1) for b in back_near]
     near = core_sum(plan, dqkv_near, w_qkv, True, "qkv_in")
+    down.cross_plane()
     heads.stay()
     heads.second()
-    down.cross_plane()
+    mixed_far = core_sum(plan, hid_far, w_d, False, "down")
+    ups.total()
     input_mine, input_other, gain_attn_part = norm_input_back(plan, s, near, far, x_near, grad_residual, gains_attn)
     input_got = ship(other_core, input_other)
     gains = mix(lambda a, b: jnp.stack((jnp.sum(a, axis=0), jnp.sum(b, axis=0))), gain_attn_part, gain_ffn_part)
     gains_got = ship(other_core, gains)
-    mixed_near = core_sum(plan, hid_near, w_d, False, "down")
+    heads.cross_plane()
+    mixed_far = post(other_chip, add_pair(plan, mixed_far))
+    ups.spread()
     input_grad = side_by_side(plan, s, input_mine, input_got)
     gains = mix(jnp.add, gains, gains_got)
     gains_got = ship(hop_one, gains)
-    heads.cross_plane()
-    mixed_far = core_sum(plan, hid_far, w_d, False, "down")
+    ups.spread_last()
+    mixed_near = core_sum(plan, hid_near, w_d, False, "down")
     gains = mix(jnp.add, gains, gains_got)
-    gains_got = ship(hop_two, gains)
-    ups.spread()
-    plan.pause()
-    mixed_far = post(other_chip, add_pair(plan, mixed_far))
     down.total()
     down.spread()
+    gains_got = ship(hop_two, gains)
+    plan.pause()
+    mixed_near = [add_pair(plan, mixed_near)]
     gains = mix(jnp.add, gains, gains_got)
     gains_got = ship(other_chip, gains)
-    ups.spread_last()
     plan.pause()
-    gains = mix(jnp.add, gains, gains_got)
     heads.total()
     heads.spread()
     down.spread_last()
+    gains = mix(jnp.add, gains, gains_got)
     gains_got = ship(far_plane, gains)
     gate_grad, up_grad = ups.finish()
     mixed_mine, mixed_other = add_mixed(plan, s, mixed_near, mixed_far, residual)

time: 955 us -> 927 us (0.971)
  Pallas kernels: 617 us -> 517 us
  local copies, waits for them, and re-layouts: 2.58 us -> 60.1 us
  waiting for transfers between devices: 173 us -> 197 us
    pallas_call x85, Pallas kernels: 617 us -> 517 us  [launch(): pl.pallas_call(body, out_shape=out_shape, compiler_params=pltpu.CompilerP...]
    unnamed x50 -> x368, local copies, waits for them, and re-layouts: 1.22 us -> 59.3 us
    ppermute x26, waiting for transfers between devices: 93.6 us -> 108 us  [hop(): return lax.ppermute(values, ('dp', 'row'), pairs)]
  transfers between devices with their start and end apart: 81 -> 82, of which waited for: 35 -> 28; matrix products, arithmetic and copies ran while one was open for 8% -> 7% of each run, Pallas kernels for 57% -> 48%
where the time goes in v3:
time: 927 us; the launch traced here: 918 us
  Pallas kernels  517 us (56%)
  waiting for transfers between devices  197 us (21%)
  other arithmetic  67.5 us (7%)
  starting transfers between devices  61.4 us (7%)
  local copies, waits for them, and re-layouts  60.1 us (6%)
  blocking collectives  11 us (1%)
    pallas_call x85, Pallas kernels, launch(): pl.pallas_call(body, out_shape=out_shape, compiler_params=pltpu.CompilerP...  517 us
    ppermute x26, waiting for transfers between devices, hop(): return lax.ppermute(values, ('dp', 'row'), pairs)  108 us
    ppermute x55, waiting for transfers between devices, swap_axis(): return lax.ppermute(values, axis, [(i, i ^ distance) for i in range(size)])  85.3 us
    unnamed x368, local copies, waits for them, and re-layouts  59.3 us
    ppermute x55, starting transfers between devices, swap_axis(): return lax.ppermute(values, axis, [(i, i ^ distance) for i in range(size)])  29 us
    ppermute x26, starting transfers between devices, hop(): return lax.ppermute(values, ('dp', 'row'), pairs)  27.5 us
  transfers between devices with their start and end apart: 82, of which 28 were waited for; matrix products, arithmetic and copies ran while one was open for 7% of the time, Pallas kernels for 48%

profile of v3, /device:TPU:0, one launch (start us, length us, event | category | flops | bytes accessed | tf_op | source)
XLA Modules:
  0.0 917.5 jit_solution(10403245422803150143)
XLA Ops:
  42.5 7.0 own.6.refs_3_.refs_1_.refs_2_.refs_5_
  63.5 6.6 qkv.4
  72.8 5.8 attend.4
  94.8 9.4 %collective-permute-done.8.refs_2_ = bf16[512,1024]{1,0:T(8,128)(2,1)} collective-permute-done((bf16[512,1024]{1,0:T(8,128)(2,1)}, bf16[512,1024]{1,0:T(8,128)(2,1)}, u32[]{:S(2)}, u32[]{:S(2)}) %collective-permute-start.8) | collective-permute-done | bytes 1048608 | tf_op jit(solution)/shard_map/ppermute | solution.py:598
  106.4 5.8 attend.5
  112.3 7.2 collective-permute-done.11.refs_4_
  127.0 5.8 attend.6
  146.5 6.8 collective-permute-done.12.refs_1_
  153.8 6.6 attend.7
  164.8 15.3 %collective-permute-done.17.refs_2_ = bf16[384,2048]{1,0:T(8,128)(2,1)} collective-permute-done((bf16[384,2048]{1,0:T(8,128)(2,1)}, bf16[384,2048]{1,0:T(8,128)(2,1)}, u32[]{:S(2)}, u32[]{:S(2)}) %collective-permute-start.17) | collective-permute-done | bytes 1572896 | tf_op jit(solution)/shard_map/ppermute | solution.py:598
  194.3 14.3 %collective-permute-done.19.refs_4_ = bf16[384,2048]{1,0:T(8,128)(2,1)} collective-permute-done((bf16[384,2048]{1,0:T(8,128)(2,1)}, bf16[384,2048]{1,0:T(8,128)(2,1)}, u32[]{:S(2)}, u32[]{:S(2)}) %collective-permute-start.19) | collective-permute-done | bytes 1572896 | tf_op jit(solution)/shard_map/ppermute | solution.py:598
  213.6 21.8 %collective-permute-done.16.refs_3_ = bf16[512,2048]{1,0:T(8,128)(2,1)} collective-permute-done((bf16[512,2048]{1,0:T(8,128)(2,1)}, bf16[512,2048]{1,0:T(8,128)(2,1)}, u32[]{:S(2)}, u32[]{:S(2)}) %collective-permute-start.16) | collective-permute-done | bytes 2097184 | tf_op jit(solution)/shard_map/ppermute | solution.py:577
  243.1 8.8 collective-permute-done.24.refs_1_
  256.2 19.4 %ffn.4 = (bf16[1024,1024]{1,0:T(8,128)(2,1)S(1)}, bf16[1024,2048]{1,0:T(8,128)(2,1)S(1)}) custom-call(bf16[1024,2048]{1,0:T(8,128)(2,1)S(1)} %join.12.refs_0_.refs_4_.refs_1_.refs_2_.refs_3_, bf16[1024,2048]{1,0:T(8,128)(2,1)} %copy-done.89, bf16[2048,2048]{1,0:T(8,128)(2,1)} %own.6.refs_3_.refs_1_.refs_2_.refs_5_, bf16[1024,2048]{1,0:T(8,128)(2,1)} %copy-done.93, ...), custom_call_target="tpu_custom_call" | custom-call | flops 999999995904 | bytes 1 | tf_op jit(solution)/shard_map/ffn/pallas_call | solution.py:92
  275.7 21.1 %collective-permute-done.28.refs_1_ = bf16[512,2048]{1,0:T(8,128)(2,1)} collective-permute-done((bf16[512,2048]{1,0:T(8,128)(2,1)}, bf16[512,2048]{1,0:T(8,128)(2,1)}, u32[]{:S(2)}, u32[]{:S(2)}) %collective-permute-start.28) | collective-permute-done | bytes 2097184 | tf_op jit(solution)/shard_map/ppermute | solution.py:577
  304.9 19.4 %ffn.5 = (bf16[1024,1024]{1,0:T(8,128)(2,1)S(1)}, bf16[1024,2048]{1,0:T(8,128)(2,1)S(1)}) custom-call(bf16[1024,2048]{1,0:T(8,128)(2,1)S(1)} %join.13.refs_0_.refs_4_.refs_5_.refs_6_.refs_7_.refs_8_, bf16[1024,2048]{1,0:T(8,128)(2,1)} %copy-done.90, bf16[2048,2048]{1,0:T(8,128)(2,1)} %own.6.refs_3_.refs_1_.refs_2_.refs_5_, bf16[1024,2048]{1,0:T(8,128)(2,1)} %copy-done.93, ...), custom_call_target="tpu_custom_call" | custom-call | flops 999999995904 | bytes 1 | tf_op jit(solution)/shard_map/ffn/pallas_call | solution.py:92
  326.4 6.1 other.5
  334.4 18.1 %ffn.6 = (bf16[1024,1024]{1,0:T(8,128)(2,1)S(1)}, bf16[1024,2048]{1,0:T(8,128)(2,1)S(1)}) custom-call(bf16[1024,2048]{1,0:T(8,128)(2,1)S(1)} %copy-done.81, bf16[1024,2048]{1,0:T(8,128)(2,1)} %copy-done.90, bf16[2048,2048]{1,0:T(8,128)(2,1)} %get-tuple-element.329.refs_2_.refs_4_.refs_6_, bf16[1024,2048]{1,0:T(8,128)(2,1)} %copy-done.91, ...), custom_call_target="tpu_custom_call" | custom-call | flops 999999995904 | bytes 1 | tf_op jit(solution)/shard_map/ffn/pallas_call | solution.py:92
  352.5 20.1 %ffn.7 = (bf16[1024,1024]{1,0:T(8,128)(2,1)S(1)}, bf16[1024,2048]{1,0:T(8,128)(2,1)S(1)}) custom-call(bf16[1024,2048]{1,0:T(8,128)(2,1)S(1)} %copy-done.76, bf16[1024,2048]{1,0:T(8,128)(2,1)} %copy-done.89, bf16[2048,2048]{1,0:T(8,128)(2,1)} %get-tuple-element.329.refs_2_.refs_4_.refs_6_, bf16[1024,2048]{1,0:T(8,128)(2,1)} %copy-done.91, ...), custom_call_target="tpu_custom_call" | custom-call | flops 999999995904 | bytes 1 | tf_op jit(solution)/shard_map/ffn/pallas_call | solution.py:92
  374.6 24.5 %gu_grad.2.refs_1_ = bf16[2,512,4096]{2,1,0:T(8,128)(2,1)} custom-call(s32[6]{0:T(128)S(1)} %stack.45.refs_0_, bf16[1024,2048]{1,0:T(8,128)(2,1)S(1)} %copy-done.76, bf16[1024,2048]{1,0:T(8,128)(2,1)S(1)} %copy-done.76, bf16[1024,2048]{1,0:T(8,128)(2,1)S(1)} %copy-done.76, bf16[1024,2048]{1,0:T(8,128)(2,1)S(1)} %copy-done.76, ...), custom_call_target="tpu_custom_call" | custom-call | flops 999999995904 | bytes 1 | tf_op jit(solution)/shard_map/gu_grad/pallas_call | solution.py:92
  406.5 21.7 %ffn_in.2 = (bf16[512,2048]{1,0:T(8,128)(2,1)}, bf16[512,2048]{1,0:T(8,128)(2,1)S(1)}) custom-call(s32[6]{0:T(128)S(1)} %stack.45.refs_0_, bf16[1024,2048]{1,0:T(8,128)(2,1)S(1)} %copy-done.84, bf16[1024,2048]{1,0:T(8,128)(2,1)S(1)} %copy-done.86, bf16[1024,2048]{1,0:T(8,128)(2,1)S(1)} %copy-done.84, bf16[1024,2048]{1,0:T(8,128)(2,1)S(1)} %copy-done.86, ...), custom_call_target="tpu_custom_call" | custom-call | flops 999999995904 | bytes 1 | tf_op jit(solution)/shard_map/ffn_in/pallas_call | solution.py:92
  440.2 22.9 %ffn_in.3 = (bf16[512,2048]{1,0:T(8,128)(2,1)}, bf16[512,2048]{1,0:T(8,128)(2,1)S(1)}) custom-call(s32[6]{0:T(128)S(1)} %stack.45.refs_0_, bf16[1024,2048]{1,0:T(8,128)(2,1)S(1)} %copy-done.79, bf16[1024,2048]{1,0:T(8,128)(2,1)S(1)} %copy-done.88, bf16[1024,2048]{1,0:T(8,128)(2,1)S(1)} %copy-done.79, bf16[1024,2048]{1,0:T(8,128)(2,1)S(1)} %copy-done.88, ...), custom_call_target="tpu_custom_call" | custom-call | flops 999999995904 | bytes 1 | tf_op jit(solution)/shard_map/ffn_in/pallas_call | solution.py:92
  463.5 24.4 %gu_grad.3.refs_7_ = bf16[2,512,4096]{2,1,0:T(8,128)(2,1)} custom-call(s32[6]{0:T(128)S(1)} %stack.45.refs_0_, bf16[1024,2048]{1,0:T(8,128)(2,1)S(1)} %copy-done.77, bf16[1024,2048]{1,0:T(8,128)(2,1)S(1)} %copy-done.77, bf16[1024,2048]{1,0:T(8,128)(2,1)S(1)} %copy-done.77, bf16[1024,2048]{1,0:T(8,128)(2,1)S(1)} %copy-done.77, ...), custom_call_target="tpu_custom_call" | custom-call | flops 999999995904 | bytes 1 | tf_op jit(solution)/shard_map/gu_grad/pallas_call | solution.py:92
  488.5 7.0 ffn_back.1
  503.7 7.1 fusion.refs_1_
  515.9 8.6 attend_back.4
  526.6 8.2 attend_back.5
  534.9 9.3 %collective-permute-done.40.refs_1_ = bf16[512,2048]{1,0:T(8,128)(2,1)} collective-permute-done((bf16[512,2048]{1,0:T(8,128)(2,1)}, bf16[512,2048]{1,0:T(8,128)(2,1)}, u32[]{:S(2)}, u32[]{:S(2)}) %collective-permute-start.40) | collective-permute-done | bytes 2097184 | tf_op jit(solution)/shard_map/ppermute | solution.py:577
  544.2 15.2 %down_grad.2.refs_2_ = bf16[2,512,2048]{2,1,0:T(8,128)(2,1)} custom-call(s32[6]{0:T(128)S(1)} %copy-done.48, bf16[1024,2048]{1,0:T(8,128)(2,1)} %copy-done.89, bf16[1024,2048]{1,0:T(8,128)(2,1)} %copy-done.89, bf16[1024,2048]{1,0:T(8,128)(2,1)} %copy-done.89, bf16[1024,2048]{1,0:T(8,128)(2,1)} %copy-done.89, bf16[1024,2048]{1,0:T(8,128)(2,1)} %copy-done.90, ...), custom_call_target="tpu_custom_call" | custom-call | flops 999999995904 | bytes 1 | tf_op jit(solution)/shard_map/down_grad/pallas_call | solution.py:92
  575.1 15.1 %down_grad.3.refs_3_ = bf16[2,512,2048]{2,1,0:T(8,128)(2,1)S(1)} custom-call(s32[6]{0:T(128)S(1)} %copy-done.48, bf16[1024,2048]{1,0:T(8,128)(2,1)} %copy-done.89, bf16[1024,2048]{1,0:T(8,128)(2,1)} %copy-done.89, bf16[1024,2048]{1,0:T(8,128)(2,1)} %copy-done.89, bf16[1024,2048]{1,0:T(8,128)(2,1)} %copy-done.89, bf16[1024,2048]{1,0:T(8,128)(2,1)} %copy-done.90, ...), custom_call_target="tpu_custom_call" | custom-call | flops 999999995904 | bytes 1 | tf_op jit(solution)/shard_map/down_grad/pallas_call | solution.py:92
  597.8 8.4 attend_back.6
  608.7 8.2 attend_back.7
  625.1 9.2 %qkv_in.2 = (bf16[512,2048]{1,0:T(8,128)(2,1)}, bf16[512,2048]{1,0:T(8,128)(2,1)S(1)}) custom-call(s32[6]{0:T(128)S(1)} %copy-done.49, bf16[1024,768]{1,0:T(8,128)(2,1)S(1)} %get-tuple-element.501.refs_1_.refs_3_, bf16[1024,768]{1,0:T(8,128)(2,1)S(1)} %get-tuple-element.502.refs_2_.refs_4_, bf16[1024,768]{1,0:T(8,128)(2,1)S(1)} %get-tuple-element.501.refs_1_.refs_3_, ...), custom_call_target="tpu_custom_call" | custom-call | flops 999999995904 | bytes 1 | tf_op jit(solution)/shard_map/qkv_in/pallas_call | solution.py:92
  635.5 19.0 %head_grad.2.refs_1_ = bf16[2,512,2048]{2,1,0:T(8,128)(2,1)} custom-call(s32[6]{0:T(128)S(1)} %copy-done.49, bf16[1024,2048]{1,0:T(8,128)(2,1)} %copy-done.70, bf16[1024,2048]{1,0:T(8,128)(2,1)} %copy-done.70, bf16[1024,2048]{1,0:T(8,128)(2,1)} %copy-done.70, bf16[1024,2048]{1,0:T(8,128)(2,1)} %copy-done.70, bf16[1024,2048]{1,0:T(8,128)(2,1)} %copy-done.72, ...), custom_call_target="tpu_custom_call" | custom-call | flops 999999995904 | bytes 1 | tf_op jit(solution)/shard_map/head_grad/pallas_call | solution.py:92
  666.2 9.2 %qkv_in.3 = (bf16[512,2048]{1,0:T(8,128)(2,1)}, bf16[512,2048]{1,0:T(8,128)(2,1)S(1)}) custom-call(s32[6]{0:T(128)S(1)} %copy-done.49, bf16[1024,768]{1,0:T(8,128)(2,1)S(1)} %get-tuple-element.503.refs_1_.refs_3_, bf16[1024,768]{1,0:T(8,128)(2,1)S(1)} %get-tuple-element.504.refs_2_.refs_4_, bf16[1024,768]{1,0:T(8,128)(2,1)S(1)} %get-tuple-element.503.refs_1_.refs_3_, ...), custom_call_target="tpu_custom_call" | custom-call | flops 999999995904 | bytes 1 | tf_op jit(solution)/shard_map/qkv_in/pallas_call | solution.py:92
  683.0 19.0 %head_grad.3.refs_2_ = bf16[2,512,2048]{2,1,0:T(8,128)(2,1)S(1)} custom-call(s32[6]{0:T(128)S(1)} %copy-done.49, bf16[1024,2048]{1,0:T(8,128)(2,1)} %copy-done.70, bf16[1024,2048]{1,0:T(8,128)(2,1)} %copy-done.70, bf16[1024,2048]{1,0:T(8,128)(2,1)} %copy-done.70, bf16[1024,2048]{1,0:T(8,128)(2,1)} %copy-done.70, bf16[1024,2048]{1,0:T(8,128)(2,1)} %copy-done.72, ...), custom_call_target="tpu_custom_call" | custom-call | flops 999999995904 | bytes 1 | tf_op jit(solution)/shard_map/head_grad/pallas_call | solution.py:92
  711.1 12.8 %down.2 = (bf16[512,2048]{1,0:T(8,128)(2,1)}, bf16[512,2048]{1,0:T(8,128)(2,1)S(1)}) custom-call(s32[6]{0:T(128)S(1)} %copy-done.50, bf16[1024,1024]{1,0:T(8,128)(2,1)S(1)} %copy-done.119, bf16[1024,1024]{1,0:T(8,128)(2,1)S(1)} %copy-done.123, bf16[1024,1024]{1,0:T(8,128)(2,1)S(1)} %copy-done.119, bf16[1024,1024]{1,0:T(8,128)(2,1)S(1)} %copy-done.123, ...), custom_call_target="tpu_custom_call" | custom-call | flops 999999995904 | bytes 1 | tf_op jit(solution)/shard_map/down/pallas_call | solution.py:92
  724.4 6.8 fusion.3.refs_8_
  742.1 7.6 input_back.1
  765.2 5.9 sides.2.refs_8_
  773.0 11.9 %down.3 = (bf16[512,2048]{1,0:T(8,128)(2,1)}, bf16[512,2048]{1,0:T(8,128)(2,1)S(1)}) custom-call(s32[6]{0:T(128)S(1)} %copy-done.50, bf16[1024,1024]{1,0:T(8,128)(2,1)S(1)} %copy-done.115, bf16[1024,1024]{1,0:T(8,128)(2,1)S(1)} %copy-done.111, bf16[1024,1024]{1,0:T(8,128)(2,1)S(1)} %copy-done.115, bf16[1024,1024]{1,0:T(8,128)(2,1)S(1)} %copy-done.111, ...), custom_call_target="tpu_custom_call" | custom-call | flops 999999995904 | bytes 1 | tf_op jit(solution)/shard_map/down/pallas_call | solution.py:92
  801.0 32.9 %collective-permute-done.70 = f32[2,2048]{1,0:T(2,128)S(1)} collective-permute-done((f32[2,2048]{1,0:T(2,128)S(1)}, f32[2,2048]{1,0:T(2,128)S(1)}, u32[]{:S(2)}, u32[]{:S(2)}) %collective-permute-start.70) | collective-permute-done | bytes 16416 | tf_op jit(solution)/shard_map/ppermute | solution.py:598
  853.7 11.5 %finish.3 = (f32[1024,2048]{1,0:T(8,128)}, f32[1024,2048]{1,0:T(8,128)}) custom-call(s32[6]{0:T(128)S(1)} %copy-done.50, bf16[2,256,2048]{2,1,0:T(8,128)(2,1)} %all-to-all-done.refs_1_, bf16[2,256,2048]{2,1,0:T(8,128)(2,1)} %collective-permute-done.55.refs_2_, bf16[2,256,2048]{2,1,0:T(8,128)(2,1)} %collective-permute-done.68.refs_3_, ...), custom_call_target="tpu_custom_call" | custom-call | flops 999999995904 | bytes 1 | tf_op jit(solution)/shard_map/finish/pallas_call | solution.py:92
  868.5 9.5 %collective-permute-done.77.refs_2_ = bf16[2,256,1024]{2,1,0:T(8,128)(2,1)} collective-permute-done((bf16[2,256,1024]{2,1,0:T(8,128)(2,1)}, bf16[2,256,1024]{2,1,0:T(8,128)(2,1)}, u32[]{:S(2)}, u32[]{:S(2)}) %collective-permute-start.77) | collective-permute-done | bytes 1048608 | tf_op jit(solution)/shard_map/ppermute | solution.py:598
  880.1 6.4 collective-permute-done.75.refs_3_
  886.5 6.7 finish.4.refs_3_
  901.3 7.7 collective-permute-done.80.refs_4_
  910.6 6.5 finish.5
  (608 shorter events, 324.9 us)
Async XLA Ops:
  0.6 35.0 %collective-permute-start = (bf16[1024,1024]{1,0:T(8,128)(2,1)}, bf16[1024,1024]{1,0:T(8,128)(2,1)}, u32[]{:S(2)}, u32[]{:S(2)}) collective-permute-start(bf16[1024,1024]{1,0:T(8,128)(2,1)} %refs_1_.16), channel_id=1, source_target_pairs={{0,4},{4,0},{1,5},{5,1},{2,6},{6,2},{3,7},{7,3},{8,12},{12,8},{9,1... | collective-permute-start | bytes 6291464 | tf_op jit(solution)/shard_map/ppermute | solution.py:577
  1.2 71.7 %collective-permute-start.6 = (bf16[1024,1024]{1,0:T(8,128)(2,1)}, bf16[1024,1024]{1,0:T(8,128)(2,1)}, u32[]{:S(2)}, u32[]{:S(2)}) collective-permute-start(bf16[1024,1024]{1,0:T(8,128)(2,1)} %refs_1_.16), channel_id=1, source_target_pairs={{0,1},{1,0},{2,3},{3,2},{4,5},{5,4},{6,7},{7,6},{8,9},{9,8},{10,11... | collective-permute-start | bytes 6291464 | tf_op jit(solution)/shard_map/ppermute | solution.py:577
  21.2 57.5 %collective-permute-start.7 = (bf16[512,1024]{1,0:T(8,128)(2,1)}, bf16[512,1024]{1,0:T(8,128)(2,1)}, u32[]{:S(2)}, u32[]{:S(2)}) collective-permute-start(bf16[512,1024]{1,0:T(8,128)(2,1)} %quarter.3.refs_4_), channel_id=1, source_target_pairs={{0,2},{1,3},{2,0},{3,1},{4,6},{5,7},{6,4},{7,5},{8,10},{9,11},{10,... | collective-permute-start | bytes 3145736 | tf_op jit(solution)/shard_map/ppermute | solution.py:577
  78.7 25.5 %collective-permute-start.8 = (bf16[512,1024]{1,0:T(8,128)(2,1)}, bf16[512,1024]{1,0:T(8,128)(2,1)}, u32[]{:S(2)}, u32[]{:S(2)}) collective-permute-start(bf16[512,1024]{1,0:T(8,128)(2,1)} %collective-permute-done.7.refs_1_), channel_id=1, source_target_pairs={{0,8},{4,20},{8,0},{12,28},{16,24},{20,4},{24,16},{28,12},{1,9},{5... | collective-permute-start | bytes 3145736 | tf_op jit(solution)/shard_map/ppermute | solution.py:598
  80.4 31.9 %collective-permute-start.9 = (bf16[512,1024]{1,0:T(8,128)(2,1)}, bf16[512,1024]{1,0:T(8,128)(2,1)}, u32[]{:S(2)}, u32[]{:S(2)}) collective-permute-start(bf16[512,1024]{1,0:T(8,128)(2,1)} %collective-permute-done.7.refs_1_), channel_id=1, source_target_pairs={{0,16},{4,12},{8,24},{12,4},{16,0},{20,28},{24,8},{28,20},{1,17},{... | collective-permute-start | bytes 3145736 | tf_op jit(solution)/shard_map/ppermute | solution.py:598
  82.0 71.3 %collective-permute-start.12 = (bf16[384,2048]{1,0:T(8,128)(2,1)}, bf16[384,2048]{1,0:T(8,128)(2,1)}, u32[]{:S(2)}, u32[]{:S(2)}) collective-permute-start(bf16[384,2048]{1,0:T(8,128)(2,1)} %quarter.4.refs_3_), channel_id=1, source_target_pairs={{0,2},{1,3},{2,0},{3,1},{4,6},{5,7},{6,4},{7,5},{8,10},{9,11},{10,... | collective-permute-start | bytes 4718600 | tf_op jit(solution)/shard_map/ppermute | solution.py:577
  83.6 99.5 %collective-permute-start.20 = (bf16[1024,1024]{1,0:T(8,128)(2,1)}, bf16[1024,1024]{1,0:T(8,128)(2,1)}, u32[]{:S(2)}, u32[]{:S(2)}) collective-permute-start(bf16[1024,1024]{1,0:T(8,128)(2,1)} %refs_1_.19), channel_id=1, source_target_pairs={{0,1},{1,0},{2,3},{3,2},{4,5},{5,4},{6,7},{7,6},{8,9},{9,8},{10,11... | collective-permute-start | bytes 6291464 | tf_op jit(solution)/shard_map/ppermute | solution.py:577
  104.2 15.4 %collective-permute-start.11 = (bf16[512,1024]{1,0:T(8,128)(2,1)}, bf16[512,1024]{1,0:T(8,128)(2,1)}, u32[]{:S(2)}, u32[]{:S(2)}) collective-permute-start(bf16[512,1024]{1,0:T(8,128)(2,1)} %collective-permute-done.8.refs_2_), channel_id=1, source_target_pairs={{0,16},{4,12},{8,24},{12,4},{16,0},{20,28},{24,8},{28,20},{1,17},{... | collective-permute-start | bytes 3145736 | tf_op jit(solution)/shard_map/ppermute | solution.py:598
  145.4 90.0 %collective-permute-start.16 = (bf16[512,2048]{1,0:T(8,128)(2,1)}, bf16[512,2048]{1,0:T(8,128)(2,1)}, u32[]{:S(2)}, u32[]{:S(2)}) collective-permute-start(bf16[512,2048]{1,0:T(8,128)(2,1)} %add_convert_fusion.7.refs_1_), channel_id=1, source_target_pairs={{0,1},{1,0},{2,3},{3,2},{4,5},{5,4},{6,7},{7,6},{8,9},{9,8},{10,11... | collective-permute-start | bytes 6291464 | tf_op jit(solution)/shard_map/ppermute | solution.py:577
  153.2 26.8 %collective-permute-start.17 = (bf16[384,2048]{1,0:T(8,128)(2,1)}, bf16[384,2048]{1,0:T(8,128)(2,1)}, u32[]{:S(2)}, u32[]{:S(2)}) collective-permute-start(bf16[384,2048]{1,0:T(8,128)(2,1)} %collective-permute-done.12.refs_1_), channel_id=1, source_target_pairs={{0,8},{4,20},{8,0},{12,28},{16,24},{20,4},{24,16},{28,12},{1,9},{5... | collective-permute-start | bytes 4718600 | tf_op jit(solution)/shard_map/ppermute | solution.py:598
  153.8 26.3 %collective-permute-start.21 = (bf16[1024,1024]{1,0:T(8,128)(2,1)}, bf16[1024,1024]{1,0:T(8,128)(2,1)}, u32[]{:S(2)}, u32[]{:S(2)}) collective-permute-start(bf16[1024,1024]{1,0:T(8,128)(2,1)} %refs_1_.19), channel_id=1, source_target_pairs={{0,4},{4,0},{1,5},{5,1},{2,6},{6,2},{3,7},{7,3},{8,12},{12,8},{9,1... | collective-permute-start | bytes 6291464 | tf_op jit(solution)/shard_map/ppermute | solution.py:577
  164.4 29.9 %collective-permute-start.18 = (bf16[384,2048]{1,0:T(8,128)(2,1)}, bf16[384,2048]{1,0:T(8,128)(2,1)}, u32[]{:S(2)}, u32[]{:S(2)}) collective-permute-start(bf16[384,2048]{1,0:T(8,128)(2,1)} %collective-permute-done.12.refs_1_), channel_id=1, source_target_pairs={{0,16},{4,12},{8,24},{12,4},{16,0},{20,28},{24,8},{28,20},{1,17},{... | collective-permute-start | bytes 4718600 | tf_op jit(solution)/shard_map/ppermute | solution.py:598
  180.1 55.4 %collective-permute-start.15 = (bf16[512,2048]{1,0:T(8,128)(2,1)}, bf16[512,2048]{1,0:T(8,128)(2,1)}, u32[]{:S(2)}, u32[]{:S(2)}) collective-permute-start(bf16[512,2048]{1,0:T(8,128)(2,1)} %get-tuple-element.307.refs_3_), channel_id=1, source_target_pairs={{0,4},{4,0},{1,5},{5,1},{2,6},{6,2},{3,7},{7,3},{8,12},{12,8},{9,1... | collective-permute-start | bytes 6291464 | tf_op jit(solution)/shard_map/ppermute | solution.py:577
  180.1 71.9 %collective-permute-start.24 = (bf16[384,2048]{1,0:T(8,128)(2,1)}, bf16[384,2048]{1,0:T(8,128)(2,1)}, u32[]{:S(2)}, u32[]{:S(2)}) collective-permute-start(bf16[384,2048]{1,0:T(8,128)(2,1)} %quarter.5.refs_5_), channel_id=1, source_target_pairs={{0,2},{1,3},{2,0},{3,1},{4,6},{5,7},{6,4},{7,5},{8,10},{9,11},{10,... | collective-permute-start | bytes 4718600 | tf_op jit(solution)/shard_map/ppermute | solution.py:577
  187.9 20.7 %collective-permute-start.19 = (bf16[384,2048]{1,0:T(8,128)(2,1)}, bf16[384,2048]{1,0:T(8,128)(2,1)}, u32[]{:S(2)}, u32[]{:S(2)}) collective-permute-start(bf16[384,2048]{1,0:T(8,128)(2,1)} %collective-permute-done.17.refs_2_), channel_id=1, source_target_pairs={{0,16},{4,12},{8,24},{12,4},{16,0},{20,28},{24,8},{28,20},{1,17},{... | collective-permute-start | bytes 4718600 | tf_op jit(solution)/shard_map/ppermute | solution.py:598
  241.1 55.7 %collective-permute-start.28 = (bf16[512,2048]{1,0:T(8,128)(2,1)}, bf16[512,2048]{1,0:T(8,128)(2,1)}, u32[]{:S(2)}, u32[]{:S(2)}) collective-permute-start(bf16[512,2048]{1,0:T(8,128)(2,1)} %get-tuple-element.311.refs_1_), channel_id=1, source_target_pairs={{0,1},{1,0},{2,3},{3,2},{4,5},{5,4},{6,7},{7,6},{8,9},{9,8},{10,11... | collective-permute-start | bytes 6291464 | tf_op jit(solution)/shard_map/ppermute | solution.py:577
  252.0 44.9 %collective-permute-start.26 = (bf16[384,2048]{1,0:T(8,128)(2,1)}, bf16[384,2048]{1,0:T(8,128)(2,1)}, u32[]{:S(2)}, u32[]{:S(2)}) collective-permute-start(bf16[384,2048]{1,0:T(8,128)(2,1)} %collective-permute-done.24.refs_1_), channel_id=1, source_target_pairs={{0,8},{4,20},{8,0},{12,28},{16,24},{20,4},{24,16},{28,12},{1,9},{5... | collective-permute-start | bytes 4718600 | tf_op jit(solution)/shard_map/ppermute | solution.py:598
  252.0 74.4 %collective-permute-start.27 = (bf16[384,2048]{1,0:T(8,128)(2,1)}, bf16[384,2048]{1,0:T(8,128)(2,1)}, u32[]{:S(2)}, u32[]{:S(2)}) collective-permute-start(bf16[384,2048]{1,0:T(8,128)(2,1)} %collective-permute-done.24.refs_1_), channel_id=1, source_target_pairs={{0,16},{4,12},{8,24},{12,4},{16,0},{20,28},{24,8},{28,20},{1,17},{... | collective-permute-start | bytes 4718600 | tf_op jit(solution)/shard_map/ppermute | solution.py:598
  297.4 28.9 %collective-permute-start.29 = (bf16[384,2048]{1,0:T(8,128)(2,1)}, bf16[384,2048]{1,0:T(8,128)(2,1)}, u32[]{:S(2)}, u32[]{:S(2)}) collective-permute-start(bf16[384,2048]{1,0:T(8,128)(2,1)} %collective-permute-done.26.refs_2_), channel_id=1, source_target_pairs={{0,16},{4,12},{8,24},{12,4},{16,0},{20,28},{24,8},{28,20},{1,17},{... | collective-permute-start | bytes 4718600 | tf_op jit(solution)/shard_map/ppermute | solution.py:598
  399.2 104.5 %collective-permute-start.34 = (bf16[2,512,4096]{2,1,0:T(8,128)(2,1)}, bf16[2,512,4096]{2,1,0:T(8,128)(2,1)}, u32[]{:S(2)}, u32[]{:S(2)}) collective-permute-start(bf16[2,512,4096]{2,1,0:T(8,128)(2,1)} %gu_grad.2.refs_1_), channel_id=1, source_target_pairs={{0,8},{4,20},{8,0},{12,28},{16,24},{20,4},{24,16},{28,12},{1,9},{5... | collective-permute-start | bytes 25165832 | tf_op jit(solution)/shard_map/ppermute | solution.py:598
  436.5 51.3 %collective-permute-start.36 = (bf16[512,2048]{1,0:T(8,128)(2,1)}, bf16[512,2048]{1,0:T(8,128)(2,1)}, u32[]{:S(2)}, u32[]{:S(2)}) collective-permute-start(bf16[512,2048]{1,0:T(8,128)(2,1)} %add_convert_fusion.6.refs_1_), channel_id=1, source_target_pairs={{0,1},{1,0},{2,3},{3,2},{4,5},{5,4},{6,7},{7,6},{8,9},{9,8},{10,11... | collective-permute-start | bytes 6291464 | tf_op jit(solution)/shard_map/ppermute | solution.py:577
  463.0 24.8 %collective-permute-start.35 = (bf16[512,2048]{1,0:T(8,128)(2,1)}, bf16[512,2048]{1,0:T(8,128)(2,1)}, u32[]{:S(2)}, u32[]{:S(2)}) collective-permute-start(bf16[512,2048]{1,0:T(8,128)(2,1)} %get-tuple-element.346.refs_13_), channel_id=1, source_target_pairs={{0,4},{4,0},{1,5},{5,1},{2,6},{6,2},{3,7},{7,3},{8,12},{12,8},{9,1... | collective-permute-start | bytes 6291464 | tf_op jit(solution)/shard_map/ppermute | solution.py:577
  495.7 48.5 %collective-permute-start.40 = (bf16[512,2048]{1,0:T(8,128)(2,1)}, bf16[512,2048]{1,0:T(8,128)(2,1)}, u32[]{:S(2)}, u32[]{:S(2)}) collective-permute-start(bf16[512,2048]{1,0:T(8,128)(2,1)} %get-tuple-element.348.refs_1_), channel_id=1, source_target_pairs={{0,1},{1,0},{2,3},{3,2},{4,5},{5,4},{6,7},{7,6},{8,9},{9,8},{10,11... | collective-permute-start | bytes 6291464 | tf_op jit(solution)/shard_map/ppermute | solution.py:577
  510.7 50.7 %collective-permute-start.39 = (bf16[512,4096]{1,0:T(8,128)(2,1)}, bf16[512,4096]{1,0:T(8,128)(2,1)}, u32[]{:S(2)}, u32[]{:S(2)}) collective-permute-start(bf16[512,4096]{1,0:T(8,128)(2,1)} %fusion.refs_1_), channel_id=1, source_target_pairs={{0,16},{4,12},{8,24},{12,4},{16,0},{20,28},{24,8},{28,20},{1,17},{... | collective-permute-start | bytes 12582920 | tf_op jit(solution)/shard_map/ppermute | solution.py:598
  559.4 57.5 %collective-permute-start.46 = (bf16[2,512,2048]{2,1,0:T(8,128)(2,1)}, bf16[2,512,2048]{2,1,0:T(8,128)(2,1)}, u32[]{:S(2)}, u32[]{:S(2)}) collective-permute-start(bf16[2,512,2048]{2,1,0:T(8,128)(2,1)} %down_grad.2.refs_2_), channel_id=1, source_target_pairs={{0,8},{4,20},{8,0},{12,28},{16,24},{20,4},{24,16},{28,12},{1,9},{5... | collective-permute-start | bytes 12582920 | tf_op jit(solution)/shard_map/ppermute | solution.py:598
  561.1 29.1 %collective-permute-start.43 = (bf16[512,2048]{1,0:T(8,128)(2,1)}, bf16[512,2048]{1,0:T(8,128)(2,1)}, u32[]{:S(2)}, u32[]{:S(2)}) collective-permute-start(bf16[512,2048]{1,0:T(8,128)(2,1)} %collective-permute-done.40.refs_1_), channel_id=1, source_target_pairs={{0,4},{4,0},{1,5},{5,1},{2,6},{6,2},{3,7},{7,3},{8,12},{12,8},{9,1... | collective-permute-start | bytes 6291464 | tf_op jit(solution)/shard_map/ppermute | solution.py:577
  567.1 156.8 %collective-permute-start.42 = (bf16[512,2048]{1,0:T(8,128)(2,1)}, bf16[512,2048]{1,0:T(8,128)(2,1)}, u32[]{:S(2)}, u32[]{:S(2)}) collective-permute-start(bf16[512,2048]{1,0:T(8,128)(2,1)} %fusion.1.refs_1_), channel_id=1, source_target_pairs={{0,2},{1,3},{2,0},{3,1},{4,6},{5,7},{6,4},{7,5},{8,10},{9,11},{10,... | collective-permute-start | bytes 6291464 | tf_op jit(solution)/shard_map/ppermute | solution.py:577
  621.2 54.7 %collective-permute-start.51 = (bf16[512,2048]{1,0:T(8,128)(2,1)}, bf16[512,2048]{1,0:T(8,128)(2,1)}, u32[]{:S(2)}, u32[]{:S(2)}) collective-permute-start(bf16[512,2048]{1,0:T(8,128)(2,1)} %fusion.4.refs_1_), channel_id=1, source_target_pairs={{0,16},{4,12},{8,24},{12,4},{16,0},{20,28},{24,8},{28,20},{1,17},{... | collective-permute-start | bytes 6291464 | tf_op jit(solution)/shard_map/ppermute | solution.py:598
  655.1 48.8 %collective-permute-start.53 = (bf16[2,512,2048]{2,1,0:T(8,128)(2,1)}, bf16[2,512,2048]{2,1,0:T(8,128)(2,1)}, u32[]{:S(2)}, u32[]{:S(2)}) collective-permute-start(bf16[2,512,2048]{2,1,0:T(8,128)(2,1)} %head_grad.2.refs_1_), channel_id=1, source_target_pairs={{0,8},{4,20},{8,0},{12,28},{16,24},{20,4},{24,16},{28,12},{1,9},{5... | collective-permute-start | bytes 12582920 | tf_op jit(solution)/shard_map/ppermute | solution.py:598
  663.0 73.2 %collective-permute-start.57 = (bf16[512,2048]{1,0:T(8,128)(2,1)}, bf16[512,2048]{1,0:T(8,128)(2,1)}, u32[]{:S(2)}, u32[]{:S(2)}) collective-permute-start(bf16[512,2048]{1,0:T(8,128)(2,1)} %add_convert_fusion.4.refs_1_), channel_id=1, source_target_pairs={{0,1},{1,0},{2,3},{3,2},{4,5},{5,4},{6,7},{7,6},{8,9},{9,8},{10,11... | collective-permute-start | bytes 6291464 | tf_op jit(solution)/shard_map/ppermute | solution.py:577
  675.5 65.1 %collective-permute-start.56 = (bf16[512,2048]{1,0:T(8,128)(2,1)}, bf16[512,2048]{1,0:T(8,128)(2,1)}, u32[]{:S(2)}, u32[]{:S(2)}) collective-permute-start(bf16[512,2048]{1,0:T(8,128)(2,1)} %get-tuple-element.403.refs_2_), channel_id=1, source_target_pairs={{0,4},{4,0},{1,5},{5,1},{2,6},{6,2},{3,7},{7,3},{8,12},{12,8},{9,1... | collective-permute-start | bytes 6291464 | tf_op jit(solution)/shard_map/ppermute | solution.py:577
  681.2 106.0 %collective-permute-start.65 = (bf16[512,1024]{1,0:T(8,128)(2,1)}, bf16[512,1024]{1,0:T(8,128)(2,1)}, u32[]{:S(2)}, u32[]{:S(2)}) collective-permute-start(bf16[512,1024]{1,0:T(8,128)(2,1)} %fusion.11.refs_1_), channel_id=1, source_target_pairs={{0,2},{1,3},{2,0},{3,1},{4,6},{5,7},{6,4},{7,5},{8,10},{9,11},{10,... | collective-permute-start | bytes 3145736 | tf_op jit(solution)/shard_map/ppermute | solution.py:577
  708.9 42.9 %collective-permute-start.60 = (bf16[512,2048]{1,0:T(8,128)(2,1)}, bf16[512,2048]{1,0:T(8,128)(2,1)}, u32[]{:S(2)}, u32[]{:S(2)}) collective-permute-start(bf16[512,2048]{1,0:T(8,128)(2,1)} %fusion.5.refs_1_), channel_id=1, source_target_pairs={{0,16},{4,12},{8,24},{12,4},{16,0},{20,28},{24,8},{28,20},{1,17},{... | collective-permute-start | bytes 6291464 | tf_op jit(solution)/shard_map/ppermute | solution.py:598
  723.9 33.4 %collective-permute-start.59 = (bf16[512,2048]{1,0:T(8,128)(2,1)}, bf16[512,2048]{1,0:T(8,128)(2,1)}, u32[]{:S(2)}, u32[]{:S(2)}) collective-permute-start(bf16[512,2048]{1,0:T(8,128)(2,1)} %get-tuple-element.416.refs_9_), channel_id=1, source_target_pairs={{0,4},{4,0},{1,5},{5,1},{2,6},{6,2},{3,7},{7,3},{8,12},{12,8},{9,1... | collective-permute-start | bytes 6291464 | tf_op jit(solution)/shard_map/ppermute | solution.py:577
  739.1 33.9 %collective-permute-start.55 = (bf16[2,256,2048]{2,1,0:T(8,128)(2,1)}, bf16[2,256,2048]{2,1,0:T(8,128)(2,1)}, u32[]{:S(2)}, u32[]{:S(2)}) collective-permute-start(bf16[2,256,2048]{2,1,0:T(8,128)(2,1)} %all-to-all-done.refs_1_), channel_id=1, source_target_pairs={{0,8},{4,20},{8,0},{12,28},{16,24},{20,4},{24,16},{28,12},{1,9},{5... | collective-permute-start | bytes 6291464 | tf_op jit(solution)/shard_map/ppermute | solution.py:598
  751.7 19.4 %collective-permute-start.63 = (f32[2,2048]{1,0:T(2,128)}, f32[2,2048]{1,0:T(2,128)}, u32[]{:S(2)}, u32[]{:S(2)}) collective-permute-start(f32[2,2048]{1,0:T(2,128)} %pad_maximum_fusion.5.refs_2_), channel_id=1, source_target_pairs={{0,4},{4,0},{1,5},{5,1},{2,6},{6,2},{3,7},{7,3},{8,12},{12,8},{9,1... | collective-permute-start | bytes 49160 | tf_op jit(solution)/shard_map/ppermute | solution.py:577
  762.5 74.0 %collective-permute-start.72 = (bf16[512,1024]{1,0:T(8,128)(2,1)}, bf16[512,1024]{1,0:T(8,128)(2,1)}, u32[]{:S(2)}, u32[]{:S(2)}) collective-permute-start(bf16[512,1024]{1,0:T(8,128)(2,1)} %fusion.10.refs_1_), channel_id=1, source_target_pairs={{0,2},{1,3},{2,0},{3,1},{4,6},{5,7},{6,4},{7,5},{8,10},{9,11},{10,... | collective-permute-start | bytes 3145736 | tf_op jit(solution)/shard_map/ppermute | solution.py:577
  763.4 101.8 %collective-permute-start.67 = (bf16[512,2048]{1,0:T(8,128)(2,1)}, bf16[512,2048]{1,0:T(8,128)(2,1)}, u32[]{:S(2)}, u32[]{:S(2)}) collective-permute-start(bf16[512,2048]{1,0:T(8,128)(2,1)} %add_convert_fusion.2.refs_1_), channel_id=1, source_target_pairs={{0,1},{1,0},{2,3},{3,2},{4,5},{5,4},{6,7},{7,6},{8,9},{9,8},{10,11... | collective-permute-start | bytes 6291464 | tf_op jit(solution)/shard_map/ppermute | solution.py:577
  784.9 66.7 %collective-permute-start.69 = (bf16[2,256,2048]{2,1,0:T(8,128)(2,1)}, bf16[2,256,2048]{2,1,0:T(8,128)(2,1)}, u32[]{:S(2)}, u32[]{:S(2)}) collective-permute-start(bf16[2,256,2048]{2,1,0:T(8,128)(2,1)} %collective-permute-done.55.refs_2_), channel_id=1, source_target_pairs={{0,16},{4,12},{8,24},{12,4},{16,0},{20,28},{24,8},{28,20},{1,17},{... | collective-permute-start | bytes 6291464 | tf_op jit(solution)/shard_map/ppermute | solution.py:598
  787.2 65.9 %collective-permute-start.68 = (bf16[2,256,2048]{2,1,0:T(8,128)(2,1)}, bf16[2,256,2048]{2,1,0:T(8,128)(2,1)}, u32[]{:S(2)}, u32[]{:S(2)}) collective-permute-start(bf16[2,256,2048]{2,1,0:T(8,128)(2,1)} %all-to-all-done.refs_1_), channel_id=1, source_target_pairs={{0,16},{4,12},{8,24},{12,4},{16,0},{20,28},{24,8},{28,20},{1,17},{... | collective-permute-start | bytes 6291464 | tf_op jit(solution)/shard_map/ppermute | solution.py:598
  797.1 36.8 %collective-permute-start.70 = (f32[2,2048]{1,0:T(2,128)S(1)}, f32[2,2048]{1,0:T(2,128)S(1)}, u32[]{:S(2)}, u32[]{:S(2)}) collective-permute-start(f32[2,2048]{1,0:T(2,128)S(1)} %add.154.refs_3_), channel_id=1, source_target_pairs={{0,16},{4,12},{8,24},{12,4},{16,0},{20,28},{24,8},{28,20},{1,17},{... | collective-permute-start | bytes 49160 | tf_op jit(solution)/shard_map/ppermute | solution.py:598
  849.0 30.6 %collective-permute-start.76 = (bf16[2,256,1024]{2,1,0:T(8,128)(2,1)}, bf16[2,256,1024]{2,1,0:T(8,128)(2,1)}, u32[]{:S(2)}, u32[]{:S(2)}) collective-permute-start(bf16[2,256,1024]{2,1,0:T(8,128)(2,1)} %collective-permute-done.71.refs_2_), channel_id=1, source_target_pairs={{0,16},{4,12},{8,24},{12,4},{16,0},{20,28},{24,8},{28,20},{1,17},{... | collective-permute-start | bytes 3145736 | tf_op jit(solution)/shard_map/ppermute | solution.py:598
  850.5 36.1 %collective-permute-start.75 = (bf16[2,256,1024]{2,1,0:T(8,128)(2,1)}, bf16[2,256,1024]{2,1,0:T(8,128)(2,1)}, u32[]{:S(2)}, u32[]{:S(2)}) collective-permute-start(bf16[2,256,1024]{2,1,0:T(8,128)(2,1)} %all_to_all.34.refs_1_), channel_id=1, source_target_pairs={{0,16},{4,12},{8,24},{12,4},{16,0},{20,28},{24,8},{28,20},{1,17},{... | collective-permute-start | bytes 3145736 | tf_op jit(solution)/shard_map/ppermute | solution.py:598
  851.7 26.4 %collective-permute-start.77 = (bf16[2,256,1024]{2,1,0:T(8,128)(2,1)}, bf16[2,256,1024]{2,1,0:T(8,128)(2,1)}, u32[]{:S(2)}, u32[]{:S(2)}) collective-permute-start(bf16[2,256,1024]{2,1,0:T(8,128)(2,1)} %all_to_all.35.refs_1_), channel_id=1, source_target_pairs={{0,8},{4,20},{8,0},{12,28},{16,24},{20,4},{24,16},{28,12},{1,9},{5... | collective-permute-start | bytes 3145736 | tf_op jit(solution)/shard_map/ppermute | solution.py:598
  853.1 46.8 %collective-permute-start.78 = (f32[2,2048]{1,0:T(2,128)}, f32[2,2048]{1,0:T(2,128)}, u32[]{:S(2)}, u32[]{:S(2)}) collective-permute-start(f32[2,2048]{1,0:T(2,128)} %add.162.refs_5_), channel_id=1, source_target_pairs={{0,2},{1,3},{2,0},{3,1},{4,6},{5,7},{6,4},{7,5},{8,10},{9,11},{10,... | collective-permute-start | bytes 49160 | tf_op jit(solution)/shard_map/ppermute | solution.py:577
  868.5 24.7 %collective-permute-start.74 = (bf16[512,1024]{1,0:T(8,128)(2,1)}, bf16[512,1024]{1,0:T(8,128)(2,1)}, u32[]{:S(2)}, u32[]{:S(2)}) collective-permute-start(bf16[512,1024]{1,0:T(8,128)(2,1)} %get-tuple-element.479), channel_id=1, source_target_pairs={{0,4},{4,0},{1,5},{5,1},{2,6},{6,2},{3,7},{7,3},{8,12},{12,8},{9,1... | collective-permute-start | bytes 3145736 | tf_op jit(solution)/shard_map/ppermute | solution.py:577
  878.1 23.2 %collective-permute-start.79 = (bf16[2,256,1024]{2,1,0:T(8,128)(2,1)}, bf16[2,256,1024]{2,1,0:T(8,128)(2,1)}, u32[]{:S(2)}, u32[]{:S(2)}) collective-permute-start(bf16[2,256,1024]{2,1,0:T(8,128)(2,1)} %all_to_all.35.refs_1_), channel_id=1, source_target_pairs={{0,16},{4,12},{8,24},{12,4},{16,0},{20,28},{24,8},{28,20},{1,17},{... | collective-permute-start | bytes 3145736 | tf_op jit(solution)/shard_map/ppermute | solution.py:598
  879.5 29.5 %collective-permute-start.80 = (bf16[2,256,1024]{2,1,0:T(8,128)(2,1)}, bf16[2,256,1024]{2,1,0:T(8,128)(2,1)}, u32[]{:S(2)}, u32[]{:S(2)}) collective-permute-start(bf16[2,256,1024]{2,1,0:T(8,128)(2,1)} %collective-permute-done.77.refs_2_), channel_id=1, source_target_pairs={{0,16},{4,12},{8,24},{12,4},{16,0},{20,28},{24,8},{28,20},{1,17},{... | collective-permute-start | bytes 3145736 | tf_op jit(solution)/shard_map/ppermute | solution.py:598
  (218 other events, 2269.8 us)

commit v4 on v3

--- a/solution.py
+++ b/solution.py
@@ -29,15 +29,15 @@
 
 class Line:
     waiting = []
+    mark = None
 
     def __init__(self):
-        self.last, self.marks = [], []
+        self.last = []
 
     def run(self, call, *values):
         Line.waiting = list(self.last)
         result = call(*values)
-        self.last = jax.tree.leaves(result)[:1] + self.marks
-        self.marks = []
+        self.last = [Line.mark]
         return result
 
     def tied(self, value):
@@ -47,10 +47,7 @@
         return value
 
     def mix(self, call, first, *values):
-        first = self.tied(first)
-        result = call(first, *values)
-        self.last = jax.tree.leaves(result)[:1] + list(self.last)
-        return result
+        return self.tied(call(self.tied(first), *values))
 
     def send(self, move, value):
         return move(self.tied(value))
@@ -66,9 +63,7 @@
         return sent
 
     def swap(self, value):
-        value = lax.all_to_all(self.tied(value), "row", split_axis=0, concat_axis=0, tiled=True)
-        self.last = [value, *self.last]
-        return value
+        return self.tied(lax.all_to_all(self.tied(value), "row", split_axis=0, concat_axis=0, tiled=True))
 
 
 ONCE = pl.Buffered(1)
@@ -77,26 +72,33 @@
 def launch(kernel, arrays, in_specs, name, prefetch=(), **rest):
     held, Line.waiting = Line.waiting, []
     skip, count = len(held), len(prefetch) + len(arrays)
+    out_shape, out_specs = rest.pop("out_shape"), rest.pop("out_specs")
+    single = not isinstance(out_shape, (list, tuple))
+    out_shape, out_specs = ([out_shape], [out_specs]) if single else (list(out_shape), list(out_specs))
+    outs = count + skip + len(out_shape)
 
     def body(*refs):
-        kernel(*refs[:count], *refs[count + skip :])
+        kernel(*refs[:count], *refs[count + skip : outs], *refs[outs + 1 :])
 
     in_specs = list(in_specs) + [pl.BlockSpec(memory_space=pl.ANY)] * skip
-    out_shape = rest.pop("out_shape")
+    out_specs = out_specs + [pl.BlockSpec(memory_space=pl.ANY)]
     if prefetch:
         layout = dict(
-            grid_spec=pltpu.PrefetchScalarGridSpec(num_scalar_prefetch=len(prefetch), in_specs=in_specs, **rest)
+            grid_spec=pltpu.PrefetchScalarGridSpec(
+                num_scalar_prefetch=len(prefetch), in_specs=in_specs, out_specs=out_specs, **rest
+            )
         )
     else:
-        layout = dict(in_specs=in_specs, **rest)
-    return pl.pallas_call(
+        layout = dict(in_specs=in_specs, out_specs=out_specs, **rest)
+    *results, Line.mark = pl.pallas_call(
         body,
-        out_shape=out_shape,
+        out_shape=out_shape + [of((8, LANES), F32)],
         compiler_params=pltpu.CompilerParams(vmem_limit_bytes=VMEM),
         cost_estimate=pl.CostEstimate(flops=COST, bytes_accessed=1, transcendentals=0),
         name=name,
         **layout,
     )(*prefetch, *arrays, *held)
+    return results[0] if single else results
 
 
 def short_kernel(values):
@@ -117,7 +119,7 @@
     return tuple(sizes)
 
 
-def place(sources, outs, phases, where, name, kept=0):
+def place(sources, outs, phases, where, name, kept=0, fixed=0):
     moves = [m for phase in phases for m in phase]
     shapes = [extent((sources[src] if src >= 0 else outs[-1 - src]).shape, src_at([0] * 8)) for src, src_at, _, _ in moves]
     count = len(sources)
@@ -141,10 +143,13 @@
                 store.wait()
             base += len(phase)
 
+    sources = [pltpu.with_memory_space_constraint(a, pltpu.HBM) for a in sources[:fixed]] + list(sources[fixed:])
     return launch(
         kernel,
         [where, *sources],
-        [pl.BlockSpec(memory_space=pltpu.SMEM)] + [pl.BlockSpec(memory_space=pl.ANY)] * count,
+        [pl.BlockSpec(memory_space=pltpu.SMEM)]
+        + [pl.BlockSpec(memory_space=pltpu.HBM)] * fixed
+        + [pl.BlockSpec(memory_space=pl.ANY)] * (count - fixed),
         name,
         out_specs=[pl.BlockSpec(memory_space=pl.ANY)] * len(outs),
         out_shape=list(outs),
@@ -646,8 +651,8 @@
     def swap(self, value):
         return self.line.swap(value)
 
-    def place(self, sources, outs, phases, name, kept=0):
-        return self.run(lambda first, *rest: place([first, *rest], outs, phases, self.where, name, kept), *sources)
+    def place(self, sources, outs, phases, name, kept=0, fixed=0):
+        return self.run(lambda first, *rest: place([first, *rest], outs, phases, self.where, name, kept, fixed), *sources)
 
     def by_core(self, low, high):
         return jnp.where(self.core == 0, low, high), jnp.where(self.core == 0, high, low)
@@ -767,7 +772,7 @@
     for i, lo, size, step in parts:
         moves.append((i, cols_at(OTHER, step, lo, size), 0, columns(at, size)))
         at += size
-    return plan.place(weights, [of((s.split, total))], [moves], name)[0]
+    return plan.place(weights, [of((s.split, total))], [moves], name, fixed=len(weights))[0]
 
 
 def own_in(plan, s, weights, got, parts):
@@ -777,14 +782,14 @@
         moves.append((i, cols_at(CORE, step, lo, size), 0, block_at(CORE, s.split, at, size)))
         at += size
     moves.append((len(weights), full, 0, rows_at(OTHER, s.split)))
-    return plan.place([*weights, got], [of((D, total))], [moves], "own")[0]
+    return plan.place([*weights, got], [of((D, total))], [moves], "own", fixed=len(weights))[0]
 
 
 def own_out(plan, s, weight, got):
     rows = got.shape[0]
     return plan.place(
         [weight, got], [of((rows, D))], [[(0, rows_at(CORE, rows), 0, cols_at(CORE, s.split)), (1, full, 0, cols_at(OTHER, s.split))]],
-        "own",
+        "own", fixed=1,
     )[0]
 
 
@@ -866,7 +871,7 @@
     gains_other = other_core(gains_mine)
     plan.line.stamp = gains_mine[:, :LANES]
     got_qkv = ship(other_core, pack_in(plan, s, [w_query, w_key, w_value], qkv_parts, "pack"))
-    pack_out = plan.place([w_out], [of((s.width, s.split))], [[(0, rows_at(OTHER, s.width), 0, full)]], "pack")[0]
+    pack_out = plan.place([w_out], [of((s.width, s.split))], [[(0, rows_at(OTHER, s.width), 0, full)]], "pack", fixed=1)[0]
     got_out = ship(other_core, pack_out)
     own_qkv = own_in(plan, s, [w_query, w_key, w_value], got_qkv, qkv_parts)
     own_o = own_out(plan, s, w_out, got_out)
@@ -890,7 +895,7 @@
     qkvo_zero = ship(far_plane, qkvo)
     gains_attn, gains_ffn = both_gains(plan, gains_mine, gains_other)
     got_gu = ship(other_core, pack_in(plan, s, [w_gate, w_up], gu_parts, "pack"))
-    pack_down = plan.place([w_down], [of((s.units, s.split))], [[(0, rows_at(OTHER, s.units), 0, full)]], "pack")[0]
+    pack_down = plan.place([w_down], [of((s.units, s.split))], [[(0, rows_at(OTHER, s.units), 0, full)]], "pack", fixed=1)[0]
     got_down = ship(other_core, pack_down)
     x_near = join_features(plan, s, tokens, near_tokens)
     own_gu = own_in(plan, s, [w_gate, w_up], got_gu, gu_parts)
@@ -1098,7 +1103,7 @@
         return [every[b] for b in range(blocks)]
 
     def pack_rows(weight, rows):
-        return plan.place([weight], [of((rows, s.split))], [[(0, rows_at(OTHER, rows), 0, full)]], "pack")[0]
+        return plan.place([weight], [of((rows, s.split))], [[(0, rows_at(OTHER, rows), 0, full)]], "pack", fixed=1)[0]
 
     got = other_core(pack_in(plan, s, [w_query, w_key, w_value], qkv_parts, "pack"))
     w_qkv = gathered(own_in(plan, s, [w_query, w_key, w_value], got, qkv_parts))

time: 927 us -> 913 us (0.985)
  Pallas kernels: 517 us -> 500 us
  waiting for transfers between devices: 197 us -> 213 us
  starting transfers between devices: 61.4 us -> 47.2 us
    pallas_call x85, Pallas kernels: 517 us -> 500 us  [launch(): pl.pallas_call(body, out_shape=out_shape + [of((8, LANES), F32)], compile...]
    ppermute x55, waiting for transfers between devices: 85.3 us -> 98.2 us  [swap_axis(): return lax.ppermute(values, axis, [(i, i ^ distance) for i in range(size)])]
    unnamed x368 -> x310, local copies, waits for them, and re-layouts: 59.3 us -> 58.1 us
  transfers between devices with their start and end apart: 82 -> 81, of which waited for: 28 -> 32; matrix products, arithmetic and copies ran while one was open for 7% -> 8% of each run, Pallas kernels for 48% -> 47%
where the time goes in v4:
time: 913 us; the launch traced here: 909 us
  Pallas kernels  500 us (55%)
  waiting for transfers between devices  213 us (23%)
  other arithmetic  68.9 us (8%)
  local copies, waits for them, and re-layouts  58.9 us (6%)
  starting transfers between devices  47.2 us (5%)
  blocking collectives  17.3 us (2%)
    pallas_call x85, Pallas kernels, launch(): pl.pallas_call(body, out_shape=out_shape + [of((8, LANES), F32)], compile...  500 us
    ppermute x26, waiting for transfers between devices, hop(): return lax.ppermute(values, ('dp', 'row'), pairs)  115 us
    ppermute x55, waiting for transfers between devices, swap_axis(): return lax.ppermute(values, axis, [(i, i ^ distance) for i in range(size)])  98.2 us
    unnamed x310, local copies, waits for them, and re-layouts  58.1 us
    ppermute x55, starting transfers between devices, swap_axis(): return lax.ppermute(values, axis, [(i, i ^ distance) for i in range(size)])  27.4 us
    ppermute x26, starting transfers between devices, hop(): return lax.ppermute(values, ('dp', 'row'), pairs)  19.8 us
  transfers between devices with their start and end apart: 81, of which 32 were waited for; matrix products, arithmetic and copies ran while one was open for 8% of the time, Pallas kernels for 47%

profile of v4, /device:TPU:0, one launch (start us, length us, event | category | flops | bytes accessed | tf_op | source)
XLA Modules:
  0.0 908.8 jit_solution(8777303337520108425)
XLA Ops:
  72.8 5.8 attend.4
  95.3 10.0 %collective-permute-done.8.refs_2_ = bf16[512,1024]{1,0:T(8,128)(2,1)} collective-permute-done((bf16[512,1024]{1,0:T(8,128)(2,1)}, bf16[512,1024]{1,0:T(8,128)(2,1)}, u32[]{:S(2)}, u32[]{:S(2)}) %collective-permute-start.8) | collective-permute-done | bytes 1048608 | tf_op jit(solution)/shard_map/ppermute | solution.py:603
  107.1 6.3 attend.5
  113.5 7.0 collective-permute-done.11.refs_4_
  128.3 5.8 attend.6
  147.6 6.4 collective-permute-done.12.refs_1_
  154.5 5.8 attend.7
  164.5 10.2 %collective-permute-done.17.refs_2_ = bf16[384,2048]{1,0:T(8,128)(2,1)} collective-permute-done((bf16[384,2048]{1,0:T(8,128)(2,1)}, bf16[384,2048]{1,0:T(8,128)(2,1)}, u32[]{:S(2)}, u32[]{:S(2)}) %collective-permute-start.17) | collective-permute-done | bytes 1572896 | tf_op jit(solution)/shard_map/ppermute | solution.py:603
  180.3 19.7 %collective-permute-done.20.refs_1_ = bf16[1024,1024]{1,0:T(8,128)(2,1)} collective-permute-done((bf16[1024,1024]{1,0:T(8,128)(2,1)}, bf16[1024,1024]{1,0:T(8,128)(2,1)}, u32[]{:S(2)}, u32[]{:S(2)}) %collective-permute-start.20) | collective-permute-done | bytes 2097184 | tf_op jit(solution)/shard_map/ppermute | solution.py:582
  210.1 15.1 %collective-permute-done.19.refs_4_ = bf16[384,2048]{1,0:T(8,128)(2,1)} collective-permute-done((bf16[384,2048]{1,0:T(8,128)(2,1)}, bf16[384,2048]{1,0:T(8,128)(2,1)}, u32[]{:S(2)}, u32[]{:S(2)}) %collective-permute-start.19) | collective-permute-done | bytes 1572896 | tf_op jit(solution)/shard_map/ppermute | solution.py:603
  230.2 13.7 %collective-permute-done.16.refs_3_ = bf16[512,2048]{1,0:T(8,128)(2,1)} collective-permute-done((bf16[512,2048]{1,0:T(8,128)(2,1)}, bf16[512,2048]{1,0:T(8,128)(2,1)}, u32[]{:S(2)}, u32[]{:S(2)}) %collective-permute-start.16) | collective-permute-done | bytes 2097184 | tf_op jit(solution)/shard_map/ppermute | solution.py:582
  243.9 5.6 norm.1
  259.9 19.4 %ffn.4 = (bf16[1024,1024]{1,0:T(8,128)(2,1)S(1)}, bf16[1024,2048]{1,0:T(8,128)(2,1)S(1)}, f32[8,128]{1,0:T(8,128)S(1)}) custom-call(bf16[1024,2048]{1,0:T(8,128)(2,1)S(1)} %get-tuple-element.498.refs_0_.refs_1_.refs_2_.refs_3_.refs_4_, bf16[1024,2048]{1,0:T(8,128)(2,1)} %copy-done.66, bf16[2048,2048]{1,0:T(8,128)(2,1)} %copy-done.43, ...), custom_call_target="tpu_custom_call" | custom-call | flops 999999995904 | bytes 1 | tf_op jit(solution)/shard_map/ffn/pallas_call | solution.py:93
  279.3 19.1 %collective-permute-done.28.refs_1_ = bf16[512,2048]{1,0:T(8,128)(2,1)} collective-permute-done((bf16[512,2048]{1,0:T(8,128)(2,1)}, bf16[512,2048]{1,0:T(8,128)(2,1)}, u32[]{:S(2)}, u32[]{:S(2)}) %collective-permute-start.28) | collective-permute-done | bytes 2097184 | tf_op jit(solution)/shard_map/ppermute | solution.py:582
  305.9 19.7 %ffn.5 = (bf16[1024,1024]{1,0:T(8,128)(2,1)S(1)}, bf16[1024,2048]{1,0:T(8,128)(2,1)S(1)}, f32[8,128]{1,0:T(8,128)S(1)}) custom-call(bf16[1024,2048]{1,0:T(8,128)(2,1)S(1)} %get-tuple-element.512.refs_0_.refs_5_.refs_6_.refs_7_.refs_8_, bf16[1024,2048]{1,0:T(8,128)(2,1)} %copy-done.67, bf16[2048,2048]{1,0:T(8,128)(2,1)} %copy-done.43, ...), custom_call_target="tpu_custom_call" | custom-call | flops 999999995904 | bytes 1 | tf_op jit(solution)/shard_map/ffn/pallas_call | solution.py:93
  336.2 18.5 %ffn.6 = (bf16[1024,1024]{1,0:T(8,128)(2,1)S(1)}, bf16[1024,2048]{1,0:T(8,128)(2,1)S(1)}, f32[8,128]{1,0:T(8,128)S(1)}) custom-call(bf16[1024,2048]{1,0:T(8,128)(2,1)S(1)} %copy-done.57, bf16[1024,2048]{1,0:T(8,128)(2,1)} %copy-done.67, bf16[2048,2048]{1,0:T(8,128)(2,1)} %get-tuple-element.516.refs_2_.refs_6_, bf16[1024,2048]{1,0:T(8,128)(2,1)} %copy-done.71, ...), custom_call_target="tpu_custom_call" | custom-call | flops 999999995904 | bytes 1 | tf_op jit(solution)/shard_map/ffn/pallas_call | solution.py:93
  356.6 18.7 %ffn.7 = (bf16[1024,1024]{1,0:T(8,128)(2,1)S(1)}, bf16[1024,2048]{1,0:T(8,128)(2,1)S(1)}, f32[8,128]{1,0:T(8,128)S(1)}) custom-call(bf16[1024,2048]{1,0:T(8,128)(2,1)S(1)} %copy-done.52, bf16[1024,2048]{1,0:T(8,128)(2,1)} %copy-done.66, bf16[2048,2048]{1,0:T(8,128)(2,1)} %get-tuple-element.516.refs_2_.refs_6_, bf16[1024,2048]{1,0:T(8,128)(2,1)} %copy-done.71, ...), custom_call_target="tpu_custom_call" | custom-call | flops 999999995904 | bytes 1 | tf_op jit(solution)/shard_map/ffn/pallas_call | solution.py:93
  380.4 24.3 %gu_grad.2 = (bf16[2,512,4096]{2,1,0:T(8,128)(2,1)}, f32[8,128]{1,0:T(8,128)S(1)}) custom-call(s32[6]{0:T(128)S(1)} %stack.45.refs_0_, bf16[1024,2048]{1,0:T(8,128)(2,1)S(1)} %copy-done.52, bf16[1024,2048]{1,0:T(8,128)(2,1)S(1)} %copy-done.52, bf16[1024,2048]{1,0:T(8,128)(2,1)S(1)} %copy-done.52, bf16[1024,2048]{1,0:T(8,128)(2,1)S(1)} %copy-done.52, ...), custom_call_target="tpu_custom_call" | custom-call | flops 999999995904 | bytes 1 | tf_op jit(solution)/shard_map/gu_grad/pallas_call | solution.py:93
  409.2 21.5 %ffn_in.2 = (bf16[512,2048]{1,0:T(8,128)(2,1)}, bf16[512,2048]{1,0:T(8,128)(2,1)S(1)}, f32[8,128]{1,0:T(8,128)S(1)}) custom-call(s32[6]{0:T(128)S(1)} %stack.45.refs_0_, bf16[1024,2048]{1,0:T(8,128)(2,1)S(1)} %copy-done.61, bf16[1024,2048]{1,0:T(8,128)(2,1)S(1)} %copy-done.63, bf16[1024,2048]{1,0:T(8,128)(2,1)S(1)} %copy-done.61, ...), custom_call_target="tpu_custom_call" | custom-call | flops 999999995904 | bytes 1 | tf_op jit(solution)/shard_map/ffn_in/pallas_call | solution.py:93
  443.6 21.0 %ffn_in.3 = (bf16[512,2048]{1,0:T(8,128)(2,1)}, bf16[512,2048]{1,0:T(8,128)(2,1)S(1)}, f32[8,128]{1,0:T(8,128)S(1)}) custom-call(s32[6]{0:T(128)S(1)} %stack.45.refs_0_, bf16[1024,2048]{1,0:T(8,128)(2,1)S(1)} %copy-done.55, bf16[1024,2048]{1,0:T(8,128)(2,1)S(1)} %copy-done.65, bf16[1024,2048]{1,0:T(8,128)(2,1)S(1)} %copy-done.55, ...), custom_call_target="tpu_custom_call" | custom-call | flops 999999995904 | bytes 1 | tf_op jit(solution)/shard_map/ffn_in/pallas_call | solution.py:93
  467.1 24.3 %gu_grad.3 = (bf16[2,512,4096]{2,1,0:T(8,128)(2,1)}, f32[8,128]{1,0:T(8,128)S(1)}) custom-call(s32[6]{0:T(128)S(1)} %stack.45.refs_0_, bf16[1024,2048]{1,0:T(8,128)(2,1)S(1)} %copy-done.52, bf16[1024,2048]{1,0:T(8,128)(2,1)S(1)} %copy-done.52, bf16[1024,2048]{1,0:T(8,128)(2,1)S(1)} %copy-done.52, bf16[1024,2048]{1,0:T(8,128)(2,1)S(1)} %copy-done.52, ...), custom_call_target="tpu_custom_call" | custom-call | flops 999999995904 | bytes 1 | tf_op jit(solution)/shard_map/gu_grad/pallas_call | solution.py:93
  492.0 7.2 ffn_back.1
  509.1 7.1 fusion
  519.5 8.2 attend_back.4
  529.8 8.4 attend_back.5
  538.2 11.3 %collective-permute-done.40.refs_1_ = bf16[512,2048]{1,0:T(8,128)(2,1)} collective-permute-done((bf16[512,2048]{1,0:T(8,128)(2,1)}, bf16[512,2048]{1,0:T(8,128)(2,1)}, u32[]{:S(2)}, u32[]{:S(2)}) %collective-permute-start.40) | collective-permute-done | bytes 2097184 | tf_op jit(solution)/shard_map/ppermute | solution.py:582
  549.5 15.1 %down_grad.2 = (bf16[2,512,2048]{2,1,0:T(8,128)(2,1)}, f32[8,128]{1,0:T(8,128)S(1)}) custom-call(s32[6]{0:T(128)S(1)} %copy-done.37, bf16[1024,2048]{1,0:T(8,128)(2,1)} %copy-done.66, bf16[1024,2048]{1,0:T(8,128)(2,1)} %copy-done.66, bf16[1024,2048]{1,0:T(8,128)(2,1)} %copy-done.66, bf16[1024,2048]{1,0:T(8,128)(2,1)} %copy-done.66, ...), custom_call_target="tpu_custom_call" | custom-call | flops 999999995904 | bytes 1 | tf_op jit(solution)/shard_map/down_grad/pallas_call | solution.py:93
  565.8 5.6 fusion.1
  576.5 14.7 %down_grad.3 = (bf16[2,512,2048]{2,1,0:T(8,128)(2,1)S(1)}, f32[8,128]{1,0:T(8,128)S(1)}) custom-call(s32[6]{0:T(128)S(1)} %copy-done.37, bf16[1024,2048]{1,0:T(8,128)(2,1)} %copy-done.66, bf16[1024,2048]{1,0:T(8,128)(2,1)} %copy-done.66, bf16[1024,2048]{1,0:T(8,128)(2,1)} %copy-done.66, bf16[1024,2048]{1,0:T(8,128)(2,1)} %copy-done.66, ...), custom_call_target="tpu_custom_call" | custom-call | flops 999999995904 | bytes 1 | tf_op jit(solution)/shard_map/down_grad/pallas_call | solution.py:93
  598.8 8.2 attend_back.6
  609.2 8.7 attend_back.7
  625.9 8.4 qkv_in.2
  636.8 18.8 %head_grad.2 = (bf16[2,512,2048]{2,1,0:T(8,128)(2,1)}, f32[8,128]{1,0:T(8,128)S(1)}) custom-call(s32[6]{0:T(128)S(1)} %copy-done.38, bf16[1024,2048]{1,0:T(8,128)(2,1)} %copy-done.45, bf16[1024,2048]{1,0:T(8,128)(2,1)} %copy-done.45, bf16[1024,2048]{1,0:T(8,128)(2,1)} %copy-done.45, bf16[1024,2048]{1,0:T(8,128)(2,1)} %copy-done.45, ...), custom_call_target="tpu_custom_call" | custom-call | flops 999999995904 | bytes 1 | tf_op jit(solution)/shard_map/head_grad/pallas_call | solution.py:93
  665.6 8.6 qkv_in.3
  680.3 18.4 %head_grad.3 = (bf16[2,512,2048]{2,1,0:T(8,128)(2,1)S(1)}, f32[8,128]{1,0:T(8,128)S(1)}) custom-call(s32[6]{0:T(128)S(1)} %copy-done.38, bf16[1024,2048]{1,0:T(8,128)(2,1)} %copy-done.45, bf16[1024,2048]{1,0:T(8,128)(2,1)} %copy-done.45, bf16[1024,2048]{1,0:T(8,128)(2,1)} %copy-done.45, bf16[1024,2048]{1,0:T(8,128)(2,1)} %copy-done.45, ...), custom_call_target="tpu_custom_call" | custom-call | flops 999999995904 | bytes 1 | tf_op jit(solution)/shard_map/head_grad/pallas_call | solution.py:93
  698.7 6.5 collective-permute-done.53
  712.4 12.3 %down.2 = (bf16[512,2048]{1,0:T(8,128)(2,1)}, bf16[512,2048]{1,0:T(8,128)(2,1)S(1)}, f32[8,128]{1,0:T(8,128)S(1)}) custom-call(s32[6]{0:T(128)S(1)} %copy-done.39, bf16[1024,1024]{1,0:T(8,128)(2,1)S(1)} %copy-done.94, bf16[1024,1024]{1,0:T(8,128)(2,1)S(1)} %copy-done.97, bf16[1024,1024]{1,0:T(8,128)(2,1)S(1)} %copy-done.94, ...), custom_call_target="tpu_custom_call" | custom-call | flops 999999995904 | bytes 1 | tf_op jit(solution)/shard_map/down/pallas_call | solution.py:93
  730.0 6.4 all_to_all.36
  737.0 7.6 input_back.1
  766.0 12.0 %down.3 = (bf16[512,2048]{1,0:T(8,128)(2,1)}, bf16[512,2048]{1,0:T(8,128)(2,1)S(1)}, f32[8,128]{1,0:T(8,128)S(1)}) custom-call(s32[6]{0:T(128)S(1)} %copy-done.40, bf16[1024,1024]{1,0:T(8,128)(2,1)S(1)} %copy-done.87, bf16[1024,1024]{1,0:T(8,128)(2,1)S(1)} %copy-done.90, bf16[1024,1024]{1,0:T(8,128)(2,1)S(1)} %copy-done.87, ...), custom_call_target="tpu_custom_call" | custom-call | flops 999999995904 | bytes 1 | tf_op jit(solution)/shard_map/down/pallas_call | solution.py:93
  784.5 5.5 all_to_all.37
  793.6 33.4 %collective-permute-done.70 = f32[2,2048]{1,0:T(2,128)S(1)} collective-permute-done((f32[2,2048]{1,0:T(2,128)S(1)}, f32[2,2048]{1,0:T(2,128)S(1)}, u32[]{:S(2)}, u32[]{:S(2)}) %collective-permute-start.70) | collective-permute-done | bytes 16416 | tf_op jit(solution)/shard_map/ppermute | solution.py:603
  847.3 10.5 %finish.3 = (f32[1024,2048]{1,0:T(8,128)}, f32[1024,2048]{1,0:T(8,128)}, f32[8,128]{1,0:T(8,128)S(1)}) custom-call(s32[6]{0:T(128)S(1)} %copy-done.40, bf16[2,256,2048]{2,1,0:T(8,128)(2,1)} %bitcast.16.refs_1_, bf16[2,256,2048]{2,1,0:T(8,128)(2,1)} %collective-permute-done.55.refs_2_, bf16[2,256,2048]{2,1,0:T(8,128)(2,1)} %collective-permute-done.68.refs_3_, ...), custom_call_target="tpu_custom_call" | custom-call | flops 999999995904 | bytes 1 | tf_op jit(solution)/shard_map/finish/pallas_call | solution.py:93
  861.8 9.3 %collective-permute-done.77.refs_2_ = bf16[2,256,1024]{2,1,0:T(8,128)(2,1)} collective-permute-done((bf16[2,256,1024]{2,1,0:T(8,128)(2,1)}, bf16[2,256,1024]{2,1,0:T(8,128)(2,1)}, u32[]{:S(2)}, u32[]{:S(2)}) %collective-permute-start.77) | collective-permute-done | bytes 1048608 | tf_op jit(solution)/shard_map/ppermute | solution.py:603
  871.6 8.0 collective-permute-done.75.refs_3_
  879.6 6.7 finish.4
  891.0 11.1 %collective-permute-done.80.refs_4_ = bf16[2,256,1024]{2,1,0:T(8,128)(2,1)} collective-permute-done((bf16[2,256,1024]{2,1,0:T(8,128)(2,1)}, bf16[2,256,1024]{2,1,0:T(8,128)(2,1)}, u32[]{:S(2)}, u32[]{:S(2)}) %collective-permute-start.80) | collective-permute-done | bytes 1048608 | tf_op jit(solution)/shard_map/ppermute | solution.py:603
  902.1 6.5 finish.5
  (549 shorter events, 323.4 us)
Async XLA Ops:
  0.6 32.6 %collective-permute-start = (bf16[1024,1024]{1,0:T(8,128)(2,1)}, bf16[1024,1024]{1,0:T(8,128)(2,1)}, u32[]{:S(2)}, u32[]{:S(2)}) collective-permute-start(bf16[1024,1024]{1,0:T(8,128)(2,1)} %refs_1_.16), channel_id=1, source_target_pairs={{0,4},{4,0},{1,5},{5,1},{2,6},{6,2},{3,7},{7,3},{8,12},{12,8},{9,1... | collective-permute-start | bytes 6291464 | tf_op jit(solution)/shard_map/ppermute | solution.py:582
  1.2 71.7 %collective-permute-start.6 = (bf16[1024,1024]{1,0:T(8,128)(2,1)}, bf16[1024,1024]{1,0:T(8,128)(2,1)}, u32[]{:S(2)}, u32[]{:S(2)}) collective-permute-start(bf16[1024,1024]{1,0:T(8,128)(2,1)} %refs_1_.16), channel_id=1, source_target_pairs={{0,1},{1,0},{2,3},{3,2},{4,5},{5,4},{6,7},{7,6},{8,9},{9,8},{10,11... | collective-permute-start | bytes 6291464 | tf_op jit(solution)/shard_map/ppermute | solution.py:582
  5.1 15.6 %collective-permute-start.3 = (f32[2,1024]{1,0:T(2,128)}, f32[2,1024]{1,0:T(2,128)}, u32[]{:S(2)}, u32[]{:S(2)}) collective-permute-start(f32[2,1024]{1,0:T(2,128)} %pad_maximum_fusion.6), channel_id=1, source_target_pairs={{0,4},{4,0},{1,5},{5,1},{2,6},{6,2},{3,7},{7,3},{8,12},{12,8},{9,1... | collective-permute-start | bytes 24584 | tf_op jit(solution)/shard_map/ppermute | solution.py:582
  22.1 57.4 %collective-permute-start.7 = (bf16[512,1024]{1,0:T(8,128)(2,1)}, bf16[512,1024]{1,0:T(8,128)(2,1)}, u32[]{:S(2)}, u32[]{:S(2)}) collective-permute-start(bf16[512,1024]{1,0:T(8,128)(2,1)} %get-tuple-element.417), channel_id=1, source_target_pairs={{0,2},{1,3},{2,0},{3,1},{4,6},{5,7},{6,4},{7,5},{8,10},{9,11},{10,... | collective-permute-start | bytes 3145736 | tf_op jit(solution)/shard_map/ppermute | solution.py:582
  32.6 18.5 %collective-permute-start.5 = (bf16[1024,1024]{1,0:T(8,128)(2,1)}, bf16[1024,1024]{1,0:T(8,128)(2,1)}, u32[]{:S(2)}, u32[]{:S(2)}) collective-permute-start(bf16[1024,1024]{1,0:T(8,128)(2,1)} %get-tuple-element.404), channel_id=1, source_target_pairs={{0,4},{4,0},{1,5},{5,1},{2,6},{6,2},{3,7},{7,3},{8,12},{12,8},{9,1... | collective-permute-start | bytes 6291464 | tf_op jit(solution)/shard_map/ppermute | solution.py:582
  79.5 34.0 %collective-permute-start.9 = (bf16[512,1024]{1,0:T(8,128)(2,1)}, bf16[512,1024]{1,0:T(8,128)(2,1)}, u32[]{:S(2)}, u32[]{:S(2)}) collective-permute-start(bf16[512,1024]{1,0:T(8,128)(2,1)} %collective-permute-done.7.refs_1_), channel_id=1, source_target_pairs={{0,16},{4,12},{8,24},{12,4},{16,0},{20,28},{24,8},{28,20},{1,17},{... | collective-permute-start | bytes 3145736 | tf_op jit(solution)/shard_map/ppermute | solution.py:603
  81.2 24.2 %collective-permute-start.8 = (bf16[512,1024]{1,0:T(8,128)(2,1)}, bf16[512,1024]{1,0:T(8,128)(2,1)}, u32[]{:S(2)}, u32[]{:S(2)}) collective-permute-start(bf16[512,1024]{1,0:T(8,128)(2,1)} %collective-permute-done.7.refs_1_), channel_id=1, source_target_pairs={{0,8},{4,20},{8,0},{12,28},{16,24},{20,4},{24,16},{28,12},{1,9},{5... | collective-permute-start | bytes 3145736 | tf_op jit(solution)/shard_map/ppermute | solution.py:603
  82.7 71.3 %collective-permute-start.12 = (bf16[384,2048]{1,0:T(8,128)(2,1)}, bf16[384,2048]{1,0:T(8,128)(2,1)}, u32[]{:S(2)}, u32[]{:S(2)}) collective-permute-start(bf16[384,2048]{1,0:T(8,128)(2,1)} %get-tuple-element.452), channel_id=1, source_target_pairs={{0,2},{1,3},{2,0},{3,1},{4,6},{5,7},{6,4},{7,5},{8,10},{9,11},{10,... | collective-permute-start | bytes 4718600 | tf_op jit(solution)/shard_map/ppermute | solution.py:582
  84.3 115.6 %collective-permute-start.20 = (bf16[1024,1024]{1,0:T(8,128)(2,1)}, bf16[1024,1024]{1,0:T(8,128)(2,1)}, u32[]{:S(2)}, u32[]{:S(2)}) collective-permute-start(bf16[1024,1024]{1,0:T(8,128)(2,1)} %refs_1_.19), channel_id=1, source_target_pairs={{0,1},{1,0},{2,3},{3,2},{4,5},{5,4},{6,7},{7,6},{8,9},{9,8},{10,11... | collective-permute-start | bytes 6291464 | tf_op jit(solution)/shard_map/ppermute | solution.py:582
  147.5 96.4 %collective-permute-start.16 = (bf16[512,2048]{1,0:T(8,128)(2,1)}, bf16[512,2048]{1,0:T(8,128)(2,1)}, u32[]{:S(2)}, u32[]{:S(2)}) collective-permute-start(bf16[512,2048]{1,0:T(8,128)(2,1)} %add_convert_fusion.7), channel_id=1, source_target_pairs={{0,1},{1,0},{2,3},{3,2},{4,5},{5,4},{6,7},{7,6},{8,9},{9,8},{10,11... | collective-permute-start | bytes 6291464 | tf_op jit(solution)/shard_map/ppermute | solution.py:582
  153.9 98.6 %collective-permute-start.24 = (bf16[384,2048]{1,0:T(8,128)(2,1)}, bf16[384,2048]{1,0:T(8,128)(2,1)}, u32[]{:S(2)}, u32[]{:S(2)}) collective-permute-start(bf16[384,2048]{1,0:T(8,128)(2,1)} %get-tuple-element.489), channel_id=1, source_target_pairs={{0,2},{1,3},{2,0},{3,1},{4,6},{5,7},{6,4},{7,5},{8,10},{9,11},{10,... | collective-permute-start | bytes 4718600 | tf_op jit(solution)/shard_map/ppermute | solution.py:582
  153.9 20.7 %collective-permute-start.17 = (bf16[384,2048]{1,0:T(8,128)(2,1)}, bf16[384,2048]{1,0:T(8,128)(2,1)}, u32[]{:S(2)}, u32[]{:S(2)}) collective-permute-start(bf16[384,2048]{1,0:T(8,128)(2,1)} %collective-permute-done.12.refs_1_), channel_id=1, source_target_pairs={{0,8},{4,20},{8,0},{12,28},{16,24},{20,4},{24,16},{28,12},{1,9},{5... | collective-permute-start | bytes 4718600 | tf_op jit(solution)/shard_map/ppermute | solution.py:603
  154.5 20.7 %collective-permute-start.21 = (bf16[1024,1024]{1,0:T(8,128)(2,1)}, bf16[1024,1024]{1,0:T(8,128)(2,1)}, u32[]{:S(2)}, u32[]{:S(2)}) collective-permute-start(bf16[1024,1024]{1,0:T(8,128)(2,1)} %refs_1_.19), channel_id=1, source_target_pairs={{0,4},{4,0},{1,5},{5,1},{2,6},{6,2},{3,7},{7,3},{8,12},{12,8},{9,1... | collective-permute-start | bytes 6291464 | tf_op jit(solution)/shard_map/ppermute | solution.py:582
  174.7 35.5 %collective-permute-start.18 = (bf16[384,2048]{1,0:T(8,128)(2,1)}, bf16[384,2048]{1,0:T(8,128)(2,1)}, u32[]{:S(2)}, u32[]{:S(2)}) collective-permute-start(bf16[384,2048]{1,0:T(8,128)(2,1)} %collective-permute-done.12.refs_1_), channel_id=1, source_target_pairs={{0,16},{4,12},{8,24},{12,4},{16,0},{20,28},{24,8},{28,20},{1,17},{... | collective-permute-start | bytes 4718600 | tf_op jit(solution)/shard_map/ppermute | solution.py:603
  175.2 68.7 %collective-permute-start.15 = (bf16[512,2048]{1,0:T(8,128)(2,1)}, bf16[512,2048]{1,0:T(8,128)(2,1)}, u32[]{:S(2)}, u32[]{:S(2)}) collective-permute-start(bf16[512,2048]{1,0:T(8,128)(2,1)} %get-tuple-element.473), channel_id=1, source_target_pairs={{0,4},{4,0},{1,5},{5,1},{2,6},{6,2},{3,7},{7,3},{8,12},{12,8},{9,1... | collective-permute-start | bytes 6291464 | tf_op jit(solution)/shard_map/ppermute | solution.py:582
  204.5 20.7 %collective-permute-start.19 = (bf16[384,2048]{1,0:T(8,128)(2,1)}, bf16[384,2048]{1,0:T(8,128)(2,1)}, u32[]{:S(2)}, u32[]{:S(2)}) collective-permute-start(bf16[384,2048]{1,0:T(8,128)(2,1)} %collective-permute-done.17.refs_2_), channel_id=1, source_target_pairs={{0,16},{4,12},{8,24},{12,4},{16,0},{20,28},{24,8},{28,20},{1,17},{... | collective-permute-start | bytes 4718600 | tf_op jit(solution)/shard_map/ppermute | solution.py:603
  251.5 46.9 %collective-permute-start.28 = (bf16[512,2048]{1,0:T(8,128)(2,1)}, bf16[512,2048]{1,0:T(8,128)(2,1)}, u32[]{:S(2)}, u32[]{:S(2)}) collective-permute-start(bf16[512,2048]{1,0:T(8,128)(2,1)} %get-tuple-element.488.refs_1_), channel_id=1, source_target_pairs={{0,1},{1,0},{2,3},{3,2},{4,5},{5,4},{6,7},{7,6},{8,9},{9,8},{10,11... | collective-permute-start | bytes 6291464 | tf_op jit(solution)/shard_map/ppermute | solution.py:582
  256.1 72.9 %collective-permute-start.27 = (bf16[384,2048]{1,0:T(8,128)(2,1)}, bf16[384,2048]{1,0:T(8,128)(2,1)}, u32[]{:S(2)}, u32[]{:S(2)}) collective-permute-start(bf16[384,2048]{1,0:T(8,128)(2,1)} %collective-permute-done.24.refs_1_), channel_id=1, source_target_pairs={{0,16},{4,12},{8,24},{12,4},{16,0},{20,28},{24,8},{28,20},{1,17},{... | collective-permute-start | bytes 4718600 | tf_op jit(solution)/shard_map/ppermute | solution.py:603
  256.6 41.9 %collective-permute-start.26 = (bf16[384,2048]{1,0:T(8,128)(2,1)}, bf16[384,2048]{1,0:T(8,128)(2,1)}, u32[]{:S(2)}, u32[]{:S(2)}) collective-permute-start(bf16[384,2048]{1,0:T(8,128)(2,1)} %collective-permute-done.24.refs_1_), channel_id=1, source_target_pairs={{0,8},{4,20},{8,0},{12,28},{16,24},{20,4},{24,16},{28,12},{1,9},{5... | collective-permute-start | bytes 4718600 | tf_op jit(solution)/shard_map/ppermute | solution.py:603
  299.0 29.9 %collective-permute-start.29 = (bf16[384,2048]{1,0:T(8,128)(2,1)}, bf16[384,2048]{1,0:T(8,128)(2,1)}, u32[]{:S(2)}, u32[]{:S(2)}) collective-permute-start(bf16[384,2048]{1,0:T(8,128)(2,1)} %collective-permute-done.26.refs_2_), channel_id=1, source_target_pairs={{0,16},{4,12},{8,24},{12,4},{16,0},{20,28},{24,8},{28,20},{1,17},{... | collective-permute-start | bytes 4718600 | tf_op jit(solution)/shard_map/ppermute | solution.py:603
  405.3 103.7 %collective-permute-start.34 = (bf16[2,512,4096]{2,1,0:T(8,128)(2,1)}, bf16[2,512,4096]{2,1,0:T(8,128)(2,1)}, u32[]{:S(2)}, u32[]{:S(2)}) collective-permute-start(bf16[2,512,4096]{2,1,0:T(8,128)(2,1)} %get-tuple-element.542), channel_id=1, source_target_pairs={{0,8},{4,20},{8,0},{12,28},{16,24},{20,4},{24,16},{28,12},{1,9},{5... | collective-permute-start | bytes 25165832 | tf_op jit(solution)/shard_map/ppermute | solution.py:603
  439.8 51.6 %collective-permute-start.36 = (bf16[512,2048]{1,0:T(8,128)(2,1)}, bf16[512,2048]{1,0:T(8,128)(2,1)}, u32[]{:S(2)}, u32[]{:S(2)}) collective-permute-start(bf16[512,2048]{1,0:T(8,128)(2,1)} %add_convert_fusion.6), channel_id=1, source_target_pairs={{0,1},{1,0},{2,3},{3,2},{4,5},{5,4},{6,7},{7,6},{8,9},{9,8},{10,11... | collective-permute-start | bytes 6291464 | tf_op jit(solution)/shard_map/ppermute | solution.py:582
  464.7 26.7 %collective-permute-start.35 = (bf16[512,2048]{1,0:T(8,128)(2,1)}, bf16[512,2048]{1,0:T(8,128)(2,1)}, u32[]{:S(2)}, u32[]{:S(2)}) collective-permute-start(bf16[512,2048]{1,0:T(8,128)(2,1)} %get-tuple-element.544), channel_id=1, source_target_pairs={{0,4},{4,0},{1,5},{5,1},{2,6},{6,2},{3,7},{7,3},{8,12},{12,8},{9,1... | collective-permute-start | bytes 6291464 | tf_op jit(solution)/shard_map/ppermute | solution.py:582
  501.3 48.2 %collective-permute-start.40 = (bf16[512,2048]{1,0:T(8,128)(2,1)}, bf16[512,2048]{1,0:T(8,128)(2,1)}, u32[]{:S(2)}, u32[]{:S(2)}) collective-permute-start(bf16[512,2048]{1,0:T(8,128)(2,1)} %get-tuple-element.548.refs_1_), channel_id=1, source_target_pairs={{0,1},{1,0},{2,3},{3,2},{4,5},{5,4},{6,7},{7,6},{8,9},{9,8},{10,11... | collective-permute-start | bytes 6291464 | tf_op jit(solution)/shard_map/ppermute | solution.py:582
  516.9 48.9 %collective-permute-start.39 = (bf16[512,4096]{1,0:T(8,128)(2,1)}, bf16[512,4096]{1,0:T(8,128)(2,1)}, u32[]{:S(2)}, u32[]{:S(2)}) collective-permute-start(bf16[512,4096]{1,0:T(8,128)(2,1)} %fusion), channel_id=1, source_target_pairs={{0,16},{4,12},{8,24},{12,4},{16,0},{20,28},{24,8},{28,20},{1,17},{... | collective-permute-start | bytes 12582920 | tf_op jit(solution)/shard_map/ppermute | solution.py:603
  549.5 41.7 %collective-permute-start.43 = (bf16[512,2048]{1,0:T(8,128)(2,1)}, bf16[512,2048]{1,0:T(8,128)(2,1)}, u32[]{:S(2)}, u32[]{:S(2)}) collective-permute-start(bf16[512,2048]{1,0:T(8,128)(2,1)} %collective-permute-done.40.refs_1_), channel_id=1, source_target_pairs={{0,4},{4,0},{1,5},{5,1},{2,6},{6,2},{3,7},{7,3},{8,12},{12,8},{9,1... | collective-permute-start | bytes 6291464 | tf_op jit(solution)/shard_map/ppermute | solution.py:582
  564.6 53.3 %collective-permute-start.46 = (bf16[2,512,2048]{2,1,0:T(8,128)(2,1)}, bf16[2,512,2048]{2,1,0:T(8,128)(2,1)}, u32[]{:S(2)}, u32[]{:S(2)}) collective-permute-start(bf16[2,512,2048]{2,1,0:T(8,128)(2,1)} %get-tuple-element.611), channel_id=1, source_target_pairs={{0,8},{4,20},{8,0},{12,28},{16,24},{20,4},{24,16},{28,12},{1,9},{5... | collective-permute-start | bytes 12582920 | tf_op jit(solution)/shard_map/ppermute | solution.py:603
  571.9 152.8 %collective-permute-start.42 = (bf16[512,2048]{1,0:T(8,128)(2,1)}, bf16[512,2048]{1,0:T(8,128)(2,1)}, u32[]{:S(2)}, u32[]{:S(2)}) collective-permute-start(bf16[512,2048]{1,0:T(8,128)(2,1)} %fusion.1), channel_id=1, source_target_pairs={{0,2},{1,3},{2,0},{3,1},{4,6},{5,7},{6,4},{7,5},{8,10},{9,11},{10,... | collective-permute-start | bytes 6291464 | tf_op jit(solution)/shard_map/ppermute | solution.py:582
  623.3 50.8 %collective-permute-start.51 = (bf16[512,2048]{1,0:T(8,128)(2,1)}, bf16[512,2048]{1,0:T(8,128)(2,1)}, u32[]{:S(2)}, u32[]{:S(2)}) collective-permute-start(bf16[512,2048]{1,0:T(8,128)(2,1)} %fusion.4), channel_id=1, source_target_pairs={{0,16},{4,12},{8,24},{12,4},{16,0},{20,28},{24,8},{28,20},{1,17},{... | collective-permute-start | bytes 6291464 | tf_op jit(solution)/shard_map/ppermute | solution.py:603
  634.3 22.8 %collective-permute-start.48 = (bf16[512,2048]{1,0:T(8,128)(2,1)}, bf16[512,2048]{1,0:T(8,128)(2,1)}, u32[]{:S(2)}, u32[]{:S(2)}) collective-permute-start(bf16[512,2048]{1,0:T(8,128)(2,1)} %get-tuple-element.617), channel_id=1, source_target_pairs={{0,4},{4,0},{1,5},{5,1},{2,6},{6,2},{3,7},{7,3},{8,12},{12,8},{9,1... | collective-permute-start | bytes 6291464 | tf_op jit(solution)/shard_map/ppermute | solution.py:582
  656.3 48.9 %collective-permute-start.53 = (bf16[2,512,2048]{2,1,0:T(8,128)(2,1)}, bf16[2,512,2048]{2,1,0:T(8,128)(2,1)}, u32[]{:S(2)}, u32[]{:S(2)}) collective-permute-start(bf16[2,512,2048]{2,1,0:T(8,128)(2,1)} %get-tuple-element.642), channel_id=1, source_target_pairs={{0,8},{4,20},{8,0},{12,28},{16,24},{20,4},{24,16},{28,12},{1,9},{5... | collective-permute-start | bytes 12582920 | tf_op jit(solution)/shard_map/ppermute | solution.py:603
  661.0 76.0 %collective-permute-start.57 = (bf16[512,2048]{1,0:T(8,128)(2,1)}, bf16[512,2048]{1,0:T(8,128)(2,1)}, u32[]{:S(2)}, u32[]{:S(2)}) collective-permute-start(bf16[512,2048]{1,0:T(8,128)(2,1)} %add_convert_fusion.4), channel_id=1, source_target_pairs={{0,1},{1,0},{2,3},{3,2},{4,5},{5,4},{6,7},{7,6},{8,9},{9,8},{10,11... | collective-permute-start | bytes 6291464 | tf_op jit(solution)/shard_map/ppermute | solution.py:582
  678.9 101.0 %collective-permute-start.65 = (bf16[512,1024]{1,0:T(8,128)(2,1)}, bf16[512,1024]{1,0:T(8,128)(2,1)}, u32[]{:S(2)}, u32[]{:S(2)}) collective-permute-start(bf16[512,1024]{1,0:T(8,128)(2,1)} %fusion.11), channel_id=1, source_target_pairs={{0,2},{1,3},{2,0},{3,1},{4,6},{5,7},{6,4},{7,5},{8,10},{9,11},{10,... | collective-permute-start | bytes 3145736 | tf_op jit(solution)/shard_map/ppermute | solution.py:582
  680.1 56.9 %collective-permute-start.56 = (bf16[512,2048]{1,0:T(8,128)(2,1)}, bf16[512,2048]{1,0:T(8,128)(2,1)}, u32[]{:S(2)}, u32[]{:S(2)}) collective-permute-start(bf16[512,2048]{1,0:T(8,128)(2,1)} %get-tuple-element.655), channel_id=1, source_target_pairs={{0,4},{4,0},{1,5},{5,1},{2,6},{6,2},{3,7},{7,3},{8,12},{12,8},{9,1... | collective-permute-start | bytes 6291464 | tf_op jit(solution)/shard_map/ppermute | solution.py:582
  710.4 36.7 %collective-permute-start.60 = (bf16[512,2048]{1,0:T(8,128)(2,1)}, bf16[512,2048]{1,0:T(8,128)(2,1)}, u32[]{:S(2)}, u32[]{:S(2)}) collective-permute-start(bf16[512,2048]{1,0:T(8,128)(2,1)} %fusion.5), channel_id=1, source_target_pairs={{0,16},{4,12},{8,24},{12,4},{16,0},{20,28},{24,8},{28,20},{1,17},{... | collective-permute-start | bytes 6291464 | tf_op jit(solution)/shard_map/ppermute | solution.py:603
  736.4 28.1 %collective-permute-start.55 = (bf16[2,256,2048]{2,1,0:T(8,128)(2,1)}, bf16[2,256,2048]{2,1,0:T(8,128)(2,1)}, u32[]{:S(2)}, u32[]{:S(2)}) collective-permute-start(bf16[2,256,2048]{2,1,0:T(8,128)(2,1)} %bitcast.16.refs_1_), channel_id=1, source_target_pairs={{0,8},{4,20},{8,0},{12,28},{16,24},{20,4},{24,16},{28,12},{1,9},{5... | collective-permute-start | bytes 6291464 | tf_op jit(solution)/shard_map/ppermute | solution.py:603
  746.6 16.5 %collective-permute-start.63 = (f32[2,2048]{1,0:T(2,128)}, f32[2,2048]{1,0:T(2,128)}, u32[]{:S(2)}, u32[]{:S(2)}) collective-permute-start(f32[2,2048]{1,0:T(2,128)} %pad_maximum_fusion.5), channel_id=1, source_target_pairs={{0,4},{4,0},{1,5},{5,1},{2,6},{6,2},{3,7},{7,3},{8,12},{12,8},{9,1... | collective-permute-start | bytes 49160 | tf_op jit(solution)/shard_map/ppermute | solution.py:582
  756.5 72.2 %collective-permute-start.72 = (bf16[512,1024]{1,0:T(8,128)(2,1)}, bf16[512,1024]{1,0:T(8,128)(2,1)}, u32[]{:S(2)}, u32[]{:S(2)}) collective-permute-start(bf16[512,1024]{1,0:T(8,128)(2,1)} %fusion.10), channel_id=1, source_target_pairs={{0,2},{1,3},{2,0},{3,1},{4,6},{5,7},{6,4},{7,5},{8,10},{9,11},{10,... | collective-permute-start | bytes 3145736 | tf_op jit(solution)/shard_map/ppermute | solution.py:582
  757.3 100.5 %collective-permute-start.67 = (bf16[512,2048]{1,0:T(8,128)(2,1)}, bf16[512,2048]{1,0:T(8,128)(2,1)}, u32[]{:S(2)}, u32[]{:S(2)}) collective-permute-start(bf16[512,2048]{1,0:T(8,128)(2,1)} %add_convert_fusion.2), channel_id=1, source_target_pairs={{0,1},{1,0},{2,3},{3,2},{4,5},{5,4},{6,7},{7,6},{8,9},{9,8},{10,11... | collective-permute-start | bytes 6291464 | tf_op jit(solution)/shard_map/ppermute | solution.py:582
  778.0 66.7 %collective-permute-start.69 = (bf16[2,256,2048]{2,1,0:T(8,128)(2,1)}, bf16[2,256,2048]{2,1,0:T(8,128)(2,1)}, u32[]{:S(2)}, u32[]{:S(2)}) collective-permute-start(bf16[2,256,2048]{2,1,0:T(8,128)(2,1)} %collective-permute-done.55.refs_2_), channel_id=1, source_target_pairs={{0,16},{4,12},{8,24},{12,4},{16,0},{20,28},{24,8},{28,20},{1,17},{... | collective-permute-start | bytes 6291464 | tf_op jit(solution)/shard_map/ppermute | solution.py:603
  779.9 65.4 %collective-permute-start.68 = (bf16[2,256,2048]{2,1,0:T(8,128)(2,1)}, bf16[2,256,2048]{2,1,0:T(8,128)(2,1)}, u32[]{:S(2)}, u32[]{:S(2)}) collective-permute-start(bf16[2,256,2048]{2,1,0:T(8,128)(2,1)} %bitcast.16.refs_1_), channel_id=1, source_target_pairs={{0,16},{4,12},{8,24},{12,4},{16,0},{20,28},{24,8},{28,20},{1,17},{... | collective-permute-start | bytes 6291464 | tf_op jit(solution)/shard_map/ppermute | solution.py:603
  790.8 36.2 %collective-permute-start.70 = (f32[2,2048]{1,0:T(2,128)S(1)}, f32[2,2048]{1,0:T(2,128)S(1)}, u32[]{:S(2)}, u32[]{:S(2)}) collective-permute-start(f32[2,2048]{1,0:T(2,128)S(1)} %copy-done.149), channel_id=1, source_target_pairs={{0,16},{4,12},{8,24},{12,4},{16,0},{20,28},{24,8},{28,20},{1,17},{... | collective-permute-start | bytes 49160 | tf_op jit(solution)/shard_map/ppermute | solution.py:603
  842.1 29.1 %collective-permute-start.76 = (bf16[2,256,1024]{2,1,0:T(8,128)(2,1)}, bf16[2,256,1024]{2,1,0:T(8,128)(2,1)}, u32[]{:S(2)}, u32[]{:S(2)}) collective-permute-start(bf16[2,256,1024]{2,1,0:T(8,128)(2,1)} %collective-permute-done.71.refs_2_), channel_id=1, source_target_pairs={{0,16},{4,12},{8,24},{12,4},{16,0},{20,28},{24,8},{28,20},{1,17},{... | collective-permute-start | bytes 3145736 | tf_op jit(solution)/shard_map/ppermute | solution.py:603
  842.5 37.1 %collective-permute-start.75 = (bf16[2,256,1024]{2,1,0:T(8,128)(2,1)}, bf16[2,256,1024]{2,1,0:T(8,128)(2,1)}, u32[]{:S(2)}, u32[]{:S(2)}) collective-permute-start(bf16[2,256,1024]{2,1,0:T(8,128)(2,1)} %bitcast.23.refs_1_), channel_id=1, source_target_pairs={{0,16},{4,12},{8,24},{12,4},{16,0},{20,28},{24,8},{28,20},{1,17},{... | collective-permute-start | bytes 3145736 | tf_op jit(solution)/shard_map/ppermute | solution.py:603
  844.7 26.4 %collective-permute-start.77 = (bf16[2,256,1024]{2,1,0:T(8,128)(2,1)}, bf16[2,256,1024]{2,1,0:T(8,128)(2,1)}, u32[]{:S(2)}, u32[]{:S(2)}) collective-permute-start(bf16[2,256,1024]{2,1,0:T(8,128)(2,1)} %bitcast.27.refs_1_), channel_id=1, source_target_pairs={{0,8},{4,20},{8,0},{12,28},{16,24},{20,4},{24,16},{28,12},{1,9},{5... | collective-permute-start | bytes 3145736 | tf_op jit(solution)/shard_map/ppermute | solution.py:603
  845.3 44.3 %collective-permute-start.78 = (f32[2,2048]{1,0:T(2,128)}, f32[2,2048]{1,0:T(2,128)}, u32[]{:S(2)}, u32[]{:S(2)}) collective-permute-start(f32[2,2048]{1,0:T(2,128)} %add.162), channel_id=1, source_target_pairs={{0,2},{1,3},{2,0},{3,1},{4,6},{5,7},{6,4},{7,5},{8,10},{9,11},{10,... | collective-permute-start | bytes 49160 | tf_op jit(solution)/shard_map/ppermute | solution.py:582
  861.2 29.7 %collective-permute-start.79 = (bf16[2,256,1024]{2,1,0:T(8,128)(2,1)}, bf16[2,256,1024]{2,1,0:T(8,128)(2,1)}, u32[]{:S(2)}, u32[]{:S(2)}) collective-permute-start(bf16[2,256,1024]{2,1,0:T(8,128)(2,1)} %bitcast.27.refs_1_), channel_id=1, source_target_pairs={{0,16},{4,12},{8,24},{12,4},{16,0},{20,28},{24,8},{28,20},{1,17},{... | collective-permute-start | bytes 3145736 | tf_op jit(solution)/shard_map/ppermute | solution.py:603
  871.2 30.9 %collective-permute-start.80 = (bf16[2,256,1024]{2,1,0:T(8,128)(2,1)}, bf16[2,256,1024]{2,1,0:T(8,128)(2,1)}, u32[]{:S(2)}, u32[]{:S(2)}) collective-permute-start(bf16[2,256,1024]{2,1,0:T(8,128)(2,1)} %collective-permute-done.77.refs_2_), channel_id=1, source_target_pairs={{0,16},{4,12},{8,24},{12,4},{16,0},{20,28},{24,8},{28,20},{1,17},{... | collective-permute-start | bytes 3145736 | tf_op jit(solution)/shard_map/ppermute | solution.py:603
  (188 other events, 2512.6 us)

commit v5 on v4

--- a/solution.py
+++ b/solution.py
@@ -11,7 +11,7 @@
 LANES = 128
 EPS = 1e-05
 ROPE_BASE = 130000.0
-VMEM = 40 * 1024 * 1024
+VMEM = 48 * 1024 * 1024
 UNIT_TILE = 256
 QB = 256
 COST = 10**12
@@ -1056,15 +1056,14 @@
     gains_got = ship(hop_two, gains)
     plan.pause()
     mixed_near = [add_pair(plan, mixed_near)]
-    gains = mix(jnp.add, gains, gains_got)
-    gains_got = ship(other_chip, gains)
-    plan.pause()
     heads.total()
     heads.spread()
     down.spread_last()
     gains = mix(jnp.add, gains, gains_got)
+    gains_got = ship(other_chip, gains)
+    gate_grad, up_grad = ups.finish()
+    gains = mix(jnp.add, gains, gains_got)
     gains_got = ship(far_plane, gains)
-    gate_grad, up_grad = ups.finish()
     mixed_mine, mixed_other = add_mixed(plan, s, mixed_near, mixed_far, residual)
     mixed_got = ship(other_core, mixed_other)
     heads.spread_last()

time: 913 us -> 906 us (level)
  Pallas kernels: 500 us -> 548 us
  local copies, waits for them, and re-layouts: 58.9 us -> 20 us
  waiting for transfers between devices: 213 us -> 187 us
  starting transfers between devices: 47.2 us -> 58.4 us
    pallas_call x85 -> x84, Pallas kernels: 500 us -> 548 us  [launch(): pl.pallas_call(body, out_shape=out_shape + [of((8, LANES), F32)], compile...]
    unnamed x310 -> x190, local copies, waits for them, and re-layouts: 58.1 us -> 19.2 us
    ppermute x26, waiting for transfers between devices: 115 us -> 94.4 us  [hop(): return lax.ppermute(values, ('dp', 'row'), pairs)]
  transfers between devices with their start and end apart: 81 -> 81, of which waited for: 32 -> 29; matrix products, arithmetic and copies ran while one was open for 8% -> 8% of each run, Pallas kernels for 47% -> 52%
where the time goes in v5:
time: 906 us; the launch traced here: 902 us
  Pallas kernels  548 us (60%)
  waiting for transfers between devices  187 us (21%)
  other arithmetic  69.1 us (8%)
  starting transfers between devices  58.4 us (6%)
  local copies, waits for them, and re-layouts  20 us (2%)
  blocking collectives  17.3 us (2%)
    pallas_call x84, Pallas kernels, launch(): pl.pallas_call(body, out_shape=out_shape + [of((8, LANES), F32)], compile...  548 us
    ppermute x26, waiting for transfers between devices, hop(): return lax.ppermute(values, ('dp', 'row'), pairs)  94.4 us
    ppermute x55, waiting for transfers between devices, swap_axis(): return lax.ppermute(values, axis, [(i, i ^ distance) for i in range(size)])  92.2 us
    ppermute x55, starting transfers between devices, swap_axis(): return lax.ppermute(values, axis, [(i, i ^ distance) for i in range(size)])  30.8 us
    ppermute x26, starting transfers between devices, hop(): return lax.ppermute(values, ('dp', 'row'), pairs)  27.6 us
    unnamed x190, local copies, waits for them, and re-layouts  19.2 us
  transfers between devices with their start and end apart: 81, of which 29 were waited for; matrix products, arithmetic and copies ran while one was open for 8% of the time, Pallas kernels for 52%

profile of v5, /device:TPU:0, one launch (start us, length us, event | category | flops | bytes accessed | tf_op | source)
XLA Modules:
  0.0 902.0 jit_solution(9886186662427450794)
XLA Ops:
  43.2 7.8 own.6
  63.5 7.8 qkv.4
  90.3 7.8 qkv.5
  98.1 6.6 collective-permute-done.8.refs_2_
  112.2 7.6 collective-permute-done.11.refs_4_
  126.1 6.1 qkv.6
  132.2 5.8 attend.6
  159.4 5.8 attend.7
  169.7 9.0 collective-permute-done.17.refs_2_
  184.3 15.0 %collective-permute-done.20.refs_1_ = bf16[1024,1024]{1,0:T(8,128)(2,1)} collective-permute-done((bf16[1024,1024]{1,0:T(8,128)(2,1)}, bf16[1024,1024]{1,0:T(8,128)(2,1)}, u32[]{:S(2)}, u32[]{:S(2)}) %collective-permute-start.20) | collective-permute-done | bytes 2097184 | tf_op jit(solution)/shard_map/ppermute | solution.py:582
  208.5 16.0 %collective-permute-done.19.refs_4_ = bf16[384,2048]{1,0:T(8,128)(2,1)} collective-permute-done((bf16[384,2048]{1,0:T(8,128)(2,1)}, bf16[384,2048]{1,0:T(8,128)(2,1)}, u32[]{:S(2)}, u32[]{:S(2)}) %collective-permute-start.19) | collective-permute-done | bytes 1572896 | tf_op jit(solution)/shard_map/ppermute | solution.py:603
  224.5 5.9 other.4
  230.4 12.8 %collective-permute-done.16.refs_3_ = bf16[512,2048]{1,0:T(8,128)(2,1)} collective-permute-done((bf16[512,2048]{1,0:T(8,128)(2,1)}, bf16[512,2048]{1,0:T(8,128)(2,1)}, u32[]{:S(2)}, u32[]{:S(2)}) %collective-permute-start.16) | collective-permute-done | bytes 2097184 | tf_op jit(solution)/shard_map/ppermute | solution.py:582
  243.2 6.1 norm.1
  258.9 19.8 %ffn.4 = (bf16[1024,1024]{1,0:T(8,128)(2,1)S(1)}, bf16[1024,2048]{1,0:T(8,128)(2,1)}, f32[8,128]{1,0:T(8,128)S(1)}) custom-call(bf16[1024,2048]{1,0:T(8,128)(2,1)} %get-tuple-element.497.refs_0_.refs_1_.refs_2_.refs_3_.refs_4_, bf16[1024,2048]{1,0:T(8,128)(2,1)} %get-tuple-element.498.refs_1_.refs_5_.refs_2_.refs_3_.refs_4_, ...), custom_call_target="tpu_custom_call" | custom-call | flops 999999995904 | bytes 1 | tf_op jit(solution)/shard_map/ffn/pallas_call | solution.py:93
  278.7 17.6 %collective-permute-done.28.refs_1_ = bf16[512,2048]{1,0:T(8,128)(2,1)} collective-permute-done((bf16[512,2048]{1,0:T(8,128)(2,1)}, bf16[512,2048]{1,0:T(8,128)(2,1)}, u32[]{:S(2)}, u32[]{:S(2)}) %collective-permute-start.28) | collective-permute-done | bytes 2097184 | tf_op jit(solution)/shard_map/ppermute | solution.py:582
  305.0 19.8 %ffn.5 = (bf16[1024,1024]{1,0:T(8,128)(2,1)S(1)}, bf16[1024,2048]{1,0:T(8,128)(2,1)}, f32[8,128]{1,0:T(8,128)S(1)}) custom-call(bf16[1024,2048]{1,0:T(8,128)(2,1)} %get-tuple-element.511.refs_0_.refs_5_.refs_6_.refs_7_.refs_8_, bf16[1024,2048]{1,0:T(8,128)(2,1)} %get-tuple-element.512.refs_1_.refs_5_.refs_6_.refs_7_.refs_8_, ...), custom_call_target="tpu_custom_call" | custom-call | flops 999999995904 | bytes 1 | tf_op jit(solution)/shard_map/ffn/pallas_call | solution.py:93
  331.9 19.8 %ffn.6 = (bf16[1024,1024]{1,0:T(8,128)(2,1)S(1)}, bf16[1024,2048]{1,0:T(8,128)(2,1)}, f32[8,128]{1,0:T(8,128)S(1)}) custom-call(bf16[1024,2048]{1,0:T(8,128)(2,1)} %get-tuple-element.511.refs_0_.refs_5_.refs_6_.refs_7_.refs_8_, bf16[1024,2048]{1,0:T(8,128)(2,1)} %get-tuple-element.512.refs_1_.refs_5_.refs_6_.refs_7_.refs_8_, ...), custom_call_target="tpu_custom_call" | custom-call | flops 999999995904 | bytes 1 | tf_op jit(solution)/shard_map/ffn/pallas_call | solution.py:93
  353.1 20.8 %ffn.7 = (bf16[1024,1024]{1,0:T(8,128)(2,1)S(1)}, bf16[1024,2048]{1,0:T(8,128)(2,1)}, f32[8,128]{1,0:T(8,128)S(1)}) custom-call(bf16[1024,2048]{1,0:T(8,128)(2,1)} %get-tuple-element.497.refs_0_.refs_1_.refs_2_.refs_3_.refs_4_, bf16[1024,2048]{1,0:T(8,128)(2,1)} %get-tuple-element.498.refs_1_.refs_5_.refs_2_.refs_3_.refs_4_, ...), custom_call_target="tpu_custom_call" | custom-call | flops 999999995904 | bytes 1 | tf_op jit(solution)/shard_map/ffn/pallas_call | solution.py:93
  373.9 25.3 %gu_grad.2 = (bf16[2,512,4096]{2,1,0:T(8,128)(2,1)}, f32[8,128]{1,0:T(8,128)S(1)}) custom-call(s32[6]{0:T(128)S(1)} %stack.45.refs_0_, bf16[1024,2048]{1,0:T(8,128)(2,1)S(1)} %copy-done.32, bf16[1024,2048]{1,0:T(8,128)(2,1)S(1)} %copy-done.32, bf16[1024,2048]{1,0:T(8,128)(2,1)S(1)} %copy-done.32, bf16[1024,2048]{1,0:T(8,128)(2,1)S(1)} %copy-done.32, ...), custom_call_target="tpu_custom_call" | custom-call | flops 999999995904 | bytes 1 | tf_op jit(solution)/shard_map/gu_grad/pallas_call | solution.py:93
  400.7 23.6 %ffn_in.2 = (bf16[512,2048]{1,0:T(8,128)(2,1)}, bf16[512,2048]{1,0:T(8,128)(2,1)S(1)}, f32[8,128]{1,0:T(8,128)S(1)}) custom-call(s32[6]{0:T(128)S(1)} %stack.45.refs_0_, bf16[1024,2048]{1,0:T(8,128)(2,1)} %get-tuple-element.522.refs_11_.refs_1_.refs_3_, bf16[1024,2048]{1,0:T(8,128)(2,1)} %get-tuple-element.523.refs_12_.refs_2_.refs_4_, ...), custom_call_target="tpu_custom_call" | custom-call | flops 999999995904 | bytes 1 | tf_op jit(solution)/shard_map/ffn_in/pallas_call | solution.py:93
  434.0 24.0 %ffn_in.3 = (bf16[512,2048]{1,0:T(8,128)(2,1)}, bf16[512,2048]{1,0:T(8,128)(2,1)S(1)}, f32[8,128]{1,0:T(8,128)S(1)}) custom-call(s32[6]{0:T(128)S(1)} %stack.45.refs_0_, bf16[1024,2048]{1,0:T(8,128)(2,1)} %get-tuple-element.520.refs_9_.refs_1_.refs_3_, bf16[1024,2048]{1,0:T(8,128)(2,1)} %get-tuple-element.521.refs_10_.refs_2_.refs_4_, ...), custom_call_target="tpu_custom_call" | custom-call | flops 999999995904 | bytes 1 | tf_op jit(solution)/shard_map/ffn_in/pallas_call | solution.py:93
  458.3 25.2 %gu_grad.3 = (bf16[2,512,4096]{2,1,0:T(8,128)(2,1)}, f32[8,128]{1,0:T(8,128)S(1)}) custom-call(s32[6]{0:T(128)S(1)} %stack.45.refs_0_, bf16[1024,2048]{1,0:T(8,128)(2,1)S(1)} %copy-done.32, bf16[1024,2048]{1,0:T(8,128)(2,1)S(1)} %copy-done.32, bf16[1024,2048]{1,0:T(8,128)(2,1)S(1)} %copy-done.32, bf16[1024,2048]{1,0:T(8,128)(2,1)S(1)} %copy-done.32, ...), custom_call_target="tpu_custom_call" | custom-call | flops 999999995904 | bytes 1 | tf_op jit(solution)/shard_map/gu_grad/pallas_call | solution.py:93
  484.1 7.8 ffn_back.1
  512.0 8.4 attend_back.4
  524.1 8.3 attend_back.5
  532.4 7.7 collective-permute-done.40.refs_1_
  540.1 15.9 %down_grad.2 = (bf16[2,512,2048]{2,1,0:T(8,128)(2,1)}, f32[8,128]{1,0:T(8,128)S(1)}) custom-call(s32[6]{0:T(128)S(1)} %copy-done.23, bf16[1024,2048]{1,0:T(8,128)(2,1)} %get-tuple-element.498.refs_1_.refs_5_.refs_2_.refs_3_.refs_4_, bf16[1024,2048]{1,0:T(8,128)(2,1)} %get-tuple-element.498.refs_1_.refs_5_.refs_2_.refs_3_.refs_4_, ...), custom_call_target="tpu_custom_call" | custom-call | flops 999999995904 | bytes 1 | tf_op jit(solution)/shard_map/down_grad/pallas_call | solution.py:93
  568.0 15.6 %down_grad.3 = (bf16[2,512,2048]{2,1,0:T(8,128)(2,1)}, f32[8,128]{1,0:T(8,128)S(1)}) custom-call(s32[6]{0:T(128)S(1)} %copy-done.23, bf16[1024,2048]{1,0:T(8,128)(2,1)} %get-tuple-element.498.refs_1_.refs_5_.refs_2_.refs_3_.refs_4_, bf16[1024,2048]{1,0:T(8,128)(2,1)} %get-tuple-element.498.refs_1_.refs_5_.refs_2_.refs_3_.refs_4_, ...), custom_call_target="tpu_custom_call" | custom-call | flops 999999995904 | bytes 1 | tf_op jit(solution)/shard_map/down_grad/pallas_call | solution.py:93
  591.7 8.2 attend_back.6
  604.3 8.2 attend_back.7
  619.9 10.4 %qkv_in.2 = (bf16[512,2048]{1,0:T(8,128)(2,1)}, bf16[512,2048]{1,0:T(8,128)(2,1)}, f32[8,128]{1,0:T(8,128)S(1)}) custom-call(s32[6]{0:T(128)S(1)} %copy-done.24, bf16[1024,768]{1,0:T(8,128)(2,1)S(1)} %get-tuple-element.765.refs_1_.refs_3_, bf16[1024,768]{1,0:T(8,128)(2,1)S(1)} %get-tuple-element.766.refs_2_.refs_4_, ...), custom_call_target="tpu_custom_call" | custom-call | flops 999999995904 | bytes 1 | tf_op jit(solution)/shard_map/qkv_in/pallas_call | solution.py:93
  630.5 19.7 %head_grad.2 = (bf16[2,512,2048]{2,1,0:T(8,128)(2,1)}, f32[8,128]{1,0:T(8,128)S(1)}) custom-call(s32[6]{0:T(128)S(1)} %copy-done.24, bf16[1024,2048]{1,0:T(8,128)(2,1)} %get-tuple-element.415.refs_0_.refs_1_.refs_2_.refs_3_.refs_4_, bf16[1024,2048]{1,0:T(8,128)(2,1)} %get-tuple-element.415.refs_0_.refs_1_.refs_2_.refs_3_.refs_4_, ...), custom_call_target="tpu_custom_call" | custom-call | flops 999999995904 | bytes 1 | tf_op jit(solution)/shard_map/head_grad/pallas_call | solution.py:93
  657.5 10.3 %qkv_in.3 = (bf16[512,2048]{1,0:T(8,128)(2,1)}, bf16[512,2048]{1,0:T(8,128)(2,1)}, f32[8,128]{1,0:T(8,128)S(1)}) custom-call(s32[6]{0:T(128)S(1)} %copy-done.24, bf16[1024,768]{1,0:T(8,128)(2,1)S(1)} %get-tuple-element.767.refs_1_.refs_3_, bf16[1024,768]{1,0:T(8,128)(2,1)S(1)} %get-tuple-element.768.refs_2_.refs_4_, ...), custom_call_target="tpu_custom_call" | custom-call | flops 999999995904 | bytes 1 | tf_op jit(solution)/shard_map/qkv_in/pallas_call | solution.py:93
  673.1 19.5 %head_grad.3 = (bf16[2,512,2048]{2,1,0:T(8,128)(2,1)}, f32[8,128]{1,0:T(8,128)S(1)}) custom-call(s32[6]{0:T(128)S(1)} %copy-done.24, bf16[1024,2048]{1,0:T(8,128)(2,1)} %get-tuple-element.415.refs_0_.refs_1_.refs_2_.refs_3_.refs_4_, bf16[1024,2048]{1,0:T(8,128)(2,1)} %get-tuple-element.415.refs_0_.refs_1_.refs_2_.refs_3_.refs_4_, ...), custom_call_target="tpu_custom_call" | custom-call | flops 999999995904 | bytes 1 | tf_op jit(solution)/shard_map/head_grad/pallas_call | solution.py:93
  692.6 7.4 collective-permute-done.53
  707.1 13.4 %down.2 = (bf16[512,2048]{1,0:T(8,128)(2,1)}, bf16[512,2048]{1,0:T(8,128)(2,1)S(1)}, f32[8,128]{1,0:T(8,128)S(1)}) custom-call(s32[6]{0:T(128)S(1)} %copy-done.24, bf16[1024,1024]{1,0:T(8,128)(2,1)} %copy-done.42, bf16[1024,1024]{1,0:T(8,128)(2,1)} %copy-done.43, bf16[1024,1024]{1,0:T(8,128)(2,1)} %copy-done.42, bf16[1024,1024]{1,0:T(8,128)(2,1)} %copy-done.43, ...), custom_call_target="tpu_custom_call" | custom-call | flops 999999995904 | bytes 1 | tf_op jit(solution)/shard_map/down/pallas_call | solution.py:93
  725.8 6.4 all_to_all.36
  732.9 7.9 input_back.1
  760.6 13.0 %down.3 = (bf16[512,2048]{1,0:T(8,128)(2,1)}, bf16[512,2048]{1,0:T(8,128)(2,1)S(1)}, f32[8,128]{1,0:T(8,128)S(1)}) custom-call(s32[6]{0:T(128)S(1)} %copy-done.25, bf16[1024,1024]{1,0:T(8,128)(2,1)} %copy-done.38, bf16[1024,1024]{1,0:T(8,128)(2,1)} %copy-done.39, bf16[1024,1024]{1,0:T(8,128)(2,1)} %copy-done.38, bf16[1024,1024]{1,0:T(8,128)(2,1)} %copy-done.39, ...), custom_call_target="tpu_custom_call" | custom-call | flops 999999995904 | bytes 1 | tf_op jit(solution)/shard_map/down/pallas_call | solution.py:93
  790.2 11.5 %collective-permute-done.69 = bf16[512,1024]{1,0:T(8,128)(2,1)} collective-permute-done((bf16[512,1024]{1,0:T(8,128)(2,1)}, bf16[512,1024]{1,0:T(8,128)(2,1)}, u32[]{:S(2)}, u32[]{:S(2)}) %collective-permute-start.69) | collective-permute-done | bytes 1048608 | tf_op jit(solution)/shard_map/ppermute | solution.py:582
  812.0 21.9 %collective-permute-done.70 = f32[2,2048]{1,0:T(2,128)S(1)} collective-permute-done((f32[2,2048]{1,0:T(2,128)S(1)}, f32[2,2048]{1,0:T(2,128)S(1)}, u32[]{:S(2)}, u32[]{:S(2)}) %collective-permute-start.70) | collective-permute-done | bytes 16416 | tf_op jit(solution)/shard_map/ppermute | solution.py:603
  838.1 10.2 %finish.3 = (f32[1024,2048]{1,0:T(8,128)}, f32[1024,2048]{1,0:T(8,128)}, f32[8,128]{1,0:T(8,128)S(1)}) custom-call(s32[6]{0:T(128)S(1)} %copy-done.26, bf16[2,256,2048]{2,1,0:T(8,128)(2,1)} %bitcast.16.refs_1_, bf16[2,256,2048]{2,1,0:T(8,128)(2,1)} %collective-permute-done.55.refs_2_, bf16[2,256,2048]{2,1,0:T(8,128)(2,1)} %collective-permute-done.71.refs_3_, ...), custom_call_target="tpu_custom_call" | custom-call | flops 999999995904 | bytes 1 | tf_op jit(solution)/shard_map/finish/pallas_call | solution.py:93
  857.4 6.4 collective-permute-done.77.refs_2_
  864.7 8.2 collective-permute-done.75.refs_3_
  872.9 6.7 finish.4
  884.2 11.1 %collective-permute-done.80.refs_4_ = bf16[2,256,1024]{2,1,0:T(8,128)(2,1)} collective-permute-done((bf16[2,256,1024]{2,1,0:T(8,128)(2,1)}, bf16[2,256,1024]{2,1,0:T(8,128)(2,1)}, u32[]{:S(2)}, u32[]{:S(2)}) %collective-permute-start.80) | collective-permute-done | bytes 1048608 | tf_op jit(solution)/shard_map/ppermute | solution.py:603
  895.3 6.5 finish.5
  (428 shorter events, 313.2 us)
Async XLA Ops:
  0.6 32.6 %collective-permute-start = (bf16[1024,1024]{1,0:T(8,128)(2,1)}, bf16[1024,1024]{1,0:T(8,128)(2,1)}, u32[]{:S(2)}, u32[]{:S(2)}) collective-permute-start(bf16[1024,1024]{1,0:T(8,128)(2,1)} %refs_1_.16), channel_id=1, source_target_pairs={{0,4},{4,0},{1,5},{5,1},{2,6},{6,2},{3,7},{7,3},{8,12},{12,8},{9,1... | collective-permute-start | bytes 6291464 | tf_op jit(solution)/shard_map/ppermute | solution.py:582
  1.2 71.7 %collective-permute-start.6 = (bf16[1024,1024]{1,0:T(8,128)(2,1)}, bf16[1024,1024]{1,0:T(8,128)(2,1)}, u32[]{:S(2)}, u32[]{:S(2)}) collective-permute-start(bf16[1024,1024]{1,0:T(8,128)(2,1)} %refs_1_.16), channel_id=1, source_target_pairs={{0,1},{1,0},{2,3},{3,2},{4,5},{5,4},{6,7},{7,6},{8,9},{9,8},{10,11... | collective-permute-start | bytes 6291464 | tf_op jit(solution)/shard_map/ppermute | solution.py:582
  22.1 56.6 %collective-permute-start.7 = (bf16[512,1024]{1,0:T(8,128)(2,1)}, bf16[512,1024]{1,0:T(8,128)(2,1)}, u32[]{:S(2)}, u32[]{:S(2)}) collective-permute-start(bf16[512,1024]{1,0:T(8,128)(2,1)} %get-tuple-element.416), channel_id=1, source_target_pairs={{0,2},{1,3},{2,0},{3,1},{4,6},{5,7},{6,4},{7,5},{8,10},{9,11},{10,... | collective-permute-start | bytes 3145736 | tf_op jit(solution)/shard_map/ppermute | solution.py:582
  32.6 18.3 %collective-permute-start.5 = (bf16[1024,1024]{1,0:T(8,128)(2,1)}, bf16[1024,1024]{1,0:T(8,128)(2,1)}, u32[]{:S(2)}, u32[]{:S(2)}) collective-permute-start(bf16[1024,1024]{1,0:T(8,128)(2,1)} %get-tuple-element.403), channel_id=1, source_target_pairs={{0,4},{4,0},{1,5},{5,1},{2,6},{6,2},{3,7},{7,3},{8,12},{12,8},{9,1... | collective-permute-start | bytes 6291464 | tf_op jit(solution)/shard_map/ppermute | solution.py:582
  78.7 33.5 %collective-permute-start.9 = (bf16[512,1024]{1,0:T(8,128)(2,1)}, bf16[512,1024]{1,0:T(8,128)(2,1)}, u32[]{:S(2)}, u32[]{:S(2)}) collective-permute-start(bf16[512,1024]{1,0:T(8,128)(2,1)} %collective-permute-done.7.refs_1_), channel_id=1, source_target_pairs={{0,16},{4,12},{8,24},{12,4},{16,0},{20,28},{24,8},{28,20},{1,17},{... | collective-permute-start | bytes 3145736 | tf_op jit(solution)/shard_map/ppermute | solution.py:603
  80.5 24.2 %collective-permute-start.8 = (bf16[512,1024]{1,0:T(8,128)(2,1)}, bf16[512,1024]{1,0:T(8,128)(2,1)}, u32[]{:S(2)}, u32[]{:S(2)}) collective-permute-start(bf16[512,1024]{1,0:T(8,128)(2,1)} %collective-permute-done.7.refs_1_), channel_id=1, source_target_pairs={{0,8},{4,20},{8,0},{12,28},{16,24},{20,4},{24,16},{28,12},{1,9},{5... | collective-permute-start | bytes 3145736 | tf_op jit(solution)/shard_map/ppermute | solution.py:603
  81.9 71.6 %collective-permute-start.12 = (bf16[384,2048]{1,0:T(8,128)(2,1)}, bf16[384,2048]{1,0:T(8,128)(2,1)}, u32[]{:S(2)}, u32[]{:S(2)}) collective-permute-start(bf16[384,2048]{1,0:T(8,128)(2,1)} %get-tuple-element.451), channel_id=1, source_target_pairs={{0,2},{1,3},{2,0},{3,1},{4,6},{5,7},{6,4},{7,5},{8,10},{9,11},{10,... | collective-permute-start | bytes 4718600 | tf_op jit(solution)/shard_map/ppermute | solution.py:582
  83.6 115.6 %collective-permute-start.20 = (bf16[1024,1024]{1,0:T(8,128)(2,1)}, bf16[1024,1024]{1,0:T(8,128)(2,1)}, u32[]{:S(2)}, u32[]{:S(2)}) collective-permute-start(bf16[1024,1024]{1,0:T(8,128)(2,1)} %refs_1_.19), channel_id=1, source_target_pairs={{0,1},{1,0},{2,3},{3,2},{4,5},{5,4},{6,7},{7,6},{8,9},{9,8},{10,11... | collective-permute-start | bytes 6291464 | tf_op jit(solution)/shard_map/ppermute | solution.py:582
  153.5 89.7 %collective-permute-start.16 = (bf16[512,2048]{1,0:T(8,128)(2,1)}, bf16[512,2048]{1,0:T(8,128)(2,1)}, u32[]{:S(2)}, u32[]{:S(2)}) collective-permute-start(bf16[512,2048]{1,0:T(8,128)(2,1)} %add_convert_fusion.7), channel_id=1, source_target_pairs={{0,1},{1,0},{2,3},{3,2},{4,5},{5,4},{6,7},{7,6},{8,9},{9,8},{10,11... | collective-permute-start | bytes 6291464 | tf_op jit(solution)/shard_map/ppermute | solution.py:582
  154.0 96.4 %collective-permute-start.24 = (bf16[384,2048]{1,0:T(8,128)(2,1)}, bf16[384,2048]{1,0:T(8,128)(2,1)}, u32[]{:S(2)}, u32[]{:S(2)}) collective-permute-start(bf16[384,2048]{1,0:T(8,128)(2,1)} %get-tuple-element.488), channel_id=1, source_target_pairs={{0,2},{1,3},{2,0},{3,1},{4,6},{5,7},{6,4},{7,5},{8,10},{9,11},{10,... | collective-permute-start | bytes 4718600 | tf_op jit(solution)/shard_map/ppermute | solution.py:582
  157.9 20.7 %collective-permute-start.17 = (bf16[384,2048]{1,0:T(8,128)(2,1)}, bf16[384,2048]{1,0:T(8,128)(2,1)}, u32[]{:S(2)}, u32[]{:S(2)}) collective-permute-start(bf16[384,2048]{1,0:T(8,128)(2,1)} %collective-permute-done.12.refs_1_), channel_id=1, source_target_pairs={{0,8},{4,20},{8,0},{12,28},{16,24},{20,4},{24,16},{28,12},{1,9},{5... | collective-permute-start | bytes 4718600 | tf_op jit(solution)/shard_map/ppermute | solution.py:603
  159.4 20.8 %collective-permute-start.21 = (bf16[1024,1024]{1,0:T(8,128)(2,1)}, bf16[1024,1024]{1,0:T(8,128)(2,1)}, u32[]{:S(2)}, u32[]{:S(2)}) collective-permute-start(bf16[1024,1024]{1,0:T(8,128)(2,1)} %refs_1_.19), channel_id=1, source_target_pairs={{0,4},{4,0},{1,5},{5,1},{2,6},{6,2},{3,7},{7,3},{8,12},{12,8},{9,1... | collective-permute-start | bytes 6291464 | tf_op jit(solution)/shard_map/ppermute | solution.py:582
  178.6 29.8 %collective-permute-start.18 = (bf16[384,2048]{1,0:T(8,128)(2,1)}, bf16[384,2048]{1,0:T(8,128)(2,1)}, u32[]{:S(2)}, u32[]{:S(2)}) collective-permute-start(bf16[384,2048]{1,0:T(8,128)(2,1)} %collective-permute-done.12.refs_1_), channel_id=1, source_target_pairs={{0,16},{4,12},{8,24},{12,4},{16,0},{20,28},{24,8},{28,20},{1,17},{... | collective-permute-start | bytes 4718600 | tf_op jit(solution)/shard_map/ppermute | solution.py:603
  180.2 63.0 %collective-permute-start.15 = (bf16[512,2048]{1,0:T(8,128)(2,1)}, bf16[512,2048]{1,0:T(8,128)(2,1)}, u32[]{:S(2)}, u32[]{:S(2)}) collective-permute-start(bf16[512,2048]{1,0:T(8,128)(2,1)} %get-tuple-element.472), channel_id=1, source_target_pairs={{0,4},{4,0},{1,5},{5,1},{2,6},{6,2},{3,7},{7,3},{8,12},{12,8},{9,1... | collective-permute-start | bytes 6291464 | tf_op jit(solution)/shard_map/ppermute | solution.py:582
  203.8 20.7 %collective-permute-start.19 = (bf16[384,2048]{1,0:T(8,128)(2,1)}, bf16[384,2048]{1,0:T(8,128)(2,1)}, u32[]{:S(2)}, u32[]{:S(2)}) collective-permute-start(bf16[384,2048]{1,0:T(8,128)(2,1)} %collective-permute-done.17.refs_2_), channel_id=1, source_target_pairs={{0,16},{4,12},{8,24},{12,4},{16,0},{20,28},{24,8},{28,20},{1,17},{... | collective-permute-start | bytes 4718600 | tf_op jit(solution)/shard_map/ppermute | solution.py:603
  249.3 46.9 %collective-permute-start.28 = (bf16[512,2048]{1,0:T(8,128)(2,1)}, bf16[512,2048]{1,0:T(8,128)(2,1)}, u32[]{:S(2)}, u32[]{:S(2)}) collective-permute-start(bf16[512,2048]{1,0:T(8,128)(2,1)} %get-tuple-element.487.refs_1_), channel_id=1, source_target_pairs={{0,1},{1,0},{2,3},{3,2},{4,5},{5,4},{6,7},{7,6},{8,9},{9,8},{10,11... | collective-permute-start | bytes 6291464 | tf_op jit(solution)/shard_map/ppermute | solution.py:582
  253.8 72.3 %collective-permute-start.27 = (bf16[384,2048]{1,0:T(8,128)(2,1)}, bf16[384,2048]{1,0:T(8,128)(2,1)}, u32[]{:S(2)}, u32[]{:S(2)}) collective-permute-start(bf16[384,2048]{1,0:T(8,128)(2,1)} %collective-permute-done.24.refs_1_), channel_id=1, source_target_pairs={{0,16},{4,12},{8,24},{12,4},{16,0},{20,28},{24,8},{28,20},{1,17},{... | collective-permute-start | bytes 4718600 | tf_op jit(solution)/shard_map/ppermute | solution.py:603
  254.3 41.9 %collective-permute-start.26 = (bf16[384,2048]{1,0:T(8,128)(2,1)}, bf16[384,2048]{1,0:T(8,128)(2,1)}, u32[]{:S(2)}, u32[]{:S(2)}) collective-permute-start(bf16[384,2048]{1,0:T(8,128)(2,1)} %collective-permute-done.24.refs_1_), channel_id=1, source_target_pairs={{0,8},{4,20},{8,0},{12,28},{16,24},{20,4},{24,16},{28,12},{1,9},{5... | collective-permute-start | bytes 4718600 | tf_op jit(solution)/shard_map/ppermute | solution.py:603
  296.8 29.3 %collective-permute-start.29 = (bf16[384,2048]{1,0:T(8,128)(2,1)}, bf16[384,2048]{1,0:T(8,128)(2,1)}, u32[]{:S(2)}, u32[]{:S(2)}) collective-permute-start(bf16[384,2048]{1,0:T(8,128)(2,1)} %collective-permute-done.26.refs_2_), channel_id=1, source_target_pairs={{0,16},{4,12},{8,24},{12,4},{16,0},{20,28},{24,8},{28,20},{1,17},{... | collective-permute-start | bytes 4718600 | tf_op jit(solution)/shard_map/ppermute | solution.py:603
  399.8 102.0 %collective-permute-start.34 = (bf16[2,512,4096]{2,1,0:T(8,128)(2,1)}, bf16[2,512,4096]{2,1,0:T(8,128)(2,1)}, u32[]{:S(2)}, u32[]{:S(2)}) collective-permute-start(bf16[2,512,4096]{2,1,0:T(8,128)(2,1)} %get-tuple-element.541), channel_id=1, source_target_pairs={{0,8},{4,20},{8,0},{12,28},{16,24},{20,4},{24,16},{28,12},{1,9},{5... | collective-permute-start | bytes 25165832 | tf_op jit(solution)/shard_map/ppermute | solution.py:603
  433.2 50.2 %collective-permute-start.36 = (bf16[512,2048]{1,0:T(8,128)(2,1)}, bf16[512,2048]{1,0:T(8,128)(2,1)}, u32[]{:S(2)}, u32[]{:S(2)}) collective-permute-start(bf16[512,2048]{1,0:T(8,128)(2,1)} %add_convert_fusion.6), channel_id=1, source_target_pairs={{0,1},{1,0},{2,3},{3,2},{4,5},{5,4},{6,7},{7,6},{8,9},{9,8},{10,11... | collective-permute-start | bytes 6291464 | tf_op jit(solution)/shard_map/ppermute | solution.py:582
  458.0 25.5 %collective-permute-start.35 = (bf16[512,2048]{1,0:T(8,128)(2,1)}, bf16[512,2048]{1,0:T(8,128)(2,1)}, u32[]{:S(2)}, u32[]{:S(2)}) collective-permute-start(bf16[512,2048]{1,0:T(8,128)(2,1)} %get-tuple-element.543), channel_id=1, source_target_pairs={{0,4},{4,0},{1,5},{5,1},{2,6},{6,2},{3,7},{7,3},{8,12},{12,8},{9,1... | collective-permute-start | bytes 6291464 | tf_op jit(solution)/shard_map/ppermute | solution.py:582
  491.9 48.2 %collective-permute-start.40 = (bf16[512,2048]{1,0:T(8,128)(2,1)}, bf16[512,2048]{1,0:T(8,128)(2,1)}, u32[]{:S(2)}, u32[]{:S(2)}) collective-permute-start(bf16[512,2048]{1,0:T(8,128)(2,1)} %get-tuple-element.547.refs_1_), channel_id=1, source_target_pairs={{0,1},{1,0},{2,3},{3,2},{4,5},{5,4},{6,7},{7,6},{8,9},{9,8},{10,11... | collective-permute-start | bytes 6291464 | tf_op jit(solution)/shard_map/ppermute | solution.py:582
  508.2 49.4 %collective-permute-start.39 = (bf16[512,4096]{1,0:T(8,128)(2,1)}, bf16[512,4096]{1,0:T(8,128)(2,1)}, u32[]{:S(2)}, u32[]{:S(2)}) collective-permute-start(bf16[512,4096]{1,0:T(8,128)(2,1)} %fusion), channel_id=1, source_target_pairs={{0,16},{4,12},{8,24},{12,4},{16,0},{20,28},{24,8},{28,20},{1,17},{... | collective-permute-start | bytes 12582920 | tf_op jit(solution)/shard_map/ppermute | solution.py:603
  540.1 43.5 %collective-permute-start.43 = (bf16[512,2048]{1,0:T(8,128)(2,1)}, bf16[512,2048]{1,0:T(8,128)(2,1)}, u32[]{:S(2)}, u32[]{:S(2)}) collective-permute-start(bf16[512,2048]{1,0:T(8,128)(2,1)} %collective-permute-done.40.refs_1_), channel_id=1, source_target_pairs={{0,4},{4,0},{1,5},{5,1},{2,6},{6,2},{3,7},{7,3},{8,12},{12,8},{9,1... | collective-permute-start | bytes 6291464 | tf_op jit(solution)/shard_map/ppermute | solution.py:582
  556.0 56.6 %collective-permute-start.46 = (bf16[2,512,2048]{2,1,0:T(8,128)(2,1)}, bf16[2,512,2048]{2,1,0:T(8,128)(2,1)}, u32[]{:S(2)}, u32[]{:S(2)}) collective-permute-start(bf16[2,512,2048]{2,1,0:T(8,128)(2,1)} %get-tuple-element.610), channel_id=1, source_target_pairs={{0,8},{4,20},{8,0},{12,28},{16,24},{20,4},{24,16},{28,12},{1,9},{5... | collective-permute-start | bytes 12582920 | tf_op jit(solution)/shard_map/ppermute | solution.py:603
  563.7 156.7 %collective-permute-start.42 = (bf16[512,2048]{1,0:T(8,128)(2,1)}, bf16[512,2048]{1,0:T(8,128)(2,1)}, u32[]{:S(2)}, u32[]{:S(2)}) collective-permute-start(bf16[512,2048]{1,0:T(8,128)(2,1)} %fusion.1), channel_id=1, source_target_pairs={{0,2},{1,3},{2,0},{3,1},{4,6},{5,7},{6,4},{7,5},{8,10},{9,11},{10,... | collective-permute-start | bytes 6291464 | tf_op jit(solution)/shard_map/ppermute | solution.py:582
  618.7 49.1 %collective-permute-start.51 = (bf16[512,2048]{1,0:T(8,128)(2,1)}, bf16[512,2048]{1,0:T(8,128)(2,1)}, u32[]{:S(2)}, u32[]{:S(2)}) collective-permute-start(bf16[512,2048]{1,0:T(8,128)(2,1)} %fusion.4), channel_id=1, source_target_pairs={{0,16},{4,12},{8,24},{12,4},{16,0},{20,28},{24,8},{28,20},{1,17},{... | collective-permute-start | bytes 6291464 | tf_op jit(solution)/shard_map/ppermute | solution.py:603
  630.3 22.1 %collective-permute-start.48 = (bf16[512,2048]{1,0:T(8,128)(2,1)}, bf16[512,2048]{1,0:T(8,128)(2,1)}, u32[]{:S(2)}, u32[]{:S(2)}) collective-permute-start(bf16[512,2048]{1,0:T(8,128)(2,1)} %get-tuple-element.616), channel_id=1, source_target_pairs={{0,4},{4,0},{1,5},{5,1},{2,6},{6,2},{3,7},{7,3},{8,12},{12,8},{9,1... | collective-permute-start | bytes 6291464 | tf_op jit(solution)/shard_map/ppermute | solution.py:582
  651.1 48.9 %collective-permute-start.53 = (bf16[2,512,2048]{2,1,0:T(8,128)(2,1)}, bf16[2,512,2048]{2,1,0:T(8,128)(2,1)}, u32[]{:S(2)}, u32[]{:S(2)}) collective-permute-start(bf16[2,512,2048]{2,1,0:T(8,128)(2,1)} %get-tuple-element.641), channel_id=1, source_target_pairs={{0,8},{4,20},{8,0},{12,28},{16,24},{20,4},{24,16},{28,12},{1,9},{5... | collective-permute-start | bytes 12582920 | tf_op jit(solution)/shard_map/ppermute | solution.py:603
  656.1 76.7 %collective-permute-start.57 = (bf16[512,2048]{1,0:T(8,128)(2,1)}, bf16[512,2048]{1,0:T(8,128)(2,1)}, u32[]{:S(2)}, u32[]{:S(2)}) collective-permute-start(bf16[512,2048]{1,0:T(8,128)(2,1)} %add_convert_fusion.4), channel_id=1, source_target_pairs={{0,1},{1,0},{2,3},{3,2},{4,5},{5,4},{6,7},{7,6},{8,9},{9,8},{10,11... | collective-permute-start | bytes 6291464 | tf_op jit(solution)/shard_map/ppermute | solution.py:582
  671.9 105.2 %collective-permute-start.65 = (bf16[512,1024]{1,0:T(8,128)(2,1)}, bf16[512,1024]{1,0:T(8,128)(2,1)}, u32[]{:S(2)}, u32[]{:S(2)}) collective-permute-start(bf16[512,1024]{1,0:T(8,128)(2,1)} %fusion.11), channel_id=1, source_target_pairs={{0,2},{1,3},{2,0},{3,1},{4,6},{5,7},{6,4},{7,5},{8,10},{9,11},{10,... | collective-permute-start | bytes 3145736 | tf_op jit(solution)/shard_map/ppermute | solution.py:582
  673.1 59.8 %collective-permute-start.56 = (bf16[512,2048]{1,0:T(8,128)(2,1)}, bf16[512,2048]{1,0:T(8,128)(2,1)}, u32[]{:S(2)}, u32[]{:S(2)}) collective-permute-start(bf16[512,2048]{1,0:T(8,128)(2,1)} %get-tuple-element.654), channel_id=1, source_target_pairs={{0,4},{4,0},{1,5},{5,1},{2,6},{6,2},{3,7},{7,3},{8,12},{12,8},{9,1... | collective-permute-start | bytes 6291464 | tf_op jit(solution)/shard_map/ppermute | solution.py:582
  705.9 37.4 %collective-permute-start.60 = (bf16[512,2048]{1,0:T(8,128)(2,1)}, bf16[512,2048]{1,0:T(8,128)(2,1)}, u32[]{:S(2)}, u32[]{:S(2)}) collective-permute-start(bf16[512,2048]{1,0:T(8,128)(2,1)} %fusion.5), channel_id=1, source_target_pairs={{0,16},{4,12},{8,24},{12,4},{16,0},{20,28},{24,8},{28,20},{1,17},{... | collective-permute-start | bytes 6291464 | tf_op jit(solution)/shard_map/ppermute | solution.py:603
  732.1 27.2 %collective-permute-start.55 = (bf16[2,256,2048]{2,1,0:T(8,128)(2,1)}, bf16[2,256,2048]{2,1,0:T(8,128)(2,1)}, u32[]{:S(2)}, u32[]{:S(2)}) collective-permute-start(bf16[2,256,2048]{2,1,0:T(8,128)(2,1)} %bitcast.16.refs_1_), channel_id=1, source_target_pairs={{0,8},{4,20},{8,0},{12,28},{16,24},{20,4},{24,16},{28,12},{1,9},{5... | collective-permute-start | bytes 6291464 | tf_op jit(solution)/shard_map/ppermute | solution.py:603
  752.5 49.2 %collective-permute-start.69 = (bf16[512,1024]{1,0:T(8,128)(2,1)}, bf16[512,1024]{1,0:T(8,128)(2,1)}, u32[]{:S(2)}, u32[]{:S(2)}) collective-permute-start(bf16[512,1024]{1,0:T(8,128)(2,1)} %fusion.10), channel_id=1, source_target_pairs={{0,2},{1,3},{2,0},{3,1},{4,6},{5,7},{6,4},{7,5},{8,10},{9,11},{10,... | collective-permute-start | bytes 3145736 | tf_op jit(solution)/shard_map/ppermute | solution.py:582
  773.7 62.5 %collective-permute-start.72 = (bf16[2,256,2048]{2,1,0:T(8,128)(2,1)}, bf16[2,256,2048]{2,1,0:T(8,128)(2,1)}, u32[]{:S(2)}, u32[]{:S(2)}) collective-permute-start(bf16[2,256,2048]{2,1,0:T(8,128)(2,1)} %collective-permute-done.55.refs_2_), channel_id=1, source_target_pairs={{0,16},{4,12},{8,24},{12,4},{16,0},{20,28},{24,8},{28,20},{1,17},{... | collective-permute-start | bytes 6291464 | tf_op jit(solution)/shard_map/ppermute | solution.py:603
  774.6 62.8 %collective-permute-start.71 = (bf16[2,256,2048]{2,1,0:T(8,128)(2,1)}, bf16[2,256,2048]{2,1,0:T(8,128)(2,1)}, u32[]{:S(2)}, u32[]{:S(2)}) collective-permute-start(bf16[2,256,2048]{2,1,0:T(8,128)(2,1)} %bitcast.16.refs_1_), channel_id=1, source_target_pairs={{0,16},{4,12},{8,24},{12,4},{16,0},{20,28},{24,8},{28,20},{1,17},{... | collective-permute-start | bytes 6291464 | tf_op jit(solution)/shard_map/ppermute | solution.py:603
  785.6 26.4 %collective-permute-start.68 = (bf16[2,256,1024]{2,1,0:T(8,128)(2,1)}, bf16[2,256,1024]{2,1,0:T(8,128)(2,1)}, u32[]{:S(2)}, u32[]{:S(2)}) collective-permute-start(bf16[2,256,1024]{2,1,0:T(8,128)(2,1)} %bitcast.23.refs_1_), channel_id=1, source_target_pairs={{0,8},{4,20},{8,0},{12,28},{16,24},{20,4},{24,16},{28,12},{1,9},{5... | collective-permute-start | bytes 3145736 | tf_op jit(solution)/shard_map/ppermute | solution.py:603
  786.9 62.8 %collective-permute-start.67 = (bf16[512,2048]{1,0:T(8,128)(2,1)}, bf16[512,2048]{1,0:T(8,128)(2,1)}, u32[]{:S(2)}, u32[]{:S(2)}) collective-permute-start(bf16[512,2048]{1,0:T(8,128)(2,1)} %add_convert_fusion.2), channel_id=1, source_target_pairs={{0,1},{1,0},{2,3},{3,2},{4,5},{5,4},{6,7},{7,6},{8,9},{9,8},{10,11... | collective-permute-start | bytes 6291464 | tf_op jit(solution)/shard_map/ppermute | solution.py:582
  801.7 32.2 %collective-permute-start.70 = (f32[2,2048]{1,0:T(2,128)S(1)}, f32[2,2048]{1,0:T(2,128)S(1)}, u32[]{:S(2)}, u32[]{:S(2)}) collective-permute-start(f32[2,2048]{1,0:T(2,128)S(1)} %copy-done.90), channel_id=1, source_target_pairs={{0,16},{4,12},{8,24},{12,4},{16,0},{20,28},{24,8},{28,20},{1,17},{... | collective-permute-start | bytes 49160 | tf_op jit(solution)/shard_map/ppermute | solution.py:603
  835.4 28.5 %collective-permute-start.76 = (bf16[2,256,1024]{2,1,0:T(8,128)(2,1)}, bf16[2,256,1024]{2,1,0:T(8,128)(2,1)}, u32[]{:S(2)}, u32[]{:S(2)}) collective-permute-start(bf16[2,256,1024]{2,1,0:T(8,128)(2,1)} %collective-permute-done.68.refs_2_), channel_id=1, source_target_pairs={{0,16},{4,12},{8,24},{12,4},{16,0},{20,28},{24,8},{28,20},{1,17},{... | collective-permute-start | bytes 3145736 | tf_op jit(solution)/shard_map/ppermute | solution.py:603
  836.2 36.6 %collective-permute-start.75 = (bf16[2,256,1024]{2,1,0:T(8,128)(2,1)}, bf16[2,256,1024]{2,1,0:T(8,128)(2,1)}, u32[]{:S(2)}, u32[]{:S(2)}) collective-permute-start(bf16[2,256,1024]{2,1,0:T(8,128)(2,1)} %bitcast.23.refs_1_), channel_id=1, source_target_pairs={{0,16},{4,12},{8,24},{12,4},{16,0},{20,28},{24,8},{28,20},{1,17},{... | collective-permute-start | bytes 3145736 | tf_op jit(solution)/shard_map/ppermute | solution.py:603
  837.4 26.4 %collective-permute-start.77 = (bf16[2,256,1024]{2,1,0:T(8,128)(2,1)}, bf16[2,256,1024]{2,1,0:T(8,128)(2,1)}, u32[]{:S(2)}, u32[]{:S(2)}) collective-permute-start(bf16[2,256,1024]{2,1,0:T(8,128)(2,1)} %bitcast.27.refs_1_), channel_id=1, source_target_pairs={{0,8},{4,20},{8,0},{12,28},{16,24},{20,4},{24,16},{28,12},{1,9},{5... | collective-permute-start | bytes 3145736 | tf_op jit(solution)/shard_map/ppermute | solution.py:603
  854.3 28.5 %collective-permute-start.78 = (f32[2,2048]{1,0:T(2,128)}, f32[2,2048]{1,0:T(2,128)}, u32[]{:S(2)}, u32[]{:S(2)}) collective-permute-start(f32[2,2048]{1,0:T(2,128)} %add.162), channel_id=1, source_target_pairs={{0,2},{1,3},{2,0},{3,1},{4,6},{5,7},{6,4},{7,5},{8,10},{9,11},{10,... | collective-permute-start | bytes 49160 | tf_op jit(solution)/shard_map/ppermute | solution.py:582
  856.1 28.1 %collective-permute-start.79 = (bf16[2,256,1024]{2,1,0:T(8,128)(2,1)}, bf16[2,256,1024]{2,1,0:T(8,128)(2,1)}, u32[]{:S(2)}, u32[]{:S(2)}) collective-permute-start(bf16[2,256,1024]{2,1,0:T(8,128)(2,1)} %bitcast.27.refs_1_), channel_id=1, source_target_pairs={{0,16},{4,12},{8,24},{12,4},{16,0},{20,28},{24,8},{28,20},{1,17},{... | collective-permute-start | bytes 3145736 | tf_op jit(solution)/shard_map/ppermute | solution.py:603
  863.8 15.8 %collective-permute-start.74 = (bf16[512,1024]{1,0:T(8,128)(2,1)}, bf16[512,1024]{1,0:T(8,128)(2,1)}, u32[]{:S(2)}, u32[]{:S(2)}) collective-permute-start(bf16[512,1024]{1,0:T(8,128)(2,1)} %get-tuple-element.732), channel_id=1, source_target_pairs={{0,4},{4,0},{1,5},{5,1},{2,6},{6,2},{3,7},{7,3},{8,12},{12,8},{9,1... | collective-permute-start | bytes 3145736 | tf_op jit(solution)/shard_map/ppermute | solution.py:582
  863.8 31.5 %collective-permute-start.80 = (bf16[2,256,1024]{2,1,0:T(8,128)(2,1)}, bf16[2,256,1024]{2,1,0:T(8,128)(2,1)}, u32[]{:S(2)}, u32[]{:S(2)}) collective-permute-start(bf16[2,256,1024]{2,1,0:T(8,128)(2,1)} %collective-permute-done.77.refs_2_), channel_id=1, source_target_pairs={{0,16},{4,12},{8,24},{12,4},{16,0},{20,28},{24,8},{28,20},{1,17},{... | collective-permute-start | bytes 3145736 | tf_op jit(solution)/shard_map/ppermute | solution.py:603
  (128 other events, 2057.0 us)

commit v6 on v5

--- a/solution.py
+++ b/solution.py
@@ -1057,15 +1057,15 @@
     plan.pause()
     mixed_near = [add_pair(plan, mixed_near)]
     heads.total()
-    heads.spread()
+    heads.one = post(hop_one, heads.both)
     down.spread_last()
+    gate_grad, up_grad = ups.finish()
     gains = mix(jnp.add, gains, gains_got)
     gains_got = ship(other_chip, gains)
-    gate_grad, up_grad = ups.finish()
+    mixed_mine, mixed_other = add_mixed(plan, s, mixed_near, mixed_far, residual)
+    mixed_got = ship(other_core, mixed_other)
     gains = mix(jnp.add, gains, gains_got)
     gains_got = ship(far_plane, gains)
-    mixed_mine, mixed_other = add_mixed(plan, s, mixed_near, mixed_far, residual)
-    mixed_got = ship(other_core, mixed_other)
     heads.spread_last()
     (down_grad,) = down.finish()
     mixed = side_by_side(plan, s, mixed_mine, mixed_got)

time: 906 us -> 905 us (level)
    ppermute x55 -> x56, waiting for transfers between devices: 92.2 us -> 93.3 us  [swap_axis(): return lax.ppermute(values, axis, [(i, i ^ distance) for i in range(size)])]
    ppermute x55 -> x56, starting transfers between devices: 30.8 us -> 31.5 us  [swap_axis(): return lax.ppermute(values, axis, [(i, i ^ distance) for i in range(size)])]
    pallas_call x84 -> x85, Pallas kernels: 548 us -> 549 us  [launch(): pl.pallas_call(body, out_shape=out_shape + [of((8, LANES), F32)], compile...]
    unnamed x190 -> x188, local copies, waits for them, and re-layouts: 19.2 us -> 18.8 us
  transfers between devices with their start and end apart: 81 -> 82, of which waited for: 29 -> 30; matrix products, arithmetic and copies ran while one was open for 8% -> 8% of each run, Pallas kernels for 52% -> 52%
where the time goes in v6:
time: 905 us; the launch traced here: 901 us
  Pallas kernels  549 us (61%)
  waiting for transfers between devices  183 us (20%)
  other arithmetic  69.8 us (8%)
  starting transfers between devices  59.2 us (7%)
  local copies, waits for them, and re-layouts  19.6 us (2%)
  blocking collectives  17.3 us (2%)
    pallas_call x85, Pallas kernels, launch(): pl.pallas_call(body, out_shape=out_shape + [of((8, LANES), F32)], compile...  549 us
    ppermute x56, waiting for transfers between devices, swap_axis(): return lax.ppermute(values, axis, [(i, i ^ distance) for i in range(size)])  93.3 us
    ppermute x26, waiting for transfers between devices, hop(): return lax.ppermute(values, ('dp', 'row'), pairs)  90.2 us
    ppermute x56, starting transfers between devices, swap_axis(): return lax.ppermute(values, axis, [(i, i ^ distance) for i in range(size)])  31.5 us
    ppermute x26, starting transfers between devices, hop(): return lax.ppermute(values, ('dp', 'row'), pairs)  27.7 us
    unnamed x188, local copies, waits for them, and re-layouts  18.8 us
  transfers between devices with their start and end apart: 82, of which 30 were waited for; matrix products, arithmetic and copies ran while one was open for 8% of the time, Pallas kernels for 52%

profile of v6, /device:TPU:0, one launch (start us, length us, event | category | flops | bytes accessed | tf_op | source)
XLA Modules:
  0.0 900.6 jit_solution(12184895496859855603)
XLA Ops:
  43.2 7.8 own.6
  63.5 7.8 qkv.4
  90.3 7.8 qkv.5
  98.1 6.6 collective-permute-done.8.refs_2_
  106.3 5.8 attend.5
  112.2 7.6 collective-permute-done.11.refs_4_
  126.1 6.1 qkv.6
  132.2 5.8 attend.6
  159.4 5.8 attend.7
  169.6 9.0 collective-permute-done.17.refs_2_
  184.3 14.9 %collective-permute-done.20.refs_1_ = bf16[1024,1024]{1,0:T(8,128)(2,1)} collective-permute-done((bf16[1024,1024]{1,0:T(8,128)(2,1)}, bf16[1024,1024]{1,0:T(8,128)(2,1)}, u32[]{:S(2)}, u32[]{:S(2)}) %collective-permute-start.20) | collective-permute-done | bytes 2097184 | tf_op jit(solution)/shard_map/ppermute | solution.py:582
  208.5 16.0 %collective-permute-done.19.refs_4_ = bf16[384,2048]{1,0:T(8,128)(2,1)} collective-permute-done((bf16[384,2048]{1,0:T(8,128)(2,1)}, bf16[384,2048]{1,0:T(8,128)(2,1)}, u32[]{:S(2)}, u32[]{:S(2)}) %collective-permute-start.19) | collective-permute-done | bytes 1572896 | tf_op jit(solution)/shard_map/ppermute | solution.py:603
  224.5 5.9 other.4
  230.4 12.8 %collective-permute-done.16.refs_3_ = bf16[512,2048]{1,0:T(8,128)(2,1)} collective-permute-done((bf16[512,2048]{1,0:T(8,128)(2,1)}, bf16[512,2048]{1,0:T(8,128)(2,1)}, u32[]{:S(2)}, u32[]{:S(2)}) %collective-permute-start.16) | collective-permute-done | bytes 2097184 | tf_op jit(solution)/shard_map/ppermute | solution.py:582
  243.2 6.1 norm.1
  258.9 19.8 %ffn.4 = (bf16[1024,1024]{1,0:T(8,128)(2,1)S(1)}, bf16[1024,2048]{1,0:T(8,128)(2,1)}, f32[8,128]{1,0:T(8,128)S(1)}) custom-call(bf16[1024,2048]{1,0:T(8,128)(2,1)} %get-tuple-element.502.refs_0_.refs_1_.refs_2_.refs_3_.refs_4_, bf16[1024,2048]{1,0:T(8,128)(2,1)} %get-tuple-element.503.refs_1_.refs_5_.refs_2_.refs_3_.refs_4_, ...), custom_call_target="tpu_custom_call" | custom-call | flops 999999995904 | bytes 1 | tf_op jit(solution)/shard_map/ffn/pallas_call | solution.py:93
  278.7 17.6 %collective-permute-done.28.refs_1_ = bf16[512,2048]{1,0:T(8,128)(2,1)} collective-permute-done((bf16[512,2048]{1,0:T(8,128)(2,1)}, bf16[512,2048]{1,0:T(8,128)(2,1)}, u32[]{:S(2)}, u32[]{:S(2)}) %collective-permute-start.28) | collective-permute-done | bytes 2097184 | tf_op jit(solution)/shard_map/ppermute | solution.py:582
  305.0 19.8 %ffn.5 = (bf16[1024,1024]{1,0:T(8,128)(2,1)S(1)}, bf16[1024,2048]{1,0:T(8,128)(2,1)}, f32[8,128]{1,0:T(8,128)S(1)}) custom-call(bf16[1024,2048]{1,0:T(8,128)(2,1)} %get-tuple-element.516.refs_0_.refs_5_.refs_6_.refs_7_.refs_8_, bf16[1024,2048]{1,0:T(8,128)(2,1)} %get-tuple-element.517.refs_1_.refs_5_.refs_6_.refs_7_.refs_8_, ...), custom_call_target="tpu_custom_call" | custom-call | flops 999999995904 | bytes 1 | tf_op jit(solution)/shard_map/ffn/pallas_call | solution.py:93
  326.1 5.8 other.5
  331.9 19.8 %ffn.6 = (bf16[1024,1024]{1,0:T(8,128)(2,1)S(1)}, bf16[1024,2048]{1,0:T(8,128)(2,1)}, f32[8,128]{1,0:T(8,128)S(1)}) custom-call(bf16[1024,2048]{1,0:T(8,128)(2,1)} %get-tuple-element.516.refs_0_.refs_5_.refs_6_.refs_7_.refs_8_, bf16[1024,2048]{1,0:T(8,128)(2,1)} %get-tuple-element.517.refs_1_.refs_5_.refs_6_.refs_7_.refs_8_, ...), custom_call_target="tpu_custom_call" | custom-call | flops 999999995904 | bytes 1 | tf_op jit(solution)/shard_map/ffn/pallas_call | solution.py:93
  353.1 20.8 %ffn.7 = (bf16[1024,1024]{1,0:T(8,128)(2,1)S(1)}, bf16[1024,2048]{1,0:T(8,128)(2,1)}, f32[8,128]{1,0:T(8,128)S(1)}) custom-call(bf16[1024,2048]{1,0:T(8,128)(2,1)} %get-tuple-element.502.refs_0_.refs_1_.refs_2_.refs_3_.refs_4_, bf16[1024,2048]{1,0:T(8,128)(2,1)} %get-tuple-element.503.refs_1_.refs_5_.refs_2_.refs_3_.refs_4_, ...), custom_call_target="tpu_custom_call" | custom-call | flops 999999995904 | bytes 1 | tf_op jit(solution)/shard_map/ffn/pallas_call | solution.py:93
  373.9 25.3 %gu_grad.2 = (bf16[2,512,4096]{2,1,0:T(8,128)(2,1)}, f32[8,128]{1,0:T(8,128)S(1)}) custom-call(s32[6]{0:T(128)S(1)} %stack.45.refs_0_, bf16[1024,2048]{1,0:T(8,128)(2,1)S(1)} %copy-done.32, bf16[1024,2048]{1,0:T(8,128)(2,1)S(1)} %copy-done.32, bf16[1024,2048]{1,0:T(8,128)(2,1)S(1)} %copy-done.32, bf16[1024,2048]{1,0:T(8,128)(2,1)S(1)} %copy-done.32, ...), custom_call_target="tpu_custom_call" | custom-call | flops 999999995904 | bytes 1 | tf_op jit(solution)/shard_map/gu_grad/pallas_call | solution.py:93
  400.7 23.6 %ffn_in.2 = (bf16[512,2048]{1,0:T(8,128)(2,1)}, bf16[512,2048]{1,0:T(8,128)(2,1)S(1)}, f32[8,128]{1,0:T(8,128)S(1)}) custom-call(s32[6]{0:T(128)S(1)} %stack.45.refs_0_, bf16[1024,2048]{1,0:T(8,128)(2,1)} %get-tuple-element.527.refs_11_.refs_1_.refs_3_, bf16[1024,2048]{1,0:T(8,128)(2,1)} %get-tuple-element.528.refs_12_.refs_2_.refs_4_, ...), custom_call_target="tpu_custom_call" | custom-call | flops 999999995904 | bytes 1 | tf_op jit(solution)/shard_map/ffn_in/pallas_call | solution.py:93
  434.1 24.0 %ffn_in.3 = (bf16[512,2048]{1,0:T(8,128)(2,1)}, bf16[512,2048]{1,0:T(8,128)(2,1)S(1)}, f32[8,128]{1,0:T(8,128)S(1)}) custom-call(s32[6]{0:T(128)S(1)} %stack.45.refs_0_, bf16[1024,2048]{1,0:T(8,128)(2,1)} %get-tuple-element.525.refs_9_.refs_1_.refs_3_, bf16[1024,2048]{1,0:T(8,128)(2,1)} %get-tuple-element.526.refs_10_.refs_2_.refs_4_, ...), custom_call_target="tpu_custom_call" | custom-call | flops 999999995904 | bytes 1 | tf_op jit(solution)/shard_map/ffn_in/pallas_call | solution.py:93
  458.3 25.2 %gu_grad.3 = (bf16[2,512,4096]{2,1,0:T(8,128)(2,1)}, f32[8,128]{1,0:T(8,128)S(1)}) custom-call(s32[6]{0:T(128)S(1)} %stack.45.refs_0_, bf16[1024,2048]{1,0:T(8,128)(2,1)S(1)} %copy-done.32, bf16[1024,2048]{1,0:T(8,128)(2,1)S(1)} %copy-done.32, bf16[1024,2048]{1,0:T(8,128)(2,1)S(1)} %copy-done.32, bf16[1024,2048]{1,0:T(8,128)(2,1)S(1)} %copy-done.32, ...), custom_call_target="tpu_custom_call" | custom-call | flops 999999995904 | bytes 1 | tf_op jit(solution)/shard_map/gu_grad/pallas_call | solution.py:93
  484.2 7.8 ffn_back.1
  512.0 8.4 attend_back.4
  524.2 8.3 attend_back.5
  532.5 7.7 collective-permute-done.40.refs_1_
  540.1 15.9 %down_grad.2 = (bf16[2,512,2048]{2,1,0:T(8,128)(2,1)}, f32[8,128]{1,0:T(8,128)S(1)}) custom-call(s32[6]{0:T(128)S(1)} %copy-done.23, bf16[1024,2048]{1,0:T(8,128)(2,1)} %get-tuple-element.503.refs_1_.refs_5_.refs_2_.refs_3_.refs_4_, bf16[1024,2048]{1,0:T(8,128)(2,1)} %get-tuple-element.503.refs_1_.refs_5_.refs_2_.refs_3_.refs_4_, ...), custom_call_target="tpu_custom_call" | custom-call | flops 999999995904 | bytes 1 | tf_op jit(solution)/shard_map/down_grad/pallas_call | solution.py:93
  568.0 15.6 %down_grad.3 = (bf16[2,512,2048]{2,1,0:T(8,128)(2,1)}, f32[8,128]{1,0:T(8,128)S(1)}) custom-call(s32[6]{0:T(128)S(1)} %copy-done.23, bf16[1024,2048]{1,0:T(8,128)(2,1)} %get-tuple-element.503.refs_1_.refs_5_.refs_2_.refs_3_.refs_4_, bf16[1024,2048]{1,0:T(8,128)(2,1)} %get-tuple-element.503.refs_1_.refs_5_.refs_2_.refs_3_.refs_4_, ...), custom_call_target="tpu_custom_call" | custom-call | flops 999999995904 | bytes 1 | tf_op jit(solution)/shard_map/down_grad/pallas_call | solution.py:93
  591.8 8.2 attend_back.6
  604.3 8.2 attend_back.7
  619.9 10.4 %qkv_in.2 = (bf16[512,2048]{1,0:T(8,128)(2,1)}, bf16[512,2048]{1,0:T(8,128)(2,1)}, f32[8,128]{1,0:T(8,128)S(1)}) custom-call(s32[6]{0:T(128)S(1)} %copy-done.24, bf16[1024,768]{1,0:T(8,128)(2,1)S(1)} %get-tuple-element.775.refs_1_.refs_3_, bf16[1024,768]{1,0:T(8,128)(2,1)S(1)} %get-tuple-element.776.refs_2_.refs_4_, ...), custom_call_target="tpu_custom_call" | custom-call | flops 999999995904 | bytes 1 | tf_op jit(solution)/shard_map/qkv_in/pallas_call | solution.py:93
  630.5 19.7 %head_grad.2 = (bf16[2,512,2048]{2,1,0:T(8,128)(2,1)}, f32[8,128]{1,0:T(8,128)S(1)}) custom-call(s32[6]{0:T(128)S(1)} %copy-done.24, bf16[1024,2048]{1,0:T(8,128)(2,1)} %get-tuple-element.420.refs_0_.refs_1_.refs_2_.refs_3_.refs_4_, bf16[1024,2048]{1,0:T(8,128)(2,1)} %get-tuple-element.420.refs_0_.refs_1_.refs_2_.refs_3_.refs_4_, ...), custom_call_target="tpu_custom_call" | custom-call | flops 999999995904 | bytes 1 | tf_op jit(solution)/shard_map/head_grad/pallas_call | solution.py:93
  657.6 10.3 %qkv_in.3 = (bf16[512,2048]{1,0:T(8,128)(2,1)}, bf16[512,2048]{1,0:T(8,128)(2,1)}, f32[8,128]{1,0:T(8,128)S(1)}) custom-call(s32[6]{0:T(128)S(1)} %copy-done.24, bf16[1024,768]{1,0:T(8,128)(2,1)S(1)} %get-tuple-element.777.refs_1_.refs_3_, bf16[1024,768]{1,0:T(8,128)(2,1)S(1)} %get-tuple-element.778.refs_2_.refs_4_, ...), custom_call_target="tpu_custom_call" | custom-call | flops 999999995904 | bytes 1 | tf_op jit(solution)/shard_map/qkv_in/pallas_call | solution.py:93
  673.2 19.5 %head_grad.3 = (bf16[2,512,2048]{2,1,0:T(8,128)(2,1)}, f32[8,128]{1,0:T(8,128)S(1)}) custom-call(s32[6]{0:T(128)S(1)} %copy-done.24, bf16[1024,2048]{1,0:T(8,128)(2,1)} %get-tuple-element.420.refs_0_.refs_1_.refs_2_.refs_3_.refs_4_, bf16[1024,2048]{1,0:T(8,128)(2,1)} %get-tuple-element.420.refs_0_.refs_1_.refs_2_.refs_3_.refs_4_, ...), custom_call_target="tpu_custom_call" | custom-call | flops 999999995904 | bytes 1 | tf_op jit(solution)/shard_map/head_grad/pallas_call | solution.py:93
  692.7 7.3 collective-permute-done.53
  707.1 13.4 %down.2 = (bf16[512,2048]{1,0:T(8,128)(2,1)}, bf16[512,2048]{1,0:T(8,128)(2,1)S(1)}, f32[8,128]{1,0:T(8,128)S(1)}) custom-call(s32[6]{0:T(128)S(1)} %copy-done.24, bf16[1024,1024]{1,0:T(8,128)(2,1)} %copy-done.42, bf16[1024,1024]{1,0:T(8,128)(2,1)} %copy-done.43, bf16[1024,1024]{1,0:T(8,128)(2,1)} %copy-done.42, bf16[1024,1024]{1,0:T(8,128)(2,1)} %copy-done.43, ...), custom_call_target="tpu_custom_call" | custom-call | flops 999999995904 | bytes 1 | tf_op jit(solution)/shard_map/down/pallas_call | solution.py:93
  725.8 6.4 all_to_all.36
  732.9 7.9 input_back.1
  761.7 13.0 %down.3 = (bf16[512,2048]{1,0:T(8,128)(2,1)}, bf16[512,2048]{1,0:T(8,128)(2,1)S(1)}, f32[8,128]{1,0:T(8,128)S(1)}) custom-call(s32[6]{0:T(128)S(1)} %copy-done.25, bf16[1024,1024]{1,0:T(8,128)(2,1)} %copy-done.38, bf16[1024,1024]{1,0:T(8,128)(2,1)} %copy-done.39, bf16[1024,1024]{1,0:T(8,128)(2,1)} %copy-done.38, bf16[1024,1024]{1,0:T(8,128)(2,1)} %copy-done.39, ...), custom_call_target="tpu_custom_call" | custom-call | flops 999999995904 | bytes 1 | tf_op jit(solution)/shard_map/down/pallas_call | solution.py:93
  790.3 11.6 %collective-permute-done.71 = bf16[512,1024]{1,0:T(8,128)(2,1)} collective-permute-done((bf16[512,1024]{1,0:T(8,128)(2,1)}, bf16[512,1024]{1,0:T(8,128)(2,1)}, u32[]{:S(2)}, u32[]{:S(2)}) %collective-permute-start.71) | collective-permute-done | bytes 1048608 | tf_op jit(solution)/shard_map/ppermute | solution.py:582
  815.8 30.3 %collective-permute-done.68.refs_3_ = bf16[2,256,2048]{2,1,0:T(8,128)(2,1)} collective-permute-done((bf16[2,256,2048]{2,1,0:T(8,128)(2,1)}, bf16[2,256,2048]{2,1,0:T(8,128)(2,1)}, u32[]{:S(2)}, u32[]{:S(2)}) %collective-permute-start.68) | collective-permute-done | bytes 2097184 | tf_op jit(solution)/shard_map/ppermute | solution.py:603
  847.0 10.2 %finish.3 = (f32[1024,2048]{1,0:T(8,128)}, f32[1024,2048]{1,0:T(8,128)}, f32[8,128]{1,0:T(8,128)S(1)}) custom-call(s32[6]{0:T(128)S(1)} %copy-done.26, bf16[2,256,2048]{2,1,0:T(8,128)(2,1)} %bitcast.16.refs_1_, bf16[2,256,2048]{2,1,0:T(8,128)(2,1)} %collective-permute-done.55.refs_2_, bf16[2,256,2048]{2,1,0:T(8,128)(2,1)} %collective-permute-done.68.refs_3_, ...), custom_call_target="tpu_custom_call" | custom-call | flops 999999995904 | bytes 1 | tf_op jit(solution)/shard_map/finish/pallas_call | solution.py:93
  869.6 6.7 finish.4
  882.7 11.2 %collective-permute-done.81.refs_4_ = bf16[2,256,1024]{2,1,0:T(8,128)(2,1)} collective-permute-done((bf16[2,256,1024]{2,1,0:T(8,128)(2,1)}, bf16[2,256,1024]{2,1,0:T(8,128)(2,1)}, u32[]{:S(2)}, u32[]{:S(2)}) %collective-permute-start.81) | collective-permute-done | bytes 1048608 | tf_op jit(solution)/shard_map/ppermute | solution.py:603
  893.9 6.5 finish.5
  (429 shorter events, 306.1 us)
Async XLA Ops:
  0.6 32.6 %collective-permute-start = (bf16[1024,1024]{1,0:T(8,128)(2,1)}, bf16[1024,1024]{1,0:T(8,128)(2,1)}, u32[]{:S(2)}, u32[]{:S(2)}) collective-permute-start(bf16[1024,1024]{1,0:T(8,128)(2,1)} %refs_1_.16), channel_id=1, source_target_pairs={{0,4},{4,0},{1,5},{5,1},{2,6},{6,2},{3,7},{7,3},{8,12},{12,8},{9,1... | collective-permute-start | bytes 6291464 | tf_op jit(solution)/shard_map/ppermute | solution.py:582
  1.2 71.7 %collective-permute-start.6 = (bf16[1024,1024]{1,0:T(8,128)(2,1)}, bf16[1024,1024]{1,0:T(8,128)(2,1)}, u32[]{:S(2)}, u32[]{:S(2)}) collective-permute-start(bf16[1024,1024]{1,0:T(8,128)(2,1)} %refs_1_.16), channel_id=1, source_target_pairs={{0,1},{1,0},{2,3},{3,2},{4,5},{5,4},{6,7},{7,6},{8,9},{9,8},{10,11... | collective-permute-start | bytes 6291464 | tf_op jit(solution)/shard_map/ppermute | solution.py:582
  5.1 15.6 %collective-permute-start.3 = (f32[2,1024]{1,0:T(2,128)}, f32[2,1024]{1,0:T(2,128)}, u32[]{:S(2)}, u32[]{:S(2)}) collective-permute-start(f32[2,1024]{1,0:T(2,128)} %pad_maximum_fusion.6), channel_id=1, source_target_pairs={{0,4},{4,0},{1,5},{5,1},{2,6},{6,2},{3,7},{7,3},{8,12},{12,8},{9,1... | collective-permute-start | bytes 24584 | tf_op jit(solution)/shard_map/ppermute | solution.py:582
  22.1 56.6 %collective-permute-start.7 = (bf16[512,1024]{1,0:T(8,128)(2,1)}, bf16[512,1024]{1,0:T(8,128)(2,1)}, u32[]{:S(2)}, u32[]{:S(2)}) collective-permute-start(bf16[512,1024]{1,0:T(8,128)(2,1)} %get-tuple-element.421), channel_id=1, source_target_pairs={{0,2},{1,3},{2,0},{3,1},{4,6},{5,7},{6,4},{7,5},{8,10},{9,11},{10,... | collective-permute-start | bytes 3145736 | tf_op jit(solution)/shard_map/ppermute | solution.py:582
  32.6 18.3 %collective-permute-start.5 = (bf16[1024,1024]{1,0:T(8,128)(2,1)}, bf16[1024,1024]{1,0:T(8,128)(2,1)}, u32[]{:S(2)}, u32[]{:S(2)}) collective-permute-start(bf16[1024,1024]{1,0:T(8,128)(2,1)} %get-tuple-element.408), channel_id=1, source_target_pairs={{0,4},{4,0},{1,5},{5,1},{2,6},{6,2},{3,7},{7,3},{8,12},{12,8},{9,1... | collective-permute-start | bytes 6291464 | tf_op jit(solution)/shard_map/ppermute | solution.py:582
  78.7 33.5 %collective-permute-start.9 = (bf16[512,1024]{1,0:T(8,128)(2,1)}, bf16[512,1024]{1,0:T(8,128)(2,1)}, u32[]{:S(2)}, u32[]{:S(2)}) collective-permute-start(bf16[512,1024]{1,0:T(8,128)(2,1)} %collective-permute-done.7.refs_1_), channel_id=1, source_target_pairs={{0,16},{4,12},{8,24},{12,4},{16,0},{20,28},{24,8},{28,20},{1,17},{... | collective-permute-start | bytes 3145736 | tf_op jit(solution)/shard_map/ppermute | solution.py:603
  80.5 24.2 %collective-permute-start.8 = (bf16[512,1024]{1,0:T(8,128)(2,1)}, bf16[512,1024]{1,0:T(8,128)(2,1)}, u32[]{:S(2)}, u32[]{:S(2)}) collective-permute-start(bf16[512,1024]{1,0:T(8,128)(2,1)} %collective-permute-done.7.refs_1_), channel_id=1, source_target_pairs={{0,8},{4,20},{8,0},{12,28},{16,24},{20,4},{24,16},{28,12},{1,9},{5... | collective-permute-start | bytes 3145736 | tf_op jit(solution)/shard_map/ppermute | solution.py:603
  81.9 71.6 %collective-permute-start.12 = (bf16[384,2048]{1,0:T(8,128)(2,1)}, bf16[384,2048]{1,0:T(8,128)(2,1)}, u32[]{:S(2)}, u32[]{:S(2)}) collective-permute-start(bf16[384,2048]{1,0:T(8,128)(2,1)} %get-tuple-element.456), channel_id=1, source_target_pairs={{0,2},{1,3},{2,0},{3,1},{4,6},{5,7},{6,4},{7,5},{8,10},{9,11},{10,... | collective-permute-start | bytes 4718600 | tf_op jit(solution)/shard_map/ppermute | solution.py:582
  83.6 115.6 %collective-permute-start.20 = (bf16[1024,1024]{1,0:T(8,128)(2,1)}, bf16[1024,1024]{1,0:T(8,128)(2,1)}, u32[]{:S(2)}, u32[]{:S(2)}) collective-permute-start(bf16[1024,1024]{1,0:T(8,128)(2,1)} %refs_1_.19), channel_id=1, source_target_pairs={{0,1},{1,0},{2,3},{3,2},{4,5},{5,4},{6,7},{7,6},{8,9},{9,8},{10,11... | collective-permute-start | bytes 6291464 | tf_op jit(solution)/shard_map/ppermute | solution.py:582
  153.5 89.7 %collective-permute-start.16 = (bf16[512,2048]{1,0:T(8,128)(2,1)}, bf16[512,2048]{1,0:T(8,128)(2,1)}, u32[]{:S(2)}, u32[]{:S(2)}) collective-permute-start(bf16[512,2048]{1,0:T(8,128)(2,1)} %add_convert_fusion.7), channel_id=1, source_target_pairs={{0,1},{1,0},{2,3},{3,2},{4,5},{5,4},{6,7},{7,6},{8,9},{9,8},{10,11... | collective-permute-start | bytes 6291464 | tf_op jit(solution)/shard_map/ppermute | solution.py:582
  154.1 96.3 %collective-permute-start.24 = (bf16[384,2048]{1,0:T(8,128)(2,1)}, bf16[384,2048]{1,0:T(8,128)(2,1)}, u32[]{:S(2)}, u32[]{:S(2)}) collective-permute-start(bf16[384,2048]{1,0:T(8,128)(2,1)} %get-tuple-element.493), channel_id=1, source_target_pairs={{0,2},{1,3},{2,0},{3,1},{4,6},{5,7},{6,4},{7,5},{8,10},{9,11},{10,... | collective-permute-start | bytes 4718600 | tf_op jit(solution)/shard_map/ppermute | solution.py:582
  157.9 20.7 %collective-permute-start.17 = (bf16[384,2048]{1,0:T(8,128)(2,1)}, bf16[384,2048]{1,0:T(8,128)(2,1)}, u32[]{:S(2)}, u32[]{:S(2)}) collective-permute-start(bf16[384,2048]{1,0:T(8,128)(2,1)} %collective-permute-done.12.refs_1_), channel_id=1, source_target_pairs={{0,8},{4,20},{8,0},{12,28},{16,24},{20,4},{24,16},{28,12},{1,9},{5... | collective-permute-start | bytes 4718600 | tf_op jit(solution)/shard_map/ppermute | solution.py:603
  159.4 20.8 %collective-permute-start.21 = (bf16[1024,1024]{1,0:T(8,128)(2,1)}, bf16[1024,1024]{1,0:T(8,128)(2,1)}, u32[]{:S(2)}, u32[]{:S(2)}) collective-permute-start(bf16[1024,1024]{1,0:T(8,128)(2,1)} %refs_1_.19), channel_id=1, source_target_pairs={{0,4},{4,0},{1,5},{5,1},{2,6},{6,2},{3,7},{7,3},{8,12},{12,8},{9,1... | collective-permute-start | bytes 6291464 | tf_op jit(solution)/shard_map/ppermute | solution.py:582
  178.6 29.8 %collective-permute-start.18 = (bf16[384,2048]{1,0:T(8,128)(2,1)}, bf16[384,2048]{1,0:T(8,128)(2,1)}, u32[]{:S(2)}, u32[]{:S(2)}) collective-permute-start(bf16[384,2048]{1,0:T(8,128)(2,1)} %collective-permute-done.12.refs_1_), channel_id=1, source_target_pairs={{0,16},{4,12},{8,24},{12,4},{16,0},{20,28},{24,8},{28,20},{1,17},{... | collective-permute-start | bytes 4718600 | tf_op jit(solution)/shard_map/ppermute | solution.py:603
  180.2 63.0 %collective-permute-start.15 = (bf16[512,2048]{1,0:T(8,128)(2,1)}, bf16[512,2048]{1,0:T(8,128)(2,1)}, u32[]{:S(2)}, u32[]{:S(2)}) collective-permute-start(bf16[512,2048]{1,0:T(8,128)(2,1)} %get-tuple-element.477), channel_id=1, source_target_pairs={{0,4},{4,0},{1,5},{5,1},{2,6},{6,2},{3,7},{7,3},{8,12},{12,8},{9,1... | collective-permute-start | bytes 6291464 | tf_op jit(solution)/shard_map/ppermute | solution.py:582
  203.8 20.7 %collective-permute-start.19 = (bf16[384,2048]{1,0:T(8,128)(2,1)}, bf16[384,2048]{1,0:T(8,128)(2,1)}, u32[]{:S(2)}, u32[]{:S(2)}) collective-permute-start(bf16[384,2048]{1,0:T(8,128)(2,1)} %collective-permute-done.17.refs_2_), channel_id=1, source_target_pairs={{0,16},{4,12},{8,24},{12,4},{16,0},{20,28},{24,8},{28,20},{1,17},{... | collective-permute-start | bytes 4718600 | tf_op jit(solution)/shard_map/ppermute | solution.py:603
  249.3 46.9 %collective-permute-start.28 = (bf16[512,2048]{1,0:T(8,128)(2,1)}, bf16[512,2048]{1,0:T(8,128)(2,1)}, u32[]{:S(2)}, u32[]{:S(2)}) collective-permute-start(bf16[512,2048]{1,0:T(8,128)(2,1)} %get-tuple-element.492.refs_1_), channel_id=1, source_target_pairs={{0,1},{1,0},{2,3},{3,2},{4,5},{5,4},{6,7},{7,6},{8,9},{9,8},{10,11... | collective-permute-start | bytes 6291464 | tf_op jit(solution)/shard_map/ppermute | solution.py:582
  253.8 72.3 %collective-permute-start.27 = (bf16[384,2048]{1,0:T(8,128)(2,1)}, bf16[384,2048]{1,0:T(8,128)(2,1)}, u32[]{:S(2)}, u32[]{:S(2)}) collective-permute-start(bf16[384,2048]{1,0:T(8,128)(2,1)} %collective-permute-done.24.refs_1_), channel_id=1, source_target_pairs={{0,16},{4,12},{8,24},{12,4},{16,0},{20,28},{24,8},{28,20},{1,17},{... | collective-permute-start | bytes 4718600 | tf_op jit(solution)/shard_map/ppermute | solution.py:603
  254.3 41.9 %collective-permute-start.26 = (bf16[384,2048]{1,0:T(8,128)(2,1)}, bf16[384,2048]{1,0:T(8,128)(2,1)}, u32[]{:S(2)}, u32[]{:S(2)}) collective-permute-start(bf16[384,2048]{1,0:T(8,128)(2,1)} %collective-permute-done.24.refs_1_), channel_id=1, source_target_pairs={{0,8},{4,20},{8,0},{12,28},{16,24},{20,4},{24,16},{28,12},{1,9},{5... | collective-permute-start | bytes 4718600 | tf_op jit(solution)/shard_map/ppermute | solution.py:603
  296.8 29.3 %collective-permute-start.29 = (bf16[384,2048]{1,0:T(8,128)(2,1)}, bf16[384,2048]{1,0:T(8,128)(2,1)}, u32[]{:S(2)}, u32[]{:S(2)}) collective-permute-start(bf16[384,2048]{1,0:T(8,128)(2,1)} %collective-permute-done.26.refs_2_), channel_id=1, source_target_pairs={{0,16},{4,12},{8,24},{12,4},{16,0},{20,28},{24,8},{28,20},{1,17},{... | collective-permute-start | bytes 4718600 | tf_op jit(solution)/shard_map/ppermute | solution.py:603
  399.9 102.0 %collective-permute-start.34 = (bf16[2,512,4096]{2,1,0:T(8,128)(2,1)}, bf16[2,512,4096]{2,1,0:T(8,128)(2,1)}, u32[]{:S(2)}, u32[]{:S(2)}) collective-permute-start(bf16[2,512,4096]{2,1,0:T(8,128)(2,1)} %get-tuple-element.546), channel_id=1, source_target_pairs={{0,8},{4,20},{8,0},{12,28},{16,24},{20,4},{24,16},{28,12},{1,9},{5... | collective-permute-start | bytes 25165832 | tf_op jit(solution)/shard_map/ppermute | solution.py:603
  433.3 50.2 %collective-permute-start.36 = (bf16[512,2048]{1,0:T(8,128)(2,1)}, bf16[512,2048]{1,0:T(8,128)(2,1)}, u32[]{:S(2)}, u32[]{:S(2)}) collective-permute-start(bf16[512,2048]{1,0:T(8,128)(2,1)} %add_convert_fusion.6), channel_id=1, source_target_pairs={{0,1},{1,0},{2,3},{3,2},{4,5},{5,4},{6,7},{7,6},{8,9},{9,8},{10,11... | collective-permute-start | bytes 6291464 | tf_op jit(solution)/shard_map/ppermute | solution.py:582
  458.0 25.5 %collective-permute-start.35 = (bf16[512,2048]{1,0:T(8,128)(2,1)}, bf16[512,2048]{1,0:T(8,128)(2,1)}, u32[]{:S(2)}, u32[]{:S(2)}) collective-permute-start(bf16[512,2048]{1,0:T(8,128)(2,1)} %get-tuple-element.548), channel_id=1, source_target_pairs={{0,4},{4,0},{1,5},{5,1},{2,6},{6,2},{3,7},{7,3},{8,12},{12,8},{9,1... | collective-permute-start | bytes 6291464 | tf_op jit(solution)/shard_map/ppermute | solution.py:582
  492.0 48.2 %collective-permute-start.40 = (bf16[512,2048]{1,0:T(8,128)(2,1)}, bf16[512,2048]{1,0:T(8,128)(2,1)}, u32[]{:S(2)}, u32[]{:S(2)}) collective-permute-start(bf16[512,2048]{1,0:T(8,128)(2,1)} %get-tuple-element.552.refs_1_), channel_id=1, source_target_pairs={{0,1},{1,0},{2,3},{3,2},{4,5},{5,4},{6,7},{7,6},{8,9},{9,8},{10,11... | collective-permute-start | bytes 6291464 | tf_op jit(solution)/shard_map/ppermute | solution.py:582
  508.2 49.4 %collective-permute-start.39 = (bf16[512,4096]{1,0:T(8,128)(2,1)}, bf16[512,4096]{1,0:T(8,128)(2,1)}, u32[]{:S(2)}, u32[]{:S(2)}) collective-permute-start(bf16[512,4096]{1,0:T(8,128)(2,1)} %fusion), channel_id=1, source_target_pairs={{0,16},{4,12},{8,24},{12,4},{16,0},{20,28},{24,8},{28,20},{1,17},{... | collective-permute-start | bytes 12582920 | tf_op jit(solution)/shard_map/ppermute | solution.py:603
  540.1 43.5 %collective-permute-start.43 = (bf16[512,2048]{1,0:T(8,128)(2,1)}, bf16[512,2048]{1,0:T(8,128)(2,1)}, u32[]{:S(2)}, u32[]{:S(2)}) collective-permute-start(bf16[512,2048]{1,0:T(8,128)(2,1)} %collective-permute-done.40.refs_1_), channel_id=1, source_target_pairs={{0,4},{4,0},{1,5},{5,1},{2,6},{6,2},{3,7},{7,3},{8,12},{12,8},{9,1... | collective-permute-start | bytes 6291464 | tf_op jit(solution)/shard_map/ppermute | solution.py:582
  556.0 56.6 %collective-permute-start.46 = (bf16[2,512,2048]{2,1,0:T(8,128)(2,1)}, bf16[2,512,2048]{2,1,0:T(8,128)(2,1)}, u32[]{:S(2)}, u32[]{:S(2)}) collective-permute-start(bf16[2,512,2048]{2,1,0:T(8,128)(2,1)} %get-tuple-element.615), channel_id=1, source_target_pairs={{0,8},{4,20},{8,0},{12,28},{16,24},{20,4},{24,16},{28,12},{1,9},{5... | collective-permute-start | bytes 12582920 | tf_op jit(solution)/shard_map/ppermute | solution.py:603
  563.8 156.8 %collective-permute-start.42 = (bf16[512,2048]{1,0:T(8,128)(2,1)}, bf16[512,2048]{1,0:T(8,128)(2,1)}, u32[]{:S(2)}, u32[]{:S(2)}) collective-permute-start(bf16[512,2048]{1,0:T(8,128)(2,1)} %fusion.1), channel_id=1, source_target_pairs={{0,2},{1,3},{2,0},{3,1},{4,6},{5,7},{6,4},{7,5},{8,10},{9,11},{10,... | collective-permute-start | bytes 6291464 | tf_op jit(solution)/shard_map/ppermute | solution.py:582
  618.7 49.1 %collective-permute-start.51 = (bf16[512,2048]{1,0:T(8,128)(2,1)}, bf16[512,2048]{1,0:T(8,128)(2,1)}, u32[]{:S(2)}, u32[]{:S(2)}) collective-permute-start(bf16[512,2048]{1,0:T(8,128)(2,1)} %fusion.4), channel_id=1, source_target_pairs={{0,16},{4,12},{8,24},{12,4},{16,0},{20,28},{24,8},{28,20},{1,17},{... | collective-permute-start | bytes 6291464 | tf_op jit(solution)/shard_map/ppermute | solution.py:603
  630.3 22.2 %collective-permute-start.48 = (bf16[512,2048]{1,0:T(8,128)(2,1)}, bf16[512,2048]{1,0:T(8,128)(2,1)}, u32[]{:S(2)}, u32[]{:S(2)}) collective-permute-start(bf16[512,2048]{1,0:T(8,128)(2,1)} %get-tuple-element.621), channel_id=1, source_target_pairs={{0,4},{4,0},{1,5},{5,1},{2,6},{6,2},{3,7},{7,3},{8,12},{12,8},{9,1... | collective-permute-start | bytes 6291464 | tf_op jit(solution)/shard_map/ppermute | solution.py:582
  651.2 48.9 %collective-permute-start.53 = (bf16[2,512,2048]{2,1,0:T(8,128)(2,1)}, bf16[2,512,2048]{2,1,0:T(8,128)(2,1)}, u32[]{:S(2)}, u32[]{:S(2)}) collective-permute-start(bf16[2,512,2048]{2,1,0:T(8,128)(2,1)} %get-tuple-element.646), channel_id=1, source_target_pairs={{0,8},{4,20},{8,0},{12,28},{16,24},{20,4},{24,16},{28,12},{1,9},{5... | collective-permute-start | bytes 12582920 | tf_op jit(solution)/shard_map/ppermute | solution.py:603
  656.2 76.7 %collective-permute-start.57 = (bf16[512,2048]{1,0:T(8,128)(2,1)}, bf16[512,2048]{1,0:T(8,128)(2,1)}, u32[]{:S(2)}, u32[]{:S(2)}) collective-permute-start(bf16[512,2048]{1,0:T(8,128)(2,1)} %add_convert_fusion.4), channel_id=1, source_target_pairs={{0,1},{1,0},{2,3},{3,2},{4,5},{5,4},{6,7},{7,6},{8,9},{9,8},{10,11... | collective-permute-start | bytes 6291464 | tf_op jit(solution)/shard_map/ppermute | solution.py:582
  672.1 105.0 %collective-permute-start.65 = (bf16[512,1024]{1,0:T(8,128)(2,1)}, bf16[512,1024]{1,0:T(8,128)(2,1)}, u32[]{:S(2)}, u32[]{:S(2)}) collective-permute-start(bf16[512,1024]{1,0:T(8,128)(2,1)} %fusion.11), channel_id=1, source_target_pairs={{0,2},{1,3},{2,0},{3,1},{4,6},{5,7},{6,4},{7,5},{8,10},{9,11},{10,... | collective-permute-start | bytes 3145736 | tf_op jit(solution)/shard_map/ppermute | solution.py:582
  673.2 59.7 %collective-permute-start.56 = (bf16[512,2048]{1,0:T(8,128)(2,1)}, bf16[512,2048]{1,0:T(8,128)(2,1)}, u32[]{:S(2)}, u32[]{:S(2)}) collective-permute-start(bf16[512,2048]{1,0:T(8,128)(2,1)} %get-tuple-element.659), channel_id=1, source_target_pairs={{0,4},{4,0},{1,5},{5,1},{2,6},{6,2},{3,7},{7,3},{8,12},{12,8},{9,1... | collective-permute-start | bytes 6291464 | tf_op jit(solution)/shard_map/ppermute | solution.py:582
  706.0 37.4 %collective-permute-start.60 = (bf16[512,2048]{1,0:T(8,128)(2,1)}, bf16[512,2048]{1,0:T(8,128)(2,1)}, u32[]{:S(2)}, u32[]{:S(2)}) collective-permute-start(bf16[512,2048]{1,0:T(8,128)(2,1)} %fusion.5), channel_id=1, source_target_pairs={{0,16},{4,12},{8,24},{12,4},{16,0},{20,28},{24,8},{28,20},{1,17},{... | collective-permute-start | bytes 6291464 | tf_op jit(solution)/shard_map/ppermute | solution.py:603
  732.2 28.2 %collective-permute-start.55 = (bf16[2,256,2048]{2,1,0:T(8,128)(2,1)}, bf16[2,256,2048]{2,1,0:T(8,128)(2,1)}, u32[]{:S(2)}, u32[]{:S(2)}) collective-permute-start(bf16[2,256,2048]{2,1,0:T(8,128)(2,1)} %bitcast.16.refs_1_), channel_id=1, source_target_pairs={{0,8},{4,20},{8,0},{12,28},{16,24},{20,4},{24,16},{28,12},{1,9},{5... | collective-permute-start | bytes 6291464 | tf_op jit(solution)/shard_map/ppermute | solution.py:603
  742.8 16.2 %collective-permute-start.63 = (f32[2,2048]{1,0:T(2,128)}, f32[2,2048]{1,0:T(2,128)}, u32[]{:S(2)}, u32[]{:S(2)}) collective-permute-start(f32[2,2048]{1,0:T(2,128)} %pad_maximum_fusion.5), channel_id=1, source_target_pairs={{0,4},{4,0},{1,5},{5,1},{2,6},{6,2},{3,7},{7,3},{8,12},{12,8},{9,1... | collective-permute-start | bytes 49160 | tf_op jit(solution)/shard_map/ppermute | solution.py:582
  752.7 49.2 %collective-permute-start.71 = (bf16[512,1024]{1,0:T(8,128)(2,1)}, bf16[512,1024]{1,0:T(8,128)(2,1)}, u32[]{:S(2)}, u32[]{:S(2)}) collective-permute-start(bf16[512,1024]{1,0:T(8,128)(2,1)} %fusion.10), channel_id=1, source_target_pairs={{0,2},{1,3},{2,0},{3,1},{4,6},{5,7},{6,4},{7,5},{8,10},{9,11},{10,... | collective-permute-start | bytes 3145736 | tf_op jit(solution)/shard_map/ppermute | solution.py:582
  753.4 105.9 %collective-permute-start.67 = (bf16[512,2048]{1,0:T(8,128)(2,1)}, bf16[512,2048]{1,0:T(8,128)(2,1)}, u32[]{:S(2)}, u32[]{:S(2)}) collective-permute-start(bf16[512,2048]{1,0:T(8,128)(2,1)} %add_convert_fusion.2), channel_id=1, source_target_pairs={{0,1},{1,0},{2,3},{3,2},{4,5},{5,4},{6,7},{7,6},{8,9},{9,8},{10,11... | collective-permute-start | bytes 6291464 | tf_op jit(solution)/shard_map/ppermute | solution.py:582
  774.7 39.7 %collective-permute-start.69 = (bf16[2,256,2048]{2,1,0:T(8,128)(2,1)}, bf16[2,256,2048]{2,1,0:T(8,128)(2,1)}, u32[]{:S(2)}, u32[]{:S(2)}) collective-permute-start(bf16[2,256,2048]{2,1,0:T(8,128)(2,1)} %collective-permute-done.55.refs_2_), channel_id=1, source_target_pairs={{0,16},{4,12},{8,24},{12,4},{16,0},{20,28},{24,8},{28,20},{1,17},{... | collective-permute-start | bytes 6291464 | tf_op jit(solution)/shard_map/ppermute | solution.py:603
  777.0 69.1 %collective-permute-start.68 = (bf16[2,256,2048]{2,1,0:T(8,128)(2,1)}, bf16[2,256,2048]{2,1,0:T(8,128)(2,1)}, u32[]{:S(2)}, u32[]{:S(2)}) collective-permute-start(bf16[2,256,2048]{2,1,0:T(8,128)(2,1)} %bitcast.16.refs_1_), channel_id=1, source_target_pairs={{0,16},{4,12},{8,24},{12,4},{16,0},{20,28},{24,8},{28,20},{1,17},{... | collective-permute-start | bytes 6291464 | tf_op jit(solution)/shard_map/ppermute | solution.py:603
  787.2 26.5 %collective-permute-start.70 = (bf16[2,256,1024]{2,1,0:T(8,128)(2,1)}, bf16[2,256,1024]{2,1,0:T(8,128)(2,1)}, u32[]{:S(2)}, u32[]{:S(2)}) collective-permute-start(bf16[2,256,1024]{2,1,0:T(8,128)(2,1)} %bitcast.23.refs_1_), channel_id=1, source_target_pairs={{0,8},{4,20},{8,0},{12,28},{16,24},{20,4},{24,16},{28,12},{1,9},{5... | collective-permute-start | bytes 3145736 | tf_op jit(solution)/shard_map/ppermute | solution.py:603
  811.9 45.3 %collective-permute-start.73 = (f32[2,2048]{1,0:T(2,128)}, f32[2,2048]{1,0:T(2,128)}, u32[]{:S(2)}, u32[]{:S(2)}) collective-permute-start(f32[2,2048]{1,0:T(2,128)} %add.154), channel_id=1, source_target_pairs={{0,16},{4,12},{8,24},{12,4},{16,0},{20,28},{24,8},{28,20},{1,17},{... | collective-permute-start | bytes 49160 | tf_op jit(solution)/shard_map/ppermute | solution.py:603
  813.7 53.9 %collective-permute-start.77 = (bf16[2,256,1024]{2,1,0:T(8,128)(2,1)}, bf16[2,256,1024]{2,1,0:T(8,128)(2,1)}, u32[]{:S(2)}, u32[]{:S(2)}) collective-permute-start(bf16[2,256,1024]{2,1,0:T(8,128)(2,1)} %bitcast.27.refs_1_), channel_id=1, source_target_pairs={{0,8},{4,20},{8,0},{12,28},{16,24},{20,4},{24,16},{28,12},{1,9},{5... | collective-permute-start | bytes 3145736 | tf_op jit(solution)/shard_map/ppermute | solution.py:603
  814.4 54.3 %collective-permute-start.76 = (bf16[2,256,1024]{2,1,0:T(8,128)(2,1)}, bf16[2,256,1024]{2,1,0:T(8,128)(2,1)}, u32[]{:S(2)}, u32[]{:S(2)}) collective-permute-start(bf16[2,256,1024]{2,1,0:T(8,128)(2,1)} %collective-permute-done.70.refs_2_), channel_id=1, source_target_pairs={{0,16},{4,12},{8,24},{12,4},{16,0},{20,28},{24,8},{28,20},{1,17},{... | collective-permute-start | bytes 3145736 | tf_op jit(solution)/shard_map/ppermute | solution.py:603
  846.1 23.5 %collective-permute-start.75 = (bf16[2,256,1024]{2,1,0:T(8,128)(2,1)}, bf16[2,256,1024]{2,1,0:T(8,128)(2,1)}, u32[]{:S(2)}, u32[]{:S(2)}) collective-permute-start(bf16[2,256,1024]{2,1,0:T(8,128)(2,1)} %bitcast.23.refs_1_), channel_id=1, source_target_pairs={{0,16},{4,12},{8,24},{12,4},{16,0},{20,28},{24,8},{28,20},{1,17},{... | collective-permute-start | bytes 3145736 | tf_op jit(solution)/shard_map/ppermute | solution.py:603
  867.5 15.1 %collective-permute-start.80 = (bf16[2,256,1024]{2,1,0:T(8,128)(2,1)}, bf16[2,256,1024]{2,1,0:T(8,128)(2,1)}, u32[]{:S(2)}, u32[]{:S(2)}) collective-permute-start(bf16[2,256,1024]{2,1,0:T(8,128)(2,1)} %bitcast.27.refs_1_), channel_id=1, source_target_pairs={{0,16},{4,12},{8,24},{12,4},{16,0},{20,28},{24,8},{28,20},{1,17},{... | collective-permute-start | bytes 3145736 | tf_op jit(solution)/shard_map/ppermute | solution.py:603
  868.7 25.2 %collective-permute-start.81 = (bf16[2,256,1024]{2,1,0:T(8,128)(2,1)}, bf16[2,256,1024]{2,1,0:T(8,128)(2,1)}, u32[]{:S(2)}, u32[]{:S(2)}) collective-permute-start(bf16[2,256,1024]{2,1,0:T(8,128)(2,1)} %collective-permute-done.77.refs_2_), channel_id=1, source_target_pairs={{0,16},{4,12},{8,24},{12,4},{16,0},{20,28},{24,8},{28,20},{1,17},{... | collective-permute-start | bytes 3145736 | tf_op jit(solution)/shard_map/ppermute | solution.py:603
  (128 other events, 2036.1 us)
